TPU v7x, 32 devices: a whole 2x2x4 slice. The times are simulated.
32 devices in a mesh: img: 8 (over z, y), rows: 4 (over x, core).
Axes of the slice: x: 2, y: 2, z: 4, core: 2. Of those that a mesh axis runs over, the one named last changes fastest.
Arguments:
- features: bfloat16 [128, 8, 8, 2048], P('img', 'rows'), may hold values from -6 to 6
- weight_in: bfloat16 [2048, 512], replicated, may hold values from -0.125 to 0.125
- gain_in: float32 [512], replicated, may hold values from 0.5 to 1.5
- bias_in: float32 [512], replicated, may hold values from -0.5 to 0.5
- weight_mid: bfloat16 [3, 3, 512, 512], replicated, may hold values from -0.09375 to 0.09375
- gain_mid: float32 [512], replicated, may hold values from 0.5 to 1.5
- bias_mid: float32 [512], replicated, may hold values from -0.5 to 0.5
- weight_out: bfloat16 [512, 2048], replicated, may hold values from -0.25 to 0.25
- gain_out: float32 [2048], replicated, may hold values from 0.5 to 1.5
- bias_out: float32 [2048], replicated, may hold values from -0.5 to 0.5
- map_size: int32 [128], P('img'), may hold values from 5 to 7
- out_grad: bfloat16 [128, 8, 8, 2048], P('img', 'rows'), may hold values from -6 to 6
- pool_grad: float32 [128, 2048], P('img'), may hold values from -24 to 24
Outputs:
- block_out: bfloat16 [128, 8, 8, 2048], P('img', 'rows')
- pooled: float32 [128, 2048], P('img')
- grad_features: float32 [128, 8, 8, 2048], P('img', 'rows')
- grad_weight_in: float32 [2048, 512], replicated
- grad_gain_in: float32 [512], replicated
- grad_bias_in: float32 [512], replicated
- grad_weight_mid: float32 [3, 3, 512, 512], replicated
- grad_gain_mid: float32 [512], replicated
- grad_bias_mid: float32 [512], replicated
- grad_weight_out: float32 [512, 2048], replicated
- grad_gain_out: float32 [2048], replicated
- grad_bias_out: float32 [2048], replicated
Inputs may be any that keep to these rules, and one draw needn't show every extreme that they name: Each image's map fills the first map_size rows and columns of its 8 x 8 array; the rest is padding.
All inputs are finite; a program needn't handle non-finite values.
Results may differ from a plain program's by a relative error of at most 0.008.
Values may be sent and summed in bfloat16 or wider, within the bound.
No kernel may reach another device: no remote copies, remote signals or barrier semaphores. Data moves between devices by JAX's collectives and lax.ppermute only.
A program may use at most 128 MiB of HBM per device.

v0:
```python
import jax
import jax.numpy as jnp
from jax import lax
from jax.sharding import PartitionSpec as P

EPSILON = 1e-05


def with_halo(block, sides, width):
    for axis, dim in sides:
        count = lax.axis_size(axis)
        forward = [(i, i + 1) for i in range(count - 1)]
        backward = [(target, source) for source, target in forward]
        low = lax.ppermute(
            lax.slice_in_dim(block, block.shape[dim] - width, None, axis=dim), axis, forward
        )
        high = lax.ppermute(lax.slice_in_dim(block, 0, width, axis=dim), axis, backward)
        block = jnp.concatenate([low, block, high], axis=dim)
    return block


def flatten(tensor):
    return tensor.reshape(-1, tensor.shape[-1])


def widen(tensor):
    return jnp.pad(tensor, ((0, 0), (0, 0), (1, 1), (0, 0)))


def patches(padded, height, width):
    pieces = []
    for row_off in range(3):
        for col_off in range(3):
            pieces.append(padded[:, row_off : row_off + height, col_off : col_off + width, :])
    return jnp.concatenate(pieces, axis=3)


def contract(left, right):
    return lax.dot_general(
        flatten(left), flatten(right), (((0,), (0,)), ((), ())), preferred_element_type=jnp.float32
    )


def times_transpose(left, weights):
    return lax.dot_general(
        flatten(left), weights, (((1,), (1,)), ((), ())), preferred_element_type=jnp.float32
    )


def smooth(values):
    return jax.nn.silu(values)


def smooth_slope(values):
    logistic = jax.nn.sigmoid(values)
    return logistic * (1.0 + values * (1.0 - logistic))


def batch_stats(hidden, inside):
    masked = hidden * inside
    total, squares, pixel_count = lax.psum(
        (
            jnp.sum(masked, axis=(0, 1, 2)),
            jnp.sum(masked * hidden, axis=(0, 1, 2)),
            jnp.sum(inside),
        ),
        ("img", "rows"),
    )
    average = total / pixel_count
    inv_std = lax.rsqrt(squares / pixel_count - average * average + EPSILON)
    return ((hidden - average) * inv_std, inv_std, pixel_count)


def norm_back(grad_z, normed, gain, inv_std, pixel_count, inside):
    grad_shift, grad_gain = lax.psum(
        (jnp.sum(grad_z, axis=(0, 1, 2)), jnp.sum(grad_z * normed, axis=(0, 1, 2))), ("img", "rows")
    )
    grad_hidden = (
        inside * (gain * inv_std) * (grad_z - (grad_shift + normed * grad_gain) / pixel_count)
    )
    return (grad_hidden, grad_gain, grad_shift)


def per_device(
    features,
    weight_in,
    gain_in,
    bias_in,
    weight_mid,
    gain_mid,
    bias_mid,
    weight_out,
    gain_out,
    bias_out,
    map_size,
    out_grad,
    pool_grad,
):
    images = features.shape[0]
    height = features.shape[1]
    width = features.shape[2]
    channels_mid = weight_mid.shape[3]
    row_pos = lax.axis_index("rows") * height + jnp.arange(height)
    col_pos = jnp.arange(width)
    sizes_col = map_size[:, None, None]
    inside = ((row_pos[None, :, None] < sizes_col) & (col_pos[None, None, :] < sizes_col)).astype(
        jnp.float32
    )[..., None]
    map_area = (map_size * map_size).astype(jnp.float32)[:, None]
    first = jnp.dot(flatten(features), weight_in, preferred_element_type=jnp.float32).reshape(
        images, height, width, -1
    )
    first_normed, first_std, pixel_count = batch_stats(first, inside)
    first_pre = gain_in * first_normed + bias_in
    first_act = (smooth(first_pre) * inside).astype(jnp.bfloat16)
    first_rim = with_halo(first_act, (("rows", 1),), 1)
    first_cols = patches(widen(first_rim), height, width)
    second = jnp.dot(
        flatten(first_cols),
        weight_mid.reshape(-1, channels_mid),
        preferred_element_type=jnp.float32,
    ).reshape(images, height, width, channels_mid)
    second_normed, second_std, pixel_count = batch_stats(second, inside)
    second_pre = gain_mid * second_normed + bias_mid
    second_act = (smooth(second_pre) * inside).astype(jnp.bfloat16)
    third = jnp.dot(flatten(second_act), weight_out, preferred_element_type=jnp.float32).reshape(
        images, height, width, -1
    )
    third_normed, third_std, pixel_count = batch_stats(third, inside)
    summed = gain_out * third_normed + bias_out + features.astype(jnp.float32)
    result = smooth(summed) * inside
    pooled = (
        lax.psum(jnp.sum(result, axis=(1, 2)).astype(jnp.bfloat16), "rows").astype(jnp.float32)
        / map_area
    )
    total_grad = out_grad.astype(jnp.float32) + (pool_grad / map_area)[:, None, None, :]
    grad_summed = total_grad * inside * smooth_slope(summed)
    grad_third, grad_gain_out, grad_bias_out = norm_back(
        grad_summed, third_normed, gain_out, third_std, pixel_count, inside
    )
    grad_third_low = grad_third.astype(jnp.bfloat16)
    grad_weight_out = contract(second_act, grad_third_low)
    grad_second_act = times_transpose(grad_third_low, weight_out).reshape(
        images, height, width, channels_mid
    )
    grad_second_pre = grad_second_act * inside * smooth_slope(second_pre)
    grad_second, grad_gain_mid, grad_bias_mid = norm_back(
        grad_second_pre, second_normed, gain_mid, second_std, pixel_count, inside
    )
    grad_second_low = grad_second.astype(jnp.bfloat16)
    grad_weight_mid = contract(first_cols, grad_second_low).reshape(
        3, 3, channels_mid, channels_mid
    )
    grad_rim = with_halo(grad_second_low, (("rows", 1),), 1)
    grad_cols = patches(widen(grad_rim), height, width)
    flipped = weight_mid[::-1, ::-1].transpose(0, 1, 3, 2).reshape(-1, channels_mid)
    grad_first_act = jnp.dot(
        flatten(grad_cols), flipped, preferred_element_type=jnp.float32
    ).reshape(images, height, width, channels_mid)
    grad_first_pre = grad_first_act * inside * smooth_slope(first_pre)
    grad_first, grad_gain_in, grad_bias_in = norm_back(
        grad_first_pre, first_normed, gain_in, first_std, pixel_count, inside
    )
    grad_first_low = grad_first.astype(jnp.bfloat16)
    grad_weight_in = contract(features, grad_first_low)
    grad_features = grad_summed + times_transpose(grad_first_low, weight_in).reshape(
        images, height, width, -1
    )
    grad_weight_in, grad_weight_mid, grad_weight_out = lax.psum(
        (grad_weight_in, grad_weight_mid, grad_weight_out), ("img", "rows")
    )
    return (
        result.astype(jnp.bfloat16),
        pooled,
        grad_features,
        grad_weight_in,
        grad_gain_in,
        grad_bias_in,
        grad_weight_mid,
        grad_gain_mid,
        grad_bias_mid,
        grad_weight_out,
        grad_gain_out,
        grad_bias_out,
    )


def solution(mesh):
    placed = (
        P("img", "rows", None, None),
        P(),
        P(),
        P(),
        P(),
        P(),
        P(),
        P(),
        P(),
        P(),
        P("img"),
        P("img", "rows", None, None),
        P("img", None),
    )
    return jax.shard_map(
        per_device,
        mesh=mesh,
        in_specs=placed,
        out_specs=(
            P("img", "rows", None, None),
            P("img", None),
            P("img", "rows", None, None),
            P(),
            P(),
            P(),
            P(),
            P(),
            P(),
            P(),
            P(),
            P(),
        ),
        check_vma=False,
    )
```

profile of v0, /device:TPU:1, one launch (start us, length us, event | category | flops | bytes accessed | tf_op | source)
XLA Modules:
  0.0 639.2 jit_solution(6611695330649976521)
XLA Ops:
  7.3 0.8 iota_compare_fusion.2
  8.1 0.7 broadcast_compare_fusion
  8.9 0.6 convert_reduce_fusion
  9.5 0.1 copy.38
  9.7 2.7 multiply_reduce_fusion.3
  12.4 41.1 %all-reduce.7 = (f32[512]{0:T(512)S(1)}, f32[]{:T(128)}, f32[512]{0:T(512)S(1)}) all-reduce(f32[512]{0:T(512)S(1)} %get-tuple-element.55, f32[]{:T(128)} %convert_reduce_fusion, f32[512]{0:T(512)S(1)} %get-tuple-element.54), channel_id=1, replica_groups=mesh['img'=8,'rows'=4] {'img','rows'}, use_global_device_ids=true, to_apply=%region_5.0 | all-reduce | flops 1025 | bytes 8200 | tf_op jit(solution)/shard_map/psum | solution.py:61
  53.5 1.3 fusion.27
  54.8 0.2 multiply_convert_fusion.4
  55.0 0.7 fusion.31
  55.7 5.0 collective-permute-start
  60.7 1.9 collective-permute-start.1
  62.7 0.5 copy-done.29
  63.3 6.6 %copy.40 = bf16[3,3,512,512]{2,3,1,0:T(8,128)(2,1)} copy(bf16[3,3,512,512]{3,2,1,0:T(8,128)(2,1)} %param.17) | data formatting | bytes 9437184 | tf_op args[4]
  69.9 4.8 rev.3
  74.7 0.5 select_maximum_fusion.2
  75.4 0.2 constant_dynamic-update-slice_fusion
  75.9 4.6 multiply_reduce_fusion.2
  80.5 38.7 %all-reduce.6 = (f32[512]{0:T(512)S(1)}, f32[512]{0:T(512)S(1)}) all-reduce(f32[512]{0:T(512)S(1)} %get-tuple-element.53, f32[512]{0:T(512)S(1)} %get-tuple-element.52), channel_id=1, replica_groups=mesh['img'=8,'rows'=4] {'img','rows'}, use_global_device_ids=true, to_apply=%region_9.10 | all-reduce | flops 1024 | bytes 8192 | tf_op jit(solution)/shard_map/psum | solution.py:61
  119.2 0.7 fusion.28
  119.9 2.2 fusion
  122.1 39.9 %all-reduce.5 = (f32[2048]{0:T(1024)S(1)}, f32[2048]{0:T(1024)S(1)}) all-reduce(f32[2048]{0:T(1024)S(1)} %get-tuple-element.49, f32[2048]{0:T(1024)S(1)} %get-tuple-element.48), channel_id=1, replica_groups=mesh['img'=8,'rows'=4] {'img','rows'}, use_global_device_ids=true, to_apply=%region_11.12 | all-reduce | flops 4096 | bytes 32768 | tf_op jit(solution)/shard_map/psum | solution.py:61
  162.0 0.7 fusion.23
  162.7 0.7 add_rsqrt_fusion
  163.4 5.2 fusion.24
  168.6 40.5 %all-reduce.4 = (f32[2048]{0:T(1024)S(1)}, f32[2048]{0:T(1024)S(1)}) all-reduce(f32[2048]{0:T(1024)S(1)} %get-tuple-element.51, f32[2048]{0:T(1024)S(1)} %get-tuple-element.50), channel_id=1, replica_groups=mesh['img'=8,'rows'=4] {'img','rows'}, use_global_device_ids=true, to_apply=%region_19.20 | all-reduce | flops 4096 | bytes 32768 | tf_op jit(solution)/shard_map/psum | solution.py:75
  209.2 3.5 multiply_convert_fusion
  212.7 1.8 fusion.26
  214.5 2.9 convolution_bitcast_fusion
  217.5 4.3 copy.41
  221.9 39.9 %all-reduce.3 = (f32[512]{0:T(512)S(1)}, f32[512]{0:T(512)S(1)}) all-reduce(f32[512]{0:T(512)S(1)} %get-tuple-element.59, f32[512]{0:T(512)S(1)} %get-tuple-element.58), channel_id=1, replica_groups=mesh['img'=8,'rows'=4] {'img','rows'}, use_global_device_ids=true, to_apply=%region_23.24 | all-reduce | flops 1024 | bytes 8192 | tf_op jit(solution)/shard_map/psum | solution.py:75
  261.8 1.0 multiply_convert_fusion.2
  262.8 5.4 collective-permute-start.2
  268.2 1.9 collective-permute-start.3
  270.2 6.9 %fusion.32 = f32[3,3,512,512]{3,2,1,0:T(8,128)} fusion(bf16[3,3,512,256]{3,2,1,0:T(8,128)(2,1)} %bitcast.68, bf16[256,512,1,1]{1,0,3,2:T(8,128)(2,1)S(1)} %bitcast.67), kind=kOutput, calls=%fused_computation.98 | convolution fusion | flops 1207959552 | bytes 12058624 | tf_op jit(solution)/shard_map/dot_general | solution.py:39
  277.0 0.5 select_maximum_fusion
  278.0 0.2 copy-done.10
  278.3 1.5 fusion.25
  279.8 38.6 %all-reduce.2 = (f32[512]{0:T(512)S(1)}, f32[512]{0:T(512)S(1)}) all-reduce(f32[512]{0:T(512)S(1)} %get-tuple-element.57, f32[512]{0:T(512)S(1)} %get-tuple-element.56), channel_id=1, replica_groups=mesh['img'=8,'rows'=4] {'img','rows'}, use_global_device_ids=true, to_apply=%region_27.28 | all-reduce | flops 1024 | bytes 8192 | tf_op jit(solution)/shard_map/psum | solution.py:75
  318.4 0.9 multiply_convert_fusion.1
  319.3 2.8 convolution_bitcast_fusion.1
  322.1 0.5 copy-done.30
  322.6 1.6 convert_divide_fusion
  324.3 3.7 convolution_add_fusion
  327.9 287.2 %all-reduce.14.cloned.1.call-done = (f32[2048,512]{0,1:T(8,128)}, f32[3,3,512,512]{3,2,1,0:T(8,128)}, f32[512,2048]{1,0:T(8,128)}) async-done(((f32[2048,512]{0,1:T(8,128)}, f32[3,3,512,512]{3,2,1,0:T(8,128)}, f32[512,2048]{1,0:T(8,128)}), (f32[2048,512]{0,1:T(8,128)}, f32[3,3,512,512]{3,2,1,0:T(8,128)}, f32[512,2048]{1,0:T(8,128)})) %all-reduce.14.cloned.1.call-update) | async-done | bytes 17825808 | tf_op jit(solution)/shard_map/psum | solution.py:169
  615.1 5.3 copy.42
  620.5 8.7 %copy.70 = f32[3,3,512,512]{3,2,1,0:T(8,128)} copy(f32[3,3,512,512]{3,2,1,0:T(8,128)} %get-tuple-element.109) | data formatting | bytes 18874368
  629.2 2.1 copy.71
  631.3 1.0 copy-done.1
  (101 shorter events, 1.3 us)
Async XLA Ops:
  7.2 112.7 %copy-start = (bf16[512,2048]{1,0:T(8,128)(2,1)S(1)}, bf16[512,2048]{1,0:T(8,128)(2,1)}, u32[]{:S(2)}) copy-start(bf16[512,2048]{1,0:T(8,128)(2,1)} %param.20) | copy-start | bytes 6291460
  7.2 314.9 %all-reduce.12.cloned.1.call-start = ((), (), s32[]{:S(2)}) async-start(), calls=%async_computation | async-start | bytes 131072 | tf_op jit(solution)/shard_map/psum | solution.py:133
  9.7 43.9 %copy-start.15 = (f32[512]{0:T(512)S(1)}, f32[512]{0:T(512)}, u32[]{:S(2)}) copy-start(f32[512]{0:T(512)} %param.15) | copy-start | bytes 6148
  9.7 45.1 %copy-start.20 = (f32[512]{0:T(512)S(1)}, f32[512]{0:T(512)}, u32[]{:S(2)}) copy-start(f32[512]{0:T(512)} %param.16) | copy-start | bytes 6148
  9.7 53.0 %copy-start.33 = (s32[16]{0:T(128)S(1)}, s32[16]{0:T(128)}, u32[]{:S(2)}) copy-start(s32[16]{0:T(128)} %param.23) | copy-start | bytes 196
  9.7 53.5 %copy-start.7 = (f32[16,2048]{1,0:T(8,128)S(1)}, f32[16,2048]{1,0:T(8,128)}, u32[]{:S(2)}) copy-start(f32[16,2048]{1,0:T(8,128)} %param.25) | copy-start | bytes 393220
  54.8 5.9 copy-start.8
  54.8 5.9 copy-start.11
  55.7 19.0 %collective-permute-start = (bf16[16,1,8,512]{3,2,1,0:T(8,128)(2,1)}, bf16[16,1,8,512]{3,2,1,0:T(8,128)(2,1)S(1)}, u32[]{:S(2)}, u32[]{:S(2)}) collective-permute-start(bf16[16,1,8,512]{3,2,1,0:T(8,128)(2,1)} %get-tuple-element.89), channel_id=1, source_target_pairs={{0,1},{1,2},{2,3},{4,5},{5,6},{6,7},{8,9},{9,10},{10,11},{12,13},{... | collective-permute-start | bytes 393224 | tf_op jit(solution)/shard_map/ppermute | solution.py:14
  60.7 13.9 %collective-permute-start.1 = (bf16[16,1,8,512]{3,2,1,0:T(8,128)(2,1)S(1)}, bf16[16,1,8,512]{3,2,1,0:T(8,128)(2,1)S(1)}, u32[]{:S(2)}, u32[]{:S(2)}) collective-permute-start(bf16[16,1,8,512]{3,2,1,0:T(8,128)(2,1)S(1)} %get-tuple-element.90), channel_id=1, source_target_pairs={{1,0},{2,1},{3,2},{5,4},{6,5},{7,6},{9,8},{10,9},{11,10},{13,12},{... | collective-permute-start | bytes 393224 | tf_op jit(solution)/shard_map/ppermute | solution.py:17
  62.7 0.5 copy-start.29
  74.7 0.7 copy-start.9
  74.7 0.7 copy-start.12
  74.7 0.7 copy-start.16
  74.7 0.7 copy-start.21
  75.8 4.7 copy-start.4
  75.8 43.3 %copy-start.31 = (f32[512]{0:T(512)S(1)}, f32[512]{0:T(512)}, u32[]{:S(2)}) copy-start(f32[512]{0:T(512)} %param.18) | copy-start | bytes 6148
  75.9 44.0 %copy-start.32 = (f32[512]{0:T(512)S(1)}, f32[512]{0:T(512)}, u32[]{:S(2)}) copy-start(f32[512]{0:T(512)} %param.19) | copy-start | bytes 6148
  119.9 42.1 %copy-start.14 = (f32[2048]{0:T(1024)S(1)}, f32[2048]{0:T(1024)}, u32[]{:S(2)}) copy-start(f32[2048]{0:T(1024)} %param.21) | copy-start | bytes 24580
  119.9 43.5 %copy-start.24 = (f32[2048]{0:T(1024)S(1)}, f32[2048]{0:T(1024)}, u32[]{:S(2)}) copy-start(f32[2048]{0:T(1024)} %param.22) | copy-start | bytes 24580
  209.2 3.6 copy-start.18
  209.2 3.6 copy-start.19
  217.5 44.3 %copy-start.6 = (f32[16,2,8,512]{3,2,1,0:T(8,128)S(1)}, f32[16,2,8,512]{3,2,1,0:T(8,128)}, u32[]{:S(2)}) copy-start(f32[16,2,8,512]{3,2,1,0:T(8,128)} %get-tuple-element.96) | copy-start | bytes 1572868
  221.8 393.3 %all-reduce.14.cloned.1.call-start = ((), (), s32[]{:S(2)}) async-start(), calls=%async_computation.1 | async-start | bytes 35651584 | tf_op jit(solution)/shard_map/psum | solution.py:169
  261.7 15.3 %copy-start.25 = (f32[512]{0:T(512)}, f32[512]{0:T(512)S(1)}, u32[]{:S(2)}) copy-start(f32[512]{0:T(512)S(1)} %get-tuple-element.110) | copy-start | bytes 6148
  261.8 15.3 %copy-start.26 = (f32[512]{0:T(512)}, f32[512]{0:T(512)S(1)}, u32[]{:S(2)}) copy-start(f32[512]{0:T(512)S(1)} %get-tuple-element.111) | copy-start | bytes 6148
  261.8 16.2 %slice-start = ((s8[4718592]{0:T(1024)(128)(4,1)}), s8[4194304]{0:T(1024)(128)(4,1)S(1)}, s32[]{:S(2)}) async-start(s8[4718592]{0:T(1024)(128)(4,1)} %bitcast.70), calls=%async_computation.2 | async-start | bytes 8388608
  262.8 14.2 %collective-permute-start.2 = (bf16[16,1,8,512]{3,2,1,0:T(8,128)(2,1)S(1)}, bf16[16,1,8,512]{3,2,1,0:T(8,128)(2,1)S(1)}, u32[]{:S(2)}, u32[]{:S(2)}) collective-permute-start(bf16[16,1,8,512]{3,2,1,0:T(8,128)(2,1)S(1)} %get-tuple-element.87), channel_id=1, source_target_pairs={{0,1},{1,2},{2,3},{4,5},{5,6},{6,7},{8,9},{9,10},{10,11},{12,13},{... | collective-permute-start | bytes 393224 | tf_op jit(solution)/shard_map/ppermute | solution.py:14
  268.2 8.8 %collective-permute-start.3 = (bf16[16,1,8,512]{3,2,1,0:T(8,128)(2,1)S(1)}, bf16[16,1,8,512]{3,2,1,0:T(8,128)(2,1)S(1)}, u32[]{:S(2)}, u32[]{:S(2)}) collective-permute-start(bf16[16,1,8,512]{3,2,1,0:T(8,128)(2,1)S(1)} %get-tuple-element.88), channel_id=1, source_target_pairs={{1,0},{2,1},{3,2},{5,4},{6,5},{7,6},{9,8},{10,9},{11,10},{13,12},{... | collective-permute-start | bytes 393224 | tf_op jit(solution)/shard_map/ppermute | solution.py:17
  270.1 7.9 %slice-start.1 = ((s8[4718592]{0:T(1024)(128)(4,1)}), s8[524288]{0:T(1024)(128)(4,1)S(1)}, s32[]{:S(2)}) async-start(s8[4718592]{0:T(1024)(128)(4,1)} %bitcast.70), calls=%async_computation.3 | async-start | bytes 1048576
  277.5 0.7 copy-start.10
  277.6 0.7 copy-start.13
  277.6 0.7 copy-start.17
  277.6 0.7 copy-start.22
  278.3 40.1 %copy-start.23 = (f32[512]{0:T(512)S(1)}, f32[512]{0:T(512)}, u32[]{:S(2)}) copy-start(f32[512]{0:T(512)} %get-tuple-element.76) | copy-start | bytes 6148
  278.3 41.0 %copy-start.5 = (bf16[16,2,8,2048]{3,2,1,0:T(8,128)(2,1)S(1)}, bf16[16,2,8,2048]{3,2,1,0:T(8,128)(2,1)}, u32[]{:S(2)}) copy-start(bf16[16,2,8,2048]{3,2,1,0:T(8,128)(2,1)} %param.13) | copy-start | bytes 3145732
  318.4 3.7 copy-start.27
  318.4 3.7 copy-start.28
  322.1 0.6 copy-start.30
  322.1 2.2 copy-start.2
  620.5 8.7 %copy-start.3 = (f32[512,2048]{1,0:T(8,128)S(1)}, f32[512,2048]{1,0:T(8,128)}, u32[]{:S(2)}) copy-start(f32[512,2048]{1,0:T(8,128)} %get-tuple-element.112) | copy-start | bytes 12582916
  629.2 3.1 copy-start.1
Sparse Core Ops, SparseCore 0:
  221.9 31.0 all-reduce.11
  322.2 292.8 all-reduce.13
where the time goes:
time: 642 us; the launch traced here: 639 us
  waiting for transfers between devices  287 us (45%)
  blocking collectives  239 us (37%)
  local copies, waits for them, and re-layouts  35.8 us (6%)
  matrix products  29 us (5%)
  other arithmetic  19.4 us (3%)
  between operations  14.7 us (2%)
  starting transfers between devices  14.3 us (2%)
    psum x1, waiting for transfers between devices, per_device(): lax.psum((grad_weight_in, grad_weight_mid, grad_weight_out), ('img', 'row...  287 us
    psum x3, blocking collectives, batch_stats(): lax.psum((jnp.sum(masked, axis=(0, 1, 2)), jnp.sum(masked * hidden, axis=...  120 us
    psum x3, blocking collectives, norm_back(): lax.psum((jnp.sum(grad_z, axis=(0, 1, 2)), jnp.sum(grad_z * normed, axis=...  119 us
    unnamed x87, local copies, waits for them, and re-layouts  25.7 us
  transfers between devices with their start and end apart: 6, of which 1 were waited for; matrix products, arithmetic and copies ran while one was open for 5% of the time, Pallas kernels for 0%

commit v1 on v0

--- a/solution.py
+++ b/solution.py
@@ -4,6 +4,65 @@
 from jax.sharding import PartitionSpec as P
 
 EPSILON = 1e-05
+
+AXES = ("img", "rows")
+
+
+def swap(value, flips):
+    count = lax.axis_size(AXES)
+    return lax.ppermute(value, AXES, [(i, i ^ flips[i & 1]) for i in range(count)])
+
+
+def bits():
+    count, found = lax.axis_size(AXES), []
+    while (1 << len(found)) < count:
+        found.append(1 << len(found))
+    return found
+
+
+def sum_all(value):
+    for bit in bits():
+        value = value + swap(value, (bit, bit))
+    return value
+
+
+def flat_index():
+    return lax.axis_index("img") * lax.axis_size("rows") + lax.axis_index("rows")
+
+
+def plan():
+    order = bits()
+    steps = [(bit, bit) for bit in order]
+    if len(order) >= 3:
+        steps[1], steps[2] = (order[1], order[2]), (order[2], order[1])
+    index = flat_index()
+    low = index % 2
+    chosen = []
+    for even, odd in steps:
+        chosen.append(((even, odd), jnp.where(low == 0, index // even % 2, index // odd % 2)))
+    return chosen
+
+
+def sum_scatter(value):
+    for flips, mine in plan():
+        halves = value.reshape((2, value.shape[0] // 2) + value.shape[1:])
+        sent = lax.dynamic_index_in_dim(halves, 1 - mine, 0, keepdims=False).astype(jnp.bfloat16)
+        kept = lax.dynamic_index_in_dim(halves, mine, 0, keepdims=False)
+        value = kept + swap(sent, flips).astype(jnp.float32)
+    return value
+
+
+def gather_back(value):
+    value = value.astype(jnp.bfloat16)
+    half = jnp.arange(2).reshape((2,) + (1,) * value.ndim)
+    for flips, mine in reversed(plan()):
+        other = swap(value, flips)
+        value = jnp.where(half == mine, value[None], other[None]).reshape((-1,) + value.shape[1:])
+    return value.astype(jnp.float32)
+
+
+def sum_weights(value):
+    return gather_back(sum_scatter(value))
 
 
 def with_halo(block, sides, width):
@@ -56,24 +115,18 @@
     return logistic * (1.0 + values * (1.0 - logistic))
 
 
-def batch_stats(hidden, inside):
+def batch_stats(hidden, inside, pixel_count):
     masked = hidden * inside
-    total, squares, pixel_count = lax.psum(
-        (
-            jnp.sum(masked, axis=(0, 1, 2)),
-            jnp.sum(masked * hidden, axis=(0, 1, 2)),
-            jnp.sum(inside),
-        ),
-        ("img", "rows"),
-    )
+    sums = jnp.stack([jnp.sum(masked, axis=(0, 1, 2)), jnp.sum(masked * hidden, axis=(0, 1, 2))])
+    total, squares = sum_all(sums)
     average = total / pixel_count
     inv_std = lax.rsqrt(squares / pixel_count - average * average + EPSILON)
-    return ((hidden - average) * inv_std, inv_std, pixel_count)
+    return ((hidden - average) * inv_std, inv_std)
 
 
 def norm_back(grad_z, normed, gain, inv_std, pixel_count, inside):
-    grad_shift, grad_gain = lax.psum(
-        (jnp.sum(grad_z, axis=(0, 1, 2)), jnp.sum(grad_z * normed, axis=(0, 1, 2))), ("img", "rows")
+    grad_shift, grad_gain = sum_all(
+        jnp.stack([jnp.sum(grad_z, axis=(0, 1, 2)), jnp.sum(grad_z * normed, axis=(0, 1, 2))])
     )
     grad_hidden = (
         inside * (gain * inv_std) * (grad_z - (grad_shift + normed * grad_gain) / pixel_count)
@@ -107,10 +160,11 @@
         jnp.float32
     )[..., None]
     map_area = (map_size * map_size).astype(jnp.float32)[:, None]
+    pixel_count = sum_all(jnp.sum(inside))
     first = jnp.dot(flatten(features), weight_in, preferred_element_type=jnp.float32).reshape(
         images, height, width, -1
     )
-    first_normed, first_std, pixel_count = batch_stats(first, inside)
+    first_normed, first_std = batch_stats(first, inside, pixel_count)
     first_pre = gain_in * first_normed + bias_in
     first_act = (smooth(first_pre) * inside).astype(jnp.bfloat16)
     first_rim = with_halo(first_act, (("rows", 1),), 1)
@@ -120,13 +174,13 @@
         weight_mid.reshape(-1, channels_mid),
         preferred_element_type=jnp.float32,
     ).reshape(images, height, width, channels_mid)
-    second_normed, second_std, pixel_count = batch_stats(second, inside)
+    second_normed, second_std = batch_stats(second, inside, pixel_count)
     second_pre = gain_mid * second_normed + bias_mid
     second_act = (smooth(second_pre) * inside).astype(jnp.bfloat16)
     third = jnp.dot(flatten(second_act), weight_out, preferred_element_type=jnp.float32).reshape(
         images, height, width, -1
     )
-    third_normed, third_std, pixel_count = batch_stats(third, inside)
+    third_normed, third_std = batch_stats(third, inside, pixel_count)
     summed = gain_out * third_normed + bias_out + features.astype(jnp.float32)
     result = smooth(summed) * inside
     pooled = (
@@ -166,9 +220,11 @@
     grad_features = grad_summed + times_transpose(grad_first_low, weight_in).reshape(
         images, height, width, -1
     )
-    grad_weight_in, grad_weight_mid, grad_weight_out = lax.psum(
-        (grad_weight_in, grad_weight_mid, grad_weight_out), ("img", "rows")
-    )
+    grad_weight_in = sum_weights(grad_weight_in)
+    grad_weight_mid = sum_weights(grad_weight_mid.reshape(-1, channels_mid)).reshape(
+        3, 3, channels_mid, channels_mid
+    )
+    grad_weight_out = sum_weights(grad_weight_out)
     return (
         result.astype(jnp.bfloat16),
         pooled,

time: 642 us -> 391 us (0.61)
  blocking collectives: 239 us -> 0 us
  waiting for transfers between devices: 287 us -> 125 us
  starting transfers between devices: 14.3 us -> 124 us
  local copies, waits for them, and re-layouts: 35.8 us -> 59.4 us
  other arithmetic: 19.4 us -> 41.4 us
  matrix products: 29 us -> 18.4 us
    psum x1 -> x0, waiting for transfers between devices: 287 us -> none  [per_device(): lax.psum((grad_weight_in, grad_weight_mid, grad_weight_out), ('img', 'row...]
    psum x6 -> x0, blocking collectives: 239 us -> none  [the longest x3 120 us: batch_stats(): lax.psum((jnp.sum(masked, axis=(0, 1, 2)), jnp.sum(masked * hidden, axis=...]
    ppermute x0 -> x65, starting transfers between devices: none -> 104 us  [swap(): lax.ppermute(value, AXES, [(i, i ^ flips[i & 1]) for i in range(count)])]
    ppermute x0 -> x65, waiting for transfers between devices: none -> 95.7 us  [swap(): lax.ppermute(value, AXES, [(i, i ^ flips[i & 1]) for i in range(count)])]
    psum x1, waiting for transfers between devices: 0.02 us -> 27.7 us  [per_device(): lax.psum(jnp.sum(result, axis=(1, 2)).astype(jnp.bfloat16), 'rows')]
    dynamic_slice x0 -> x3, local copies, waits for them, and re-layouts: none -> 13.1 us  [the longest x2 9.86 us: sum_scatter(): kept = lax.dynamic_index_in_dim(halves, mine, 0, keepdims=False)]
    convert_element_type x0 -> x7, other arithmetic: none -> 11.9 us  [the longest x3 11.6 us: gather_back(): return value.astype(jnp.float32)]
    add x0 -> x42, other arithmetic: none -> 11.5 us  [the longest x12 11.2 us: sum_scatter(): value = kept + swap(sent, flips).astype(jnp.float32)]
  transfers between devices with their start and end apart: 6 -> 70, of which waited for: 1 -> 49; matrix products, arithmetic and copies ran while one was open for 5% -> 24% of each run, Pallas kernels for 0% -> 0%
where the time goes in v1:
time: 391 us; the launch traced here: 388 us
  waiting for transfers between devices  125 us (32%)
  starting transfers between devices  124 us (32%)
  local copies, waits for them, and re-layouts  59.4 us (15%)
  other arithmetic  41.4 us (11%)
  between operations  19.3 us (5%)
  matrix products  18.4 us (5%)
    ppermute x65, starting transfers between devices, swap(): lax.ppermute(value, AXES, [(i, i ^ flips[i & 1]) for i in range(count)])  104 us
    ppermute x65, waiting for transfers between devices, swap(): lax.ppermute(value, AXES, [(i, i ^ flips[i & 1]) for i in range(count)])  95.7 us
    psum x1, waiting for transfers between devices, per_device(): lax.psum(jnp.sum(result, axis=(1, 2)).astype(jnp.bfloat16), 'rows')  27.7 us
    unnamed x115, local copies, waits for them, and re-layouts  16.9 us
    ppermute x2, starting transfers between devices, with_halo(): lax.ppermute(lax.slice_in_dim(block, 0, width, axis=dim), axis, backward)  13.4 us
    convert_element_type x3, other arithmetic, gather_back(): return value.astype(jnp.float32)  11.6 us
    add x12, other arithmetic, sum_scatter(): value = kept + swap(sent, flips).astype(jnp.float32)  11.2 us
    dynamic_slice x2, local copies, waits for them, and re-layouts, sum_scatter(): kept = lax.dynamic_index_in_dim(halves, mine, 0, keepdims=False)  9.86 us
  transfers between devices with their start and end apart: 70, of which 49 were waited for; matrix products, arithmetic and copies ran while one was open for 24% of the time, Pallas kernels for 0%

profile of v1, /device:TPU:1, one launch (start us, length us, event | category | flops | bytes accessed | tf_op | source)
XLA Modules:
  0.0 387.7 jit_solution(1823711610754003461)
XLA Ops:
  9.1 2.6 multiply_reduce_fusion.3
  21.5 2.5 collective-permute-start.4
  24.6 4.1 %collective-permute-start.5 = (f32[]{:T(128)}, f32[]{:T(128)}, u32[]{:S(2)}, u32[]{:S(2)}) collective-permute-start(f32[]{:T(128)} %convert_reduce_fusion), channel_id=1, source_target_pairs={{0,1},{1,0},{2,3},{3,2},{4,5},{5,4},{6,7},{7,6},{8,9},{9,8},{10,11... | collective-permute-start | bytes 20 | tf_op jit(solution)/shard_map/ppermute | solution.py:13
  41.0 2.5 collective-permute-done.9
  45.0 7.4 %collective-permute-start.11 = (bf16[16,1,8,512]{3,2,1,0:T(8,128)(2,1)S(1)}, bf16[16,1,8,512]{3,2,1,0:T(8,128)(2,1)S(1)}, u32[]{:S(2)}, u32[]{:S(2)}) collective-permute-start(bf16[16,1,8,512]{3,2,1,0:T(8,128)(2,1)S(1)} %get-tuple-element.32), channel_id=1, source_target_pairs={{1,0},{2,1},{3,2},{5,4},{6,5},{7,6},{9,8},{10,9},{11,10},{13,12},{... | collective-permute-start | bytes 393224 | tf_op jit(solution)/shard_map/ppermute | solution.py:76
  52.4 3.0 collective-permute-start.10
  58.5 2.6 copy-done.12
  72.0 3.3 collective-permute-done.16
  76.5 4.7 %collective-permute-start.17 = (f32[2,2048]{1,0:T(2,128)S(1)}, f32[2,2048]{1,0:T(2,128)S(1)}, u32[]{:S(2)}, u32[]{:S(2)}) collective-permute-start(f32[2,2048]{1,0:T(2,128)S(1)} %pad_maximum_fusion.4), channel_id=1, source_target_pairs={{0,1},{1,0},{2,3},{3,2},{4,5},{5,4},{6,7},{7,6},{8,9},{9,8},{10,11... | collective-permute-start | bytes 49160 | tf_op jit(solution)/shard_map/ppermute | solution.py:13
  90.6 3.3 collective-permute-done.21
  94.0 3.4 fusion.51
  97.5 4.7 %collective-permute-start.22 = (f32[2,2048]{1,0:T(2,128)S(1)}, f32[2,2048]{1,0:T(2,128)S(1)}, u32[]{:S(2)}, u32[]{:S(2)}) collective-permute-start(f32[2,2048]{1,0:T(2,128)S(1)} %pad_maximum_fusion.5), channel_id=1, source_target_pairs={{0,1},{1,0},{2,3},{3,2},{4,5},{5,4},{6,7},{7,6},{8,9},{9,8},{10,11... | collective-permute-start | bytes 49160 | tf_op jit(solution)/shard_map/ppermute | solution.py:13
  111.5 3.4 collective-permute-done.26
  117.5 4.7 %collective-permute-start.27 = (f32[2,512]{1,0:T(2,128)S(1)}, f32[2,512]{1,0:T(2,128)S(1)}, u32[]{:S(2)}, u32[]{:S(2)}) collective-permute-start(f32[2,512]{1,0:T(2,128)S(1)} %pad_maximum_fusion.8), channel_id=1, source_target_pairs={{0,1},{1,0},{2,3},{3,2},{4,5},{5,4},{6,7},{7,6},{8,9},{9,8},{10,11... | collective-permute-start | bytes 12296 | tf_op jit(solution)/shard_map/ppermute | solution.py:13
  130.9 6.6 %copy.40 = bf16[3,3,512,512]{2,3,1,0:T(8,128)(2,1)} copy(bf16[3,3,512,512]{3,2,1,0:T(8,128)(2,1)} %param.17) | data formatting | bytes 9437184 | tf_op args[4]
  137.6 4.8 %rev.3 = bf16[3,3,512,512]{2,3,1,0:T(8,128)(2,1)} reverse(bf16[3,3,512,512]{2,3,1,0:T(8,128)(2,1)} %copy.40), dimensions={0,1} | reverse | bytes 9437184 | tf_op jit(solution)/shard_map/rev | solution.py:210
  142.4 4.3 %copy.43 = bf16[4608,256]{1,0:T(8,128)(2,1)} copy(bf16[4608,256]{0,1:T(8,128)(2,1)} %bitcast.264) | data formatting | bytes 4718592 | tf_op jit(solution)/shard_map/dot_general | solution.py:98
  147.0 6.0 %collective-permute-start.33 = (bf16[16,1,8,512]{3,2,1,0:T(8,128)(2,1)S(1)}, bf16[16,1,8,512]{3,2,1,0:T(8,128)(2,1)S(1)}, u32[]{:S(2)}, u32[]{:S(2)}) collective-permute-start(bf16[16,1,8,512]{3,2,1,0:T(8,128)(2,1)S(1)} %get-tuple-element.30), channel_id=1, source_target_pairs={{1,0},{2,1},{3,2},{5,4},{6,5},{7,6},{9,8},{10,9},{11,10},{13,12},{... | collective-permute-start | bytes 393224 | tf_op jit(solution)/shard_map/ppermute | solution.py:76
  153.0 3.7 collective-permute-start.32
  156.7 3.1 fusion.60
  178.7 3.0 collective-permute-start.59
  181.9 3.8 bitcast_add_fusion
  188.9 2.8 convolution_bitcast_fusion
  191.7 6.6 %reshape.624 = f32[2,1024,512]{1,0,2:T(2,128)} reshape(f32[2048,512]{0,1:T(8,128)} %convolution_bitcast_fusion) | data formatting | bytes 8388608 | tf_op jit(solution)/shard_map/reshape | solution.py:48
  198.2 5.3 %constant_dynamic-slice_fusion.1 = f32[1,1024,512]{1,0,2:T(1,128)} fusion(f32[2,1024,512]{1,0,2:T(2,128)} %reshape.624, s32[]{:T(128)S(6)} %select_n.448), kind=kLoop, calls=%fused_computation.146 | loop fusion | bytes 4194308 | tf_op jit(solution)/shard_map/jit(dynamic_index_in_dim)/dynamic_slice | solution.py:50
  210.8 3.2 constant_dynamic-slice_fusion
  214.0 4.6 %copy.41 = f32[1,1024,512]{2,1,0:T(8,128)S(1)} copy(f32[1,1024,512]{1,0,2:T(1,128)} %constant_dynamic-slice_fusion.1) | data formatting | bytes 4194304 | tf_op jit(solution)/shard_map/jit(dynamic_index_in_dim)/dynamic_slice | solution.py:50
  218.6 4.8 %copy.50 = bf16[1,1024,512]{2,1,0:T(8,128)(2,1)S(1)} copy(bf16[1,1024,512]{1,0,2:T(2,128)(2,1)} %constant_dynamic-slice_fusion) | data formatting | bytes 2097152
  229.9 5.9 %collective-permute-done.52 = bf16[288,512]{1,0:T(8,128)(2,1)S(1)} collective-permute-done((bf16[288,512]{1,0:T(8,128)(2,1)S(1)}, bf16[288,512]{1,0:T(8,128)(2,1)S(1)}, u32[]{:S(2)}, u32[]{:S(2)}) %collective-permute-start.52) | collective-permute-done | bytes 294944 | tf_op jit(solution)/shard_map/ppermute | solution.py:13
  239.7 5.1 %collective-permute-done.53 = bf16[144,512]{1,0:T(8,128)(2,1)S(1)} collective-permute-done((bf16[144,512]{1,0:T(8,128)(2,1)S(1)}, bf16[144,512]{1,0:T(8,128)(2,1)S(1)}, u32[]{:S(2)}, u32[]{:S(2)}) %collective-permute-start.53) | collective-permute-done | bytes 147488 | tf_op jit(solution)/shard_map/ppermute | solution.py:13
  246.1 3.6 collective-permute-done.54
  249.9 3.6 collective-permute-start.55
  253.6 4.5 %collective-permute-done.55 = bf16[288,512]{1,0:T(8,128)(2,1)S(1)} collective-permute-done((bf16[288,512]{1,0:T(8,128)(2,1)S(1)}, bf16[288,512]{1,0:T(8,128)(2,1)S(1)}, u32[]{:S(2)}, u32[]{:S(2)}) %collective-permute-start.55) | collective-permute-done | bytes 294944 | tf_op jit(solution)/shard_map/ppermute | solution.py:13
  262.0 5.3 %collective-permute-done.56 = bf16[576,512]{1,0:T(8,128)(2,1)S(1)} collective-permute-done((bf16[576,512]{1,0:T(8,128)(2,1)S(1)}, bf16[576,512]{1,0:T(8,128)(2,1)S(1)}, u32[]{:S(2)}, u32[]{:S(2)}) %collective-permute-start.56) | collective-permute-done | bytes 589856 | tf_op jit(solution)/shard_map/ppermute | solution.py:13
  272.2 2.8 collective-permute-start.63
  275.1 2.9 collective-permute-start.43
  278.0 9.7 %collective-permute-done.57 = bf16[1152,512]{1,0:T(8,128)(2,1)S(1)} collective-permute-done((bf16[1152,512]{1,0:T(8,128)(2,1)S(1)}, bf16[1152,512]{1,0:T(8,128)(2,1)S(1)}, u32[]{:S(2)}, u32[]{:S(2)}) %collective-permute-start.57) | collective-permute-done | bytes 1179680 | tf_op jit(solution)/shard_map/ppermute | solution.py:13
  289.6 3.4 collective-permute-start.58
  296.1 3.2 collective-permute-done.64
  303.3 2.5 collective-permute-start.66
  314.6 6.8 %collective-permute-done.67 = bf16[128,2048]{1,0:T(8,128)(2,1)} collective-permute-done((bf16[128,2048]{1,0:T(8,128)(2,1)S(1)}, bf16[128,2048]{1,0:T(8,128)(2,1)}, u32[]{:S(2)}, u32[]{:S(2)}) %collective-permute-start.67) | collective-permute-done | bytes 524320 | tf_op jit(solution)/shard_map/ppermute | solution.py:13
  324.4 2.5 collective-permute-done.47
  329.4 2.6 collective-permute-start.48
  332.3 27.7 %all-reduce.4.cloned.1.call-done = bf16[16,2048]{1,0:T(8,128)(2,1)} async-done(((bf16[16,2048]{1,0:T(8,128)(2,1)}), bf16[16,2048]{1,0:T(8,128)(2,1)}) %all-reduce.4.cloned.1.call-update) | async-done | bytes 65552 | tf_op jit(solution)/shard_map/psum | solution.py:187
  361.6 3.7 convolution_add_fusion
  365.3 3.6 fusion.2
  368.9 4.0 %fusion.3 = f32[2048,512]{1,0:T(8,128)} fusion(pred[2048]{0:T(1024)(128)(4,1)S(1)} %broadcast_in_dim.520, bf16[1024,512]{1,0:T(8,128)(2,1)} %collective-permute-done.48, bf16[1024,512]{1,0:T(8,128)(2,1)} %bitcast_select_fusion.5), kind=kLoop, calls=%fused_computation.18 | loop fusion | flops 2097152 | bytes 6293504 | tf_op jit(solution)/shard_map/convert_element_type | solution.py:61
  376.8 4.1 %select_convert_fusion = f32[3,3,512,512]{3,2,1,0:T(8,128)} fusion(bf16[3,3,512,512]{3,2,1,0:T(8,128)(2,1)S(1)} %bitcast.241, bf16[3,3,512,512]{3,2,1,0:T(8,128)(2,1)S(1)} %bitcast.242, pred[3,3,512]{2,1,0:T(4,128)(4,1)S(1)} %broadcast_in_dim.555), kind=kLoop, calls=%fused_computation.1 | loop fusion | flops 4718592 | bytes 18878976 | tf_op jit(solution)/shard_map/convert_element_type | solution.py:61
  (376 shorter events, 146.0 us)
Async XLA Ops:
  7.2 352.8 %all-reduce.4.cloned.1.call-start = ((), (), s32[]{:S(2)}) async-start(), calls=%async_computation | async-start | bytes 131072 | tf_op jit(solution)/shard_map/psum | solution.py:187
  13.0 3.4 collective-permute-start.1
  21.5 22.6 %collective-permute-start.4 = (f32[2,512]{1,0:T(2,128)S(1)}, f32[2,512]{1,0:T(2,128)S(1)}, u32[]{:S(2)}, u32[]{:S(2)}) collective-permute-start(f32[2,512]{1,0:T(2,128)S(1)} %add.446), channel_id=1, source_target_pairs={{0,16},{1,17},{2,18},{3,19},{4,20},{5,21},{6,22},{7,23},{8,24},{9,... | collective-permute-start | bytes 12296 | tf_op jit(solution)/shard_map/ppermute | solution.py:13
  24.6 5.2 %collective-permute-start.5 = (f32[]{:T(128)}, f32[]{:T(128)}, u32[]{:S(2)}, u32[]{:S(2)}) collective-permute-start(f32[]{:T(128)} %convert_reduce_fusion), channel_id=1, source_target_pairs={{0,1},{1,0},{2,3},{3,2},{4,5},{5,4},{6,7},{7,6},{8,9},{9,8},{10,11... | collective-permute-start | bytes 20 | tf_op jit(solution)/shard_map/ppermute | solution.py:13
  40.2 3.3 collective-permute-start.9
  45.0 11.2 %collective-permute-start.11 = (bf16[16,1,8,512]{3,2,1,0:T(8,128)(2,1)S(1)}, bf16[16,1,8,512]{3,2,1,0:T(8,128)(2,1)S(1)}, u32[]{:S(2)}, u32[]{:S(2)}) collective-permute-start(bf16[16,1,8,512]{3,2,1,0:T(8,128)(2,1)S(1)} %get-tuple-element.32), channel_id=1, source_target_pairs={{1,0},{2,1},{3,2},{5,4},{6,5},{7,6},{9,8},{10,9},{11,10},{13,12},{... | collective-permute-start | bytes 393224 | tf_op jit(solution)/shard_map/ppermute | solution.py:76
  52.4 5.0 %collective-permute-start.10 = (bf16[16,1,8,512]{3,2,1,0:T(8,128)(2,1)S(1)}, bf16[16,1,8,512]{3,2,1,0:T(8,128)(2,1)S(1)}, u32[]{:S(2)}, u32[]{:S(2)}) collective-permute-start(bf16[16,1,8,512]{3,2,1,0:T(8,128)(2,1)S(1)} %get-tuple-element.31), channel_id=1, source_target_pairs={{0,1},{1,2},{2,3},{4,5},{5,6},{6,7},{8,9},{9,10},{10,11},{12,13},{... | collective-permute-start | bytes 393224 | tf_op jit(solution)/shard_map/ppermute | solution.py:73
  72.0 3.4 collective-permute-start.16
  76.5 5.6 %collective-permute-start.17 = (f32[2,2048]{1,0:T(2,128)S(1)}, f32[2,2048]{1,0:T(2,128)S(1)}, u32[]{:S(2)}, u32[]{:S(2)}) collective-permute-start(f32[2,2048]{1,0:T(2,128)S(1)} %pad_maximum_fusion.4), channel_id=1, source_target_pairs={{0,1},{1,0},{2,3},{3,2},{4,5},{5,4},{6,7},{7,6},{8,9},{9,8},{10,11... | collective-permute-start | bytes 49160 | tf_op jit(solution)/shard_map/ppermute | solution.py:13
  90.4 3.6 collective-permute-start.21
  97.5 5.6 %collective-permute-start.22 = (f32[2,2048]{1,0:T(2,128)S(1)}, f32[2,2048]{1,0:T(2,128)S(1)}, u32[]{:S(2)}, u32[]{:S(2)}) collective-permute-start(f32[2,2048]{1,0:T(2,128)S(1)} %pad_maximum_fusion.5), channel_id=1, source_target_pairs={{0,1},{1,0},{2,3},{3,2},{4,5},{5,4},{6,7},{7,6},{8,9},{9,8},{10,11... | collective-permute-start | bytes 49160 | tf_op jit(solution)/shard_map/ppermute | solution.py:13
  111.4 3.6 collective-permute-start.26
  117.5 5.6 %collective-permute-start.27 = (f32[2,512]{1,0:T(2,128)S(1)}, f32[2,512]{1,0:T(2,128)S(1)}, u32[]{:S(2)}, u32[]{:S(2)}) collective-permute-start(f32[2,512]{1,0:T(2,128)S(1)} %pad_maximum_fusion.8), channel_id=1, source_target_pairs={{0,1},{1,0},{2,3},{3,2},{4,5},{5,4},{6,7},{7,6},{8,9},{9,8},{10,11... | collective-permute-start | bytes 12296 | tf_op jit(solution)/shard_map/ppermute | solution.py:13
  130.9 15.8 %collective-permute-start.31 = (f32[2,512]{1,0:T(2,128)S(1)}, f32[2,512]{1,0:T(2,128)S(1)}, u32[]{:S(2)}, u32[]{:S(2)}) collective-permute-start(f32[2,512]{1,0:T(2,128)S(1)} %add.492), channel_id=1, source_target_pairs={{0,16},{1,17},{2,18},{3,19},{4,20},{5,21},{6,22},{7,23},{8,24},{9,... | collective-permute-start | bytes 12296 | tf_op jit(solution)/shard_map/ppermute | solution.py:13
  147.0 14.8 %collective-permute-start.33 = (bf16[16,1,8,512]{3,2,1,0:T(8,128)(2,1)S(1)}, bf16[16,1,8,512]{3,2,1,0:T(8,128)(2,1)S(1)}, u32[]{:S(2)}, u32[]{:S(2)}) collective-permute-start(bf16[16,1,8,512]{3,2,1,0:T(8,128)(2,1)S(1)} %get-tuple-element.30), channel_id=1, source_target_pairs={{1,0},{2,1},{3,2},{5,4},{6,5},{7,6},{9,8},{10,9},{11,10},{13,12},{... | collective-permute-start | bytes 393224 | tf_op jit(solution)/shard_map/ppermute | solution.py:76
  153.0 8.8 %collective-permute-start.32 = (bf16[16,1,8,512]{3,2,1,0:T(8,128)(2,1)S(1)}, bf16[16,1,8,512]{3,2,1,0:T(8,128)(2,1)S(1)}, u32[]{:S(2)}, u32[]{:S(2)}) collective-permute-start(bf16[16,1,8,512]{3,2,1,0:T(8,128)(2,1)S(1)} %get-tuple-element.29), channel_id=1, source_target_pairs={{0,1},{1,2},{2,3},{4,5},{5,6},{6,7},{8,9},{9,10},{10,11},{12,13},{... | collective-permute-start | bytes 393224 | tf_op jit(solution)/shard_map/ppermute | solution.py:73
  161.8 20.1 %collective-permute-start.49 = (bf16[2304,512]{1,0:T(8,128)(2,1)}, bf16[2304,512]{1,0:T(8,128)(2,1)}, u32[]{:S(2)}, u32[]{:S(2)}) collective-permute-start(bf16[2304,512]{1,0:T(8,128)(2,1)} %fusion), channel_id=1, source_target_pairs={{0,1},{1,0},{2,3},{3,2},{4,5},{5,4},{6,7},{7,6},{8,9},{9,8},{10,11... | collective-permute-start | bytes 7077896 | tf_op jit(solution)/shard_map/ppermute | solution.py:13
  168.9 3.8 collective-permute-start.36
  175.2 6.4 %collective-permute-start.38 = (f32[2,512]{1,0:T(2,128)S(1)}, f32[2,512]{1,0:T(2,128)S(1)}, u32[]{:S(2)}, u32[]{:S(2)}) collective-permute-start(f32[2,512]{1,0:T(2,128)S(1)} %add.501), channel_id=1, source_target_pairs={{0,16},{1,17},{2,18},{3,19},{4,20},{5,21},{6,22},{7,23},{8,24},{9,... | collective-permute-start | bytes 12296 | tf_op jit(solution)/shard_map/ppermute | solution.py:13
  178.7 28.7 %collective-permute-start.59 = (bf16[256,2048]{1,0:T(8,128)(2,1)}, bf16[256,2048]{1,0:T(8,128)(2,1)}, u32[]{:S(2)}, u32[]{:S(2)}) collective-permute-start(bf16[256,2048]{1,0:T(8,128)(2,1)} %fusion.20), channel_id=1, source_target_pairs={{0,1},{1,0},{2,3},{3,2},{4,5},{5,4},{6,7},{7,6},{8,9},{9,8},{10,11... | collective-permute-start | bytes 3145736 | tf_op jit(solution)/shard_map/ppermute | solution.py:13
  188.1 15.5 %collective-permute-start.50 = (bf16[1152,512]{1,0:T(8,128)(2,1)S(1)}, bf16[1152,512]{1,0:T(8,128)(2,1)S(1)}, u32[]{:S(2)}, u32[]{:S(2)}) collective-permute-start(bf16[1152,512]{1,0:T(8,128)(2,1)S(1)} %fusion.19), channel_id=1, source_target_pairs={{0,2},{1,5},{2,0},{3,7},{4,6},{5,1},{6,4},{7,3},{8,10},{9,13},{10,... | collective-permute-start | bytes 3538952 | tf_op jit(solution)/shard_map/ppermute | solution.py:13
  206.8 18.8 %collective-permute-start.51 = (bf16[576,512]{1,0:T(8,128)(2,1)}, bf16[576,512]{1,0:T(8,128)(2,1)}, u32[]{:S(2)}, u32[]{:S(2)}) collective-permute-start(bf16[576,512]{1,0:T(8,128)(2,1)} %fusion.22), channel_id=1, source_target_pairs={{0,4},{1,3},{2,6},{3,1},{4,0},{5,7},{6,2},{7,5},{8,12},{9,11},{10,... | collective-permute-start | bytes 1769480 | tf_op jit(solution)/shard_map/ppermute | solution.py:13
  210.1 18.7 %collective-permute-start.60 = (bf16[128,2048]{1,0:T(8,128)(2,1)}, bf16[128,2048]{1,0:T(8,128)(2,1)}, u32[]{:S(2)}, u32[]{:S(2)}) collective-permute-start(bf16[128,2048]{1,0:T(8,128)(2,1)} %fusion.26), channel_id=1, source_target_pairs={{0,2},{1,5},{2,0},{3,7},{4,6},{5,1},{6,4},{7,3},{8,10},{9,13},{10,... | collective-permute-start | bytes 1572872 | tf_op jit(solution)/shard_map/ppermute | solution.py:13
  223.4 21.5 %collective-permute-start.39 = (bf16[1024,512]{1,0:T(8,128)(2,1)S(1)}, bf16[1024,512]{1,0:T(8,128)(2,1)S(1)}, u32[]{:S(2)}, u32[]{:S(2)}) collective-permute-start(bf16[1024,512]{1,0:T(8,128)(2,1)S(1)} %bitcast.271), channel_id=1, source_target_pairs={{0,1},{1,0},{2,3},{3,2},{4,5},{5,4},{6,7},{7,6},{8,9},{9,8},{10,11... | collective-permute-start | bytes 3145736 | tf_op jit(solution)/shard_map/ppermute | solution.py:13
  227.3 8.5 %collective-permute-start.52 = (bf16[288,512]{1,0:T(8,128)(2,1)S(1)}, bf16[288,512]{1,0:T(8,128)(2,1)S(1)}, u32[]{:S(2)}, u32[]{:S(2)}) collective-permute-start(bf16[288,512]{1,0:T(8,128)(2,1)S(1)} %fusion.27), channel_id=1, source_target_pairs={{0,8},{1,9},{2,10},{3,11},{4,12},{5,13},{6,14},{7,15},{8,0},{9,1},... | collective-permute-start | bytes 884744 | tf_op jit(solution)/shard_map/ppermute | solution.py:13
  236.0 8.8 %collective-permute-start.53 = (bf16[144,512]{1,0:T(8,128)(2,1)S(1)}, bf16[144,512]{1,0:T(8,128)(2,1)S(1)}, u32[]{:S(2)}, u32[]{:S(2)}) collective-permute-start(bf16[144,512]{1,0:T(8,128)(2,1)S(1)} %fusion.35), channel_id=1, source_target_pairs={{0,16},{1,17},{2,18},{3,19},{4,20},{5,21},{6,22},{7,23},{8,24},{9,... | collective-permute-start | bytes 442376 | tf_op jit(solution)/shard_map/ppermute | solution.py:13
  238.4 15.1 %collective-permute-start.61 = (bf16[64,2048]{1,0:T(8,128)(2,1)S(1)}, bf16[64,2048]{1,0:T(8,128)(2,1)S(1)}, u32[]{:S(2)}, u32[]{:S(2)}) collective-permute-start(bf16[64,2048]{1,0:T(8,128)(2,1)S(1)} %fusion.30), channel_id=1, source_target_pairs={{0,4},{1,3},{2,6},{3,1},{4,0},{5,7},{6,2},{7,5},{8,12},{9,11},{10,... | collective-permute-start | bytes 786440 | tf_op jit(solution)/shard_map/ppermute | solution.py:13
  244.8 5.0 %collective-permute-start.54 = (bf16[144,512]{1,0:T(8,128)(2,1)S(1)}, bf16[144,512]{1,0:T(8,128)(2,1)S(1)}, u32[]{:S(2)}, u32[]{:S(2)}) collective-permute-start(bf16[144,512]{1,0:T(8,128)(2,1)S(1)} %fusion.28), channel_id=1, source_target_pairs={{0,16},{1,17},{2,18},{3,19},{4,20},{5,21},{6,22},{7,23},{8,24},{9,... | collective-permute-start | bytes 442376 | tf_op jit(solution)/shard_map/ppermute | solution.py:13
  245.3 16.2 %collective-permute-start.40 = (bf16[512,512]{1,0:T(8,128)(2,1)S(1)}, bf16[512,512]{1,0:T(8,128)(2,1)S(1)}, u32[]{:S(2)}, u32[]{:S(2)}) collective-permute-start(bf16[512,512]{1,0:T(8,128)(2,1)S(1)} %fusion.25), channel_id=1, source_target_pairs={{0,2},{1,5},{2,0},{3,7},{4,6},{5,1},{6,4},{7,3},{8,10},{9,13},{10,... | collective-permute-start | bytes 1572872 | tf_op jit(solution)/shard_map/ppermute | solution.py:13
  249.9 8.2 %collective-permute-start.55 = (bf16[288,512]{1,0:T(8,128)(2,1)S(1)}, bf16[288,512]{1,0:T(8,128)(2,1)S(1)}, u32[]{:S(2)}, u32[]{:S(2)}) collective-permute-start(bf16[288,512]{1,0:T(8,128)(2,1)S(1)} %bitcast_select_fusion.9), channel_id=1, source_target_pairs={{0,8},{1,9},{2,10},{3,11},{4,12},{5,13},{6,14},{7,15},{8,0},{9,1},... | collective-permute-start | bytes 884744 | tf_op jit(solution)/shard_map/ppermute | solution.py:13
  258.2 9.1 %collective-permute-start.56 = (bf16[576,512]{1,0:T(8,128)(2,1)S(1)}, bf16[576,512]{1,0:T(8,128)(2,1)S(1)}, u32[]{:S(2)}, u32[]{:S(2)}) collective-permute-start(bf16[576,512]{1,0:T(8,128)(2,1)S(1)} %bitcast_select_fusion.6), channel_id=1, source_target_pairs={{0,4},{1,3},{2,6},{3,1},{4,0},{5,7},{6,2},{7,5},{8,12},{9,11},{10,... | collective-permute-start | bytes 1769480 | tf_op jit(solution)/shard_map/ppermute | solution.py:13
  259.5 8.9 %collective-permute-start.62 = (bf16[32,2048]{1,0:T(8,128)(2,1)S(1)}, bf16[32,2048]{1,0:T(8,128)(2,1)S(1)}, u32[]{:S(2)}, u32[]{:S(2)}) collective-permute-start(bf16[32,2048]{1,0:T(8,128)(2,1)S(1)} %fusion.37), channel_id=1, source_target_pairs={{0,8},{1,9},{2,10},{3,11},{4,12},{5,13},{6,14},{7,15},{8,0},{9,1},... | collective-permute-start | bytes 393224 | tf_op jit(solution)/shard_map/ppermute | solution.py:13
  261.7 8.4 %collective-permute-start.41 = (bf16[256,512]{1,0:T(8,128)(2,1)S(1)}, bf16[256,512]{1,0:T(8,128)(2,1)S(1)}, u32[]{:S(2)}, u32[]{:S(2)}) collective-permute-start(bf16[256,512]{1,0:T(8,128)(2,1)S(1)} %fusion.29), channel_id=1, source_target_pairs={{0,4},{1,3},{2,6},{3,1},{4,0},{5,7},{6,2},{7,5},{8,12},{9,11},{10,... | collective-permute-start | bytes 786440 | tf_op jit(solution)/shard_map/ppermute | solution.py:13
  267.6 20.1 %collective-permute-start.57 = (bf16[1152,512]{1,0:T(8,128)(2,1)S(1)}, bf16[1152,512]{1,0:T(8,128)(2,1)S(1)}, u32[]{:S(2)}, u32[]{:S(2)}) collective-permute-start(bf16[1152,512]{1,0:T(8,128)(2,1)S(1)} %bitcast_select_fusion.3), channel_id=1, source_target_pairs={{0,2},{1,5},{2,0},{3,7},{4,6},{5,1},{6,4},{7,3},{8,10},{9,13},{10,... | collective-permute-start | bytes 3538952 | tf_op jit(solution)/shard_map/ppermute | solution.py:13
  270.2 4.7 %collective-permute-start.42 = (bf16[128,512]{1,0:T(8,128)(2,1)S(1)}, bf16[128,512]{1,0:T(8,128)(2,1)S(1)}, u32[]{:S(2)}, u32[]{:S(2)}) collective-permute-start(bf16[128,512]{1,0:T(8,128)(2,1)S(1)} %fusion.36), channel_id=1, source_target_pairs={{0,8},{1,9},{2,10},{3,11},{4,12},{5,13},{6,14},{7,15},{8,0},{9,1},... | collective-permute-start | bytes 393224 | tf_op jit(solution)/shard_map/ppermute | solution.py:13
  272.2 20.8 %collective-permute-start.63 = (bf16[16,2048]{1,0:T(8,128)(2,1)S(1)}, bf16[16,2048]{1,0:T(8,128)(2,1)S(1)}, u32[]{:S(2)}, u32[]{:S(2)}) collective-permute-start(bf16[16,2048]{1,0:T(8,128)(2,1)S(1)} %fusion.41), channel_id=1, source_target_pairs={{0,16},{1,17},{2,18},{3,19},{4,20},{5,21},{6,22},{7,23},{8,24},{9,... | collective-permute-start | bytes 196616 | tf_op jit(solution)/shard_map/ppermute | solution.py:13
  275.1 18.1 %collective-permute-start.43 = (bf16[64,512]{1,0:T(8,128)(2,1)S(1)}, bf16[64,512]{1,0:T(8,128)(2,1)S(1)}, u32[]{:S(2)}, u32[]{:S(2)}) collective-permute-start(bf16[64,512]{1,0:T(8,128)(2,1)S(1)} %fusion.40), channel_id=1, source_target_pairs={{0,16},{1,17},{2,18},{3,19},{4,20},{5,21},{6,22},{7,23},{8,24},{9,... | collective-permute-start | bytes 196616 | tf_op jit(solution)/shard_map/ppermute | solution.py:13
  289.6 83.3 %collective-permute-start.58 = (bf16[2304,512]{1,0:T(8,128)(2,1)}, bf16[2304,512]{1,0:T(8,128)(2,1)}, u32[]{:S(2)}, u32[]{:S(2)}) collective-permute-start(bf16[2304,512]{1,0:T(8,128)(2,1)} %bitcast_select_fusion), channel_id=1, source_target_pairs={{0,1},{1,0},{2,3},{3,2},{4,5},{5,4},{6,7},{7,6},{8,9},{9,8},{10,11... | collective-permute-start | bytes 7077896 | tf_op jit(solution)/shard_map/ppermute | solution.py:13
  293.0 6.2 %collective-permute-start.64 = (bf16[16,2048]{1,0:T(8,128)(2,1)S(1)}, bf16[16,2048]{1,0:T(8,128)(2,1)S(1)}, u32[]{:S(2)}, u32[]{:S(2)}) collective-permute-start(bf16[16,2048]{1,0:T(8,128)(2,1)S(1)} %fusion.38), channel_id=1, source_target_pairs={{0,16},{1,17},{2,18},{3,19},{4,20},{5,21},{6,22},{7,23},{8,24},{9,... | collective-permute-start | bytes 196616 | tf_op jit(solution)/shard_map/ppermute | solution.py:13
  293.2 7.5 %collective-permute-start.44 = (bf16[64,512]{1,0:T(8,128)(2,1)S(1)}, bf16[64,512]{1,0:T(8,128)(2,1)S(1)}, u32[]{:S(2)}, u32[]{:S(2)}) collective-permute-start(bf16[64,512]{1,0:T(8,128)(2,1)S(1)} %fusion.39), channel_id=1, source_target_pairs={{0,16},{1,17},{2,18},{3,19},{4,20},{5,21},{6,22},{7,23},{8,24},{9,... | collective-permute-start | bytes 196616 | tf_op jit(solution)/shard_map/ppermute | solution.py:13
  299.3 3.9 %collective-permute-start.65 = (bf16[32,2048]{1,0:T(8,128)(2,1)S(1)}, bf16[32,2048]{1,0:T(8,128)(2,1)S(1)}, u32[]{:S(2)}, u32[]{:S(2)}) collective-permute-start(bf16[32,2048]{1,0:T(8,128)(2,1)S(1)} %bitcast_select_fusion.12), channel_id=1, source_target_pairs={{0,8},{1,9},{2,10},{3,11},{4,12},{5,13},{6,14},{7,15},{8,0},{9,1},... | collective-permute-start | bytes 393224 | tf_op jit(solution)/shard_map/ppermute | solution.py:13
  300.7 5.5 %collective-permute-start.45 = (bf16[128,512]{1,0:T(8,128)(2,1)S(1)}, bf16[128,512]{1,0:T(8,128)(2,1)S(1)}, u32[]{:S(2)}, u32[]{:S(2)}) collective-permute-start(bf16[128,512]{1,0:T(8,128)(2,1)S(1)} %bitcast_select_fusion.13), channel_id=1, source_target_pairs={{0,8},{1,9},{2,10},{3,11},{4,12},{5,13},{6,14},{7,15},{8,0},{9,1},... | collective-permute-start | bytes 393224 | tf_op jit(solution)/shard_map/ppermute | solution.py:13
  303.3 6.3 %collective-permute-start.66 = (bf16[64,2048]{1,0:T(8,128)(2,1)S(1)}, bf16[64,2048]{1,0:T(8,128)(2,1)S(1)}, u32[]{:S(2)}, u32[]{:S(2)}) collective-permute-start(bf16[64,2048]{1,0:T(8,128)(2,1)S(1)} %bitcast_select_fusion.10), channel_id=1, source_target_pairs={{0,4},{1,3},{2,6},{3,1},{4,0},{5,7},{6,2},{7,5},{8,12},{9,11},{10,... | collective-permute-start | bytes 786440 | tf_op jit(solution)/shard_map/ppermute | solution.py:13
  306.3 6.3 %collective-permute-start.46 = (bf16[256,512]{1,0:T(8,128)(2,1)S(1)}, bf16[256,512]{1,0:T(8,128)(2,1)S(1)}, u32[]{:S(2)}, u32[]{:S(2)}) collective-permute-start(bf16[256,512]{1,0:T(8,128)(2,1)S(1)} %bitcast_select_fusion.11), channel_id=1, source_target_pairs={{0,4},{1,3},{2,6},{3,1},{4,0},{5,7},{6,2},{7,5},{8,12},{9,11},{10,... | collective-permute-start | bytes 786440 | tf_op jit(solution)/shard_map/ppermute | solution.py:13
  309.7 11.7 %collective-permute-start.67 = (bf16[128,2048]{1,0:T(8,128)(2,1)S(1)}, bf16[128,2048]{1,0:T(8,128)(2,1)}, u32[]{:S(2)}, u32[]{:S(2)}) collective-permute-start(bf16[128,2048]{1,0:T(8,128)(2,1)S(1)} %bitcast_select_fusion.7), channel_id=1, source_target_pairs={{0,2},{1,5},{2,0},{3,7},{4,6},{5,1},{6,4},{7,3},{8,10},{9,13},{10,... | collective-permute-start | bytes 1572872 | tf_op jit(solution)/shard_map/ppermute | solution.py:13
  313.6 13.4 %collective-permute-start.47 = (bf16[512,512]{1,0:T(8,128)(2,1)}, bf16[512,512]{1,0:T(8,128)(2,1)}, u32[]{:S(2)}, u32[]{:S(2)}) collective-permute-start(bf16[512,512]{1,0:T(8,128)(2,1)} %bitcast_select_fusion.8), channel_id=1, source_target_pairs={{0,2},{1,5},{2,0},{3,7},{4,6},{5,1},{6,4},{7,3},{8,10},{9,13},{10,... | collective-permute-start | bytes 1572872 | tf_op jit(solution)/shard_map/ppermute | solution.py:13
  322.7 42.5 %collective-permute-start.68 = (bf16[256,2048]{1,0:T(8,128)(2,1)S(1)}, bf16[256,2048]{1,0:T(8,128)(2,1)}, u32[]{:S(2)}, u32[]{:S(2)}) collective-permute-start(bf16[256,2048]{1,0:T(8,128)(2,1)S(1)} %bitcast_select_fusion.4), channel_id=1, source_target_pairs={{0,1},{1,0},{2,3},{3,2},{4,5},{5,4},{6,7},{7,6},{8,9},{9,8},{10,11... | collective-permute-start | bytes 3145736 | tf_op jit(solution)/shard_map/ppermute | solution.py:13
  329.4 39.5 %collective-permute-start.48 = (bf16[1024,512]{1,0:T(8,128)(2,1)}, bf16[1024,512]{1,0:T(8,128)(2,1)}, u32[]{:S(2)}, u32[]{:S(2)}) collective-permute-start(bf16[1024,512]{1,0:T(8,128)(2,1)} %bitcast_select_fusion.5), channel_id=1, source_target_pairs={{0,1},{1,0},{2,3},{3,2},{4,5},{5,4},{6,7},{7,6},{8,9},{9,8},{10,11... | collective-permute-start | bytes 3145736 | tf_op jit(solution)/shard_map/ppermute | solution.py:13
  (73 other events, 751.2 us)
Sparse Core Ops, SparseCore 0:
  332.1 27.8 all-reduce.3

commit v2 on v1

v2 whole, which is shorter than its diff:
```python
import jax
import jax.numpy as jnp
from jax import lax
from jax.experimental import pallas as pl
from jax.experimental.pallas import tpu as pltpu
from jax.sharding import PartitionSpec as P

EPSILON = 1e-05
AXES = ("img", "rows")
MIB = 1 << 20
LOW = jnp.bfloat16
FULL = jnp.float32
GROUP = 16


def swap(value, flips):
    count = lax.axis_size(AXES)
    return lax.ppermute(value, AXES, [(i, i ^ flips[i & 1]) for i in range(count)])


def bits():
    count, found = lax.axis_size(AXES), []
    while (1 << len(found)) < count:
        found.append(1 << len(found))
    return found


def sum_all(value):
    for bit in bits():
        value = value + swap(value, (bit, bit))
    return value


def flat_index():
    return lax.axis_index("img") * lax.axis_size("rows") + lax.axis_index("rows")


def plan():
    order = bits()
    steps = [(bit, bit) for bit in order]
    if len(order) >= 3:
        steps[1], steps[2] = (order[1], order[2]), (order[2], order[1])
    index = flat_index()
    low = index % 2
    chosen = []
    for even, odd in steps:
        chosen.append(((even, odd), jnp.where(low == 0, index // even % 2, index // odd % 2)))
    return chosen


def half_of(value, which):
    size = value.shape[0] // 2
    return lax.dynamic_slice_in_dim(value, which * size, size, axis=0)


def sum_scatter(value):
    for flips, mine in plan():
        sent = half_of(value, 1 - mine).astype(LOW)
        value = half_of(value, mine) + swap(sent, flips).astype(FULL)
    return value


def gather_back(value):
    value = value.astype(LOW)
    half = jnp.arange(2).reshape(2, 1, 1)
    for flips, mine in reversed(plan()):
        other = swap(value, flips)
        value = jnp.where(half == mine, value[None], other[None]).reshape(-1, value.shape[1])
    return value


def sum_rows_axis(value):
    count, bit = lax.axis_size("rows"), 1
    while bit < count:
        value = value + lax.ppermute(value, "rows", [(i, i ^ bit) for i in range(count)])
        bit *= 2
    return value


def rim(block):
    count = lax.axis_size("rows")
    odd = lax.axis_index("rows") % 2 == 1
    top, bottom = block[:, :1], block[:, -1:]
    first = lax.ppermute(jnp.where(odd, top, bottom), "rows", [(i, i ^ 1) for i in range(count)])
    pairs = [(i, i + 1) for i in range(1, count - 1, 2)]
    second = lax.ppermute(
        jnp.where(odd, bottom, top), "rows", pairs + [(b, a) for a, b in pairs]
    )
    return jnp.where(odd, first, second), jnp.where(odd, second, first)


def call(kernel, outs, *args):
    vmem = pl.BlockSpec(memory_space=pltpu.VMEM)
    return pl.pallas_call(
        kernel,
        out_shape=[jax.ShapeDtypeStruct(shape, kind) for shape, kind in outs],
        in_specs=[vmem] * len(args),
        out_specs=[vmem] * len(outs),
        compiler_params=pltpu.CompilerParams(vmem_limit_bytes=48 * MIB),
    )(*args)


def logistic(values):
    return 1.0 / (1.0 + jnp.exp(-values))


def slope(values):
    s = logistic(values)
    return s * (1.0 + values * (1.0 - s))


def shifted(values, by):
    return pltpu.roll(values, (-by) % values.shape[0], 0)


def spread(images, height, width, main, above, below):
    channels = main.shape[-1]
    main = main.reshape(images, height, width, channels)
    above = above.reshape(images, 1, width, channels)
    below = below.reshape(images, 1, width, channels)
    flat = (images * height * width, channels)
    return (
        jnp.concatenate([above, main[:, :-1]], axis=1).reshape(flat),
        main.reshape(flat),
        jnp.concatenate([main[:, 1:], below], axis=1).reshape(flat),
    )


def mid_forward(dims, first, above, below, mask, mask_above, mask_below, scale, shift, weight, x3, second, sums):
    def act(hidden, inside):
        pre = hidden[...] * scale[...] + shift[...]
        return pre * logistic(pre) * inside[...]

    three = spread(*dims, act(first, mask), act(above, mask_above), act(below, mask_below))
    for i in range(3):
        x3[i] = three[i].astype(LOW)
    total = None
    for j in range(3):
        part = None
        for i in range(3):
            term = jnp.dot(x3[i], weight[i, j], preferred_element_type=FULL)
            part = term if part is None else part + term
        part = shifted(part, j - 1) if j != 1 else part
        total = part if total is None else total + part
    second[...] = total
    masked = total * mask[...]
    sums[0:1] = jnp.sum(masked, axis=0, keepdims=True)
    sums[1:2] = jnp.sum(masked * total, axis=0, keepdims=True)


def mid_weights(x3, grad, total):
    groups, _, size, channels = total.shape
    for j in range(3):
        turned = grad[...].astype(FULL)
        turned = shifted(turned, 1 - j) if j != 1 else turned
        turned = turned.astype(LOW)
        for i in range(3):
            part = lax.dot_general(
                x3[i], turned, (((0,), (0,)), ((), ())), preferred_element_type=FULL
            )
            total[:, 3 * i + j] = part.reshape(groups, size, channels)


def mid_backward(dims, grad, above, below, first, mask, scale, shift, average, inv_std, weight, pre_grad, sums):
    def flat(ref):
        return ref[...].astype(FULL)

    three = spread(*dims, flat(grad), flat(above), flat(below))
    low = [part.astype(LOW) for part in three]
    total = None
    for j in range(3):
        part = None
        for i in range(3):
            term = lax.dot_general(
                low[2 - i], weight[i, j], (((1,), (1,)), ((), ())), preferred_element_type=FULL
            )
            part = term if part is None else part + term
        part = shifted(part, 1 - j) if j != 1 else part
        total = part if total is None else total + part
    hidden = first[...]
    pre = hidden * scale[...] + shift[...]
    total = total * mask[...] * slope(pre)
    pre_grad[...] = total
    normed = (hidden - average[...]) * inv_std[...]
    sums[0:1] = jnp.sum(total, axis=0, keepdims=True)
    sums[1:2] = jnp.sum(total * normed, axis=0, keepdims=True)


def dot(left, right):
    return jnp.dot(left, right, preferred_element_type=FULL)


def contract(left, right):
    return lax.dot_general(left, right, (((0,), (0,)), ((), ())), preferred_element_type=FULL)


def times_transpose(left, weights):
    return lax.dot_general(left, weights, (((1,), (1,)), ((), ())), preferred_element_type=FULL)


def both(values, others):
    return jnp.stack([jnp.sum(values, axis=0), jnp.sum(values * others, axis=0)])


def moments(sums, pixel_count):
    average = sums[0] / pixel_count
    inv_std = lax.rsqrt(sums[1] / pixel_count - average * average + EPSILON)
    return average, inv_std


def norm_back(grad_z, normed, gain, inv_std, sums, pixel_count, mask):
    return mask * (gain * inv_std) * (grad_z - (sums[0] + normed * sums[1]) / pixel_count)


def per_device(
    features,
    weight_in,
    gain_in,
    bias_in,
    weight_mid,
    gain_mid,
    bias_mid,
    weight_out,
    gain_out,
    bias_out,
    map_size,
    out_grad,
    pool_grad,
):
    images, height, width, channels = features.shape
    middle = weight_mid.shape[3]
    dims = (images, height, width)
    pixels = images * height * width

    def inside_rows(start, count):
        rows = start + jnp.arange(count)
        sizes = map_size[:, None, None]
        inside = (rows[None, :, None] >= 0) & (rows[None, :, None] < sizes)
        inside = inside & (jnp.arange(width)[None, None, :] < sizes)
        return inside.astype(FULL).reshape(-1, 1)

    start = lax.axis_index("rows") * height
    mask = inside_rows(start, height)
    mask_above = inside_rows(start - 1, 1)
    mask_below = inside_rows(start + height, 1)
    area = (map_size * map_size).astype(FULL)[:, None]
    flat_features = features.reshape(pixels, channels)

    first = dot(flat_features, weight_in)
    sums = jnp.concatenate(
        [both(first * mask, first), jnp.broadcast_to(jnp.sum(mask), (1, middle))], axis=0
    )
    above, below = rim(first.reshape(images, height, width, middle))
    sums = sum_all(sums)
    pixel_count = sums[2, 0]
    first_avg, first_std = moments(sums, pixel_count)
    first_scale = first_std * gain_in
    first_shift = bias_in - first_avg * first_scale
    x3, second, sums = call(
        lambda *refs: mid_forward(dims, *refs),
        [((3, pixels, middle), LOW), ((pixels, middle), FULL), ((2, middle), FULL)],
        first,
        above.reshape(-1, middle),
        below.reshape(-1, middle),
        mask,
        mask_above,
        mask_below,
        first_scale[None],
        first_shift[None],
        weight_mid,
    )
    second_avg, second_std = moments(sum_all(sums), pixel_count)
    second_normed = (second - second_avg) * second_std
    second_pre = gain_mid * second_normed + bias_mid
    second_act = (second_pre * logistic(second_pre) * mask).astype(LOW)
    third = dot(second_act, weight_out)
    third_avg, third_std = moments(sum_all(both(third * mask, third)), pixel_count)
    third_normed = (third - third_avg) * third_std
    summed = gain_out * third_normed + bias_out + flat_features.astype(FULL)
    gate = logistic(summed)
    result = summed * gate * mask
    pooled = jnp.sum(result.reshape(images, height * width, channels), axis=1)
    pooled = sum_rows_axis(pooled.astype(LOW).astype(FULL)) / area

    total_grad = out_grad.astype(FULL) + (pool_grad / area)[:, None, None, :]
    grad_summed = total_grad.reshape(pixels, channels) * mask * (gate * (1.0 + summed * (1.0 - gate)))
    sums_out = sum_all(both(grad_summed, third_normed))
    grad_third = norm_back(
        grad_summed, third_normed, gain_out, third_std, sums_out, pixel_count, mask
    ).astype(LOW)
    grad_second_act = times_transpose(grad_third, weight_out)
    grad_second_pre = grad_second_act * mask * slope(second_pre)
    sums_mid = sum_all(both(grad_second_pre, second_normed))
    grad_second = norm_back(
        grad_second_pre, second_normed, gain_mid, second_std, sums_mid, pixel_count, mask
    ).astype(LOW)
    above, below = rim(grad_second.reshape(images, height, width, middle))
    grad_first_pre, sums_in = call(
        lambda *refs: mid_backward(dims, *refs),
        [((pixels, middle), FULL), ((2, middle), FULL)],
        grad_second,
        above.reshape(-1, middle),
        below.reshape(-1, middle),
        first,
        mask,
        first_scale[None],
        first_shift[None],
        first_avg[None],
        first_std[None],
        weight_mid,
    )
    sums_in = sum_all(sums_in)
    first_normed = (first - first_avg) * first_std
    grad_first = norm_back(
        grad_first_pre, first_normed, gain_in, first_std, sums_in, pixel_count, mask
    ).astype(LOW)
    grad_features = grad_summed + times_transpose(grad_first, weight_in)

    grad_weight_out = contract(second_act, grad_third)
    (grad_weight_mid,) = call(
        mid_weights,
        [((middle // GROUP, 9, GROUP, middle), FULL)],
        x3,
        grad_second,
    )
    grad_weight_mid = grad_weight_mid.reshape(-1, middle)
    grad_weight_in = contract(flat_features, grad_first)
    grad_weight_out = gather_back(sum_scatter(grad_weight_out)).astype(FULL)
    grad_weight_mid = gather_back(sum_scatter(grad_weight_mid)).astype(FULL)
    grad_weight_mid = grad_weight_mid.reshape(-1, 9, GROUP, middle).transpose(1, 0, 2, 3)
    grad_weight_mid = grad_weight_mid.reshape(weight_mid.shape)
    grad_weight_in = gather_back(sum_scatter(grad_weight_in)).astype(FULL)
    whole = (images, height, width, channels)
    return (
        result.astype(LOW).reshape(whole),
        pooled,
        grad_features.reshape(whole),
        grad_weight_in,
        sums_in[1],
        sums_in[0],
        grad_weight_mid,
        sums_mid[1],
        sums_mid[0],
        grad_weight_out,
        sums_out[1],
        sums_out[0],
    )


def solution(mesh):
    tiles, single = P("img", "rows", None, None), P()
    return jax.shard_map(
        per_device,
        mesh=mesh,
        in_specs=(tiles,) + (single,) * 9 + (P("img"), tiles, P("img", None)),
        out_specs=(tiles, P("img", None), tiles) + (single,) * 9,
        check_vma=False,
    )
```

time: 391 us -> 315 us (0.81)
  local copies, waits for them, and re-layouts: 59.4 us -> 22 us
  between operations: 19.3 us -> 1.98 us
  Pallas kernels: 0 us -> 13.3 us
  starting transfers between devices: 124 us -> 112 us
  waiting for transfers between devices: 125 us -> 116 us
  matrix products: 18.4 us -> 10.7 us
    psum x1 -> x0, waiting for transfers between devices: 27.7 us -> none  [per_device(): lax.psum(jnp.sum(result, axis=(1, 2)).astype(jnp.bfloat16), 'rows')]
    unnamed x115 -> x52, local copies, waits for them, and re-layouts: 16.9 us -> 2.03 us
    pallas_call x0 -> x3, Pallas kernels: none -> 13.3 us  [call(): pl.pallas_call(kernel, out_shape=[jax.ShapeDtypeStruct(shape, kind) for s...]
    dynamic_slice x3 -> x0, local copies, waits for them, and re-layouts: 13.1 us -> none  [the longest x2 9.86 us: sum_scatter(): kept = lax.dynamic_index_in_dim(halves, mine, 0, keepdims=False)]
    ppermute x65 -> x60, waiting for transfers between devices: 95.7 us -> 109 us  [swap(): lax.ppermute(value, AXES, [(i, i ^ flips[i & 1]) for i in range(count)])]
    dot_general x9 -> x6, matrix products: 18.4 us -> 10.7 us  [the longest x2 5.54 us: times_transpose(): lax.dot_general(left, weights, (((1,), (1,)), ((), ())), preferred_elemen...]
    ppermute x65 -> x60, starting transfers between devices: 104 us -> 96.4 us  [swap(): lax.ppermute(value, AXES, [(i, i ^ flips[i & 1]) for i in range(count)])]
    add x13 -> x15, other arithmetic: 11.2 us -> 5.76 us  [the longest x12 5.51 us: sum_scatter(): value = half_of(value, mine) + swap(sent, flips).astype(FULL)]
  transfers between devices with their start and end apart: 70 -> 66, of which waited for: 49 -> 50; matrix products, arithmetic and copies ran while one was open for 24% -> 10% of each run, Pallas kernels for 0% -> 1%
where the time goes in v2:
time: 315 us; the launch traced here: 314 us
  waiting for transfers between devices  116 us (37%)
  starting transfers between devices  112 us (36%)
  other arithmetic  39 us (12%)
  local copies, waits for them, and re-layouts  22 us (7%)
  Pallas kernels  13.3 us (4%)
  matrix products  10.7 us (3%)
    ppermute x60, waiting for transfers between devices, swap(): lax.ppermute(value, AXES, [(i, i ^ flips[i & 1]) for i in range(count)])  109 us
    ppermute x60, starting transfers between devices, swap(): lax.ppermute(value, AXES, [(i, i ^ flips[i & 1]) for i in range(count)])  96.4 us
    pallas_call x3, Pallas kernels, call(): pl.pallas_call(kernel, out_shape=[jax.ShapeDtypeStruct(shape, kind) for s...  13.3 us
    broadcast_in_dim x30, local copies, waits for them, and re-layouts, gather_back(): jnp.where(half == mine, value[None], other[None])  8.04 us
    select_n x12, other arithmetic, gather_back(): jnp.where(half == mine, value[None], other[None])  7.51 us
    ppermute x2, starting transfers between devices, rim(): lax.ppermute(jnp.where(odd, bottom, top), 'rows', pairs + [(b, a) for a,...  6.92 us
    ppermute x2, starting transfers between devices, sum_rows_axis(): lax.ppermute(value, 'rows', [(i, i ^ bit) for i in range(count)])  6.53 us
  transfers between devices with their start and end apart: 66, of which 50 were waited for; matrix products, arithmetic and copies ran while one was open for 10% of the time, Pallas kernels for 1%

profile of v2, /device:TPU:1, one launch (start us, length us, event | category | flops | bytes accessed | tf_op | source)
XLA Modules:
  0.0 314.3 jit_solution(13984899684299168315)
XLA Ops:
  4.0 2.7 multiply_reduce_fusion.2
  8.0 2.4 collective-permute-start.3
  15.5 3.0 collective-permute-start.1
  27.0 4.1 %shard_map.220 = (bf16[3,256,512]{2,1,0:T(8,128)(2,1)S(1)}, f32[256,512]{1,0:T(8,128)S(1)}, f32[2,512]{1,0:T(2,128)S(1)}) custom-call(f32[256,512]{1,0:T(8,128)S(1)} %get-tuple-element.62.refs_0_.refs_3_, f32[128,512]{1,0:T(8,128)S(1)} %get-tuple-element.43.refs_1_, f32[128,512]{1,0:T(8,128)S(1)} %get-tuple-element.42.refs_2_, ...), custom_call_target="tpu_custom_call" | custom-call | tf_op jit(solution)/shard_map/pallas_call | solution.py:94
  32.4 2.5 collective-permute-start.8
  45.8 4.7 %collective-permute-start.12 = (f32[2,2048]{1,0:T(2,128)S(1)}, f32[2,2048]{1,0:T(2,128)S(1)}, u32[]{:S(2)}, u32[]{:S(2)}) collective-permute-start(f32[2,2048]{1,0:T(2,128)S(1)} %pad_maximum_fusion), channel_id=1, source_target_pairs={{0,1},{1,0},{2,3},{3,2},{4,5},{5,4},{6,7},{7,6},{8,9},{9,8},{10,11... | collective-permute-start | bytes 49160 | tf_op jit(solution)/shard_map/ppermute | solution.py:18
  54.7 2.4 collective-permute-done.14
  59.7 2.4 collective-permute-start.16
  66.0 4.7 %collective-permute-start.17 = (f32[16,2048]{1,0:T(8,128)S(1)}, f32[16,2048]{1,0:T(8,128)S(1)}, u32[]{:S(2)}, u32[]{:S(2)}) collective-permute-start(f32[16,2048]{1,0:T(8,128)S(1)} %convert_element_type.312), channel_id=1, source_target_pairs={{0,1},{1,0},{2,3},{3,2},{4,5},{5,4},{6,7},{7,6},{8,9},{9,8},{10,11... | collective-permute-start | bytes 393224 | tf_op jit(solution)/shard_map/ppermute | solution.py:75
  73.6 3.6 %collective-permute-done.18 = f32[16,2048]{1,0:T(8,128)S(1)} collective-permute-done((f32[16,2048]{1,0:T(8,128)S(1)}, f32[16,2048]{1,0:T(8,128)S(1)}, u32[]{:S(2)}, u32[]{:S(2)}) %collective-permute-start.18) | collective-permute-done | bytes 131104 | tf_op jit(solution)/shard_map/ppermute | solution.py:75
  84.4 2.4 collective-permute-done.21
  96.1 5.0 %collective-permute-start.24 = (f32[2,512]{1,0:T(2,128)S(1)}, f32[2,512]{1,0:T(2,128)S(1)}, u32[]{:S(2)}, u32[]{:S(2)}) collective-permute-start(f32[2,512]{1,0:T(2,128)S(1)} %pad_maximum_fusion.2), channel_id=1, source_target_pairs={{0,1},{1,0},{2,3},{3,2},{4,5},{5,4},{6,7},{7,6},{8,9},{9,8},{10,11... | collective-permute-start | bytes 12296 | tf_op jit(solution)/shard_map/ppermute | solution.py:18
  115.8 5.2 %shard_map.222 = f32[32,9,16,512]{3,2,1,0:T(8,128)} custom-call(bf16[3,256,512]{2,1,0:T(8,128)(2,1)S(1)} %copy-done.3, bf16[256,512]{1,0:T(8,128)(2,1)S(1)} %multiply_convert_fusion.2.refs_0_.grad), custom_call_target="tpu_custom_call" | custom-call | tf_op jit(solution)/shard_map/pallas_call | solution.py:94
  121.0 4.0 %dynamic-slice_convert_fusion = bf16[2304,512]{1,0:T(8,128)(2,1)} fusion(f32[4608,512]{1,0:T(8,128)} %bitcast.150, s32[]{:T(128)S(6)} %select_n.543), kind=kLoop, calls=%fused_computation.2 | loop fusion | bytes 4718596 | tf_op jit(solution)/shard_map/convert_element_type | solution.py:58
  125.1 4.9 %collective-permute-start.46 = (bf16[2304,512]{1,0:T(8,128)(2,1)}, bf16[2304,512]{1,0:T(8,128)(2,1)}, u32[]{:S(2)}, u32[]{:S(2)}) collective-permute-start(bf16[2304,512]{1,0:T(8,128)(2,1)} %dynamic-slice_convert_fusion), channel_id=1, source_target_pairs={{0,1},{1,0},{2,3},{3,2},{4,5},{5,4},{6,7},{7,6},{8,9},{9,8},{10,11... | collective-permute-start | bytes 7077896 | tf_op jit(solution)/shard_map/ppermute | solution.py:18
  130.1 3.9 %collective-permute-start.30 = (bf16[16,1,8,512]{3,2,1,0:T(8,128)(2,1)S(1)}, bf16[16,1,8,512]{3,2,1,0:T(8,128)(2,1)S(1)}, u32[]{:S(2)}, u32[]{:S(2)}) collective-permute-start(bf16[16,1,8,512]{3,2,1,0:T(8,128)(2,1)S(1)} %get-tuple-element.48), channel_id=1, source_target_pairs={{1,2},{2,1},{5,6},{6,5},{9,10},{10,9},{13,14},{14,13},{17,18},{18,... | collective-permute-start | bytes 393224 | tf_op jit(solution)/shard_map/ppermute | solution.py:86
  136.5 4.0 %shard_map.221 = (f32[256,512]{1,0:T(8,128)S(1)}, f32[2,512]{1,0:T(2,128)S(1)}) custom-call(bf16[256,512]{1,0:T(8,128)(2,1)S(1)} %multiply_convert_fusion.2.refs_0_.grad, bf16[128,512]{1,0:T(8,128)(2,1)S(1)} %get-tuple-element.47.refs_1_, bf16[128,512]{1,0:T(8,128)(2,1)S(1)} %get-tuple-element.46.refs_2_, f32[256,512]{1,0:T(8,128)S(1)} %get-tuple-element.62.refs_0_.refs_3_, ...), custom_call_target="tpu_custom_call" | custom-call | tf_op jit(solution)/shard_map/pallas_call | solution.py:94
  148.0 3.8 %convert_add_fusion = f32[2304,512]{1,0:T(8,128)S(1)} fusion(bf16[2304,512]{1,0:T(8,128)(2,1)} %collective-permute-done.46, f32[4608,512]{1,0:T(8,128)} %bitcast.151, s32[]{:T(128)S(6)} %select_n.542), kind=kLoop, calls=%fused_computation.1 | loop fusion | flops 2359296 | bytes 11796484 | tf_op jit(solution)/shard_map/add | solution.py:59
  154.0 2.4 collective-permute-start.35
  156.6 4.0 %collective-permute-start.56 = (bf16[256,2048]{1,0:T(8,128)(2,1)S(1)}, bf16[256,2048]{1,0:T(8,128)(2,1)S(1)}, u32[]{:S(2)}, u32[]{:S(2)}) collective-permute-start(bf16[256,2048]{1,0:T(8,128)(2,1)S(1)} %dynamic-slice_convert_fusion.2), channel_id=1, source_target_pairs={{0,1},{1,0},{2,3},{3,2},{4,5},{5,4},{6,7},{7,6},{8,9},{9,8},{10,11... | collective-permute-start | bytes 3145736 | tf_op jit(solution)/shard_map/ppermute | solution.py:18
  162.2 5.2 %collective-permute-done.47 = bf16[1152,512]{1,0:T(8,128)(2,1)S(1)} collective-permute-done((bf16[1152,512]{1,0:T(8,128)(2,1)S(1)}, bf16[1152,512]{1,0:T(8,128)(2,1)S(1)}, u32[]{:S(2)}, u32[]{:S(2)}) %collective-permute-start.47) | collective-permute-done | bytes 1179680 | tf_op jit(solution)/shard_map/ppermute | solution.py:18
  170.2 4.5 %collective-permute-start.36 = (bf16[1024,512]{0,1:T(8,128)(2,1)S(1)}, bf16[1024,512]{0,1:T(8,128)(2,1)S(1)}, u32[]{:S(2)}, u32[]{:S(2)}) collective-permute-start(bf16[1024,512]{0,1:T(8,128)(2,1)S(1)} %fusion.5), channel_id=1, source_target_pairs={{0,1},{1,0},{2,3},{3,2},{4,5},{5,4},{6,7},{7,6},{8,9},{9,8},{10,11... | collective-permute-start | bytes 3145736 | tf_op jit(solution)/shard_map/ppermute | solution.py:18
  174.7 3.6 %collective-permute-done.48 = bf16[576,512]{1,0:T(8,128)(2,1)S(1)} collective-permute-done((bf16[576,512]{1,0:T(8,128)(2,1)S(1)}, bf16[576,512]{1,0:T(8,128)(2,1)S(1)}, u32[]{:S(2)}, u32[]{:S(2)}) %collective-permute-start.48) | collective-permute-done | bytes 589856 | tf_op jit(solution)/shard_map/ppermute | solution.py:18
  178.9 2.7 collective-permute-done.57
  181.7 2.8 collective-permute-done.49
  184.6 2.4 collective-permute-start.50
  188.3 2.9 collective-permute-done.50
  191.2 2.4 collective-permute-start.51
  196.7 6.9 %collective-permute-done.52 = bf16[288,512]{1,0:T(8,128)(2,1)S(1)} collective-permute-done((bf16[288,512]{1,0:T(8,128)(2,1)S(1)}, bf16[288,512]{1,0:T(8,128)(2,1)S(1)}, u32[]{:S(2)}, u32[]{:S(2)}) %collective-permute-start.52) | collective-permute-done | bytes 294944 | tf_op jit(solution)/shard_map/ppermute | solution.py:18
  203.8 5.6 %collective-permute-start.53 = (bf16[576,512]{1,0:T(8,128)(2,1)S(1)}, bf16[576,512]{1,0:T(8,128)(2,1)S(1)}, u32[]{:S(2)}, u32[]{:S(2)}) collective-permute-start(bf16[576,512]{1,0:T(8,128)(2,1)S(1)} %bitcast_select_fusion.6), channel_id=1, source_target_pairs={{0,4},{1,3},{2,6},{3,1},{4,0},{5,7},{6,2},{7,5},{8,12},{9,11},{10,... | collective-permute-start | bytes 1769480 | tf_op jit(solution)/shard_map/ppermute | solution.py:18
  209.9 6.8 %collective-permute-done.53 = bf16[576,512]{1,0:T(8,128)(2,1)S(1)} collective-permute-done((bf16[576,512]{1,0:T(8,128)(2,1)S(1)}, bf16[576,512]{1,0:T(8,128)(2,1)S(1)}, u32[]{:S(2)}, u32[]{:S(2)}) %collective-permute-start.53) | collective-permute-done | bytes 589856 | tf_op jit(solution)/shard_map/ppermute | solution.py:18
  219.7 2.9 collective-permute-start.39
  222.7 2.5 collective-permute-done.39
  226.9 14.7 %collective-permute-done.54 = bf16[1152,512]{1,0:T(8,128)(2,1)S(1)} collective-permute-done((bf16[1152,512]{1,0:T(8,128)(2,1)S(1)}, bf16[1152,512]{1,0:T(8,128)(2,1)S(1)}, u32[]{:S(2)}, u32[]{:S(2)}) %collective-permute-start.54) | collective-permute-done | bytes 1179680 | tf_op jit(solution)/shard_map/ppermute | solution.py:18
  243.5 8.1 %collective-permute-start.55 = (bf16[2304,512]{1,0:T(8,128)(2,1)}, bf16[2304,512]{1,0:T(8,128)(2,1)}, u32[]{:S(2)}, u32[]{:S(2)}) collective-permute-start(bf16[2304,512]{1,0:T(8,128)(2,1)} %bitcast_select_fusion), channel_id=1, source_target_pairs={{0,1},{1,0},{2,3},{3,2},{4,5},{5,4},{6,7},{7,6},{8,9},{9,8},{10,11... | collective-permute-start | bytes 7077896 | tf_op jit(solution)/shard_map/ppermute | solution.py:18
  251.8 2.4 collective-permute-start.41
  254.7 3.5 %collective-permute-done.61 = bf16[16,2048]{1,0:T(8,128)(2,1)S(1)} collective-permute-done((bf16[16,2048]{1,0:T(8,128)(2,1)S(1)}, bf16[16,2048]{1,0:T(8,128)(2,1)S(1)}, u32[]{:S(2)}, u32[]{:S(2)}) %collective-permute-start.61) | collective-permute-done | bytes 65568 | tf_op jit(solution)/shard_map/ppermute | solution.py:18
  258.5 2.5 collective-permute-done.41
  268.8 2.8 collective-permute-done.43
  272.7 6.3 %collective-permute-done.64 = bf16[128,2048]{1,0:T(8,128)(2,1)} collective-permute-done((bf16[128,2048]{1,0:T(8,128)(2,1)S(1)}, bf16[128,2048]{1,0:T(8,128)(2,1)}, u32[]{:S(2)}, u32[]{:S(2)}) %collective-permute-start.64) | collective-permute-done | bytes 524320 | tf_op jit(solution)/shard_map/ppermute | solution.py:18
  281.7 3.0 collective-permute-done.44
  284.7 2.4 bitcast_select_fusion.5
  288.7 3.8 %convolution_add_fusion = f32[256,2048]{1,0:T(8,128)} fusion(f32[256,2048]{1,0:T(8,128)S(1)} %copy-done.5, bf16[256,512]{1,0:T(8,128)(2,1)S(1)} %multiply_convert_fusion.1, bf16[2048,512]{1,0:T(8,128)(2,1)} %param.14), kind=kOutput, calls=%fused_computation.5 | convolution fusion | flops 537395200 | bytes 6553600 | tf_op jit(solution)/shard_map/dot_general | solution.py:198
  292.6 3.6 %fusion.1 = f32[512,2048]{1,0:T(8,128)} fusion(pred[512]{0:T(512)(128)(4,1)S(1)} %broadcast_in_dim.608, bf16[256,2048]{1,0:T(8,128)(2,1)} %collective-permute-done.65, bf16[256,2048]{1,0:T(8,128)(2,1)S(1)} %bitcast_select_fusion.4), kind=kLoop, calls=%fused_computation.11 | loop fusion | flops 2097152 | bytes 6291968 | tf_op jit(solution)/shard_map/convert_element_type | solution.py:328
  296.2 4.0 %fusion.2 = f32[2048,512]{1,0:T(8,128)} fusion(pred[2048]{0:T(1024)(128)(4,1)S(1)} %broadcast_in_dim.538, bf16[1024,512]{1,0:T(8,128)(2,1)} %collective-permute-done.45, bf16[1024,512]{1,0:T(8,128)(2,1)} %bitcast_select_fusion.5), kind=kLoop, calls=%fused_computation.13 | loop fusion | flops 2097152 | bytes 6293504 | tf_op jit(solution)/shard_map/convert_element_type | solution.py:332
  302.1 4.2 %broadcast_in_dim.603 = bf16[2,2304,512]{2,1,0:T(8,128)(2,1)} broadcast(bf16[2304,512]{1,0:T(8,128)(2,1)} %bitcast_select_fusion), dimensions={1,2} | broadcast | bytes 7077888 | tf_op jit(solution)/shard_map/jit(_where)/broadcast_in_dim | solution.py:68
  306.3 3.1 convert_bitcast_fusion
  309.4 4.9 %copy.49 = f32[9,32,16,512]{3,2,1,0:T(8,128)} copy(f32[9,32,16,512]{3,2,0,1:T(8,128)S(1)} %convert_bitcast_fusion) | data formatting | bytes 18874368 | tf_op jit(solution)/shard_map/reshape | solution.py:331
  (300 shorter events, 119.8 us)
Async XLA Ops:
  8.0 3.4 %collective-permute-start.3 = (f32[3,512]{1,0:T(4,128)S(1)}, f32[3,512]{1,0:T(4,128)S(1)}, u32[]{:S(2)}, u32[]{:S(2)}) collective-permute-start(f32[3,512]{1,0:T(4,128)S(1)} %fusion.14), channel_id=1, source_target_pairs={{0,2},{1,3},{2,0},{3,1},{4,6},{5,7},{6,4},{7,5},{8,10},{9,11},{10,... | collective-permute-start | bytes 18440 | tf_op jit(solution)/shard_map/ppermute | solution.py:18
  11.5 7.0 %collective-permute-start.4 = (f32[3,512]{1,0:T(4,128)S(1)}, f32[3,512]{1,0:T(4,128)S(1)}, u32[]{:S(2)}, u32[]{:S(2)}) collective-permute-start(f32[3,512]{1,0:T(4,128)S(1)} %fusion.39), channel_id=1, source_target_pairs={{0,4},{1,5},{2,6},{3,7},{4,0},{5,1},{6,2},{7,3},{8,12},{9,13},{10,... | collective-permute-start | bytes 18440 | tf_op jit(solution)/shard_map/ppermute | solution.py:18
  13.7 12.2 %collective-permute-start = (f32[16,1,8,512]{3,2,1,0:T(8,128)}, f32[16,1,8,512]{3,2,1,0:T(8,128)S(1)}, u32[]{:S(2)}, u32[]{:S(2)}) collective-permute-start(f32[16,1,8,512]{3,2,1,0:T(8,128)} %get-tuple-element.45), channel_id=1, source_target_pairs={{0,1},{1,0},{2,3},{3,2},{4,5},{5,4},{6,7},{7,6},{8,9},{9,8},{10,11... | collective-permute-start | bytes 786440 | tf_op jit(solution)/shard_map/ppermute | solution.py:84
  15.5 10.5 %collective-permute-start.1 = (f32[16,1,8,512]{3,2,1,0:T(8,128)S(1)}, f32[16,1,8,512]{3,2,1,0:T(8,128)}, u32[]{:S(2)}, u32[]{:S(2)}) collective-permute-start(f32[16,1,8,512]{3,2,1,0:T(8,128)S(1)} %get-tuple-element.44), channel_id=1, source_target_pairs={{1,2},{2,1},{5,6},{6,5},{9,10},{10,9},{13,14},{14,13},{17,18},{18,... | collective-permute-start | bytes 786440 | tf_op jit(solution)/shard_map/ppermute | solution.py:86
  21.1 3.6 %collective-permute-start.6 = (f32[3,512]{1,0:T(4,128)S(1)}, f32[3,512]{1,0:T(4,128)S(1)}, u32[]{:S(2)}, u32[]{:S(2)}) collective-permute-start(f32[3,512]{1,0:T(4,128)S(1)} %add.445), channel_id=1, source_target_pairs={{0,16},{1,17},{2,18},{3,19},{4,20},{5,21},{6,22},{7,23},{8,24},{9,... | collective-permute-start | bytes 18440 | tf_op jit(solution)/shard_map/ppermute | solution.py:18
  32.4 3.5 %collective-permute-start.8 = (f32[2,512]{1,0:T(2,128)S(1)}, f32[2,512]{1,0:T(2,128)S(1)}, u32[]{:S(2)}, u32[]{:S(2)}) collective-permute-start(f32[2,512]{1,0:T(2,128)S(1)} %add.448), channel_id=1, source_target_pairs={{0,2},{1,3},{2,0},{3,1},{4,6},{5,7},{6,4},{7,5},{8,10},{9,11},{10,... | collective-permute-start | bytes 12296 | tf_op jit(solution)/shard_map/ppermute | solution.py:18
  40.8 3.4 %collective-permute-start.11 = (f32[2,512]{1,0:T(2,128)S(1)}, f32[2,512]{1,0:T(2,128)S(1)}, u32[]{:S(2)}, u32[]{:S(2)}) collective-permute-start(f32[2,512]{1,0:T(2,128)S(1)} %add.451), channel_id=1, source_target_pairs={{0,16},{1,17},{2,18},{3,19},{4,20},{5,21},{6,22},{7,23},{8,24},{9,... | collective-permute-start | bytes 12296 | tf_op jit(solution)/shard_map/ppermute | solution.py:18
  45.8 5.6 %collective-permute-start.12 = (f32[2,2048]{1,0:T(2,128)S(1)}, f32[2,2048]{1,0:T(2,128)S(1)}, u32[]{:S(2)}, u32[]{:S(2)}) collective-permute-start(f32[2,2048]{1,0:T(2,128)S(1)} %pad_maximum_fusion), channel_id=1, source_target_pairs={{0,1},{1,0},{2,3},{3,2},{4,5},{5,4},{6,7},{7,6},{8,9},{9,8},{10,11... | collective-permute-start | bytes 49160 | tf_op jit(solution)/shard_map/ppermute | solution.py:18
  59.7 3.6 %collective-permute-start.16 = (f32[2,2048]{1,0:T(2,128)S(1)}, f32[2,2048]{1,0:T(2,128)S(1)}, u32[]{:S(2)}, u32[]{:S(2)}) collective-permute-start(f32[2,2048]{1,0:T(2,128)S(1)} %add.460), channel_id=1, source_target_pairs={{0,16},{1,17},{2,18},{3,19},{4,20},{5,21},{6,22},{7,23},{8,24},{9,... | collective-permute-start | bytes 49160 | tf_op jit(solution)/shard_map/ppermute | solution.py:18
  66.0 5.7 %collective-permute-start.17 = (f32[16,2048]{1,0:T(8,128)S(1)}, f32[16,2048]{1,0:T(8,128)S(1)}, u32[]{:S(2)}, u32[]{:S(2)}) collective-permute-start(f32[16,2048]{1,0:T(8,128)S(1)} %convert_element_type.312), channel_id=1, source_target_pairs={{0,1},{1,0},{2,3},{3,2},{4,5},{5,4},{6,7},{7,6},{8,9},{9,8},{10,11... | collective-permute-start | bytes 393224 | tf_op jit(solution)/shard_map/ppermute | solution.py:75
  71.8 5.4 %collective-permute-start.18 = (f32[16,2048]{1,0:T(8,128)S(1)}, f32[16,2048]{1,0:T(8,128)S(1)}, u32[]{:S(2)}, u32[]{:S(2)}) collective-permute-start(f32[16,2048]{1,0:T(8,128)S(1)} %fusion.11), channel_id=1, source_target_pairs={{0,2},{1,3},{2,0},{3,1},{4,6},{5,7},{6,4},{7,5},{8,10},{9,11},{10,... | collective-permute-start | bytes 393224 | tf_op jit(solution)/shard_map/ppermute | solution.py:75
  89.5 3.6 %collective-permute-start.23 = (f32[2,2048]{1,0:T(2,128)S(1)}, f32[2,2048]{1,0:T(2,128)S(1)}, u32[]{:S(2)}, u32[]{:S(2)}) collective-permute-start(f32[2,2048]{1,0:T(2,128)S(1)} %add.478), channel_id=1, source_target_pairs={{0,16},{1,17},{2,18},{3,19},{4,20},{5,21},{6,22},{7,23},{8,24},{9,... | collective-permute-start | bytes 49160 | tf_op jit(solution)/shard_map/ppermute | solution.py:18
  96.1 5.8 %collective-permute-start.24 = (f32[2,512]{1,0:T(2,128)S(1)}, f32[2,512]{1,0:T(2,128)S(1)}, u32[]{:S(2)}, u32[]{:S(2)}) collective-permute-start(f32[2,512]{1,0:T(2,128)S(1)} %pad_maximum_fusion.2), channel_id=1, source_target_pairs={{0,1},{1,0},{2,3},{3,2},{4,5},{5,4},{6,7},{7,6},{8,9},{9,8},{10,11... | collective-permute-start | bytes 12296 | tf_op jit(solution)/shard_map/ppermute | solution.py:18
  109.5 3.4 %collective-permute-start.28 = (f32[2,512]{1,0:T(2,128)S(1)}, f32[2,512]{1,0:T(2,128)S(1)}, u32[]{:S(2)}, u32[]{:S(2)}) collective-permute-start(f32[2,512]{1,0:T(2,128)S(1)} %add.487), channel_id=1, source_target_pairs={{0,16},{1,17},{2,18},{3,19},{4,20},{5,21},{6,22},{7,23},{8,24},{9,... | collective-permute-start | bytes 12296 | tf_op jit(solution)/shard_map/ppermute | solution.py:18
  125.1 23.0 %collective-permute-start.46 = (bf16[2304,512]{1,0:T(8,128)(2,1)}, bf16[2304,512]{1,0:T(8,128)(2,1)}, u32[]{:S(2)}, u32[]{:S(2)}) collective-permute-start(bf16[2304,512]{1,0:T(8,128)(2,1)} %dynamic-slice_convert_fusion), channel_id=1, source_target_pairs={{0,1},{1,0},{2,3},{3,2},{4,5},{5,4},{6,7},{7,6},{8,9},{9,8},{10,11... | collective-permute-start | bytes 7077896 | tf_op jit(solution)/shard_map/ppermute | solution.py:18
  130.0 4.2 %collective-permute-start.29 = (bf16[16,1,8,512]{3,2,1,0:T(8,128)(2,1)S(1)}, bf16[16,1,8,512]{3,2,1,0:T(8,128)(2,1)S(1)}, u32[]{:S(2)}, u32[]{:S(2)}) collective-permute-start(bf16[16,1,8,512]{3,2,1,0:T(8,128)(2,1)S(1)} %get-tuple-element.49), channel_id=1, source_target_pairs={{0,1},{1,0},{2,3},{3,2},{4,5},{5,4},{6,7},{7,6},{8,9},{9,8},{10,11... | collective-permute-start | bytes 393224 | tf_op jit(solution)/shard_map/ppermute | solution.py:84
  130.1 6.4 %collective-permute-start.30 = (bf16[16,1,8,512]{3,2,1,0:T(8,128)(2,1)S(1)}, bf16[16,1,8,512]{3,2,1,0:T(8,128)(2,1)S(1)}, u32[]{:S(2)}, u32[]{:S(2)}) collective-permute-start(bf16[16,1,8,512]{3,2,1,0:T(8,128)(2,1)S(1)} %get-tuple-element.48), channel_id=1, source_target_pairs={{1,2},{2,1},{5,6},{6,5},{9,10},{10,9},{13,14},{14,13},{17,18},{18,... | collective-permute-start | bytes 393224 | tf_op jit(solution)/shard_map/ppermute | solution.py:86
  146.8 7.2 %collective-permute-start.34 = (f32[2,512]{1,0:T(2,128)S(1)}, f32[2,512]{1,0:T(2,128)S(1)}, u32[]{:S(2)}, u32[]{:S(2)}) collective-permute-start(f32[2,512]{1,0:T(2,128)S(1)} %add.495), channel_id=1, source_target_pairs={{0,8},{1,9},{2,10},{3,11},{4,12},{5,13},{6,14},{7,15},{8,0},{9,1},... | collective-permute-start | bytes 12296 | tf_op jit(solution)/shard_map/ppermute | solution.py:18
  152.0 15.4 %collective-permute-start.47 = (bf16[1152,512]{1,0:T(8,128)(2,1)S(1)}, bf16[1152,512]{1,0:T(8,128)(2,1)S(1)}, u32[]{:S(2)}, u32[]{:S(2)}) collective-permute-start(bf16[1152,512]{1,0:T(8,128)(2,1)S(1)} %dynamic-slice_convert_fusion.1), channel_id=1, source_target_pairs={{0,2},{1,5},{2,0},{3,7},{4,6},{5,1},{6,4},{7,3},{8,10},{9,13},{10,... | collective-permute-start | bytes 3538952 | tf_op jit(solution)/shard_map/ppermute | solution.py:18
  154.0 6.6 %collective-permute-start.35 = (f32[2,512]{1,0:T(2,128)S(1)}, f32[2,512]{1,0:T(2,128)S(1)}, u32[]{:S(2)}, u32[]{:S(2)}) collective-permute-start(f32[2,512]{1,0:T(2,128)S(1)} %add.496), channel_id=1, source_target_pairs={{0,16},{1,17},{2,18},{3,19},{4,20},{5,21},{6,22},{7,23},{8,24},{9,... | collective-permute-start | bytes 12296 | tf_op jit(solution)/shard_map/ppermute | solution.py:18
  156.6 12.9 %collective-permute-start.56 = (bf16[256,2048]{1,0:T(8,128)(2,1)S(1)}, bf16[256,2048]{1,0:T(8,128)(2,1)S(1)}, u32[]{:S(2)}, u32[]{:S(2)}) collective-permute-start(bf16[256,2048]{1,0:T(8,128)(2,1)S(1)} %dynamic-slice_convert_fusion.2), channel_id=1, source_target_pairs={{0,1},{1,0},{2,3},{3,2},{4,5},{5,4},{6,7},{7,6},{8,9},{9,8},{10,11... | collective-permute-start | bytes 3145736 | tf_op jit(solution)/shard_map/ppermute | solution.py:18
  167.9 10.4 %collective-permute-start.48 = (bf16[576,512]{1,0:T(8,128)(2,1)S(1)}, bf16[576,512]{1,0:T(8,128)(2,1)S(1)}, u32[]{:S(2)}, u32[]{:S(2)}) collective-permute-start(bf16[576,512]{1,0:T(8,128)(2,1)S(1)} %dynamic-slice_convert_fusion.4), channel_id=1, source_target_pairs={{0,4},{1,3},{2,6},{3,1},{4,0},{5,7},{6,2},{7,5},{8,12},{9,11},{10,... | collective-permute-start | bytes 1769480 | tf_op jit(solution)/shard_map/ppermute | solution.py:18
  169.8 11.8 %collective-permute-start.57 = (bf16[128,2048]{1,0:T(8,128)(2,1)S(1)}, bf16[128,2048]{1,0:T(8,128)(2,1)S(1)}, u32[]{:S(2)}, u32[]{:S(2)}) collective-permute-start(bf16[128,2048]{1,0:T(8,128)(2,1)S(1)} %dynamic-slice_convert_fusion.5), channel_id=1, source_target_pairs={{0,2},{1,5},{2,0},{3,7},{4,6},{5,1},{6,4},{7,3},{8,10},{9,13},{10,... | collective-permute-start | bytes 1572872 | tf_op jit(solution)/shard_map/ppermute | solution.py:18
  170.2 23.4 %collective-permute-start.36 = (bf16[1024,512]{0,1:T(8,128)(2,1)S(1)}, bf16[1024,512]{0,1:T(8,128)(2,1)S(1)}, u32[]{:S(2)}, u32[]{:S(2)}) collective-permute-start(bf16[1024,512]{0,1:T(8,128)(2,1)S(1)} %fusion.5), channel_id=1, source_target_pairs={{0,1},{1,0},{2,3},{3,2},{4,5},{5,4},{6,7},{7,6},{8,9},{9,8},{10,11... | collective-permute-start | bytes 3145736 | tf_op jit(solution)/shard_map/ppermute | solution.py:18
  178.6 5.9 %collective-permute-start.49 = (bf16[288,512]{1,0:T(8,128)(2,1)S(1)}, bf16[288,512]{1,0:T(8,128)(2,1)S(1)}, u32[]{:S(2)}, u32[]{:S(2)}) collective-permute-start(bf16[288,512]{1,0:T(8,128)(2,1)S(1)} %dynamic-slice_convert_fusion.7), channel_id=1, source_target_pairs={{0,8},{1,9},{2,10},{3,11},{4,12},{5,13},{6,14},{7,15},{8,0},{9,1},... | collective-permute-start | bytes 884744 | tf_op jit(solution)/shard_map/ppermute | solution.py:18
  184.6 6.5 %collective-permute-start.50 = (bf16[144,512]{1,0:T(8,128)(2,1)S(1)}, bf16[144,512]{1,0:T(8,128)(2,1)S(1)}, u32[]{:S(2)}, u32[]{:S(2)}) collective-permute-start(bf16[144,512]{1,0:T(8,128)(2,1)S(1)} %dynamic-slice_convert_fusion.10), channel_id=1, source_target_pairs={{0,16},{1,17},{2,18},{3,19},{4,20},{5,21},{6,22},{7,23},{8,24},{9,... | collective-permute-start | bytes 442376 | tf_op jit(solution)/shard_map/ppermute | solution.py:18
  187.1 9.6 %collective-permute-start.58 = (bf16[64,2048]{1,0:T(8,128)(2,1)S(1)}, bf16[64,2048]{1,0:T(8,128)(2,1)S(1)}, u32[]{:S(2)}, u32[]{:S(2)}) collective-permute-start(bf16[64,2048]{1,0:T(8,128)(2,1)S(1)} %dynamic-slice_convert_fusion.8), channel_id=1, source_target_pairs={{0,4},{1,3},{2,6},{3,1},{4,0},{5,7},{6,2},{7,5},{8,12},{9,11},{10,... | collective-permute-start | bytes 786440 | tf_op jit(solution)/shard_map/ppermute | solution.py:18
  191.2 5.3 %collective-permute-start.51 = (bf16[144,512]{1,0:T(8,128)(2,1)S(1)}, bf16[144,512]{1,0:T(8,128)(2,1)S(1)}, u32[]{:S(2)}, u32[]{:S(2)}) collective-permute-start(bf16[144,512]{1,0:T(8,128)(2,1)S(1)} %add_convert_fusion), channel_id=1, source_target_pairs={{0,16},{1,17},{2,18},{3,19},{4,20},{5,21},{6,22},{7,23},{8,24},{9,... | collective-permute-start | bytes 442376 | tf_op jit(solution)/shard_map/ppermute | solution.py:18
  194.0 15.5 %collective-permute-start.37 = (bf16[512,512]{0,1:T(8,128)(2,1)S(1)}, bf16[512,512]{0,1:T(8,128)(2,1)S(1)}, u32[]{:S(2)}, u32[]{:S(2)}) collective-permute-start(bf16[512,512]{0,1:T(8,128)(2,1)S(1)} %dynamic-slice_convert_fusion.6), channel_id=1, source_target_pairs={{0,2},{1,5},{2,0},{3,7},{4,6},{5,1},{6,4},{7,3},{8,10},{9,13},{10,... | collective-permute-start | bytes 1572872 | tf_op jit(solution)/shard_map/ppermute | solution.py:18
  196.6 7.1 %collective-permute-start.52 = (bf16[288,512]{1,0:T(8,128)(2,1)S(1)}, bf16[288,512]{1,0:T(8,128)(2,1)S(1)}, u32[]{:S(2)}, u32[]{:S(2)}) collective-permute-start(bf16[288,512]{1,0:T(8,128)(2,1)S(1)} %bitcast_select_fusion.9), channel_id=1, source_target_pairs={{0,8},{1,9},{2,10},{3,11},{4,12},{5,13},{6,14},{7,15},{8,0},{9,1},... | collective-permute-start | bytes 884744 | tf_op jit(solution)/shard_map/ppermute | solution.py:18
  203.8 12.9 %collective-permute-start.53 = (bf16[576,512]{1,0:T(8,128)(2,1)S(1)}, bf16[576,512]{1,0:T(8,128)(2,1)S(1)}, u32[]{:S(2)}, u32[]{:S(2)}) collective-permute-start(bf16[576,512]{1,0:T(8,128)(2,1)S(1)} %bitcast_select_fusion.6), channel_id=1, source_target_pairs={{0,4},{1,3},{2,6},{3,1},{4,0},{5,7},{6,2},{7,5},{8,12},{9,11},{10,... | collective-permute-start | bytes 1769480 | tf_op jit(solution)/shard_map/ppermute | solution.py:18
  209.5 9.1 %collective-permute-start.59 = (bf16[32,2048]{1,0:T(8,128)(2,1)S(1)}, bf16[32,2048]{1,0:T(8,128)(2,1)S(1)}, u32[]{:S(2)}, u32[]{:S(2)}) collective-permute-start(bf16[32,2048]{1,0:T(8,128)(2,1)S(1)} %dynamic-slice_convert_fusion.11), channel_id=1, source_target_pairs={{0,8},{1,9},{2,10},{3,11},{4,12},{5,13},{6,14},{7,15},{8,0},{9,1},... | collective-permute-start | bytes 393224 | tf_op jit(solution)/shard_map/ppermute | solution.py:18
  209.8 9.7 %collective-permute-start.38 = (bf16[256,512]{0,1:T(8,128)(2,1)S(1)}, bf16[256,512]{0,1:T(8,128)(2,1)S(1)}, u32[]{:S(2)}, u32[]{:S(2)}) collective-permute-start(bf16[256,512]{0,1:T(8,128)(2,1)S(1)} %dynamic-slice_convert_fusion.9), channel_id=1, source_target_pairs={{0,4},{1,3},{2,6},{3,1},{4,0},{5,7},{6,2},{7,5},{8,12},{9,11},{10,... | collective-permute-start | bytes 786440 | tf_op jit(solution)/shard_map/ppermute | solution.py:18
  217.0 24.6 %collective-permute-start.54 = (bf16[1152,512]{1,0:T(8,128)(2,1)S(1)}, bf16[1152,512]{1,0:T(8,128)(2,1)S(1)}, u32[]{:S(2)}, u32[]{:S(2)}) collective-permute-start(bf16[1152,512]{1,0:T(8,128)(2,1)S(1)} %bitcast_select_fusion.3), channel_id=1, source_target_pairs={{0,2},{1,5},{2,0},{3,7},{4,6},{5,1},{6,4},{7,3},{8,10},{9,13},{10,... | collective-permute-start | bytes 3538952 | tf_op jit(solution)/shard_map/ppermute | solution.py:18
  219.7 5.6 %collective-permute-start.39 = (bf16[128,512]{0,1:T(8,128)(2,1)S(1)}, bf16[128,512]{0,1:T(8,128)(2,1)S(1)}, u32[]{:S(2)}, u32[]{:S(2)}) collective-permute-start(bf16[128,512]{0,1:T(8,128)(2,1)S(1)} %dynamic-slice_convert_fusion.13), channel_id=1, source_target_pairs={{0,8},{1,9},{2,10},{3,11},{4,12},{5,13},{6,14},{7,15},{8,0},{9,1},... | collective-permute-start | bytes 393224 | tf_op jit(solution)/shard_map/ppermute | solution.py:18
  222.6 28.9 %collective-permute-start.60 = (bf16[16,2048]{1,0:T(8,128)(2,1)S(1)}, bf16[16,2048]{1,0:T(8,128)(2,1)S(1)}, u32[]{:S(2)}, u32[]{:S(2)}) collective-permute-start(bf16[16,2048]{1,0:T(8,128)(2,1)S(1)} %dynamic-slice_convert_fusion.14), channel_id=1, source_target_pairs={{0,16},{1,17},{2,18},{3,19},{4,20},{5,21},{6,22},{7,23},{8,24},{9,... | collective-permute-start | bytes 196616 | tf_op jit(solution)/shard_map/ppermute | solution.py:18
  225.4 26.3 %collective-permute-start.40 = (bf16[64,512]{0,1:T(8,128)(2,1)S(1)}, bf16[64,512]{0,1:T(8,128)(2,1)S(1)}, u32[]{:S(2)}, u32[]{:S(2)}) collective-permute-start(bf16[64,512]{0,1:T(8,128)(2,1)S(1)} %dynamic-slice_convert_fusion.12), channel_id=1, source_target_pairs={{0,16},{1,17},{2,18},{3,19},{4,20},{5,21},{6,22},{7,23},{8,24},{9,... | collective-permute-start | bytes 196616 | tf_op jit(solution)/shard_map/ppermute | solution.py:18
  243.5 56.7 %collective-permute-start.55 = (bf16[2304,512]{1,0:T(8,128)(2,1)}, bf16[2304,512]{1,0:T(8,128)(2,1)}, u32[]{:S(2)}, u32[]{:S(2)}) collective-permute-start(bf16[2304,512]{1,0:T(8,128)(2,1)} %bitcast_select_fusion), channel_id=1, source_target_pairs={{0,1},{1,0},{2,3},{3,2},{4,5},{5,4},{6,7},{7,6},{8,9},{9,8},{10,11... | collective-permute-start | bytes 7077896 | tf_op jit(solution)/shard_map/ppermute | solution.py:18
  251.6 6.6 %collective-permute-start.61 = (bf16[16,2048]{1,0:T(8,128)(2,1)S(1)}, bf16[16,2048]{1,0:T(8,128)(2,1)S(1)}, u32[]{:S(2)}, u32[]{:S(2)}) collective-permute-start(bf16[16,2048]{1,0:T(8,128)(2,1)S(1)} %add_convert_fusion.2), channel_id=1, source_target_pairs={{0,16},{1,17},{2,18},{3,19},{4,20},{5,21},{6,22},{7,23},{8,24},{9,... | collective-permute-start | bytes 196616 | tf_op jit(solution)/shard_map/ppermute | solution.py:18
  251.8 9.2 %collective-permute-start.41 = (bf16[64,512]{0,1:T(8,128)(2,1)S(1)}, bf16[64,512]{0,1:T(8,128)(2,1)S(1)}, u32[]{:S(2)}, u32[]{:S(2)}) collective-permute-start(bf16[64,512]{0,1:T(8,128)(2,1)S(1)} %add_convert_fusion.1), channel_id=1, source_target_pairs={{0,16},{1,17},{2,18},{3,19},{4,20},{5,21},{6,22},{7,23},{8,24},{9,... | collective-permute-start | bytes 196616 | tf_op jit(solution)/shard_map/ppermute | solution.py:18
  258.3 4.7 %collective-permute-start.62 = (bf16[32,2048]{1,0:T(8,128)(2,1)S(1)}, bf16[32,2048]{1,0:T(8,128)(2,1)S(1)}, u32[]{:S(2)}, u32[]{:S(2)}) collective-permute-start(bf16[32,2048]{1,0:T(8,128)(2,1)S(1)} %bitcast_select_fusion.12), channel_id=1, source_target_pairs={{0,8},{1,9},{2,10},{3,11},{4,12},{5,13},{6,14},{7,15},{8,0},{9,1},... | collective-permute-start | bytes 393224 | tf_op jit(solution)/shard_map/ppermute | solution.py:18
  261.2 4.7 %collective-permute-start.42 = (bf16[128,512]{1,0:T(8,128)(2,1)S(1)}, bf16[128,512]{1,0:T(8,128)(2,1)S(1)}, u32[]{:S(2)}, u32[]{:S(2)}) collective-permute-start(bf16[128,512]{1,0:T(8,128)(2,1)S(1)} %bitcast_select_fusion.13), channel_id=1, source_target_pairs={{0,8},{1,9},{2,10},{3,11},{4,12},{5,13},{6,14},{7,15},{8,0},{9,1},... | collective-permute-start | bytes 393224 | tf_op jit(solution)/shard_map/ppermute | solution.py:18
  263.0 5.6 %collective-permute-start.63 = (bf16[64,2048]{1,0:T(8,128)(2,1)S(1)}, bf16[64,2048]{1,0:T(8,128)(2,1)S(1)}, u32[]{:S(2)}, u32[]{:S(2)}) collective-permute-start(bf16[64,2048]{1,0:T(8,128)(2,1)S(1)} %bitcast_select_fusion.10), channel_id=1, source_target_pairs={{0,4},{1,3},{2,6},{3,1},{4,0},{5,7},{6,2},{7,5},{8,12},{9,11},{10,... | collective-permute-start | bytes 786440 | tf_op jit(solution)/shard_map/ppermute | solution.py:18
  266.0 5.6 %collective-permute-start.43 = (bf16[256,512]{1,0:T(8,128)(2,1)S(1)}, bf16[256,512]{1,0:T(8,128)(2,1)S(1)}, u32[]{:S(2)}, u32[]{:S(2)}) collective-permute-start(bf16[256,512]{1,0:T(8,128)(2,1)S(1)} %bitcast_select_fusion.11), channel_id=1, source_target_pairs={{0,4},{1,3},{2,6},{3,1},{4,0},{5,7},{6,2},{7,5},{8,12},{9,11},{10,... | collective-permute-start | bytes 786440 | tf_op jit(solution)/shard_map/ppermute | solution.py:18
  268.8 10.3 %collective-permute-start.64 = (bf16[128,2048]{1,0:T(8,128)(2,1)S(1)}, bf16[128,2048]{1,0:T(8,128)(2,1)}, u32[]{:S(2)}, u32[]{:S(2)}) collective-permute-start(bf16[128,2048]{1,0:T(8,128)(2,1)S(1)} %bitcast_select_fusion.7), channel_id=1, source_target_pairs={{0,2},{1,5},{2,0},{3,7},{4,6},{5,1},{6,4},{7,3},{8,10},{9,13},{10,... | collective-permute-start | bytes 1572872 | tf_op jit(solution)/shard_map/ppermute | solution.py:18
  272.6 12.1 %collective-permute-start.44 = (bf16[512,512]{1,0:T(8,128)(2,1)}, bf16[512,512]{1,0:T(8,128)(2,1)}, u32[]{:S(2)}, u32[]{:S(2)}) collective-permute-start(bf16[512,512]{1,0:T(8,128)(2,1)} %bitcast_select_fusion.8), channel_id=1, source_target_pairs={{0,2},{1,5},{2,0},{3,7},{4,6},{5,1},{6,4},{7,3},{8,10},{9,13},{10,... | collective-permute-start | bytes 1572872 | tf_op jit(solution)/shard_map/ppermute | solution.py:18
  280.4 12.1 %collective-permute-start.65 = (bf16[256,2048]{1,0:T(8,128)(2,1)S(1)}, bf16[256,2048]{1,0:T(8,128)(2,1)}, u32[]{:S(2)}, u32[]{:S(2)}) collective-permute-start(bf16[256,2048]{1,0:T(8,128)(2,1)S(1)} %bitcast_select_fusion.4), channel_id=1, source_target_pairs={{0,1},{1,0},{2,3},{3,2},{4,5},{5,4},{6,7},{7,6},{8,9},{9,8},{10,11... | collective-permute-start | bytes 3145736 | tf_op jit(solution)/shard_map/ppermute | solution.py:18
  287.1 9.1 %collective-permute-start.45 = (bf16[1024,512]{1,0:T(8,128)(2,1)}, bf16[1024,512]{1,0:T(8,128)(2,1)}, u32[]{:S(2)}, u32[]{:S(2)}) collective-permute-start(bf16[1024,512]{1,0:T(8,128)(2,1)} %bitcast_select_fusion.5), channel_id=1, source_target_pairs={{0,1},{1,0},{2,3},{3,2},{4,5},{5,4},{6,7},{7,6},{8,9},{9,8},{10,11... | collective-permute-start | bytes 3145736 | tf_op jit(solution)/shard_map/ppermute | solution.py:18
  (44 other events, 353.6 us)

commit v3 on v2

v3 whole, which is shorter than its diff:
```python
import jax
import jax.numpy as jnp
from jax import lax
from jax.experimental import pallas as pl
from jax.experimental.pallas import tpu as pltpu
from jax.sharding import PartitionSpec as P

EPSILON = 1e-05
AXES = ("img", "rows")
MIB = 1 << 20
LOW = jnp.bfloat16
FULL = jnp.float32
GROUP = 16
LANES = 128


def swap(value, flips):
    count = lax.axis_size(AXES)
    return lax.ppermute(value, AXES, [(i, i ^ flips[i & 1]) for i in range(count)])


def bits():
    count, found = lax.axis_size(AXES), []
    while (1 << len(found)) < count:
        found.append(1 << len(found))
    return found


def everyone(copies):
    return lax.all_to_all(copies, AXES, 0, 0)


def sum_wide(value, *beside):
    order = bits()
    value = value + swap(value, order[:1] * 2)
    arrived = []
    for at in range(1, len(order) - 1, 2):
        p, q = order[at : at + 2]
        one, two, three = swap(value, (p, p)), swap(value, (q, q)), swap(value, (p ^ q, p ^ q))
        value = (value + one) + (two + three)
        travels = beside[len(arrived)] if len(arrived) < len(beside) else ()
        value, *came = tie(value, *(swap(*pair) for pair in travels))
        arrived.append(came)
    if len(order) % 2 == 0:
        value = value + swap(value, order[-1:] * 2)
    return value, *arrived[: len(beside)]


def tie(*values):
    return lax.optimization_barrier(values)


def flat_index():
    return lax.axis_index("img") * lax.axis_size("rows") + lax.axis_index("rows")


def plan():
    order = bits()
    steps = [(bit, bit) for bit in order]
    if len(order) >= 3:
        steps[1], steps[2] = (order[1], order[2]), (order[2], order[1])
    index = flat_index()
    low = index % 2
    chosen = []
    for even, odd in steps:
        chosen.append(((even, odd), jnp.where(low == 0, index // even % 2, index // odd % 2)))
    return chosen


def half_of(value, which, axis=0):
    size = value.shape[axis] // 2
    return lax.dynamic_slice_in_dim(value, which * size, size, axis=axis)


def stack(mine, value, other):
    low = mine == 0
    return jnp.stack([jnp.where(low, value, other), jnp.where(low, other, value)])


def scatter_step(value, step):
    _, mine = step
    return half_of(value, 1 - mine).astype(LOW), half_of(value, mine)


def merge(value, other, step):
    return stack(step[1], value, other).reshape((-1,) + value.shape[1:])


def reduce_chain(value, steps):
    for step in steps:
        sent, kept = scatter_step(value, step)
        came = yield sent, step[0]
        value = kept + came.astype(FULL)
    return value


def gather_chain(value, steps):
    for step in steps:
        came = yield value, step[0]
        value = merge(value, came, step)
    return value


def advance(chains, state, slots, extra=()):
    names = [name for name in slots if name in chains]
    came = [swap(*state[name]) for name in names]
    done = tie(*came, *extra)
    for name, value in zip(names, done):
        try:
            state[name] = chains[name].send(value)
        except StopIteration as end:
            state[name] = end.value
            del chains[name]
    return done[len(names) :]


def sum_rows_axis(value):
    count, bit = lax.axis_size("rows"), 1
    while bit < count:
        value = value + lax.ppermute(value, "rows", [(i, i ^ bit) for i in range(count)])
        bit *= 2
    return value


def rim(block):
    count = lax.axis_size("rows")
    odd = lax.axis_index("rows") % 2 == 1
    top, bottom = block[:, :1], block[:, -1:]
    near = lax.ppermute(jnp.where(odd, top, bottom), "rows", [(i, i ^ 1) for i in range(count)])
    pairs = [(i, i + 1) for i in range(1, count - 1, 2)]
    far = lax.ppermute(jnp.where(odd, bottom, top), "rows", pairs + [(b, a) for a, b in pairs])
    return near.reshape(-1, near.shape[-1]), far.reshape(-1, far.shape[-1])


def call(kernel, outs, *args, scratch=(), left=(), limit=48):
    def place(at, arg):
        if at in left:
            return pl.BlockSpec(memory_space=pltpu.HBM)
        whole = arg.dtype == jnp.int32
        return pl.BlockSpec(memory_space=pltpu.SMEM if whole else pltpu.VMEM)

    return pl.pallas_call(
        kernel,
        out_shape=[jax.ShapeDtypeStruct(shape, kind) for shape, kind in outs],
        in_specs=[place(at, arg) for at, arg in enumerate(args)],
        out_specs=[pl.BlockSpec(memory_space=pltpu.VMEM)] * len(outs),
        scratch_shapes=list(scratch),
        compiler_params=pltpu.CompilerParams(vmem_limit_bytes=limit * MIB),
    )(*args)


def logistic(values):
    return 1.0 / (1.0 + jnp.exp(-values))


def slope(values):
    s = logistic(values)
    return s * (1.0 + values * (1.0 - s))


def shifted(values, by):
    return pltpu.roll(values, (-by) % values.shape[0], 0)


def spread(images, height, width, main, above, below):
    channels = main.shape[-1]
    main = main.reshape(images, height, width, channels)
    above = above.reshape(images, 1, width, channels)
    below = below.reshape(images, 1, width, channels)
    flat = (images * height * width, channels)
    return (
        jnp.concatenate([above, main[:, :-1]], axis=1).reshape(flat),
        main.reshape(flat),
        jnp.concatenate([main[:, 1:], below], axis=1).reshape(flat),
    )


def wide(mask, like):
    return jnp.concatenate([mask] * (like.shape[1] // mask.shape[1]), axis=1)


def first_forward(
    dims, place, map_size, gain, bias, gain_mid, bias_mid, features, weight,
    first, sums, params, params_mid, areas, mask, mask_above, mask_below,
    sizes, rows, left, right, few, sems,
):
    images, height, width = dims
    lanes = mask.shape[1]
    parts = sems.shape[1]
    deep = left.shape[1] // parts
    small = [pltpu.make_async_copy(map_size, sizes, few.at[0])]
    for k, source in enumerate((gain, bias, gain_mid, bias_mid)):
        small.append(pltpu.make_async_copy(source, rows.at[k], few.at[k + 1]))
    for copy in small:
        copy.start()

    def load(k):
        span = pl.ds(k * deep, deep)
        return (
            pltpu.make_async_copy(features.at[:, span], left.at[:, span], sems.at[0, k]),
            pltpu.make_async_copy(weight.at[span, :], right.at[span, :], sems.at[1, k]),
        )

    for k in range(parts):
        for copy in load(k):
            copy.start()
    for copy in small:
        copy.wait()

    def inside(start, count):
        spot = lax.broadcasted_iota(jnp.int32, (count * width, lanes), 0)
        row, column = start + spot // width, spot % width
        parts = []
        for n in range(images):
            size = sizes[0, n]
            here = (row >= 0) & (row < size) & (column < size)
            parts.append(jnp.where(here, 1.0, 0.0))
        return jnp.concatenate(parts, axis=0)

    start = place[0, 0] * height
    kept = inside(start, height)
    mask[...] = kept
    mask_above[...] = inside(start - 1, 1)
    mask_below[...] = inside(start + height, 1)
    params[0:1], params[1:2] = rows[0], rows[1]
    params_mid[0:1], params_mid[1:2] = rows[2], rows[3]
    spot = lax.broadcasted_iota(jnp.int32, areas.shape, 0)
    area = jnp.zeros(areas.shape, FULL)
    for n in range(images):
        area = jnp.where(spot == n, (sizes[0, n] * sizes[0, n]).astype(FULL), area)
    areas[...] = area
    total = None
    for k in range(parts):
        for copy in load(k):
            copy.wait()
        span = pl.ds(k * deep, deep)
        part = jnp.dot(left[:, span], right[span, :], preferred_element_type=FULL)
        total = part if total is None else total + part
    first[...] = total
    masked = total * wide(kept, total)
    middle = total.shape[1]
    sums[:, 0, 0:middle] = spread_sum(sums, masked)
    sums[:, 1, 0:middle] = spread_sum(sums, masked * total)
    sums[:, 0, middle:] = spread_sum(sums, kept)
    sums[:, 1, middle:] = spread_sum(sums, kept)


def spread_sum(copies, values):
    total = jnp.sum(values, axis=0, keepdims=True)
    return jnp.broadcast_to(total, (copies.shape[0], total.shape[1]))


def fetch(weight, held, sems):
    def load(i, j):
        return pltpu.make_async_copy(weight.at[i, j], held.at[i, j], sems.at[i, j])

    for j in range(3):
        for i in range(3):
            load(i, j).start()

    def tap(i, j):
        load(i, j).wait()
        return held[i, j]

    return tap


def affine(sums, count, gain, bias):
    average = sums[0:1] / count
    inv_std = lax.rsqrt(sums[1:2] / count - average * average + EPSILON)
    scale = inv_std * gain
    return average, inv_std, scale, bias - average * scale


def mid_forward(
    dims, place, came, params, first, near, far, mask, mask_above, mask_below, weight,
    split, second, sums, sums_first, held, sems, edges, edge_sems,
):
    near_in = pltpu.make_async_copy(near, edges.at[0], edge_sems.at[0])
    far_in = pltpu.make_async_copy(far, edges.at[1], edge_sems.at[1])
    near_in.start()
    far_in.start()
    tap = fetch(weight, held, sems)
    middle = first.shape[1]
    totals = jnp.sum(came[...], axis=0)
    sums_first[...] = totals
    count = totals[0:1, middle : middle + 1]
    _, _, scale, shift = affine(totals[:, 0:middle], count, params[0:1], params[1:2])

    def act(hidden, inside):
        pre = hidden * scale + shift
        return pre * logistic(pre) * wide(inside[...], pre)

    odd = place[0, 0] % 2 == 1
    centre = act(first[...], mask)
    near_in.wait()
    far_in.wait()
    above = act(jnp.where(odd, edges[0], edges[1]), mask_above)
    below = act(jnp.where(odd, edges[1], edges[0]), mask_below)
    three = spread(*dims, centre, above, below)
    x3 = [part.astype(LOW) for part in three]
    flat_rows(dims, centre, split)
    total = None
    for j in range(3):
        part = None
        for i in range(3):
            term = jnp.dot(x3[i], tap(i, j), preferred_element_type=FULL)
            part = term if part is None else part + term
        part = shifted(part, j - 1) if j != 1 else part
        total = part if total is None else total + part
    second[...] = total
    masked = total * wide(mask[...], total)
    sums[:, 0] = spread_sum(sums, masked)
    sums[:, 1] = spread_sum(sums, masked * total)


def flat_rows(dims, value, out):
    images, height, width = dims
    value = value.reshape(images, height, width, -1)
    for r in range(height):
        out[r] = value[:, r].reshape(images * width, -1).astype(LOW)


def out_forward(dims, sums_first, came, params_mid, second, mask, weight, act, normed_rows, third, sums, sums_second):
    middle = second.shape[1]
    totals = jnp.sum(came[...], axis=0)
    sums_second[...] = totals
    count = sums_first[0:1, middle : middle + 1]
    average, inv_std, scale, shift = affine(totals, count, params_mid[0:1], params_mid[1:2])
    hidden = second[...]
    pre = hidden * scale + shift
    act[...] = (pre * logistic(pre) * wide(mask[...], pre)).astype(LOW)
    flat_rows(dims, (hidden - average) * inv_std, normed_rows)
    inside = wide(mask[...], hidden)
    for at in range(0, third.shape[1], middle):
        span = pl.ds(at, middle)
        total = jnp.dot(act[...], weight[:, span], preferred_element_type=FULL)
        third[:, span] = total
        masked = total * inside
        sums[0:1, span] = jnp.sum(masked, axis=0, keepdims=True)
        sums[1:2, span] = jnp.sum(masked * total, axis=0, keepdims=True)


def out_result(
    dims, sums_first, sums_third, params_out, third, features, out_grad, pool_grad, areas, mask,
    result, pooled, grad, sums,
):
    images, height, width = dims
    chunk = sums_first.shape[1] - mask.shape[1]
    count = sums_first[0:1, chunk : chunk + 1]
    inside = jnp.concatenate([mask[...]] * (chunk // mask.shape[1]), axis=1)
    area = jnp.concatenate([areas[...]] * (chunk // mask.shape[1]), axis=1)
    for at in range(0, third.shape[1], chunk):
        span = pl.ds(at, chunk)
        average, inv_std, _, _ = affine(sums_third[:, span], count, 1.0, 0.0)
        normed = (third[:, span] - average) * inv_std
        summed = params_out[0:1, span] * normed + params_out[1:2, span] + features[:, span].astype(FULL)
        gate = logistic(summed)
        value = summed * gate * inside
        result[:, span] = value.astype(LOW)
        pooled[:, span] = jnp.sum(value.reshape(images, height * width, chunk), axis=1)
        share = (pool_grad[:, span] / area)[:, None]
        total = out_grad[:, span].astype(FULL).reshape(images, height * width, chunk) + share
        total = total.reshape(inside.shape) * inside * (gate * (1.0 + summed * (1.0 - gate)))
        grad[:, span] = total
        sums[0:1, span] = jnp.sum(total, axis=0, keepdims=True)
        sums[1:2, span] = jnp.sum(total * normed, axis=0, keepdims=True)


def out_backward(
    dims, sums_first, sums_second, sums_third, sums_out, params_mid, params_out, third, grad, second, mask, weight,
    grad_third, pre_grad, rows, sums,
):
    chunk = second.shape[1]
    count = sums_first[0:1, chunk : chunk + 1]
    inside = wide(mask[...], second)
    back = None
    for at in range(0, third.shape[1], chunk):
        span = pl.ds(at, chunk)
        average, inv_std, scale, _ = affine(sums_third[:, span], count, params_out[0:1, span], 0.0)
        normed = (third[:, span] - average) * inv_std
        mean = (sums_out[0:1, span] + normed * sums_out[1:2, span]) / count
        low = (inside * scale * (grad[:, span] - mean)).astype(LOW)
        grad_third[:, span] = low
        part = lax.dot_general(
            low, weight[:, span], (((1,), (1,)), ((), ())), preferred_element_type=FULL
        )
        back = part if back is None else back + part
    average, inv_std, scale, shift = affine(sums_second[...], count, params_mid[0:1], params_mid[1:2])
    hidden = second[...]
    back = back * inside * slope(hidden * scale + shift)
    pre_grad[...] = back
    flat_rows(dims, back, rows)
    sums[:, 0] = spread_sum(sums, back)
    sums[:, 1] = spread_sum(sums, back * ((hidden - average) * inv_std))


def mid_weights(
    place, sizes, sums_first, sums_second, sums_grad, params_mid, acts, normed, grads, total, left, right
):
    groups, _, size, channels = total.shape
    pixels = acts.shape[2]
    images = sizes.shape[1]
    width = pixels // images
    swapped = place[0, 0] == 1
    middle = sums_grad.shape[1]
    count = sums_first[0:1, middle : middle + 1]
    span = pl.ds(pl.multiple_of(place[0, 1] * channels, channels), channels)
    average = sums_second[0:1, span] / count
    inv_std = lax.rsqrt(sums_second[1:2, span] / count - average * average + EPSILON)
    scale = inv_std * params_mid[0:1, span]
    mean_grad, mean_gain = sums_grad[0:1, span] / count, sums_grad[1:2, span] / count
    column = lax.broadcasted_iota(jnp.int32, (width, channels), 0)
    for y in range(2):
        for x in range(2):
            for c in range(2):
                spot = jnp.where(swapped, 4 * x + 2 * y + c, 4 * y + 2 * x + c)
                rows = pl.ds(((2 * y + x) * 2 + c) * pixels, pixels)
                for r in range(2):
                    left[r, rows, :] = acts[spot, r]
                    row = (2 * x + c) * 2 + r
                    inside = []
                    for n in range(images):
                        extent = jnp.where(row < sizes[y, n], sizes[y, n], 0)
                        inside.append(jnp.where(column < extent, 1.0, 0.0))
                    value = grads[spot, r].astype(FULL)
                    value = value - (mean_grad + normed[spot, r].astype(FULL) * mean_gain)
                    value = value * scale * jnp.concatenate(inside, axis=0)
                    right[r, rows, 0:channels] = value.astype(LOW)
    for r in range(2):
        grad = right[r, :, 0:channels].astype(FULL)
        right[r, :, channels : 2 * channels] = shifted(grad, 1).astype(LOW)
        right[r, :, 2 * channels :] = shifted(grad, -1).astype(LOW)
    span, image = 3 * pixels, 4 * pixels

    def product(r_left, at_left, r_right, at_right, count):
        return lax.dot_general(
            left[r_left, pl.ds(at_left, count), :],
            right[r_right, pl.ds(at_right, count), :],
            (((0,), (0,)), ((), ())),
            preferred_element_type=FULL,
        )

    def crossed(r_left, r_right, skip_left, skip_right):
        part = product(r_left, 0, r_right, 0, 2 * image)
        for y in range(2):
            part = part + product(
                r_right, y * image + skip_left, r_left, y * image + skip_right, span
            )
        return part

    taps = (
        crossed(0, 1, 0, pixels),
        product(0, 0, 0, 0, 2 * image) + product(1, 0, 1, 0, 2 * image),
        crossed(1, 0, pixels, 0),
    )
    for i in range(3):
        for j, place in ((1, 0), (0, 1), (2, 2)):
            part = taps[i][:, place * channels : (place + 1) * channels]
            total[:, 3 * i + j] = part.reshape(groups, size, channels)


def mid_assemble(odd, mine, other, total):
    quarters, groups, _, size, lanes = mine.shape
    half = groups * size
    swapped = odd[0, 0] == 1
    for q in range(quarters):
        a = mine[q, :, 0].astype(FULL).reshape(half, lanes)
        b = other[q, :, 0].astype(FULL).reshape(half, lanes)
        total[0, 0:half, q * lanes : (q + 1) * lanes] = jnp.where(swapped, b, a)
        total[0, half:, q * lanes : (q + 1) * lanes] = jnp.where(swapped, a, b)


def mid_backward(
    dims, place, sums_first, sums_second, came, params, params_mid, grad, near, far,
    second, second_near, second_far, first, mask, mask_above, mask_below, weight,
    pre_grad, sums, sums_mid, held, sems, edges, edge_sems,
):
    copies = []
    for k, source in enumerate((near, far, second_near, second_far)):
        copies.append(pltpu.make_async_copy(source, edges.at[k], edge_sems.at[k]))
        copies[-1].start()
    tap = fetch(weight, held, sems)
    middle = first.shape[1]
    count = sums_first[0:1, middle : middle + 1]
    totals = jnp.sum(came[...], axis=0)
    sums_mid[...] = totals
    average, inv_std, scale, shift = affine(sums_second[...], count, params_mid[0:1], params_mid[1:2])
    mean_grad, mean_gain = totals[0:1] / count, totals[1:2] / count

    def normed_grad(value, hidden, inside):
        normed = (hidden - average) * inv_std
        return wide(inside[...], value) * scale * (value - (mean_grad + normed * mean_gain))

    odd = place[0, 0] % 2 == 1

    def beside(one, other, inside):
        value = jnp.where(odd, edges[one], edges[other])
        return normed_grad(value, jnp.where(odd, edges[one + 2], edges[other + 2]), inside)

    centre = normed_grad(grad[...], second[...], mask)
    for copy in copies:
        copy.wait()
    above = beside(0, 1, mask_above)
    below = beside(1, 0, mask_below)
    three = spread(*dims, centre, above, below)
    average, inv_std, scale, shift = affine(sums_first[:, 0:middle], count, params[0:1], params[1:2])
    low = [part.astype(LOW) for part in three]
    total = None
    for j in range(3):
        part = None
        for i in range(3):
            term = lax.dot_general(
                low[2 - i], tap(i, j), (((1,), (1,)), ((), ())), preferred_element_type=FULL
            )
            part = term if part is None else part + term
        part = shifted(part, 1 - j) if j != 1 else part
        total = part if total is None else total + part
    hidden = first[...]
    total = total * wide(mask[...], total) * slope(hidden * scale + shift)
    pre_grad[...] = total
    sums[:, 0] = spread_sum(sums, total)
    sums[:, 1] = spread_sum(sums, total * ((hidden - average) * inv_std))


def first_backward(sums_first, came, params, first, grad, mask, low, sums_in):
    middle = first.shape[1]
    count = sums_first[0:1, middle : middle + 1]
    totals = jnp.sum(came[...], axis=0)
    sums_in[...] = totals
    average, inv_std, scale, _ = affine(sums_first[:, 0:middle], count, params[0:1], 0.0)
    normed = (first[...] - average) * inv_std
    value = grad[...] - (totals[0:1] + normed * totals[1:2]) / count
    low[...] = (wide(mask[...], value) * scale * value).astype(LOW)


def assemble(odd, mine, other, shape):
    groups, taps, size, lanes = shape
    quarters = mine.shape[0] // (groups * taps * size)
    channels = quarters * lanes
    pieces = pl.BlockSpec((quarters, groups, 1, size, lanes), lambda t: (0, 0, t, 0, 0))
    return pl.pallas_call(
        mid_assemble,
        grid=(taps,),
        out_shape=jax.ShapeDtypeStruct((taps, channels, channels), FULL),
        in_specs=[pl.BlockSpec(memory_space=pltpu.SMEM), pieces, pieces],
        out_specs=pl.BlockSpec((1, channels, channels), lambda t: (t, 0, 0)),
        compiler_params=pltpu.CompilerParams(vmem_limit_bytes=48 * MIB),
    )(
        odd,
        mine.reshape(quarters, groups, taps, size, lanes),
        other.reshape(quarters, groups, taps, size, lanes),
    )


def halves(value, step):
    _, mine = step
    return half_of(value, 1 - mine, 3), half_of(value, mine, 3)


def contract(left, right):
    return lax.dot_general(left, right, (((0,), (0,)), ((), ())), preferred_element_type=FULL)


def times_transpose(left, weights):
    return lax.dot_general(left, weights, (((1,), (1,)), ((), ())), preferred_element_type=FULL)


def per_device(
    features,
    weight_in,
    gain_in,
    bias_in,
    weight_mid,
    gain_mid,
    bias_mid,
    weight_out,
    gain_out,
    bias_out,
    map_size,
    out_grad,
    pool_grad,
):
    images, height, width, channels = features.shape
    middle = weight_mid.shape[3]
    dims = (images, height, width)
    pixels = images * height * width

    count = lax.axis_size(AXES)
    place = lax.axis_index("rows").astype(jnp.int32).reshape(1, 1)
    index = flat_index()
    flat_features = features.reshape(pixels, channels)
    params_out = jnp.stack([gain_out, bias_out])
    steps = plan()
    core, mine, far_steps = steps[0], steps[0][1], steps[3:]
    plane, narrow, broad = (pixels, middle), (2, middle), (2, channels)
    edge = (images * width, middle)

    def sides(value):
        return rim(value.reshape(images, height, width, middle))

    first, sums, params, params_mid, areas, mask, mask_above, mask_below = call(
        lambda *refs: first_forward(dims, *refs),
        [
            (plane, FULL),
            ((count, 2, middle + LANES), FULL),
            (narrow, FULL),
            (narrow, FULL),
            ((images, LANES), FULL),
            ((pixels, LANES), FULL),
            ((images * width, LANES), FULL),
            ((images * width, LANES), FULL),
        ],
        place,
        map_size[None],
        gain_in[None],
        bias_in[None],
        gain_mid[None],
        bias_mid[None],
        flat_features,
        weight_in,
        scratch=[
            pltpu.SMEM((1, images), jnp.int32),
            pltpu.VMEM((4, 1, middle), FULL),
            pltpu.VMEM((pixels, channels), LOW),
            pltpu.VMEM((channels, middle), LOW),
            pltpu.SemaphoreType.DMA((5,)),
            pltpu.SemaphoreType.DMA((2, 4)),
        ],
        left=(1, 2, 3, 4, 5, 6, 7),
        limit=56,
    )
    taps = [pltpu.VMEM(weight_mid.shape, LOW), pltpu.SemaphoreType.DMA((3, 3))]
    near, far = sides(first)
    came, near, far = tie(everyone(sums), near, far)
    split, second, sums, sums_first = call(
        lambda *refs: mid_forward(dims, *refs),
        [
            ((height, images * width, middle), LOW),
            (plane, FULL),
            ((count, 2, middle), FULL),
            ((2, middle + LANES), FULL),
        ],
        place,
        came,
        params,
        first,
        near,
        far,
        mask,
        mask_above,
        mask_below,
        weight_mid,
        scratch=taps + [pltpu.VMEM((2, *edge), FULL), pltpu.SemaphoreType.DMA((2,))],
        left=(4, 5, 9),
    )
    second_near, second_far = sides(second)
    acts = swap(half_of(split, 1 - mine, 2), core[0])
    sizes = map_size.astype(FULL)[None]
    other_sizes = swap(sizes, (lax.axis_size("rows"),) * 2)
    came, acts, second_near, second_far, other_sizes = tie(
        everyone(sums), acts, second_near, second_far, other_sizes
    )
    sizes = stack(lax.axis_index("img") % 2, sizes, other_sizes)[:, 0].astype(jnp.int32)
    second_act, normed, third, sums, sums_second = call(
        lambda *refs: out_forward(dims, *refs),
        [
            (plane, LOW),
            ((height, images * width, middle), LOW),
            ((pixels, channels), FULL),
            (broad, FULL),
            (narrow, FULL),
        ],
        sums_first,
        came,
        params_mid,
        second,
        mask,
        weight_out,
    )
    acts = stack(mine, half_of(split, mine, 2), acts)
    sums, acts, normed = tie(sums, acts, normed)
    sums_third, (came,), (acts_came,) = sum_wide(sums, ((normed, core[0]),), ((acts, steps[1][0]),))
    result, pooled, grad_summed, sums = call(
        lambda *refs: out_result(dims, *refs),
        [
            ((pixels, channels), LOW),
            ((images, channels), FULL),
            ((pixels, channels), FULL),
            (broad, FULL),
        ],
        sums_first,
        sums_third,
        params_out,
        third,
        flat_features,
        out_grad.reshape(pixels, channels),
        pool_grad,
        areas,
        mask,
    )

    acts = merge(acts, acts_came, steps[1])
    sent, kept = halves(stack(mine, normed, came), steps[1])
    sums, acts, sent = tie(sums, acts, sent)
    sums_out, (came,), (acts_came,) = sum_wide(
        sums, ((sent, steps[1][0]),), ((acts, steps[2][0]),)
    )
    grad_third, grad_second_pre, grads, sums = call(
        lambda *refs: out_backward(dims, *refs),
        [
            ((pixels, channels), LOW),
            (plane, FULL),
            ((height, images * width, middle), LOW),
            ((count, 2, middle), FULL),
        ],
        sums_first,
        sums_second,
        sums_third,
        sums_out,
        params_mid,
        params_out,
        third,
        grad_summed,
        second,
        mask,
        weight_out,
    )

    normed_sent, normed_kept = halves(merge(kept, came, steps[1]), steps[2])
    out_sent = contract(half_of(second_act, 1 - mine, 1), grad_third).astype(LOW)
    sums, grads, out_sent, normed_sent = tie(sums, grads, out_sent, normed_sent)
    came, out_came = swap(grads, core[0]), swap(out_sent, core[0])
    near, far = sides(grad_second_pre)
    sums = everyone(sums)
    sent, kept = halves(stack(mine, grads, came), steps[1])
    came, normed_came = swap(sent, steps[1][0]), swap(normed_sent, steps[2][0])
    out_kept = contract(half_of(second_act, mine, 1), grad_third)
    acts = merge(acts, acts_came, steps[2])
    sums, came, normed_came, out_came, out_kept, acts, near, far = tie(
        sums, came, normed_came, out_came, out_kept, acts, near, far
    )
    sent, kept = halves(merge(kept, came, steps[1]), steps[2])
    sent, sums = tie(sent, sums)
    came = swap(sent, steps[2][0])
    grad_first_pre, sums, sums_mid = call(
        lambda *refs: mid_backward(dims, *refs),
        [(plane, FULL), ((count, 2, middle), FULL), (narrow, FULL)],
        place,
        sums_first,
        sums_second,
        sums,
        params,
        params_mid,
        grad_second_pre,
        near,
        far,
        second,
        second_near,
        second_far,
        first,
        mask,
        mask_above,
        mask_below,
        weight_mid,
        scratch=taps + [pltpu.VMEM((4, *edge), FULL), pltpu.SemaphoreType.DMA((4,))],
        left=(7, 8, 10, 11, 16),
    )
    sums, came, out_came, out_kept = tie(sums, came, out_came, out_kept)
    grads = merge(kept, came, steps[2])
    normed = merge(normed_kept, normed_came, steps[2])

    odd = (index % 2).astype(jnp.int32).reshape(1, 1)
    chains, state = {}, {}

    def begin(name, chain):
        chains[name] = chain
        state[name] = next(chain)

    def out_chain():
        value = out_kept + out_came.astype(FULL)
        value = yield from reduce_chain(value, steps[1:])
        value = yield from gather_chain(value.astype(LOW), steps[:0:-1])
        other = yield value, core[0]
        return stack(mine, value, other).reshape(-1, channels).astype(FULL)

    def mid_chain():
        chunk = 2 * steps[1][1] + steps[2][1]
        lanes, deep = grads.shape[-1], acts.shape[-1]
        span = acts.shape[0] * images * width
        (block,) = call(
            mid_weights,
            [((deep // GROUP, 9, GROUP, lanes), FULL)],
            jnp.stack([index % 2, chunk]).astype(jnp.int32)[None],
            sizes,
            sums_first,
            sums_second,
            sums_mid,
            params_mid,
            acts,
            normed,
            grads,
            scratch=[pltpu.VMEM((2, span, deep), LOW), pltpu.VMEM((2, span, 3 * lanes), LOW)],
        )
        value = yield from reduce_chain(block.reshape(-1, lanes), far_steps)
        value = yield from gather_chain(value.astype(LOW), steps[:0:-1])
        other = yield value, core[0]
        return assemble(odd, value, other, block.shape)

    def in_chain():
        sent = contract(half_of(flat_features, 1 - mine, 1), grad_first).astype(LOW)
        kept = contract(half_of(flat_features, mine, 1), grad_first)
        came = yield sent, core[0]
        value = kept + came.astype(FULL)
        value = yield from reduce_chain(value, steps[1:])
        value = yield from gather_chain(value.astype(LOW), steps[:0:-1])
        other = yield value, core[0]
        return stack(mine, value, other).reshape(-1, middle).astype(FULL)

    begin("out", out_chain())
    begin("mid", mid_chain())
    (came,) = advance(chains, state, ("mid", "out"), (everyone(sums),))
    grad_first, sums_in = call(
        first_backward,
        [(plane, LOW), (narrow, FULL)],
        sums_first,
        came,
        params,
        first,
        grad_first_pre,
        mask,
    )
    begin("in", in_chain())
    advance(chains, state, ("in", "mid", "out"))
    grad_features = grad_summed + times_transpose(grad_first, weight_in)
    grad_features, pooled = advance(chains, state, ("in", "mid", "out"), (grad_features, pooled))
    pooled = sum_rows_axis(pooled.astype(LOW).astype(FULL)) / areas[:, :1]
    while chains:
        (pooled,) = advance(chains, state, ("in", "mid", "out"), (pooled,))
    grad_weight_in, grad_weight_mid, grad_weight_out = state["in"], state["mid"], state["out"]
    whole = (images, height, width, channels)
    return (
        result.astype(LOW).reshape(whole),
        pooled,
        grad_features.reshape(whole),
        grad_weight_in,
        sums_in[1],
        sums_in[0],
        grad_weight_mid.reshape(weight_mid.shape),
        sums_mid[1],
        sums_mid[0],
        grad_weight_out,
        sums_out[1],
        sums_out[0],
    )


def solution(mesh):
    tiles, single = P("img", "rows", None, None), P()
    return jax.shard_map(
        per_device,
        mesh=mesh,
        in_specs=(tiles,) + (single,) * 9 + (P("img"), tiles, P("img", None)),
        out_specs=(tiles, P("img", None), tiles) + (single,) * 9,
        check_vma=False,
    )
```

time: 315 us -> 260 us (0.83)
  waiting for transfers between devices: 116 us -> 87.6 us
  starting transfers between devices: 112 us -> 85 us
  Pallas kernels: 13.3 us -> 33.1 us
  other arithmetic: 39 us -> 24.9 us
  matrix products: 10.7 us -> 6.23 us
    ppermute x60 -> x51, starting transfers between devices: 96.4 us -> 49.9 us  [swap(): lax.ppermute(value, AXES, [(i, i ^ flips[i & 1]) for i in range(count)])]
    ppermute x60 -> x51, waiting for transfers between devices: 109 us -> 69.6 us  [swap(): lax.ppermute(value, AXES, [(i, i ^ flips[i & 1]) for i in range(count)])]
    all_to_all x0 -> x4, starting transfers between devices: none -> 20.3 us  [everyone(): return lax.all_to_all(copies, AXES, 0, 0)]
    pallas_call x3 -> x8, Pallas kernels: 13.3 us -> 25.3 us  [call(): pl.pallas_call(kernel, out_shape=[jax.ShapeDtypeStruct(shape, kind) for s...]
    unnamed x52 -> x142, local copies, waits for them, and re-layouts: 2.03 us -> 14 us
    all_to_all x0 -> x4, waiting for transfers between devices: none -> 10.7 us  [everyone(): return lax.all_to_all(copies, AXES, 0, 0)]
    another operation x3 -> x48, other arithmetic: 0.05 us -> 10.7 us  [the longest x47 10.6 us: stack(): jnp.stack([jnp.where(low, value, other), jnp.where(low, other, value)])]
    broadcast_in_dim x30 -> x0, local copies, waits for them, and re-layouts: 8.04 us -> none  [gather_back(): jnp.where(half == mine, value[None], other[None])]
  transfers between devices with their start and end apart: 66 -> 63, of which waited for: 50 -> 28; matrix products, arithmetic and copies ran while one was open for 10% -> 9% of each run, Pallas kernels for 1% -> 6%
where the time goes in v3:
time: 260 us; the launch traced here: 258 us
  waiting for transfers between devices  87.6 us (34%)
  starting transfers between devices  85 us (33%)
  Pallas kernels  33.1 us (13%)
  other arithmetic  24.9 us (10%)
  local copies, waits for them, and re-layouts  19.4 us (7%)
  matrix products  6.23 us (2%)
    ppermute x51, waiting for transfers between devices, swap(): lax.ppermute(value, AXES, [(i, i ^ flips[i & 1]) for i in range(count)])  69.6 us
    ppermute x51, starting transfers between devices, swap(): lax.ppermute(value, AXES, [(i, i ^ flips[i & 1]) for i in range(count)])  49.9 us
    pallas_call x8, Pallas kernels, call(): pl.pallas_call(kernel, out_shape=[jax.ShapeDtypeStruct(shape, kind) for s...  25.3 us
    all_to_all x4, starting transfers between devices, everyone(): return lax.all_to_all(copies, AXES, 0, 0)  20.3 us
    unnamed x142, local copies, waits for them, and re-layouts  14 us
    all_to_all x4, waiting for transfers between devices, everyone(): return lax.all_to_all(copies, AXES, 0, 0)  10.7 us
    another operation x47, other arithmetic, stack(): jnp.stack([jnp.where(low, value, other), jnp.where(low, other, value)])  10.6 us
    ppermute x3, starting transfers between devices, rim(): lax.ppermute(jnp.where(odd, bottom, top), 'rows', pairs + [(b, a) for a,...  10.4 us
  transfers between devices with their start and end apart: 63, of which 28 were waited for; matrix products, arithmetic and copies ran while one was open for 9% of the time, Pallas kernels for 6%

profile of v3, /device:TPU:1, one launch (start us, length us, event | category | flops | bytes accessed | tf_op | source)
XLA Modules:
  0.0 258.5 jit_solution(12817453238404994839)
XLA Ops:
  0.6 3.4 %shard_map.220 = (f32[256,512]{1,0:T(8,128)}, f32[32,2,640]{2,1,0:T(2,128)}, f32[2,512]{1,0:T(2,128)}, f32[2,512]{1,0:T(2,128)}, f32[16,128]{1,0:T(8,128)}, /*in...) custom-call(s32[1,1]{1,0:T(1,128)} %bitcast.refs_0_, s32[1,16]{1,0:T(1,128)} %bitcast.270, ...), custom_call_target="tpu_custom_call" | custom-call | tf_op jit(solution)/shard_map/pallas_call | solution.py:142
  4.1 7.1 %all-to-all-start = ((f32[32,2,640]{2,1,0:T(2,128)}), f32[32,2,640]{2,1,0:T(2,128)S(1)}, u32[]{:S(2)}, u32[]{:S(2)}) async-start(f32[32,2,640]{2,1,0:T(2,128)} %get-tuple-element.119), calls=%async_computation | async-start | bytes 327680 | tf_op jit(solution)/shard_map/all_to_all | solution.py:30
  12.6 3.4 %collective-permute-start.1 = (f32[16,1,8,512]{3,2,0,1:T(8,128)S(1)}, f32[16,1,8,512]{3,2,0,1:T(8,128)S(1)}, u32[]{:S(2)}, u32[]{:S(2)}) collective-permute-start(f32[16,1,8,512]{3,2,0,1:T(8,128)S(1)} %get-tuple-element.264), channel_id=1, source_target_pairs={{1,2},{2,1},{5,6},{6,5},{9,10},{10,9},{13,14},{14,13},{17,18},{18,... | collective-permute-start | bytes 786440 | tf_op jit(solution)/shard_map/ppermute | solution.py:131
  16.0 4.5 %collective-permute-done.1 = f32[16,1,8,512]{3,2,0,1:T(8,128)S(1)} collective-permute-done((f32[16,1,8,512]{3,2,0,1:T(8,128)S(1)}, f32[16,1,8,512]{3,2,0,1:T(8,128)S(1)}, u32[]{:S(2)}, u32[]{:S(2)}) %collective-permute-start.1) | collective-permute-done | bytes 262176 | tf_op jit(solution)/shard_map/ppermute | solution.py:131
  24.9 3.4 %shard_map.221 = (bf16[2,128,512]{2,1,0:T(8,128)(2,1)S(1)}, f32[256,512]{1,0:T(8,128)S(1)}, f32[32,2,512]{2,1,0:T(2,128)S(1)}, f32[2,640]{1,0:T(2,128)S(1)}) custom-call(s32[1,1]{1,0:T(1,128)} %bitcast.refs_0_, f32[32,2,640]{2,1,0:T(2,128)S(1)} %all-to-all-done.refs_1_, f32[2,512]{1,0:T(2,128)S(1)} %copy-done.39, f32[256,512]{1,0:T(8,128)S(1)} %copy-done.6, ...), custom_call_target="tpu_custom_call" | custom-call | tf_op jit(solution)/shard_map/pallas_call | solution.py:142
  29.8 3.3 %collective-permute-start.4 = (f32[16,1,8,512]{3,2,0,1:T(8,128)}, f32[16,1,8,512]{3,2,0,1:T(8,128)S(1)}, u32[]{:S(2)}, u32[]{:S(2)}) collective-permute-start(f32[16,1,8,512]{3,2,0,1:T(8,128)} %get-tuple-element.262), channel_id=1, source_target_pairs={{1,2},{2,1},{5,6},{6,5},{9,10},{10,9},{13,14},{14,13},{17,18},{18,... | collective-permute-start | bytes 786440 | tf_op jit(solution)/shard_map/ppermute | solution.py:131
  33.2 4.6 %all-to-all-start.1 = ((f32[32,2,512]{2,1,0:T(2,128)}), f32[32,2,512]{2,1,0:T(2,128)S(1)}, u32[]{:S(2)}, u32[]{:S(2)}) async-start(f32[32,2,512]{2,1,0:T(2,128)} %copy-done.37), calls=%async_computation.1 | async-start | bytes 262144 | tf_op jit(solution)/shard_map/all_to_all | solution.py:30
  42.6 3.4 %all-to-all-done.1.refs_1_ = f32[32,2,512]{2,1,0:T(2,128)S(1)} async-done(((f32[32,2,512]{2,1,0:T(2,128)}), f32[32,2,512]{2,1,0:T(2,128)S(1)}, u32[]{:S(2)}, u32[]{:S(2)}) %all-to-all-start.1) | async-done | bytes 131104 | tf_op jit(solution)/shard_map/all_to_all | solution.py:30
  53.7 1.8 collective-permute-start.9
  60.1 2.2 collective-permute-start.13
  64.8 5.7 %shard_map.223 = (bf16[256,2048]{1,0:T(8,128)(2,1)}, f32[16,2048]{1,0:T(8,128)S(1)}, f32[256,2048]{1,0:T(8,128)S(1)}, f32[2,2048]{1,0:T(2,128)S(1)}) custom-call(f32[2,640]{1,0:T(2,128)S(1)} %get-tuple-element.128.refs_0_.refs_1_.sums_first, f32[2,2048]{1,0:T(2,128)S(1)} %add_add_fusion.2.refs_1_.refs_2_, f32[2,2048]{1,0:T(2,128)S(1)} %pad_maximum_fusion.21.refs_2_.refs_5_, ...), custom_call_target="tpu_custom_call" | custom-call | tf_op jit(solution)/shard_map/pallas_call | solution.py:142
  71.7 3.3 %collective-permute-start.15 = (f32[2,2048]{1,0:T(2,128)S(1)}, f32[2,2048]{1,0:T(2,128)S(1)}, u32[]{:S(2)}, u32[]{:S(2)}) collective-permute-start(f32[2,2048]{1,0:T(2,128)S(1)} %get-tuple-element.150), channel_id=1, source_target_pairs={{0,1},{1,0},{2,3},{3,2},{4,5},{5,4},{6,7},{7,6},{8,9},{9,8},{10,11... | collective-permute-start | bytes 49160 | tf_op jit(solution)/shard_map/ppermute | solution.py:19
  77.0 1.6 collective-permute-start.18
  80.5 6.0 %collective-permute-done.19 = bf16[2,2,128,256]{3,2,1,0:T(8,128)(2,1)S(1)} collective-permute-done((bf16[2,2,128,256]{3,2,1,0:T(8,128)(2,1)S(1)}, bf16[2,2,128,256]{3,2,1,0:T(8,128)(2,1)S(1)}, u32[]{:S(2)}, u32[]{:S(2)}) %collective-permute-start.19) | collective-permute-done | bytes 262176 | tf_op jit(solution)/shard_map/ppermute | solution.py:19
  86.5 3.2 %collective-permute-start.21 = (f32[2,2048]{1,0:T(2,128)S(1)}, f32[2,2048]{1,0:T(2,128)S(1)}, u32[]{:S(2)}, u32[]{:S(2)}) collective-permute-start(f32[2,2048]{1,0:T(2,128)S(1)} %add_add_fusion.1), channel_id=1, source_target_pairs={{0,16},{1,17},{2,18},{3,19},{4,20},{5,21},{6,22},{7,23},{8,24},{9,... | collective-permute-start | bytes 49160 | tf_op jit(solution)/shard_map/ppermute | solution.py:19
  91.1 3.1 %collective-permute-done.22 = f32[2,2048]{1,0:T(2,128)S(1)} collective-permute-done((f32[2,2048]{1,0:T(2,128)S(1)}, f32[2,2048]{1,0:T(2,128)S(1)}, u32[]{:S(2)}, u32[]{:S(2)}) %collective-permute-start.22) | collective-permute-done | bytes 16416 | tf_op jit(solution)/shard_map/ppermute | solution.py:19
  95.0 4.2 %shard_map.224 = (bf16[256,2048]{1,0:T(8,128)(2,1)S(1)}, f32[256,512]{1,0:T(8,128)S(1)}, bf16[2,128,512]{2,1,0:T(8,128)(2,1)}, f32[32,2,512]{2,1,0:T(2,128)}) custom-call(f32[2,640]{1,0:T(2,128)S(1)} %get-tuple-element.128.refs_0_.refs_1_.sums_first, f32[2,512]{1,0:T(2,128)S(1)} %get-tuple-element.146.refs_1_.refs_2_.sums_second, ...), custom_call_target="tpu_custom_call" | custom-call | tf_op jit(solution)/shard_map/pallas_call | solution.py:142
  101.7 4.1 %collective-permute-start.24 = (bf16[2,128,512]{2,1,0:T(8,128)(2,1)}, bf16[2,128,512]{2,1,0:T(8,128)(2,1)}, u32[]{:S(2)}, u32[]{:S(2)}) collective-permute-start(bf16[2,128,512]{2,1,0:T(8,128)(2,1)} %get-tuple-element.161), channel_id=1, source_target_pairs={{0,1},{1,0},{2,3},{3,2},{4,5},{5,4},{6,7},{7,6},{8,9},{9,8},{10,11... | collective-permute-start | bytes 786440 | tf_op jit(solution)/shard_map/ppermute | solution.py:19
  106.8 3.4 %all-to-all-start.2 = ((f32[32,2,512]{2,1,0:T(2,128)}), f32[32,2,512]{2,1,0:T(2,128)S(1)}, u32[]{:S(2)}, u32[]{:S(2)}) async-start(f32[32,2,512]{2,1,0:T(2,128)} %get-tuple-element.162), calls=%async_computation.2 | async-start | bytes 262144 | tf_op jit(solution)/shard_map/all_to_all | solution.py:30
  111.3 3.6 %collective-permute-start.29 = (f32[16,1,8,512]{3,2,0,1:T(8,128)}, f32[16,1,8,512]{3,2,0,1:T(8,128)}, u32[]{:S(2)}, u32[]{:S(2)}) collective-permute-start(f32[16,1,8,512]{3,2,0,1:T(8,128)} %get-tuple-element.254), channel_id=1, source_target_pairs={{1,2},{2,1},{5,6},{6,5},{9,10},{10,9},{13,14},{14,13},{17,18},{18,... | collective-permute-start | bytes 786440 | tf_op jit(solution)/shard_map/ppermute | solution.py:131
  118.4 1.8 fusion.13
  120.2 2.5 collective-permute-done.25
  124.3 4.6 %shard_map.225 = (f32[256,512]{1,0:T(8,128)S(1)}, f32[32,2,512]{2,1,0:T(2,128)}, f32[2,512]{1,0:T(2,128)S(1)}) custom-call(s32[1,1]{1,0:T(1,128)} %bitcast.refs_0_, f32[2,640]{1,0:T(2,128)S(1)} %get-tuple-element.128.refs_0_.refs_1_.sums_first, f32[2,512]{1,0:T(2,128)S(1)} %copy-done.42, f32[32,2,512]{2,1,0:T(2,128)S(1)} %all-to-all-done.2.refs_3_, ...), custom_call_target="tpu_custom_call" | custom-call | tf_op jit(solution)/shard_map/pallas_call | solution.py:142
  130.8 1.6 convert_add_fusion.1
  134.8 2.7 %shard_map.226 = f32[16,9,16,128]{3,2,1,0:T(8,128)S(1)} custom-call(s32[1,2]{1,0:T(1,128)S(1)} %copy-done.48, s32[2,16]{1,0:T(2,128)S(1)} %bitcast.246, f32[2,640]{1,0:T(2,128)S(1)} %get-tuple-element.128.refs_0_.refs_1_.sums_first, f32[2,512]{1,0:T(2,128)S(1)} %copy-done.42, f32[2,512]{1,0:T(2,128)S(1)} %get-tuple-element.174.sums_grad, ...), custom_call_target="tpu_custom_call" | custom-call | tf_op jit(solution)/shard_map/pallas_call | solution.py:142
  139.7 5.2 %all-to-all-start.3 = ((f32[32,2,512]{2,1,0:T(2,128)}), f32[32,2,512]{2,1,0:T(2,128)S(1)}, u32[]{:S(2)}, u32[]{:S(2)}) async-start(f32[32,2,512]{2,1,0:T(2,128)} %get-tuple-element.184), calls=%async_computation.3 | async-start | bytes 262144 | tf_op jit(solution)/shard_map/all_to_all | solution.py:30
  145.7 7.4 %all-to-all-done.3.came = f32[32,2,512]{2,1,0:T(2,128)S(1)} async-done(((f32[32,2,512]{2,1,0:T(2,128)}), f32[32,2,512]{2,1,0:T(2,128)S(1)}, u32[]{:S(2)}, u32[]{:S(2)}) %all-to-all-start.3) | async-done | bytes 131104 | tf_op jit(solution)/shard_map/all_to_all | solution.py:30
  158.3 8.8 %collective-permute-done.34 = bf16[576,128]{1,0:T(8,128)(2,1)S(1)} collective-permute-done((bf16[576,128]{1,0:T(8,128)(2,1)S(1)}, bf16[576,128]{1,0:T(8,128)(2,1)S(1)}, u32[]{:S(2)}, u32[]{:S(2)}) %collective-permute-start.34) | collective-permute-done | bytes 147488 | tf_op jit(solution)/shard_map/ppermute | solution.py:19
  168.1 1.8 collective-permute-start.37
  169.9 2.1 convolution_add_fusion
  172.0 3.3 %collective-permute-done.37 = bf16[576,128]{1,0:T(8,128)(2,1)S(1)} collective-permute-done((bf16[576,128]{1,0:T(8,128)(2,1)S(1)}, bf16[576,128]{1,0:T(8,128)(2,1)S(1)}, u32[]{:S(2)}, u32[]{:S(2)}) %collective-permute-start.37) | collective-permute-done | bytes 147488 | tf_op jit(solution)/shard_map/ppermute | solution.py:19
  176.1 2.5 collective-permute-start.42
  182.5 2.7 %collective-permute-done.43 = f32[16,2048]{1,0:T(8,128)S(1)} collective-permute-done((f32[16,2048]{1,0:T(8,128)S(1)}, f32[16,2048]{1,0:T(8,128)S(1)}, u32[]{:S(2)}, u32[]{:S(2)}) %collective-permute-start.43) | collective-permute-done | bytes 131104 | tf_op jit(solution)/shard_map/ppermute | solution.py:120
  186.0 3.1 %collective-permute-done.39 = bf16[256,512]{1,0:T(8,128)(2,1)S(1)} collective-permute-done((bf16[256,512]{1,0:T(8,128)(2,1)S(1)}, bf16[256,512]{1,0:T(8,128)(2,1)S(1)}, u32[]{:S(2)}, u32[]{:S(2)}) %collective-permute-start.39) | collective-permute-done | bytes 262176 | tf_op jit(solution)/shard_map/ppermute | solution.py:19
  191.0 2.3 collective-permute-start.46
  193.3 1.9 collective-permute-done.46
  196.0 2.7 %collective-permute-done.45 = bf16[2304,128]{1,0:T(8,128)(2,1)S(1)} collective-permute-done((bf16[2304,128]{1,0:T(8,128)(2,1)S(1)}, bf16[2304,128]{1,0:T(8,128)(2,1)S(1)}, u32[]{:S(2)}, u32[]{:S(2)}) %collective-permute-start.45) | collective-permute-done | bytes 589856 | tf_op jit(solution)/shard_map/ppermute | solution.py:19
  199.8 2.3 collective-permute-start.47
  202.0 1.9 collective-permute-done.47
  204.3 10.1 %collective-permute-done.48 = bf16[4608,128]{1,0:T(8,128)(2,1)S(1)} collective-permute-done((bf16[4608,128]{1,0:T(8,128)(2,1)S(1)}, bf16[4608,128]{1,0:T(8,128)(2,1)S(1)}, u32[]{:S(2)}, u32[]{:S(2)}) %collective-permute-start.48) | collective-permute-done | bytes 1179680 | tf_op jit(solution)/shard_map/ppermute | solution.py:19
  214.9 2.5 collective-permute-start.51
  219.7 5.3 %collective-permute-done.50 = bf16[64,512]{1,0:T(8,128)(2,1)S(1)} collective-permute-done((bf16[64,512]{1,0:T(8,128)(2,1)S(1)}, bf16[64,512]{1,0:T(8,128)(2,1)S(1)}, u32[]{:S(2)}, u32[]{:S(2)}) %collective-permute-start.50) | collective-permute-done | bytes 65568 | tf_op jit(solution)/shard_map/ppermute | solution.py:19
  225.9 4.7 %collective-permute-done.53 = bf16[128,512]{1,0:T(8,128)(2,1)S(1)} collective-permute-done((bf16[128,512]{1,0:T(8,128)(2,1)S(1)}, bf16[128,512]{1,0:T(8,128)(2,1)S(1)}, u32[]{:S(2)}, u32[]{:S(2)}) %collective-permute-start.53) | collective-permute-done | bytes 131104 | tf_op jit(solution)/shard_map/ppermute | solution.py:19
  230.6 2.9 %collective-permute-done.54 = bf16[128,2048]{1,0:T(8,128)(2,1)S(1)} collective-permute-done((bf16[128,2048]{1,0:T(8,128)(2,1)S(1)}, bf16[128,2048]{1,0:T(8,128)(2,1)S(1)}, u32[]{:S(2)}, u32[]{:S(2)}) %collective-permute-start.54) | collective-permute-done | bytes 524320 | tf_op jit(solution)/shard_map/ppermute | solution.py:19
  235.5 5.2 %collective-permute-done.55 = bf16[256,512]{1,0:T(8,128)(2,1)S(1)} collective-permute-done((bf16[256,512]{1,0:T(8,128)(2,1)S(1)}, bf16[256,512]{1,0:T(8,128)(2,1)S(1)}, u32[]{:S(2)}, u32[]{:S(2)}) %collective-permute-start.55) | collective-permute-done | bytes 262176 | tf_op jit(solution)/shard_map/ppermute | solution.py:19
  243.3 7.8 %shard_map.228 = f32[9,512,512]{2,1,0:T(8,128)} custom-call(s32[1,1]{1,0:T(1,128)} %bitcast.94.odd, bf16[4,16,9,16,128]{4,3,2,1,0:T(8,128)(2,1)S(1)} %bitcast.228, bf16[4,16,9,16,128]{4,3,2,1,0:T(8,128)(2,1)} %bitcast.96.other), custom_call_target="tpu_custom_call" | custom-call | tf_op jit(solution)/shard_map/pallas_call | solution.py:542
  252.7 2.7 %bitcast_convert_fusion = f32[512,2048]{1,0:T(8,128)} fusion(bf16[2,256,2048]{2,1,0:T(8,128)(2,1)S(1)} %pad_maximum_fusion.2), kind=kLoop, calls=%fused_computation.5 | loop fusion | flops 1048576 | bytes 6291456 | tf_op jit(solution)/shard_map/convert_element_type | solution.py:785
  255.7 2.7 %bitcast_convert_fusion.1 = f32[2048,512]{1,0:T(8,128)} fusion(bf16[2,1024,512]{2,1,0:T(8,128)(2,1)S(1)} %pad_maximum_fusion.1), kind=kLoop, calls=%fused_computation.6 | loop fusion | flops 1048576 | bytes 6291456 | tf_op jit(solution)/shard_map/convert_element_type | solution.py:818
  (328 shorter events, 76.0 us)
Async XLA Ops:
  4.1 16.5 %all-to-all-start = ((f32[32,2,640]{2,1,0:T(2,128)}), f32[32,2,640]{2,1,0:T(2,128)S(1)}, u32[]{:S(2)}, u32[]{:S(2)}) async-start(f32[32,2,640]{2,1,0:T(2,128)} %get-tuple-element.119), calls=%async_computation | async-start | bytes 327680 | tf_op jit(solution)/shard_map/all_to_all | solution.py:30
  12.6 8.0 %collective-permute-start.1 = (f32[16,1,8,512]{3,2,0,1:T(8,128)S(1)}, f32[16,1,8,512]{3,2,0,1:T(8,128)S(1)}, u32[]{:S(2)}, u32[]{:S(2)}) collective-permute-start(f32[16,1,8,512]{3,2,0,1:T(8,128)S(1)} %get-tuple-element.264), channel_id=1, source_target_pairs={{1,2},{2,1},{5,6},{6,5},{9,10},{10,9},{13,14},{14,13},{17,18},{18,... | collective-permute-start | bytes 786440 | tf_op jit(solution)/shard_map/ppermute | solution.py:131
  29.8 16.2 %collective-permute-start.3 = (f32[16,1,8,512]{3,2,0,1:T(8,128)}, f32[16,1,8,512]{3,2,0,1:T(8,128)S(1)}, u32[]{:S(2)}, u32[]{:S(2)}) collective-permute-start(f32[16,1,8,512]{3,2,0,1:T(8,128)} %get-tuple-element.263), channel_id=1, source_target_pairs={{0,1},{1,0},{2,3},{3,2},{4,5},{5,4},{6,7},{7,6},{8,9},{9,8},{10,11... | collective-permute-start | bytes 786440 | tf_op jit(solution)/shard_map/ppermute | solution.py:129
  29.8 16.2 %collective-permute-start.4 = (f32[16,1,8,512]{3,2,0,1:T(8,128)}, f32[16,1,8,512]{3,2,0,1:T(8,128)S(1)}, u32[]{:S(2)}, u32[]{:S(2)}) collective-permute-start(f32[16,1,8,512]{3,2,0,1:T(8,128)} %get-tuple-element.262), channel_id=1, source_target_pairs={{1,2},{2,1},{5,6},{6,5},{9,10},{10,9},{13,14},{14,13},{17,18},{18,... | collective-permute-start | bytes 786440 | tf_op jit(solution)/shard_map/ppermute | solution.py:131
  33.2 12.8 %all-to-all-start.1 = ((f32[32,2,512]{2,1,0:T(2,128)}), f32[32,2,512]{2,1,0:T(2,128)S(1)}, u32[]{:S(2)}, u32[]{:S(2)}) async-start(f32[32,2,512]{2,1,0:T(2,128)} %copy-done.37), calls=%async_computation.1 | async-start | bytes 262144 | tf_op jit(solution)/shard_map/all_to_all | solution.py:30
  52.8 5.0 %collective-permute-start.7 = (f32[2,2048]{1,0:T(2,128)S(1)}, f32[2,2048]{1,0:T(2,128)S(1)}, u32[]{:S(2)}, u32[]{:S(2)}) collective-permute-start(f32[2,2048]{1,0:T(2,128)S(1)} %add.226), channel_id=1, source_target_pairs={{0,2},{1,3},{2,0},{3,1},{4,6},{5,7},{6,4},{7,5},{8,10},{9,11},{10,... | collective-permute-start | bytes 49160 | tf_op jit(solution)/shard_map/ppermute | solution.py:19
  53.0 4.8 %collective-permute-start.8 = (f32[2,2048]{1,0:T(2,128)S(1)}, f32[2,2048]{1,0:T(2,128)S(1)}, u32[]{:S(2)}, u32[]{:S(2)}) collective-permute-start(f32[2,2048]{1,0:T(2,128)S(1)} %add.226), channel_id=1, source_target_pairs={{0,4},{1,5},{2,6},{3,7},{4,0},{5,1},{6,2},{7,3},{8,12},{9,13},{10,... | collective-permute-start | bytes 49160 | tf_op jit(solution)/shard_map/ppermute | solution.py:19
  57.4 7.1 %collective-permute-start.14 = (bf16[2,2,128,256]{3,2,1,0:T(8,128)(2,1)}, bf16[2,2,128,256]{3,2,1,0:T(8,128)(2,1)S(1)}, u32[]{:S(2)}, u32[]{:S(2)}) collective-permute-start(bf16[2,2,128,256]{3,2,1,0:T(8,128)(2,1)} %pad_maximum_fusion.16), channel_id=1, source_target_pairs={{0,2},{1,5},{2,0},{3,7},{4,6},{5,1},{6,4},{7,3},{8,10},{9,13},{10,... | collective-permute-start | bytes 786440 | tf_op jit(solution)/shard_map/ppermute | solution.py:19
  58.8 4.6 %collective-permute-start.11 = (f32[2,2048]{1,0:T(2,128)S(1)}, f32[2,2048]{1,0:T(2,128)S(1)}, u32[]{:S(2)}, u32[]{:S(2)}) collective-permute-start(f32[2,2048]{1,0:T(2,128)S(1)} %add_add_fusion.3), channel_id=1, source_target_pairs={{0,8},{1,9},{2,10},{3,11},{4,12},{5,13},{6,14},{7,15},{8,0},{9,1},... | collective-permute-start | bytes 49160 | tf_op jit(solution)/shard_map/ppermute | solution.py:19
  79.1 15.1 %collective-permute-start.23 = (bf16[4,2,128,256]{3,2,1,0:T(8,128)(2,1)S(1)}, bf16[4,2,128,256]{3,2,1,0:T(8,128)(2,1)S(1)}, u32[]{:S(2)}, u32[]{:S(2)}) collective-permute-start(bf16[4,2,128,256]{3,2,1,0:T(8,128)(2,1)S(1)} %bitcast.253), channel_id=1, source_target_pairs={{0,4},{1,3},{2,6},{3,1},{4,0},{5,7},{6,2},{7,5},{8,12},{9,11},{10,... | collective-permute-start | bytes 1572872 | tf_op jit(solution)/shard_map/ppermute | solution.py:19
  79.4 7.1 %collective-permute-start.19 = (bf16[2,2,128,256]{3,2,1,0:T(8,128)(2,1)S(1)}, bf16[2,2,128,256]{3,2,1,0:T(8,128)(2,1)S(1)}, u32[]{:S(2)}, u32[]{:S(2)}) collective-permute-start(bf16[2,2,128,256]{3,2,1,0:T(8,128)(2,1)S(1)} %fusion.6), channel_id=1, source_target_pairs={{0,2},{1,5},{2,0},{3,7},{4,6},{5,1},{6,4},{7,3},{8,10},{9,13},{10,... | collective-permute-start | bytes 786440 | tf_op jit(solution)/shard_map/ppermute | solution.py:19
  86.5 4.6 %collective-permute-start.20 = (f32[2,2048]{1,0:T(2,128)S(1)}, f32[2,2048]{1,0:T(2,128)S(1)}, u32[]{:S(2)}, u32[]{:S(2)}) collective-permute-start(f32[2,2048]{1,0:T(2,128)S(1)} %add_add_fusion.1), channel_id=1, source_target_pairs={{0,8},{1,9},{2,10},{3,11},{4,12},{5,13},{6,14},{7,15},{8,0},{9,1},... | collective-permute-start | bytes 49160 | tf_op jit(solution)/shard_map/ppermute | solution.py:19
  86.5 4.6 %collective-permute-start.21 = (f32[2,2048]{1,0:T(2,128)S(1)}, f32[2,2048]{1,0:T(2,128)S(1)}, u32[]{:S(2)}, u32[]{:S(2)}) collective-permute-start(f32[2,2048]{1,0:T(2,128)S(1)} %add_add_fusion.1), channel_id=1, source_target_pairs={{0,16},{1,17},{2,18},{3,19},{4,20},{5,21},{6,22},{7,23},{8,24},{9,... | collective-permute-start | bytes 49160 | tf_op jit(solution)/shard_map/ppermute | solution.py:19
  89.7 4.5 %collective-permute-start.22 = (f32[2,2048]{1,0:T(2,128)S(1)}, f32[2,2048]{1,0:T(2,128)S(1)}, u32[]{:S(2)}, u32[]{:S(2)}) collective-permute-start(f32[2,2048]{1,0:T(2,128)S(1)} %add_add_fusion.1), channel_id=1, source_target_pairs={{0,24},{1,25},{2,26},{3,27},{4,28},{5,29},{6,30},{7,31},{8,16},{9,... | collective-permute-start | bytes 49160 | tf_op jit(solution)/shard_map/ppermute | solution.py:19
  101.7 13.5 %collective-permute-start.24 = (bf16[2,128,512]{2,1,0:T(8,128)(2,1)}, bf16[2,128,512]{2,1,0:T(8,128)(2,1)}, u32[]{:S(2)}, u32[]{:S(2)}) collective-permute-start(bf16[2,128,512]{2,1,0:T(8,128)(2,1)} %get-tuple-element.161), channel_id=1, source_target_pairs={{0,1},{1,0},{2,3},{3,2},{4,5},{5,4},{6,7},{7,6},{8,9},{9,8},{10,11... | collective-permute-start | bytes 786440 | tf_op jit(solution)/shard_map/ppermute | solution.py:19
  105.7 17.0 %collective-permute-start.27 = (bf16[256,2048]{1,0:T(8,128)(2,1)}, bf16[256,2048]{1,0:T(8,128)(2,1)}, u32[]{:S(2)}, u32[]{:S(2)}) collective-permute-start(bf16[256,2048]{1,0:T(8,128)(2,1)} %convolution_convert_fusion), channel_id=1, source_target_pairs={{0,1},{1,0},{2,3},{3,2},{4,5},{5,4},{6,7},{7,6},{8,9},{9,8},{10,11... | collective-permute-start | bytes 3145736 | tf_op jit(solution)/shard_map/ppermute | solution.py:19
  105.7 14.5 %collective-permute-start.26 = (bf16[4,2,128,128]{3,2,1,0:T(8,128)(2,1)}, bf16[4,2,128,128]{3,2,1,0:T(8,128)(2,1)}, u32[]{:S(2)}, u32[]{:S(2)}) collective-permute-start(bf16[4,2,128,128]{3,2,1,0:T(8,128)(2,1)} %constant_dynamic-slice_fusion.1), channel_id=1, source_target_pairs={{0,4},{1,3},{2,6},{3,1},{4,0},{5,7},{6,2},{7,5},{8,12},{9,11},{10,... | collective-permute-start | bytes 786440 | tf_op jit(solution)/shard_map/ppermute | solution.py:19
  106.8 13.4 %all-to-all-start.2 = ((f32[32,2,512]{2,1,0:T(2,128)}), f32[32,2,512]{2,1,0:T(2,128)S(1)}, u32[]{:S(2)}, u32[]{:S(2)}) async-start(f32[32,2,512]{2,1,0:T(2,128)} %get-tuple-element.162), calls=%async_computation.2 | async-start | bytes 262144 | tf_op jit(solution)/shard_map/all_to_all | solution.py:30
  111.0 9.2 %collective-permute-start.28 = (f32[16,1,8,512]{3,2,0,1:T(8,128)}, f32[16,1,8,512]{3,2,0,1:T(8,128)}, u32[]{:S(2)}, u32[]{:S(2)}) collective-permute-start(f32[16,1,8,512]{3,2,0,1:T(8,128)} %get-tuple-element.255), channel_id=1, source_target_pairs={{0,1},{1,0},{2,3},{3,2},{4,5},{5,4},{6,7},{7,6},{8,9},{9,8},{10,11... | collective-permute-start | bytes 786440 | tf_op jit(solution)/shard_map/ppermute | solution.py:129
  111.3 9.0 %collective-permute-start.29 = (f32[16,1,8,512]{3,2,0,1:T(8,128)}, f32[16,1,8,512]{3,2,0,1:T(8,128)}, u32[]{:S(2)}, u32[]{:S(2)}) collective-permute-start(f32[16,1,8,512]{3,2,0,1:T(8,128)} %get-tuple-element.254), channel_id=1, source_target_pairs={{1,2},{2,1},{5,6},{6,5},{9,10},{10,9},{13,14},{14,13},{17,18},{18,... | collective-permute-start | bytes 786440 | tf_op jit(solution)/shard_map/ppermute | solution.py:131
  117.2 5.5 %collective-permute-start.25 = (bf16[2,2,128,256]{3,2,1,0:T(8,128)(2,1)}, bf16[2,2,128,256]{3,2,1,0:T(8,128)(2,1)}, u32[]{:S(2)}, u32[]{:S(2)}) collective-permute-start(bf16[2,2,128,256]{3,2,1,0:T(8,128)(2,1)} %fusion.3), channel_id=1, source_target_pairs={{0,2},{1,5},{2,0},{3,7},{4,6},{5,1},{6,4},{7,3},{8,10},{9,13},{10,... | collective-permute-start | bytes 786440 | tf_op jit(solution)/shard_map/ppermute | solution.py:19
  124.1 6.2 %collective-permute-start.30 = (bf16[4,2,128,128]{3,2,1,0:T(8,128)(2,1)S(1)}, bf16[4,2,128,128]{3,2,1,0:T(8,128)(2,1)S(1)}, u32[]{:S(2)}, u32[]{:S(2)}) collective-permute-start(bf16[4,2,128,128]{3,2,1,0:T(8,128)(2,1)S(1)} %constant_dynamic-slice_fusion), channel_id=1, source_target_pairs={{0,4},{1,3},{2,6},{3,1},{4,0},{5,7},{6,2},{7,5},{8,12},{9,11},{10,... | collective-permute-start | bytes 786440 | tf_op jit(solution)/shard_map/ppermute | solution.py:19
  133.3 19.8 %collective-permute-start.32 = (bf16[128,2048]{1,0:T(8,128)(2,1)}, bf16[128,2048]{1,0:T(8,128)(2,1)}, u32[]{:S(2)}, u32[]{:S(2)}) collective-permute-start(bf16[128,2048]{1,0:T(8,128)(2,1)} %dynamic-slice_convert_fusion.1), channel_id=1, source_target_pairs={{0,2},{1,5},{2,0},{3,7},{4,6},{5,1},{6,4},{7,3},{8,10},{9,13},{10,... | collective-permute-start | bytes 1572872 | tf_op jit(solution)/shard_map/ppermute | solution.py:19
  138.6 14.5 %collective-permute-start.31 = (bf16[1152,128]{1,0:T(8,128)(2,1)S(1)}, bf16[1152,128]{1,0:T(8,128)(2,1)S(1)}, u32[]{:S(2)}, u32[]{:S(2)}) collective-permute-start(bf16[1152,128]{1,0:T(8,128)(2,1)S(1)} %dynamic-slice_convert_fusion.2), channel_id=1, source_target_pairs={{0,8},{1,9},{2,10},{3,11},{4,12},{5,13},{6,14},{7,15},{8,0},{9,1},... | collective-permute-start | bytes 884744 | tf_op jit(solution)/shard_map/ppermute | solution.py:19
  139.7 13.4 %all-to-all-start.3 = ((f32[32,2,512]{2,1,0:T(2,128)}), f32[32,2,512]{2,1,0:T(2,128)S(1)}, u32[]{:S(2)}, u32[]{:S(2)}) async-start(f32[32,2,512]{2,1,0:T(2,128)} %get-tuple-element.184), calls=%async_computation.3 | async-start | bytes 262144 | tf_op jit(solution)/shard_map/all_to_all | solution.py:30
  155.2 11.9 %collective-permute-start.33 = (bf16[1024,512]{1,0:T(8,128)(2,1)S(1)}, bf16[1024,512]{1,0:T(8,128)(2,1)S(1)}, u32[]{:S(2)}, u32[]{:S(2)}) collective-permute-start(bf16[1024,512]{1,0:T(8,128)(2,1)S(1)} %convolution_convert_fusion.1), channel_id=1, source_target_pairs={{0,1},{1,0},{2,3},{3,2},{4,5},{5,4},{6,7},{7,6},{8,9},{9,8},{10,11... | collective-permute-start | bytes 3145736 | tf_op jit(solution)/shard_map/ppermute | solution.py:19
  157.1 10.0 %collective-permute-start.35 = (bf16[64,2048]{1,0:T(8,128)(2,1)S(1)}, bf16[64,2048]{1,0:T(8,128)(2,1)S(1)}, u32[]{:S(2)}, u32[]{:S(2)}) collective-permute-start(bf16[64,2048]{1,0:T(8,128)(2,1)S(1)} %dynamic-slice_convert_fusion.4), channel_id=1, source_target_pairs={{0,4},{1,3},{2,6},{3,1},{4,0},{5,7},{6,2},{7,5},{8,12},{9,11},{10,... | collective-permute-start | bytes 786440 | tf_op jit(solution)/shard_map/ppermute | solution.py:19
  157.3 9.8 %collective-permute-start.34 = (bf16[576,128]{1,0:T(8,128)(2,1)S(1)}, bf16[576,128]{1,0:T(8,128)(2,1)S(1)}, u32[]{:S(2)}, u32[]{:S(2)}) collective-permute-start(bf16[576,128]{1,0:T(8,128)(2,1)S(1)} %dynamic-slice_convert_fusion.5), channel_id=1, source_target_pairs={{0,16},{1,17},{2,18},{3,19},{4,20},{5,21},{6,22},{7,23},{8,24},{9,... | collective-permute-start | bytes 442376 | tf_op jit(solution)/shard_map/ppermute | solution.py:19
  167.2 4.8 %collective-permute-start.38 = (bf16[32,2048]{1,0:T(8,128)(2,1)S(1)}, bf16[32,2048]{1,0:T(8,128)(2,1)S(1)}, u32[]{:S(2)}, u32[]{:S(2)}) collective-permute-start(bf16[32,2048]{1,0:T(8,128)(2,1)S(1)} %dynamic-slice_convert_fusion.7), channel_id=1, source_target_pairs={{0,8},{1,9},{2,10},{3,11},{4,12},{5,13},{6,14},{7,15},{8,0},{9,1},... | collective-permute-start | bytes 393224 | tf_op jit(solution)/shard_map/ppermute | solution.py:19
  167.7 8.4 %collective-permute-start.36 = (bf16[512,512]{1,0:T(8,128)(2,1)S(1)}, bf16[512,512]{1,0:T(8,128)(2,1)S(1)}, u32[]{:S(2)}, u32[]{:S(2)}) collective-permute-start(bf16[512,512]{1,0:T(8,128)(2,1)S(1)} %dynamic-slice_convert_fusion), channel_id=1, source_target_pairs={{0,2},{1,5},{2,0},{3,7},{4,6},{5,1},{6,4},{7,3},{8,10},{9,13},{10,... | collective-permute-start | bytes 1572872 | tf_op jit(solution)/shard_map/ppermute | solution.py:19
  168.1 7.2 %collective-permute-start.37 = (bf16[576,128]{1,0:T(8,128)(2,1)S(1)}, bf16[576,128]{1,0:T(8,128)(2,1)S(1)}, u32[]{:S(2)}, u32[]{:S(2)}) collective-permute-start(bf16[576,128]{1,0:T(8,128)(2,1)S(1)} %add_convert_fusion), channel_id=1, source_target_pairs={{0,16},{1,17},{2,18},{3,19},{4,20},{5,21},{6,22},{7,23},{8,24},{9,... | collective-permute-start | bytes 442376 | tf_op jit(solution)/shard_map/ppermute | solution.py:19
  176.1 4.6 %collective-permute-start.42 = (f32[16,2048]{1,0:T(8,128)S(1)}, f32[16,2048]{1,0:T(8,128)S(1)}, u32[]{:S(2)}, u32[]{:S(2)}) collective-permute-start(f32[16,2048]{1,0:T(8,128)S(1)} %convert_convert_fusion), channel_id=1, source_target_pairs={{0,1},{1,0},{2,3},{3,2},{4,5},{5,4},{6,7},{7,6},{8,9},{9,8},{10,11... | collective-permute-start | bytes 393224 | tf_op jit(solution)/shard_map/ppermute | solution.py:120
  178.6 7.3 %collective-permute-start.41 = (bf16[16,2048]{1,0:T(8,128)(2,1)S(1)}, bf16[16,2048]{1,0:T(8,128)(2,1)S(1)}, u32[]{:S(2)}, u32[]{:S(2)}) collective-permute-start(bf16[16,2048]{1,0:T(8,128)(2,1)S(1)} %dynamic-slice_convert_fusion.9), channel_id=1, source_target_pairs={{0,16},{1,17},{2,18},{3,19},{4,20},{5,21},{6,22},{7,23},{8,24},{9,... | collective-permute-start | bytes 196616 | tf_op jit(solution)/shard_map/ppermute | solution.py:19
  179.3 10.2 %collective-permute-start.40 = (bf16[1152,128]{1,0:T(8,128)(2,1)S(1)}, bf16[1152,128]{1,0:T(8,128)(2,1)S(1)}, u32[]{:S(2)}, u32[]{:S(2)}) collective-permute-start(bf16[1152,128]{1,0:T(8,128)(2,1)S(1)} %bitcast.261), channel_id=1, source_target_pairs={{0,8},{1,9},{2,10},{3,11},{4,12},{5,13},{6,14},{7,15},{8,0},{9,1},... | collective-permute-start | bytes 884744 | tf_op jit(solution)/shard_map/ppermute | solution.py:19
  180.7 4.5 %collective-permute-start.43 = (f32[16,2048]{1,0:T(8,128)S(1)}, f32[16,2048]{1,0:T(8,128)S(1)}, u32[]{:S(2)}, u32[]{:S(2)}) collective-permute-start(f32[16,2048]{1,0:T(8,128)S(1)} %fusion.22), channel_id=1, source_target_pairs={{0,2},{1,3},{2,0},{3,1},{4,6},{5,7},{6,4},{7,5},{8,10},{9,11},{10,... | collective-permute-start | bytes 393224 | tf_op jit(solution)/shard_map/ppermute | solution.py:120
  182.3 6.8 %collective-permute-start.39 = (bf16[256,512]{1,0:T(8,128)(2,1)S(1)}, bf16[256,512]{1,0:T(8,128)(2,1)S(1)}, u32[]{:S(2)}, u32[]{:S(2)}) collective-permute-start(bf16[256,512]{1,0:T(8,128)(2,1)S(1)} %dynamic-slice_convert_fusion.3), channel_id=1, source_target_pairs={{0,4},{1,3},{2,6},{3,1},{4,0},{5,7},{6,2},{7,5},{8,12},{9,11},{10,... | collective-permute-start | bytes 786440 | tf_op jit(solution)/shard_map/ppermute | solution.py:19
  189.7 9.1 %collective-permute-start.45 = (bf16[2304,128]{1,0:T(8,128)(2,1)S(1)}, bf16[2304,128]{1,0:T(8,128)(2,1)S(1)}, u32[]{:S(2)}, u32[]{:S(2)}) collective-permute-start(bf16[2304,128]{1,0:T(8,128)(2,1)S(1)} %bitcast.251), channel_id=1, source_target_pairs={{0,4},{1,3},{2,6},{3,1},{4,0},{5,7},{6,2},{7,5},{8,12},{9,11},{10,... | collective-permute-start | bytes 1769480 | tf_op jit(solution)/shard_map/ppermute | solution.py:19
  190.9 5.2 %collective-permute-start.44 = (bf16[128,512]{1,0:T(8,128)(2,1)S(1)}, bf16[128,512]{1,0:T(8,128)(2,1)S(1)}, u32[]{:S(2)}, u32[]{:S(2)}) collective-permute-start(bf16[128,512]{1,0:T(8,128)(2,1)S(1)} %dynamic-slice_convert_fusion.6), channel_id=1, source_target_pairs={{0,8},{1,9},{2,10},{3,11},{4,12},{5,13},{6,14},{7,15},{8,0},{9,1},... | collective-permute-start | bytes 393224 | tf_op jit(solution)/shard_map/ppermute | solution.py:19
  199.0 15.4 %collective-permute-start.48 = (bf16[4608,128]{1,0:T(8,128)(2,1)S(1)}, bf16[4608,128]{1,0:T(8,128)(2,1)S(1)}, u32[]{:S(2)}, u32[]{:S(2)}) collective-permute-start(bf16[4608,128]{1,0:T(8,128)(2,1)S(1)} %bitcast.248), channel_id=1, source_target_pairs={{0,2},{1,5},{2,0},{3,7},{4,6},{5,1},{6,4},{7,3},{8,10},{9,13},{10,... | collective-permute-start | bytes 3538952 | tf_op jit(solution)/shard_map/ppermute | solution.py:19
  199.5 4.9 %collective-permute-start.49 = (bf16[32,2048]{1,0:T(8,128)(2,1)S(1)}, bf16[32,2048]{1,0:T(8,128)(2,1)S(1)}, u32[]{:S(2)}, u32[]{:S(2)}) collective-permute-start(bf16[32,2048]{1,0:T(8,128)(2,1)S(1)} %bitcast.264), channel_id=1, source_target_pairs={{0,8},{1,9},{2,10},{3,11},{4,12},{5,13},{6,14},{7,15},{8,0},{9,1},... | collective-permute-start | bytes 393224 | tf_op jit(solution)/shard_map/ppermute | solution.py:19
  214.9 10.1 %collective-permute-start.51 = (bf16[9216,128]{1,0:T(8,128)(2,1)S(1)}, bf16[9216,128]{1,0:T(8,128)(2,1)}, u32[]{:S(2)}, u32[]{:S(2)}) collective-permute-start(bf16[9216,128]{1,0:T(8,128)(2,1)S(1)} %bitcast.227), channel_id=1, source_target_pairs={{0,1},{1,0},{2,3},{3,2},{4,5},{5,4},{6,7},{7,6},{8,9},{9,8},{10,11... | collective-permute-start | bytes 7077896 | tf_op jit(solution)/shard_map/ppermute | solution.py:19
  217.4 7.5 %collective-permute-start.52 = (bf16[64,2048]{1,0:T(8,128)(2,1)S(1)}, bf16[64,2048]{1,0:T(8,128)(2,1)S(1)}, u32[]{:S(2)}, u32[]{:S(2)}) collective-permute-start(bf16[64,2048]{1,0:T(8,128)(2,1)S(1)} %bitcast.262), channel_id=1, source_target_pairs={{0,4},{1,3},{2,6},{3,1},{4,0},{5,7},{6,2},{7,5},{8,12},{9,11},{10,... | collective-permute-start | bytes 786440 | tf_op jit(solution)/shard_map/ppermute | solution.py:19
  218.7 6.3 %collective-permute-start.50 = (bf16[64,512]{1,0:T(8,128)(2,1)S(1)}, bf16[64,512]{1,0:T(8,128)(2,1)S(1)}, u32[]{:S(2)}, u32[]{:S(2)}) collective-permute-start(bf16[64,512]{1,0:T(8,128)(2,1)S(1)} %add_convert_fusion.1), channel_id=1, source_target_pairs={{0,16},{1,17},{2,18},{3,19},{4,20},{5,21},{6,22},{7,23},{8,24},{9,... | collective-permute-start | bytes 196616 | tf_op jit(solution)/shard_map/ppermute | solution.py:19
  225.1 8.4 %collective-permute-start.54 = (bf16[128,2048]{1,0:T(8,128)(2,1)S(1)}, bf16[128,2048]{1,0:T(8,128)(2,1)S(1)}, u32[]{:S(2)}, u32[]{:S(2)}) collective-permute-start(bf16[128,2048]{1,0:T(8,128)(2,1)S(1)} %bitcast.260), channel_id=1, source_target_pairs={{0,2},{1,5},{2,0},{3,7},{4,6},{5,1},{6,4},{7,3},{8,10},{9,13},{10,... | collective-permute-start | bytes 1572872 | tf_op jit(solution)/shard_map/ppermute | solution.py:19
  225.8 4.8 %collective-permute-start.53 = (bf16[128,512]{1,0:T(8,128)(2,1)S(1)}, bf16[128,512]{1,0:T(8,128)(2,1)S(1)}, u32[]{:S(2)}, u32[]{:S(2)}) collective-permute-start(bf16[128,512]{1,0:T(8,128)(2,1)S(1)} %bitcast.265), channel_id=1, source_target_pairs={{0,8},{1,9},{2,10},{3,11},{4,12},{5,13},{6,14},{7,15},{8,0},{9,1},... | collective-permute-start | bytes 393224 | tf_op jit(solution)/shard_map/ppermute | solution.py:19
  233.7 7.0 %collective-permute-start.56 = (bf16[256,2048]{1,0:T(8,128)(2,1)S(1)}, bf16[256,2048]{1,0:T(8,128)(2,1)S(1)}, u32[]{:S(2)}, u32[]{:S(2)}) collective-permute-start(bf16[256,2048]{1,0:T(8,128)(2,1)S(1)} %bitcast.249), channel_id=1, source_target_pairs={{0,1},{1,0},{2,3},{3,2},{4,5},{5,4},{6,7},{7,6},{8,9},{9,8},{10,11... | collective-permute-start | bytes 3145736 | tf_op jit(solution)/shard_map/ppermute | solution.py:19
  235.1 5.6 %collective-permute-start.55 = (bf16[256,512]{1,0:T(8,128)(2,1)S(1)}, bf16[256,512]{1,0:T(8,128)(2,1)S(1)}, u32[]{:S(2)}, u32[]{:S(2)}) collective-permute-start(bf16[256,512]{1,0:T(8,128)(2,1)S(1)} %bitcast.263), channel_id=1, source_target_pairs={{0,4},{1,3},{2,6},{3,1},{4,0},{5,7},{6,2},{7,5},{8,12},{9,11},{10,... | collective-permute-start | bytes 786440 | tf_op jit(solution)/shard_map/ppermute | solution.py:19
  240.8 10.3 %collective-permute-start.57 = (bf16[512,512]{1,0:T(8,128)(2,1)S(1)}, bf16[512,512]{1,0:T(8,128)(2,1)S(1)}, u32[]{:S(2)}, u32[]{:S(2)}) collective-permute-start(bf16[512,512]{1,0:T(8,128)(2,1)S(1)} %bitcast.259), channel_id=1, source_target_pairs={{0,2},{1,5},{2,0},{3,7},{4,6},{5,1},{6,4},{7,3},{8,10},{9,13},{10,... | collective-permute-start | bytes 1572872 | tf_op jit(solution)/shard_map/ppermute | solution.py:19
  (86 other events, 546.5 us)

commit v4 on v3

v4 whole, which is shorter than its diff:
```python
import jax
import jax.numpy as jnp
from jax import lax
from jax.experimental import pallas as pl
from jax.experimental.pallas import tpu as pltpu
from jax.sharding import Mesh
from jax.sharding import PartitionSpec as P

EPSILON = 1e-05
ROWS = ("half", "low")
AXES = ("img", *ROWS)
MIB = 1 << 20
LOW = jnp.bfloat16
FULL = jnp.float32
GROUP = 16
LANES = 128


def swap(value, flips):
    count = lax.axis_size(AXES)
    return lax.ppermute(value, AXES, [(i, i ^ flips[i & 1]) for i in range(count)])


def bits():
    count, found = lax.axis_size(AXES), []
    while (1 << len(found)) < count:
        found.append(1 << len(found))
    return found


def everyone(copies):
    return lax.all_to_all(copies, AXES, 0, 0)


def everyone_wide(sent, kept, low_step):
    value = kept + swap(sent, low_step[0])
    count = lax.axis_size(AXES[:2])
    mine = lax.all_to_all(jnp.broadcast_to(value[None], (count, *value.shape)), AXES[:2], 0, 0)
    return mine, swap(mine, low_step[0])


def tie(*values):
    return lax.optimization_barrier(values)


def flat_index():
    return lax.axis_index("img") * lax.axis_size(ROWS) + lax.axis_index(ROWS)


def plan():
    order = bits()
    steps = [(bit, bit) for bit in order]
    if len(order) >= 3:
        steps[1], steps[2] = (order[1], order[2]), (order[2], order[1])
    index = flat_index()
    low = index % 2
    chosen = []
    for even, odd in steps:
        chosen.append(((even, odd), jnp.where(low == 0, index // even % 2, index // odd % 2)))
    return chosen


def half_of(value, which, axis=0):
    size = value.shape[axis] // 2
    return lax.dynamic_slice_in_dim(value, which * size, size, axis=axis)


def stack(mine, value, other):
    low = mine == 0
    return jnp.stack([jnp.where(low, value, other), jnp.where(low, other, value)])


def scatter_step(value, step):
    _, mine = step
    return half_of(value, 1 - mine).astype(LOW), half_of(value, mine)


def merge(value, other, step):
    return stack(step[1], value, other).reshape((-1,) + value.shape[1:])


def reduce_chain(value, steps):
    for step in steps:
        sent, kept = scatter_step(value, step)
        came = yield sent, step[0]
        value = kept + came.astype(FULL)
    return value


def gather_chain(value, steps):
    for step in steps:
        came = yield value, step[0]
        value = merge(value, came, step)
    return value


class Chains:
    def __init__(self):
        self.running, self.flying, self.results = {}, {}, {}

    def begin(self, name, chain, spans, sent=None):
        self.running[name] = (chain, list(spans))
        self.load(name, next(chain) if sent is None else sent)

    def load(self, name, sent):
        spans = self.running[name][1]
        self.flying[name] = [sent, None, spans.pop(0) if spans else 1]

    def slot(self, *extra):
        due = []
        for name, flight in self.flying.items():
            if flight[1] is None:
                flight[1] = swap(*flight[0])
            flight[2] -= 1
            if flight[2] <= 0:
                due.append(name)
        done = tie(*(self.flying[name][1] for name in due), *extra) if due or extra else ()
        for name, value in zip(due, done):
            try:
                self.load(name, self.running[name][0].send(value))
            except StopIteration as end:
                self.results[name] = end.value
                del self.running[name], self.flying[name]
        return done[len(due) :]


def sum_rows_axis(value):
    count, bit = lax.axis_size(ROWS), 1
    while bit < count:
        value = value + lax.ppermute(value, ROWS, [(i, i ^ bit) for i in range(count)])
        bit *= 2
    return value


def trade(near, far):
    count = lax.axis_size(ROWS)
    pairs = [(i, i + 1) for i in range(1, count - 1, 2)]
    return (
        lax.ppermute(near, ROWS, [(i, i ^ 1) for i in range(count)]),
        lax.ppermute(far, ROWS, pairs + [(b, a) for a, b in pairs]),
    )


def call(kernel, outs, *args, scratch=(), left=(), limit=60):
    def place(at, arg):
        if at in left:
            return pl.BlockSpec(memory_space=pltpu.HBM)
        return pl.BlockSpec(memory_space=pltpu.SMEM if arg.dtype == jnp.int32 else pltpu.VMEM)

    return pl.pallas_call(
        kernel,
        out_shape=[jax.ShapeDtypeStruct(shape, kind) for shape, kind in outs],
        in_specs=[place(at, arg) for at, arg in enumerate(args)],
        out_specs=[pl.BlockSpec(memory_space=pltpu.VMEM)] * len(outs),
        scratch_shapes=list(scratch),
        compiler_params=pltpu.CompilerParams(vmem_limit_bytes=limit * MIB),
    )(*args)


def logistic(values):
    return 0.5 * jnp.tanh(0.5 * values) + 0.5


def slope(values):
    s = logistic(values)
    return s * (1.0 + values * (1.0 - s))


def shifted(values, by):
    return pltpu.roll(values, (-by) % values.shape[0], 0)


def spread(images, height, width, main, above, below):
    channels = main.shape[-1]
    main = main.reshape(images, height, width, channels)
    above = above.reshape(images, 1, width, channels)
    below = below.reshape(images, 1, width, channels)
    flat = (images * height * width, channels)
    return (
        jnp.concatenate([above, main[:, :-1]], axis=1).reshape(flat),
        main.reshape(flat),
        jnp.concatenate([main[:, 1:], below], axis=1).reshape(flat),
    )


def wide(mask, like):
    return jnp.concatenate([mask] * (like.shape[1] // mask.shape[1]), axis=1)


def edges_of(dims, place, value, near, far):
    images, height, width = dims
    value = value.reshape(images, height, width, -1)
    top = value[:, 0].reshape(images * width, -1)
    bottom = value[:, height - 1].reshape(images * width, -1)
    odd = place[0, 0] % 2 == 1
    near[...] = jnp.where(odd, top, bottom)
    far[...] = jnp.where(odd, bottom, top)


def first_forward(
    dims, place, map_size, gain, bias, gain_mid, bias_mid, features, weight,
    first, near, far, sums, params, params_mid, areas, mask, mask_other, mask_above, mask_below,
    sizes, few, left, right, few_sems, sems,
):
    images, height, width = dims
    lanes = mask.shape[1]
    parts = sems.shape[1]
    deep = left.shape[1] // parts
    small = [pltpu.make_async_copy(map_size, sizes, few_sems.at[0])]
    for k, source in enumerate((gain, bias, gain_mid, bias_mid)):
        small.append(pltpu.make_async_copy(source, few.at[k], few_sems.at[k + 1]))
    for copy in small:
        copy.start()

    def load(k):
        span = pl.ds(k * deep, deep)
        return (
            pltpu.make_async_copy(features.at[:, span], left.at[:, span], sems.at[0, k]),
            pltpu.make_async_copy(weight.at[span, :], right.at[span, :], sems.at[1, k]),
        )

    for k in range(parts):
        for copy in load(k):
            copy.start()
    for copy in small:
        copy.wait()

    def inside(start, count):
        spot = lax.broadcasted_iota(jnp.int32, (count * width, lanes), 0)
        row, column = start + spot // width, spot % width
        parts = []
        for n in range(images):
            size = sizes[0, n]
            here = (row >= 0) & (row < size) & (column < size)
            parts.append(jnp.where(here, 1.0, 0.0))
        return jnp.concatenate(parts, axis=0)

    start = place[0, 0] * height
    kept = inside(start, height)
    mask[...] = kept
    mask_other[...] = inside((place[0, 0] + 1 - 2 * (place[0, 0] % 2)) * height, height)
    mask_above[...] = inside(start - 1, 1)
    mask_below[...] = inside(start + height, 1)
    params[0:1], params[1:2] = few[0], few[1]
    params_mid[0:1], params_mid[1:2] = few[2], few[3]
    spot = lax.broadcasted_iota(jnp.int32, areas.shape, 0)
    area = jnp.zeros(areas.shape, FULL)
    for n in range(images):
        area = jnp.where(spot == n, (sizes[0, n] * sizes[0, n]).astype(FULL), area)
    areas[...] = area
    total = None
    for k in range(parts):
        for copy in load(k):
            copy.wait()
        span = pl.ds(k * deep, deep)
        part = jnp.dot(left[:, span], right[span, :], preferred_element_type=FULL)
        total = part if total is None else total + part
    first[...] = total
    masked = total * wide(kept, total)
    middle = total.shape[1]
    sums[:, 0, 0:middle] = spread_sum(sums, masked)
    sums[:, 1, 0:middle] = spread_sum(sums, masked * total)
    sums[:, 0, middle:] = spread_sum(sums, kept)
    lane = lax.broadcasted_iota(jnp.int32, (1, lanes), 1)
    told = jnp.zeros((1, lanes), FULL)
    for n in range(images):
        told = jnp.where(lane == n, sizes[0, n].astype(FULL), told)
    sums[:, 1, middle:] = jnp.broadcast_to(told, (sums.shape[0], lanes))
    edges_of(dims, place, total, near, far)


def spread_sum(copies, values):
    total = jnp.sum(values, axis=0, keepdims=True)
    return jnp.broadcast_to(total, (copies.shape[0], total.shape[1]))


def fetch(weight, held, sems):
    def load(i, j):
        return pltpu.make_async_copy(weight.at[i, j], held.at[i, j], sems.at[i, j])

    for j in range(3):
        for i in range(3):
            load(i, j).start()

    def tap(i, j):
        load(i, j).wait()
        return held[i, j]

    return tap


def put_sums(dims, place, at, values, others, sent, kept):
    chunk, half = values.shape[1], sent.shape[1]
    span = pl.ds(at % half, chunk)
    mine = (place[0, 0] % 2 == 1) == (at >= half)
    for k, value in enumerate((values, others)):
        total = jnp.sum(value, axis=0, keepdims=True)
        kept[k : k + 1, span] = jnp.where(mine, total, kept[k : k + 1, span])
        sent[k : k + 1, span] = jnp.where(mine, sent[k : k + 1, span], total)


def take_sums(place, at, chunk, mine, other):
    half = mine.shape[2]
    span = pl.ds(at % half, chunk)
    here = (place[0, 0] % 2 == 1) == (at >= half)
    return jnp.where(here, jnp.sum(mine[:, :, span], axis=0), jnp.sum(other[:, :, span], axis=0))


def affine(sums, count, gain, bias):
    average = sums[0:1] / count
    inv_std = lax.rsqrt(sums[1:2] / count - average * average + EPSILON)
    scale = inv_std * gain
    return average, inv_std, scale, bias - average * scale


def mid_forward(
    dims, place, came, params, first, near, far, mask, mask_above, mask_below, weight,
    split, second, sums, sums_first, sizes, held, sems,
):
    tap = fetch(weight, held, sems)
    middle = first.shape[1]
    totals = jnp.sum(came[...], axis=0)
    sums_first[...] = totals
    for y in range(2):
        sizes[y : y + 1] = came[place[0, 1] + y * place[0, 2], 1:2, middle:]
    count = totals[0:1, middle : middle + 1]
    _, _, scale, shift = affine(totals[:, 0:middle], count, params[0:1], params[1:2])

    def act(hidden, inside):
        pre = hidden * scale + shift
        return pre * logistic(pre) * wide(inside[...], pre)

    odd = place[0, 0] % 2 == 1
    centre = act(first[...], mask)
    above = act(jnp.where(odd, near[...], far[...]), mask_above)
    below = act(jnp.where(odd, far[...], near[...]), mask_below)
    three = spread(*dims, centre, above, below)
    x3 = [part.astype(LOW) for part in three]
    flat_rows(dims, centre, split)
    total = None
    for j in range(3):
        part = None
        for i in range(3):
            term = jnp.dot(x3[i], tap(i, j), preferred_element_type=FULL)
            part = term if part is None else part + term
        part = shifted(part, j - 1) if j != 1 else part
        total = part if total is None else total + part
    second[...] = total
    masked = total * wide(mask[...], total)
    sums[:, 0] = spread_sum(sums, masked)
    sums[:, 1] = spread_sum(sums, masked * total)


def flat_rows(dims, value, out):
    images, height, width = dims
    value = value.reshape(images, height, width, -1)
    for r in range(height):
        out[r] = value[:, r].reshape(images * width, -1).astype(LOW)


def flat_halves(dims, place, value, sent, kept):
    quarter = value.shape[1] // 4
    odd, high = place[0, 0] % 2 == 1, place[0, 3] == 1
    parts = [value[:, k * quarter : (k + 1) * quarter] for k in range(4)]
    parts[1], parts[2] = jnp.where(odd, parts[2], parts[1]), jnp.where(odd, parts[1], parts[2])
    one, two = jnp.concatenate(parts[:2], axis=1), jnp.concatenate(parts[2:], axis=1)
    flat_rows(dims, jnp.where(high, one, two), sent)
    flat_rows(dims, jnp.where(high, two, one), kept)


def out_forward(
    dims, place, sums_first, came, params_mid, second, mask, weight,
    act, normed_sent, normed_kept, third, sums_sent, sums_kept, sums_second,
):
    middle = second.shape[1]
    totals = jnp.sum(came[...], axis=0)
    sums_second[...] = totals
    count = sums_first[0:1, middle : middle + 1]
    average, inv_std, scale, shift = affine(totals, count, params_mid[0:1], params_mid[1:2])
    hidden = second[...]
    pre = hidden * scale + shift
    inside = wide(mask[...], hidden)
    act[...] = (pre * logistic(pre) * inside).astype(LOW)
    flat_halves(dims, place, (hidden - average) * inv_std, normed_sent, normed_kept)
    for at in range(0, third.shape[1], middle):
        span = pl.ds(at, middle)
        total = jnp.dot(act[...], weight[:, span], preferred_element_type=FULL)
        third[:, span] = total
        masked = total * inside
        put_sums(dims, place, at, masked, masked * total, sums_sent, sums_kept)


def out_result(
    dims, place, sums_first, came, other, params_out, third, features, out_grad, pool_grad, areas, mask,
    result, pooled, grad, sums_sent, sums_kept, sums_third,
):
    images, height, width = dims
    chunk = sums_first.shape[1] - mask.shape[1]
    count = sums_first[0:1, chunk : chunk + 1]
    inside = jnp.concatenate([mask[...]] * (chunk // mask.shape[1]), axis=1)
    area = jnp.concatenate([areas[...]] * (chunk // mask.shape[1]), axis=1)
    for at in range(0, third.shape[1], chunk):
        span = pl.ds(at, chunk)
        totals = take_sums(place, at, chunk, came, other)
        sums_third[:, span] = totals
        average, inv_std, _, _ = affine(totals, count, 1.0, 0.0)
        normed = (third[:, span] - average) * inv_std
        summed = params_out[0:1, span] * normed + params_out[1:2, span] + features[:, span].astype(FULL)
        gate = logistic(summed)
        value = summed * gate * inside
        result[:, span] = value.astype(LOW)
        pooled[:, span] = jnp.sum(value.reshape(images, height * width, chunk), axis=1)
        share = (pool_grad[:, span] / area)[:, None]
        total = out_grad[:, span].astype(FULL).reshape(images, height * width, chunk) + share
        total = total.reshape(inside.shape) * inside * (gate * (1.0 + summed * (1.0 - gate)))
        grad[:, span] = total
        put_sums(dims, place, at, total, total * normed, sums_sent, sums_kept)


def out_backward(
    dims, place, sums_first, sums_second, sums_third, came, other, params_mid, params_out, third, grad, second,
    mask, weight, third_sent, third_kept, pre_grad, rows_sent, rows_kept, near, far, sums, sums_out, lows,
):
    chunk = second.shape[1]
    count = sums_first[0:1, chunk : chunk + 1]
    inside = wide(mask[...], second)
    back = None
    for at in range(0, third.shape[1], chunk):
        span = pl.ds(at, chunk)
        average, inv_std, scale, _ = affine(sums_third[:, span], count, params_out[0:1, span], 0.0)
        normed = (third[:, span] - average) * inv_std
        totals = take_sums(place, at, chunk, came, other)
        sums_out[:, span] = totals
        mean = (totals[0:1] + normed * totals[1:2]) / count
        low = (inside * scale * (grad[:, span] - mean)).astype(LOW)
        lows[:, span] = low
        part = lax.dot_general(
            low, weight[:, span], (((1,), (1,)), ((), ())), preferred_element_type=FULL
        )
        back = part if back is None else back + part
    average, inv_std, scale, shift = affine(sums_second[...], count, params_mid[0:1], params_mid[1:2])
    hidden = second[...]
    back = back * inside * slope(hidden * scale + shift)
    pre_grad[...] = back
    flat_halves(dims, place, back, rows_sent, rows_kept)
    odd, half = place[0, 0] % 2 == 1, third.shape[1] // 2
    one, two = lows[:, 0:half], lows[:, half:]
    third_sent[...] = jnp.where(odd, one, two)
    third_kept[...] = jnp.where(odd, two, one)
    sums[:, 0] = spread_sum(sums, back)
    sums[:, 1] = spread_sum(sums, back * ((hidden - average) * inv_std))
    edges_of(dims, place, jnp.concatenate([back, hidden], axis=1), near, far)


def mid_weights(
    place, sizes, sums_first, sums_second, sums_grad, params_mid,
    acts_mine, acts_came, normed_mine, normed_came, grads_mine, grads_came, sent, kept, left, right,
):
    groups, _, size, channels = kept.shape
    pixels = acts_mine.shape[2]
    images = sizes.shape[1]
    width = pixels // images
    swapped, high = place[0, 0] == 1, place[0, 3] == 1
    middle = sums_grad.shape[1]
    count = sums_first[0:1, middle : middle + 1]
    span = pl.ds(pl.multiple_of(place[0, 1] * channels, channels), channels)
    average = sums_second[0:1, span] / count
    inv_std = lax.rsqrt(sums_second[1:2, span] / count - average * average + EPSILON)
    scale = inv_std * params_mid[0:1, span]
    mean_grad, mean_gain = sums_grad[0:1, span] / count, sums_grad[1:2, span] / count
    column = lax.broadcasted_iota(jnp.int32, (width, channels), 0)
    for y in range(2):
        for x in range(2):
            for c in range(2):
                spot = jnp.where(swapped, 2 * y + c, 2 * x + c)
                here = jnp.where(swapped, x, y) == place[0, 2]
                four = 2 * x + y if c else 2 * y + x
                own = place[0, 0] == c
                rows = pl.ds(((2 * y + x) * 2 + c) * pixels, pixels)
                for r in range(2):
                    left[r, rows, :] = jnp.where(here, acts_mine[spot, r], acts_came[spot, r])
                    row = (2 * x + c) * 2 + r
                    inside = []
                    for n in range(images):
                        extent = jnp.where(row < sizes[y, n], sizes[y, n], 0)
                        inside.append(jnp.where(column < extent, 1.0, 0.0))
                    value = jnp.where(own, grads_mine[four, r], grads_came[four, r]).astype(FULL)
                    normed = jnp.where(own, normed_mine[four, r], normed_came[four, r])
                    value = value - (mean_grad + normed.astype(FULL) * mean_gain)
                    value = value * scale * jnp.concatenate(inside, axis=0)
                    right[r, rows, 0:channels] = value.astype(LOW)
    for r in range(2):
        grad = right[r, :, 0:channels].astype(FULL)
        right[r, :, channels : 2 * channels] = shifted(grad, 1).astype(LOW)
        right[r, :, 2 * channels :] = shifted(grad, -1).astype(LOW)
    span, image = 3 * pixels, 4 * pixels

    def product(r_left, at_left, r_right, at_right, count):
        return lax.dot_general(
            left[r_left, pl.ds(at_left, count), :],
            right[r_right, pl.ds(at_right, count), :],
            (((0,), (0,)), ((), ())),
            preferred_element_type=FULL,
        )

    def crossed(r_left, r_right, skip_left, skip_right):
        part = product(r_left, 0, r_right, 0, 2 * image)
        for y in range(2):
            part = part + product(
                r_right, y * image + skip_left, r_left, y * image + skip_right, span
            )
        return part

    taps = (
        crossed(0, 1, 0, pixels),
        product(0, 0, 0, 0, 2 * image) + product(1, 0, 1, 0, 2 * image),
        crossed(1, 0, pixels, 0),
    )
    for i in range(3):
        for j, place in ((1, 0), (0, 1), (2, 2)):
            part = taps[i][:, place * channels : (place + 1) * channels]
            one = part[0 : groups * size].reshape(groups, size, channels)
            two = part[groups * size :].reshape(groups, size, channels)
            sent[:, 3 * i + j] = jnp.where(high, one, two).astype(LOW)
            kept[:, 3 * i + j] = jnp.where(high, two, one)


def mid_assemble(odd, mine, other, total):
    quarters, groups, _, size, lanes = mine.shape
    half = groups * size
    swapped = odd[0, 0] == 1
    for q, turned in enumerate((0, 2, 1, 3)):
        span = pl.ds(q * lanes, lanes)
        even = jnp.where(swapped, other[q, :, 0], mine[q, :, 0])
        total[0, 0:half, span] = even.astype(FULL).reshape(half, lanes)
        uneven = jnp.where(swapped, mine[turned, :, 0], other[turned, :, 0])
        total[0, half:, span] = uneven.astype(FULL).reshape(half, lanes)


def mid_backward(
    dims, place, sums_first, sums_second, came, params, params_mid, grad, near, far,
    second, first, mask, mask_above, mask_below, weight, pre_grad, low_grad, sums, sums_mid, held, sems,
):
    tap = fetch(weight, held, sems)
    middle = first.shape[1]
    count = sums_first[0:1, middle : middle + 1]
    totals = jnp.sum(came[...], axis=0)
    sums_mid[...] = totals
    average, inv_std, scale, shift = affine(sums_second[...], count, params_mid[0:1], params_mid[1:2])
    mean_grad, mean_gain = totals[0:1] / count, totals[1:2] / count

    def normed_grad(value, hidden, inside):
        normed = (hidden - average) * inv_std
        return wide(inside[...], value) * scale * (value - (mean_grad + normed * mean_gain))

    odd = place[0, 0] % 2 == 1

    def beside(one, other, inside):
        value = jnp.where(odd, one[:, 0:middle], other[:, 0:middle])
        return normed_grad(value, jnp.where(odd, one[:, middle:], other[:, middle:]), inside)

    centre = normed_grad(grad[...], second[...], mask)
    above = beside(near, far, mask_above)
    below = beside(far, near, mask_below)
    three = spread(*dims, centre, above, below)
    average, inv_std, scale, shift = affine(sums_first[:, 0:middle], count, params[0:1], params[1:2])
    low = [part.astype(LOW) for part in three]
    total = None
    for j in range(3):
        part = None
        for i in range(3):
            term = lax.dot_general(
                low[2 - i], tap(i, j), (((1,), (1,)), ((), ())), preferred_element_type=FULL
            )
            part = term if part is None else part + term
        part = shifted(part, 1 - j) if j != 1 else part
        total = part if total is None else total + part
    hidden = first[...]
    total = total * wide(mask[...], total) * slope(hidden * scale + shift)
    pre_grad[...] = total
    low_grad[...] = total.astype(LOW)
    sums[:, 0] = spread_sum(sums, total)
    sums[:, 1] = spread_sum(sums, total * ((hidden - average) * inv_std))


def first_backward(sums_first, came, params, first, grad, mask, first_other, grad_other, mask_other, low, sums_in):
    pixels, middle = first.shape
    count = sums_first[0:1, middle : middle + 1]
    totals = jnp.sum(came[...], axis=0)
    sums_in[...] = totals
    average, inv_std, scale, _ = affine(sums_first[:, 0:middle], count, params[0:1], 0.0)
    pairs = ((first, grad, mask), (first_other, grad_other, mask_other))
    for k, (hidden, source, inside) in enumerate(pairs):
        normed = (hidden[...] - average) * inv_std
        value = source[...].astype(FULL) - (totals[0:1] + normed * totals[1:2]) / count
        low[k * pixels : (k + 1) * pixels] = (wide(inside[...], value) * scale * value).astype(LOW)


def assemble(odd, mine, other, shape):
    groups, taps, size, lanes = shape
    quarters = mine.shape[0] // (groups * taps * size)
    channels = quarters * lanes
    pieces = pl.BlockSpec((quarters, groups, 1, size, lanes), lambda t: (0, 0, t, 0, 0))
    return pl.pallas_call(
        mid_assemble,
        grid=(taps,),
        out_shape=jax.ShapeDtypeStruct((taps, channels, channels), FULL),
        in_specs=[pl.BlockSpec(memory_space=pltpu.SMEM), pieces, pieces],
        out_specs=pl.BlockSpec((1, channels, channels), lambda t: (t, 0, 0)),
        compiler_params=pltpu.CompilerParams(vmem_limit_bytes=48 * MIB),
    )(
        odd,
        mine.reshape(quarters, groups, taps, size, lanes),
        other.reshape(quarters, groups, taps, size, lanes),
    )


def halves(value, step):
    _, mine = step
    return half_of(value, 1 - mine, 3), half_of(value, mine, 3)


def contract(left, right):
    return lax.dot_general(left, right, (((0,), (0,)), ((), ())), preferred_element_type=FULL)


def times_transpose(left, weights):
    return lax.dot_general(left, weights, (((1,), (1,)), ((), ())), preferred_element_type=FULL)


def per_device(
    features,
    weight_in,
    gain_in,
    bias_in,
    weight_mid,
    gain_mid,
    bias_mid,
    weight_out,
    gain_out,
    bias_out,
    map_size,
    out_grad,
    pool_grad,
):
    images, height, width, channels = features.shape
    middle = weight_mid.shape[3]
    dims = (images, height, width)
    pixels = images * height * width

    count = lax.axis_size(AXES)
    place = lax.axis_index(ROWS).astype(jnp.int32)
    index = flat_index()
    rows_count = lax.axis_size(ROWS)
    base = index - lax.axis_index("img") % 2 * rows_count

    count = lax.axis_size(AXES)
    flat_features = features.reshape(pixels, channels)
    params_out = jnp.stack([gain_out, bias_out])
    steps = plan()
    core, mine, far_steps = steps[0], steps[0][1], steps[3:]
    place = jnp.stack([place, base, jnp.int32(rows_count), steps[1][1]]).astype(jnp.int32)[None]
    plane, narrow, broad, large = (pixels, middle), (2, middle), (2, channels), (pixels, channels)
    edge, split_rows = (images * width, middle), (height, images * width, middle)
    half_broad = (2, channels // 2)
    half_rows = (height, images * width, middle // 2)
    taps = [pltpu.VMEM(weight_mid.shape, LOW), pltpu.SemaphoreType.DMA((3, 3))]

    first, near, far, sums, params, params_mid, areas, mask, mask_other, mask_above, mask_below = call(
        lambda *refs: first_forward(dims, *refs),
        [
            (plane, FULL),
            (edge, FULL),
            (edge, FULL),
            ((count, 2, middle + LANES), FULL),
            (narrow, FULL),
            (narrow, FULL),
            ((images, LANES), FULL),
            ((pixels, LANES), FULL),
            ((pixels, LANES), FULL),
            ((images * width, LANES), FULL),
            ((images * width, LANES), FULL),
        ],
        place,
        map_size[None],
        gain_in[None],
        bias_in[None],
        gain_mid[None],
        bias_mid[None],
        flat_features,
        weight_in,
        scratch=[
            pltpu.SMEM((1, images), jnp.int32),
            pltpu.VMEM((4, 1, middle), FULL),
            pltpu.VMEM((pixels, channels), LOW),
            pltpu.VMEM((channels, middle), LOW),
            pltpu.SemaphoreType.DMA((5,)),
            pltpu.SemaphoreType.DMA((2, 4)),
        ],
        left=(1, 2, 3, 4, 5, 6, 7),
        limit=60,
    )
    near, far = trade(near, far)
    came, near, far = tie(everyone(sums), near, far)
    split, second, sums, sums_first, sizes = call(
        lambda *refs: mid_forward(dims, *refs),
        [
            (split_rows, LOW),
            (plane, FULL),
            ((count, 2, middle), FULL),
            ((2, middle + LANES), FULL),
            ((2, LANES), FULL),
        ],
        place,
        came,
        params,
        first,
        near,
        far,
        mask,
        mask_above,
        mask_below,
        weight_mid,
        scratch=taps,
        left=(9,),
    )
    acts = swap(half_of(split, 1 - mine, 2), core[0])
    came, acts, first_other = tie(everyone(sums), acts, swap(first, core[0]))
    second_act, normed_sent, normed_kept, third, sums_sent, sums_kept, sums_second = call(
        lambda *refs: out_forward(dims, *refs),
        [
            (plane, LOW),
            (half_rows, LOW),
            (half_rows, LOW),
            (large, FULL),
            (half_broad, FULL),
            (half_broad, FULL),
            (narrow, FULL),
        ],
        place,
        sums_first,
        came,
        params_mid,
        second,
        mask,
        weight_out,
    )
    acts = stack(mine, half_of(split, mine, 2), acts)
    features_came = swap(half_of(flat_features, 1 - mine, 1), core[0])
    came, came_other, acts_came, normed_came, act_other, features_came = tie(
        *everyone_wide(sums_sent, sums_kept, core),
        swap(acts, steps[1][0]),
        swap(normed_sent[None], steps[1][0]),
        swap(second_act, core[0]),
        features_came,
    )
    result, pooled, grad_summed, sums_sent, sums_kept, sums_third = call(
        lambda *refs: out_result(dims, *refs),
        [
            (large, LOW),
            ((images, channels), FULL),
            (large, FULL),
            (half_broad, FULL),
            (half_broad, FULL),
            (broad, FULL),
        ],
        place,
        sums_first,
        came,
        came_other,
        params_out,
        third,
        flat_features,
        out_grad.reshape(pixels, channels),
        pool_grad,
        areas,
        mask,
    )

    acts = merge(acts, acts_came, steps[1])
    normed_sent, normed_kept = halves(merge(normed_kept[None], normed_came, steps[1]), steps[2])
    sums_sent, acts, normed_sent = tie(sums_sent, acts, normed_sent)
    features_pair = jnp.concatenate([half_of(flat_features, mine, 1), features_came])
    features_sent = half_of(features_pair, 1 - steps[1][1], 1)
    features_kept = half_of(features_pair, steps[1][1], 1)
    normed = merge(normed_kept, swap(normed_sent, steps[2][0]), steps[2])
    came, came_other, acts_came, normed, features_sent, features_kept = tie(
        *everyone_wide(sums_sent, sums_kept, core),
        swap(acts, steps[2][0]),
        normed,
        features_sent,
        features_kept,
    )
    third_sent, third_kept, grad_second_pre, grads_sent, grads_kept, near, far, sums, sums_out = call(
        lambda *refs: out_backward(dims, *refs),
        [
            ((pixels, channels // 2), LOW),
            ((pixels, channels // 2), LOW),
            (plane, FULL),
            (half_rows, LOW),
            (half_rows, LOW),
            ((edge[0], 2 * middle), FULL),
            ((edge[0], 2 * middle), FULL),
            ((count, 2, middle), FULL),
            (broad, FULL),
        ],
        place,
        sums_first,
        sums_second,
        sums_third,
        came,
        came_other,
        params_mid,
        params_out,
        third,
        grad_summed,
        second,
        mask,
        weight_out,
        scratch=[pltpu.VMEM(large, LOW)],
    )

    near, far = trade(near, far)
    sums = everyone(sums)
    came = swap(grads_sent[None], steps[1][0])
    sent, kept = halves(merge(grads_kept[None], came, steps[1]), steps[2])
    came = swap(sent, steps[2][0])
    third_came = swap(third_sent, core[0])
    sums, came, third_came, near, far = tie(sums, came, third_came, near, far)
    grads = merge(kept, came, steps[2])
    grad_first_pre, low_grad, sums, sums_mid = call(
        lambda *refs: mid_backward(dims, *refs),
        [(plane, FULL), (plane, LOW), ((count, 2, middle), FULL), (narrow, FULL)],
        place,
        sums_first,
        sums_second,
        sums,
        params,
        params_mid,
        grad_second_pre,
        near,
        far,
        second,
        first,
        mask,
        mask_above,
        mask_below,
        weight_mid,
        scratch=taps,
        left=(14,),
    )
    sums = everyone(sums)
    grad_other = swap(low_grad, core[0])
    grads_came, normed_came = swap(grads, core[0]), swap(normed, core[0])

    def out_rows(which):
        one, two = (half_of(act, which, 1) for act in (second_act, act_other))
        return contract(one, third_kept) + contract(two, third_came)

    odd = (index % 2).astype(jnp.int32).reshape(1, 1)
    def out_chain():
        came = yield out_rows(1 - steps[1][1]).astype(LOW), steps[1][0]
        value = out_rows(steps[1][1]) + came.astype(FULL)
        value = yield from reduce_chain(value, steps[2:])
        value = yield from gather_chain(value.astype(LOW), steps[:0:-1])
        other = yield value, core[0]
        low = mine == 0
        parts = [jnp.where(low, value, other), jnp.where(low, other, value)]
        return jnp.concatenate(parts, axis=1).astype(FULL)

    def mid_chain():
        high, low = steps[1][1], steps[2][1]
        chunk = jnp.where(index % 2 == 0, 2 * high + low, 2 * low + high)
        lanes, deep = grads.shape[-1], acts.shape[-1]
        span = 2 * acts.shape[0] * images * width
        shape = (deep // GROUP // 2, 9, GROUP, lanes)
        sent, kept = call(
            mid_weights,
            [(shape, LOW), (shape, FULL)],
            jnp.stack([index % 2, chunk, steps[2][1], far_steps[0][1]]).astype(jnp.int32)[None],
            sizes[:, :images].astype(jnp.int32),
            sums_first,
            sums_second,
            sums_mid,
            params_mid,
            acts,
            acts_came,
            normed,
            normed_came,
            grads,
            grads_came,
            scratch=[pltpu.VMEM((2, span, deep), LOW), pltpu.VMEM((2, span, 3 * lanes), LOW)],
        )
        came = yield sent.reshape(-1, lanes), far_steps[0][0]
        value = kept.reshape(-1, lanes) + came.astype(FULL)
        value = yield from reduce_chain(value, far_steps[1:])
        value = yield from gather_chain(value.astype(LOW), steps[:0:-1])
        other = yield value, core[0]
        return assemble(odd, value, other, (2 * shape[0], *shape[1:]))

    def in_chain():
        came = yield contract(features_sent, grad_first).astype(LOW), steps[1][0]
        value = contract(features_kept, grad_first) + came.astype(FULL)
        value = yield from reduce_chain(value, steps[2:])
        value = yield from gather_chain(value.astype(LOW), steps[:0:-1])
        other = yield value, core[0]
        return stack(mine, value, other).reshape(-1, middle).astype(FULL)

    chains = Chains()
    mid = mid_chain()
    mid_sent, flips = next(mid)
    chains.begin("out", out_chain(), ())
    came, mid_sent, grad_other = chains.slot(sums, mid_sent, grad_other)
    chains.begin("mid", mid, (), (mid_sent, flips))
    pooled = sum_rows_axis(pooled)
    grad_first, sums_in = call(
        first_backward,
        [((2 * pixels, middle), LOW), (narrow, FULL)],
        sums_first,
        came,
        params,
        first,
        grad_first_pre,
        mask,
        first_other,
        grad_other,
        mask_other,
    )
    entry = in_chain()
    in_sent, in_flips = next(entry)
    in_sent, pooled = chains.slot(in_sent, pooled)
    chains.begin("in", entry, (), (in_sent, in_flips))
    pooled = pooled / areas[:, :1]
    grad_features = grad_summed + times_transpose(grad_first[:pixels], weight_in)
    (grad_features,) = chains.slot(grad_features)
    while chains.running:
        chains.slot()
    grad_weight_in, grad_weight_mid, grad_weight_out = (
        chains.results[name] for name in ("in", "mid", "out")
    )
    whole = (images, height, width, channels)
    return (
        result.astype(LOW).reshape(whole),
        pooled,
        grad_features.reshape(whole),
        grad_weight_in,
        sums_in[1],
        sums_in[0],
        grad_weight_mid.reshape(weight_mid.shape),
        sums_mid[1],
        sums_mid[0],
        grad_weight_out,
        sums_out[1],
        sums_out[0],
    )


def solution(mesh):
    images, rows = mesh.devices.shape
    mesh = Mesh(mesh.devices.reshape(images, rows // 2, 2), AXES)
    tiles, single = P("img", ROWS, None, None), P()
    return jax.shard_map(
        per_device,
        mesh=mesh,
        in_specs=(tiles,) + (single,) * 9 + (P("img"), tiles, P("img", None)),
        out_specs=(tiles, P("img", None), tiles) + (single,) * 9,
        check_vma=False,
    )
```

time: 260 us -> 247 us (0.950)
  Pallas kernels: 33.1 us -> 47.6 us
  local copies, waits for them, and re-layouts: 19.4 us -> 7.32 us
  other arithmetic: 24.9 us -> 17.5 us
  waiting for transfers between devices: 87.6 us -> 82 us
  starting transfers between devices: 85 us -> 80 us
  matrix products: 6.23 us -> 10.5 us
    pallas_call x8, Pallas kernels: 25.3 us -> 41.7 us  [call(): pl.pallas_call(kernel, out_shape=[jax.ShapeDtypeStruct(shape, kind) for s...]
    unnamed x142 -> x74, local copies, waits for them, and re-layouts: 14 us -> 2.85 us
    all_to_all x0 -> x2, starting transfers between devices: none -> 9.1 us  [everyone_wide(): lax.all_to_all(jnp.broadcast_to(value[None], (count, *value.shape)), AXES...]
    ppermute x51 -> x43, waiting for transfers between devices: 69.6 us -> 61.3 us  [swap(): lax.ppermute(value, AXES, [(i, i ^ flips[i & 1]) for i in range(count)])]
    ppermute x51 -> x43, starting transfers between devices: 49.9 us -> 42.6 us  [swap(): lax.ppermute(value, AXES, [(i, i ^ flips[i & 1]) for i in range(count)])]
    ppermute x8 -> x6, starting transfers between devices: 14.9 us -> 9.17 us  [the longest x2 6.4 us: trade(): lax.ppermute(far, ROWS, pairs + [(b, a) for a, b in pairs])]
    another operation x47 -> x36, other arithmetic: 10.6 us -> 5.18 us  [stack(): jnp.stack([jnp.where(low, value, other), jnp.where(low, other, value)])]
    all_to_all x0 -> x2, waiting for transfers between devices: none -> 4.29 us  [everyone_wide(): lax.all_to_all(jnp.broadcast_to(value[None], (count, *value.shape)), AXES...]
  transfers between devices with their start and end apart: 63 -> 55, of which waited for: 28 -> 28; matrix products, arithmetic and copies ran while one was open for 9% -> 10% of each run, Pallas kernels for 6% -> 13%
where the time goes in v4:
time: 247 us; the launch traced here: 246 us
  waiting for transfers between devices  82 us (33%)
  starting transfers between devices  80 us (32%)
  Pallas kernels  47.6 us (19%)
  other arithmetic  17.5 us (7%)
  matrix products  10.5 us (4%)
  local copies, waits for them, and re-layouts  7.32 us (3%)
    ppermute x43, waiting for transfers between devices, swap(): lax.ppermute(value, AXES, [(i, i ^ flips[i & 1]) for i in range(count)])  61.3 us
    ppermute x43, starting transfers between devices, swap(): lax.ppermute(value, AXES, [(i, i ^ flips[i & 1]) for i in range(count)])  42.6 us
    pallas_call x8, Pallas kernels, call(): pl.pallas_call(kernel, out_shape=[jax.ShapeDtypeStruct(shape, kind) for s...  41.7 us
    all_to_all x4, starting transfers between devices, everyone(): return lax.all_to_all(copies, AXES, 0, 0)  19.2 us
    all_to_all x4, waiting for transfers between devices, everyone(): return lax.all_to_all(copies, AXES, 0, 0)  11.3 us
    all_to_all x2, starting transfers between devices, everyone_wide(): lax.all_to_all(jnp.broadcast_to(value[None], (count, *value.shape)), AXES...  9.1 us
    dot_general x6, matrix products, contract(): lax.dot_general(left, right, (((0,), (0,)), ((), ())), preferred_element_...  8.4 us
    ppermute x2, starting transfers between devices, trade(): lax.ppermute(far, ROWS, pairs + [(b, a) for a, b in pairs])  6.4 us
  transfers between devices with their start and end apart: 55, of which 28 were waited for; matrix products, arithmetic and copies ran while one was open for 10% of the time, Pallas kernels for 13%

profile of v4, /device:TPU:1, one launch (start us, length us, event | category | flops | bytes accessed | tf_op | source)
XLA Modules:
  0.0 246.4 jit_solution(17780645451569876319)
XLA Ops:
  1.3 4.3 %shard_map.220 = (f32[256,512]{1,0:T(8,128)}, f32[128,512]{1,0:T(8,128)}, f32[128,512]{1,0:T(8,128)}, f32[32,2,640]{2,1,0:T(2,128)}, f32[2,512]{1,0:T(2,128)}, /...) custom-call(s32[1,4]{1,0:T(1,128)} %add_bitcast_fusion.refs_0_, ...), custom_call_target="tpu_custom_call" | custom-call | tf_op jit(solution)/shard_map/pallas_call | solution.py:150
  5.6 7.1 %all-to-all-start = ((f32[32,2,640]{2,1,0:T(2,128)}), f32[32,2,640]{2,1,0:T(2,128)S(1)}, u32[]{:S(2)}, u32[]{:S(2)}) async-start(f32[32,2,640]{2,1,0:T(2,128)} %get-tuple-element.113), calls=%async_computation | async-start | bytes 327680 | tf_op jit(solution)/shard_map/all_to_all | solution.py:32
  13.3 3.5 %collective-permute-start.1 = (f32[128,512]{1,0:T(8,128)}, f32[128,512]{1,0:T(8,128)S(1)}, u32[]{:S(2)}, u32[]{:S(2)}) collective-permute-start(f32[128,512]{1,0:T(8,128)} %get-tuple-element.115), channel_id=1, source_target_pairs={{1,2},{2,1},{5,6},{6,5},{9,10},{10,9},{13,14},{14,13},{17,18},{18,... | collective-permute-start | bytes 786440 | tf_op jit(solution)/shard_map/ppermute | solution.py:140
  16.8 4.8 %collective-permute-done.1.refs_5_ = f32[128,512]{1,0:T(8,128)S(1)} collective-permute-done((f32[128,512]{1,0:T(8,128)}, f32[128,512]{1,0:T(8,128)S(1)}, u32[]{:S(2)}, u32[]{:S(2)}) %collective-permute-start.1) | collective-permute-done | bytes 262176 | tf_op jit(solution)/shard_map/ppermute | solution.py:140
  22.4 5.5 %shard_map.221 = (bf16[2,128,512]{2,1,0:T(8,128)(2,1)}, f32[256,512]{1,0:T(8,128)}, f32[32,2,512]{2,1,0:T(2,128)}, f32[2,640]{1,0:T(2,128)}, f32[2,128]{1,0:T(2,128)}) custom-call(s32[1,4]{1,0:T(1,128)} %add_bitcast_fusion.refs_0_, f32[32,2,640]{2,1,0:T(2,128)} %copy-done.8, f32[2,512]{1,0:T(2,128)} %get-tuple-element.117.refs_2_.refs_4_.params, ...), custom_call_target="tpu_custom_call" | custom-call | tf_op jit(solution)/shard_map/pallas_call | solution.py:150
  27.9 5.4 %all-to-all-start.1 = ((f32[32,2,512]{2,1,0:T(2,128)}), f32[32,2,512]{2,1,0:T(2,128)S(1)}, u32[]{:S(2)}, u32[]{:S(2)}) async-start(f32[32,2,512]{2,1,0:T(2,128)} %get-tuple-element.125), calls=%async_computation.1 | async-start | bytes 262144 | tf_op jit(solution)/shard_map/all_to_all | solution.py:32
  35.6 5.8 %all-to-all-done.1.refs_2_ = f32[32,2,512]{2,1,0:T(2,128)S(1)} async-done(((f32[32,2,512]{2,1,0:T(2,128)}), f32[32,2,512]{2,1,0:T(2,128)S(1)}, u32[]{:S(2)}, u32[]{:S(2)}) %all-to-all-start.1) | async-done | bytes 131104 | tf_op jit(solution)/shard_map/all_to_all | solution.py:32
  42.1 4.2 %shard_map.222 = (bf16[256,512]{1,0:T(8,128)(2,1)}, bf16[2,128,256]{2,1,0:T(8,128)(2,1)}, bf16[2,128,256]{2,1,0:T(8,128)(2,1)}, f32[256,2048]{1,0:T(8,128)}, f32...) custom-call(s32[1,4]{1,0:T(1,128)} %add_bitcast_fusion.refs_0_, ...), custom_call_target="tpu_custom_call" | custom-call | tf_op jit(solution)/shard_map/pallas_call | solution.py:150
  48.5 3.5 %all-to-all-start.2 = ((f32[16,2,1024]{2,1,0:T(2,128)}), f32[16,2,1024]{2,1,0:T(2,128)S(1)}, u32[]{:S(2)}, u32[]{:S(2)}) async-start(f32[16,2,1024]{2,1,0:T(2,128)} %broadcast_in_dim.51), calls=%async_computation.2 | async-start | bytes 262144 | tf_op jit(solution)/shard_map/all_to_all | solution.py:38
  55.5 3.3 %all-to-all-done.2.refs_2_ = f32[16,2,1024]{2,1,0:T(2,128)S(1)} async-done(((f32[16,2,1024]{2,1,0:T(2,128)}), f32[16,2,1024]{2,1,0:T(2,128)S(1)}, u32[]{:S(2)}, u32[]{:S(2)}) %all-to-all-start.2) | async-done | bytes 131104 | tf_op jit(solution)/shard_map/all_to_all | solution.py:38
  58.8 1.6 collective-permute-start.5
  62.5 7.4 %shard_map.223 = (bf16[256,2048]{1,0:T(8,128)(2,1)}, f32[16,2048]{1,0:T(8,128)}, f32[256,2048]{1,0:T(8,128)}, f32[2,1024]{1,0:T(2,128)}, f32[2,1024]{1,0:T(2,128)}, /*index=5*/f32[2,2048]{1,0:T(2,128)}) custom-call(s32[1,4]{1,0:T(1,128)} %add_bitcast_fusion.refs_0_, f32[2,640]{1,0:T(2,128)} %get-tuple-element.124.refs_1_.sums_first, ...), custom_call_target="tpu_custom_call" | custom-call | tf_op jit(solution)/shard_map/pallas_call | solution.py:150
  72.7 5.6 %all-to-all-start.3 = ((f32[16,2,1024]{2,1,0:T(2,128)}), f32[16,2,1024]{2,1,0:T(2,128)S(1)}, u32[]{:S(2)}, u32[]{:S(2)}) async-start(f32[16,2,1024]{2,1,0:T(2,128)} %broadcast_in_dim.54), calls=%async_computation.3 | async-start | bytes 262144 | tf_op jit(solution)/shard_map/all_to_all | solution.py:38
  85.0 1.8 collective-permute-start.11
  88.4 6.2 %shard_map.224 = (bf16[256,1024]{1,0:T(8,128)(2,1)}, bf16[256,1024]{1,0:T(8,128)(2,1)}, f32[256,512]{1,0:T(8,128)}, bf16[2,128,256]{2,1,0:T(8,128)(2,1)}, bf16[2...) custom-call(s32[1,4]{1,0:T(1,128)} %add_bitcast_fusion.refs_0_, ...), custom_call_target="tpu_custom_call" | custom-call | tf_op jit(solution)/shard_map/pallas_call | solution.py:150
  96.8 2.9 %collective-permute-start.18 = (f32[128,1024]{1,0:T(8,128)}, f32[128,1024]{1,0:T(8,128)}, u32[]{:S(2)}, u32[]{:S(2)}) collective-permute-start(f32[128,1024]{1,0:T(8,128)} %get-tuple-element.161), channel_id=1, source_target_pairs={{1,2},{2,1},{5,6},{6,5},{9,10},{10,9},{13,14},{14,13},{17,18},{18,... | collective-permute-start | bytes 1572872 | tf_op jit(solution)/shard_map/ppermute | solution.py:140
  99.7 2.6 %all-to-all-start.4 = ((f32[32,2,512]{2,1,0:T(2,128)}), f32[32,2,512]{2,1,0:T(2,128)S(1)}, u32[]{:S(2)}, u32[]{:S(2)}) async-start(f32[32,2,512]{2,1,0:T(2,128)} %get-tuple-element.156), calls=%async_computation.4 | async-start | bytes 262144 | tf_op jit(solution)/shard_map/all_to_all | solution.py:32
  107.2 3.3 %all-to-all-done.4.refs_3_ = f32[32,2,512]{2,1,0:T(2,128)S(1)} async-done(((f32[32,2,512]{2,1,0:T(2,128)}), f32[32,2,512]{2,1,0:T(2,128)S(1)}, u32[]{:S(2)}, u32[]{:S(2)}) %all-to-all-start.4) | async-done | bytes 131104 | tf_op jit(solution)/shard_map/all_to_all | solution.py:32
  110.5 2.2 fusion.1
  115.1 6.5 %shard_map.225 = (f32[256,512]{1,0:T(8,128)}, bf16[256,512]{1,0:T(8,128)(2,1)}, f32[32,2,512]{2,1,0:T(2,128)}, f32[2,512]{1,0:T(2,128)}) custom-call(s32[1,4]{1,0:T(1,128)} %add_bitcast_fusion.refs_0_, f32[2,640]{1,0:T(2,128)} %get-tuple-element.124.refs_1_.sums_first, f32[2,512]{1,0:T(2,128)} %get-tuple-element.140.refs_2_.sums_second, ...), custom_call_target="tpu_custom_call" | custom-call | tf_op jit(solution)/shard_map/pallas_call | solution.py:150
  122.0 4.1 %all-to-all-start.5 = ((f32[32,2,512]{2,1,0:T(2,128)}), f32[32,2,512]{2,1,0:T(2,128)S(1)}, u32[]{:S(2)}, u32[]{:S(2)}) async-start(f32[32,2,512]{2,1,0:T(2,128)} %get-tuple-element.167), calls=%async_computation.5 | async-start | bytes 262144 | tf_op jit(solution)/shard_map/all_to_all | solution.py:32
  127.3 4.8 %shard_map.226 = (bf16[8,9,16,128]{3,2,1,0:T(8,128)(2,1)}, f32[8,9,16,128]{3,2,1,0:T(8,128)}) custom-call(s32[1,4]{1,0:T(1,128)} %add_bitcast_fusion.1.place, s32[2,16]{1,0:T(2,128)} %slice_convert_fusion.sizes, f32[2,640]{1,0:T(2,128)} %get-tuple-element.124.refs_1_.sums_first, f32[2,512]{1,0:T(2,128)} %get-tuple-element.140.refs_2_.sums_second, ...), custom_call_target="tpu_custom_call" | custom-call | tf_op jit(solution)/shard_map/pallas_call | solution.py:150
  132.1 2.2 all-to-all-done.5.came
  136.9 3.1 %shard_map.227 = (bf16[512,512]{1,0:T(8,128)(2,1)}, f32[2,512]{1,0:T(2,128)}) custom-call(f32[2,640]{1,0:T(2,128)} %get-tuple-element.124.refs_1_.sums_first, f32[32,2,512]{2,1,0:T(2,128)} %copy-done.14, f32[2,512]{1,0:T(2,128)} %get-tuple-element.117.refs_2_.refs_4_.params, f32[256,512]{1,0:T(8,128)} %get-tuple-element.118.refs_3_.refs_10_.first, ...), custom_call_target="tpu_custom_call" | custom-call | tf_op jit(solution)/shard_map/pallas_call | solution.py:150
  140.0 1.7 convolution_convert_fusion
  147.4 2.1 convolution_add_fusion
  149.5 2.5 %collective-permute-done.27 = bf16[64,1024]{1,0:T(8,128)(2,1)S(1)} collective-permute-done((bf16[64,1024]{1,0:T(8,128)(2,1)S(1)}, bf16[64,1024]{1,0:T(8,128)(2,1)S(1)}, u32[]{:S(2)}, u32[]{:S(2)}) %collective-permute-start.27) | collective-permute-done | bytes 131104 | tf_op jit(solution)/shard_map/ppermute | solution.py:21
  152.0 2.3 collective-permute-done.28
  157.5 9.2 %collective-permute-done.30 = bf16[32,1024]{1,0:T(8,128)(2,1)S(1)} collective-permute-done((bf16[32,1024]{1,0:T(8,128)(2,1)S(1)}, bf16[32,1024]{1,0:T(8,128)(2,1)S(1)}, u32[]{:S(2)}, u32[]{:S(2)}) %collective-permute-start.30) | collective-permute-done | bytes 65568 | tf_op jit(solution)/shard_map/ppermute | solution.py:21
  166.9 1.5 collective-permute-start.35
  168.4 1.7 collective-permute-start.33
  170.2 5.9 %collective-permute-done.33 = bf16[32,1024]{1,0:T(8,128)(2,1)S(1)} collective-permute-done((bf16[32,1024]{1,0:T(8,128)(2,1)S(1)}, bf16[32,1024]{1,0:T(8,128)(2,1)S(1)}, u32[]{:S(2)}, u32[]{:S(2)}) %collective-permute-start.33) | collective-permute-done | bytes 65568 | tf_op jit(solution)/shard_map/ppermute | solution.py:21
  176.1 1.9 collective-permute-done.35
  178.1 1.6 collective-permute-start.37
  182.4 3.4 %collective-permute-done.38 = bf16[64,512]{1,0:T(8,128)(2,1)S(1)} collective-permute-done((bf16[64,512]{1,0:T(8,128)(2,1)S(1)}, bf16[64,512]{1,0:T(8,128)(2,1)S(1)}, u32[]{:S(2)}, u32[]{:S(2)}) %collective-permute-start.38) | collective-permute-done | bytes 65568 | tf_op jit(solution)/shard_map/ppermute | solution.py:21
  185.8 1.5 collective-permute-done.37
  191.3 3.1 %collective-permute-done.41 = bf16[64,512]{1,0:T(8,128)(2,1)S(1)} collective-permute-done((bf16[64,512]{1,0:T(8,128)(2,1)S(1)}, bf16[64,512]{1,0:T(8,128)(2,1)S(1)}, u32[]{:S(2)}, u32[]{:S(2)}) %collective-permute-start.41) | collective-permute-done | bytes 65568 | tf_op jit(solution)/shard_map/ppermute | solution.py:21
  194.7 11.0 %collective-permute-done.40 = bf16[4608,128]{1,0:T(8,128)(2,1)S(1)} collective-permute-done((bf16[4608,128]{1,0:T(8,128)(2,1)S(1)}, bf16[4608,128]{1,0:T(8,128)(2,1)S(1)}, u32[]{:S(2)}, u32[]{:S(2)}) %collective-permute-start.40) | collective-permute-done | bytes 1179680 | tf_op jit(solution)/shard_map/ppermute | solution.py:21
  206.2 1.7 collective-permute-start.43
  209.0 2.0 collective-permute-start.44
  211.0 3.2 %collective-permute-done.44 = bf16[128,512]{1,0:T(8,128)(2,1)S(1)} collective-permute-done((bf16[128,512]{1,0:T(8,128)(2,1)S(1)}, bf16[128,512]{1,0:T(8,128)(2,1)S(1)}, u32[]{:S(2)}, u32[]{:S(2)}) %collective-permute-start.44) | collective-permute-done | bytes 131104 | tf_op jit(solution)/shard_map/ppermute | solution.py:21
  214.2 2.3 collective-permute-done.42
  219.3 4.0 %collective-permute-done.46 = bf16[256,512]{1,0:T(8,128)(2,1)S(1)} collective-permute-done((bf16[256,512]{1,0:T(8,128)(2,1)S(1)}, bf16[256,512]{1,0:T(8,128)(2,1)S(1)}, u32[]{:S(2)}, u32[]{:S(2)}) %collective-permute-start.46) | collective-permute-done | bytes 262176 | tf_op jit(solution)/shard_map/ppermute | solution.py:21
  226.1 5.7 %collective-permute-done.47 = bf16[512,512]{1,0:T(8,128)(2,1)S(1)} collective-permute-done((bf16[512,512]{1,0:T(8,128)(2,1)S(1)}, bf16[512,512]{1,0:T(8,128)(2,1)S(1)}, u32[]{:S(2)}, u32[]{:S(2)}) %collective-permute-start.47) | collective-permute-done | bytes 524320 | tf_op jit(solution)/shard_map/ppermute | solution.py:21
  232.0 1.8 collective-permute-start.48
  234.6 5.9 %shard_map.228 = f32[9,512,512]{2,1,0:T(8,128)} custom-call(s32[1,1]{1,0:T(1,128)} %bitcast.86.odd, bf16[4,16,9,16,128]{4,3,2,1,0:T(8,128)(2,1)S(1)} %bitcast.193, bf16[4,16,9,16,128]{4,3,2,1,0:T(8,128)(2,1)S(1)} %bitcast.194), custom_call_target="tpu_custom_call" | custom-call | tf_op jit(solution)/shard_map/pallas_call | solution.py:604
  240.7 2.6 %maximum_convert_fusion = f32[512,2048]{1,0:T(8,128)} fusion(bf16[512,1024]{1,0:T(8,128)(2,1)S(1)} %get-tuple-element.217, bf16[512,1024]{1,0:T(8,128)(2,1)S(1)} %get-tuple-element.216), kind=kLoop, calls=%fused_computation.3 | loop fusion | flops 4194304 | bytes 6291456 | tf_op jit(solution)/shard_map/convert_element_type | solution.py:869
  243.6 2.7 %bitcast_convert_fusion = f32[2048,512]{1,0:T(8,128)} fusion(bf16[2,1024,512]{2,1,0:T(8,128)(2,1)S(1)} %pad_maximum_fusion.1), kind=kLoop, calls=%fused_computation.4 | loop fusion | flops 1048576 | bytes 6291456 | tf_op jit(solution)/shard_map/convert_element_type | solution.py:907
  (226 shorter events, 62.3 us)
Async XLA Ops:
  5.6 16.0 %all-to-all-start = ((f32[32,2,640]{2,1,0:T(2,128)}), f32[32,2,640]{2,1,0:T(2,128)S(1)}, u32[]{:S(2)}, u32[]{:S(2)}) async-start(f32[32,2,640]{2,1,0:T(2,128)} %get-tuple-element.113), calls=%async_computation | async-start | bytes 327680 | tf_op jit(solution)/shard_map/all_to_all | solution.py:32
  12.7 22.9 %collective-permute-start.3 = (f32[256,512]{1,0:T(8,128)}, f32[256,512]{1,0:T(8,128)S(1)}, u32[]{:S(2)}, u32[]{:S(2)}) collective-permute-start(f32[256,512]{1,0:T(8,128)} %get-tuple-element.118.refs_3_.refs_10_.first), channel_id=1, source_target_pairs={{0,1},{1,0},{2,3},{3,2},{4,5},{5,4},{6,7},{7,6},{8,9},{9,8},{10,11... | collective-permute-start | bytes 1572872 | tf_op jit(solution)/shard_map/ppermute | solution.py:21
  13.3 8.3 %collective-permute-start.1 = (f32[128,512]{1,0:T(8,128)}, f32[128,512]{1,0:T(8,128)S(1)}, u32[]{:S(2)}, u32[]{:S(2)}) collective-permute-start(f32[128,512]{1,0:T(8,128)} %get-tuple-element.115), channel_id=1, source_target_pairs={{1,2},{2,1},{5,6},{6,5},{9,10},{10,9},{13,14},{14,13},{17,18},{18,... | collective-permute-start | bytes 786440 | tf_op jit(solution)/shard_map/ppermute | solution.py:140
  27.9 13.6 %all-to-all-start.1 = ((f32[32,2,512]{2,1,0:T(2,128)}), f32[32,2,512]{2,1,0:T(2,128)S(1)}, u32[]{:S(2)}, u32[]{:S(2)}) async-start(f32[32,2,512]{2,1,0:T(2,128)} %get-tuple-element.125), calls=%async_computation.1 | async-start | bytes 262144 | tf_op jit(solution)/shard_map/all_to_all | solution.py:32
  46.8 14.2 %collective-permute-start.9 = (bf16[256,1024]{1,0:T(8,128)(2,1)S(1)}, bf16[256,1024]{1,0:T(8,128)(2,1)S(1)}, u32[]{:S(2)}, u32[]{:S(2)}) collective-permute-start(bf16[256,1024]{1,0:T(8,128)(2,1)S(1)} %get-tuple-element.229), channel_id=1, source_target_pairs={{0,1},{1,0},{2,3},{3,2},{4,5},{5,4},{6,7},{7,6},{8,9},{9,8},{10,11... | collective-permute-start | bytes 1572872 | tf_op jit(solution)/shard_map/ppermute | solution.py:21
  48.5 10.3 %all-to-all-start.2 = ((f32[16,2,1024]{2,1,0:T(2,128)}), f32[16,2,1024]{2,1,0:T(2,128)S(1)}, u32[]{:S(2)}, u32[]{:S(2)}) async-start(f32[16,2,1024]{2,1,0:T(2,128)} %broadcast_in_dim.51), calls=%async_computation.2 | async-start | bytes 262144 | tf_op jit(solution)/shard_map/all_to_all | solution.py:38
  52.2 8.9 %collective-permute-start.6 = (bf16[2,2,128,256]{3,2,1,0:T(8,128)(2,1)S(1)}, bf16[2,2,128,256]{3,2,1,0:T(8,128)(2,1)S(1)}, u32[]{:S(2)}, u32[]{:S(2)}) collective-permute-start(bf16[2,2,128,256]{3,2,1,0:T(8,128)(2,1)S(1)} %pad_maximum_fusion.10), channel_id=1, source_target_pairs={{0,2},{1,5},{2,0},{3,7},{4,6},{5,1},{6,4},{7,3},{8,10},{9,13},{10,... | collective-permute-start | bytes 786440 | tf_op jit(solution)/shard_map/ppermute | solution.py:21
  53.5 7.6 %collective-permute-start.8 = (bf16[256,512]{1,0:T(8,128)(2,1)S(1)}, bf16[256,512]{1,0:T(8,128)(2,1)S(1)}, u32[]{:S(2)}, u32[]{:S(2)}) collective-permute-start(bf16[256,512]{1,0:T(8,128)(2,1)S(1)} %copy-done.19), channel_id=1, source_target_pairs={{0,1},{1,0},{2,3},{3,2},{4,5},{5,4},{6,7},{7,6},{8,9},{9,8},{10,11... | collective-permute-start | bytes 786440 | tf_op jit(solution)/shard_map/ppermute | solution.py:21
  54.3 6.7 %collective-permute-start.7 = (bf16[1,2,128,256]{3,2,1,0:T(8,128)(2,1)}, bf16[1,2,128,256]{3,2,1,0:T(8,128)(2,1)}, u32[]{:S(2)}, u32[]{:S(2)}) collective-permute-start(bf16[1,2,128,256]{3,2,1,0:T(8,128)(2,1)} %bitcast.233), channel_id=1, source_target_pairs={{0,2},{1,5},{2,0},{3,7},{4,6},{5,1},{6,4},{7,3},{8,10},{9,13},{10,... | collective-permute-start | bytes 393224 | tf_op jit(solution)/shard_map/ppermute | solution.py:21
  70.3 17.4 %collective-permute-start.12 = (bf16[4,2,128,256]{3,2,1,0:T(8,128)(2,1)S(1)}, bf16[4,2,128,256]{3,2,1,0:T(8,128)(2,1)S(1)}, u32[]{:S(2)}, u32[]{:S(2)}) collective-permute-start(bf16[4,2,128,256]{3,2,1,0:T(8,128)(2,1)S(1)} %bitcast.206), channel_id=1, source_target_pairs={{0,4},{1,3},{2,6},{3,1},{4,0},{5,7},{6,2},{7,5},{8,12},{9,11},{10,... | collective-permute-start | bytes 1572872 | tf_op jit(solution)/shard_map/ppermute | solution.py:21
  72.7 12.2 %all-to-all-start.3 = ((f32[16,2,1024]{2,1,0:T(2,128)}), f32[16,2,1024]{2,1,0:T(2,128)S(1)}, u32[]{:S(2)}, u32[]{:S(2)}) async-start(f32[16,2,1024]{2,1,0:T(2,128)} %broadcast_in_dim.54), calls=%async_computation.3 | async-start | bytes 262144 | tf_op jit(solution)/shard_map/all_to_all | solution.py:38
  78.9 7.8 %collective-permute-start.13 = (bf16[2,2,128,128]{3,2,1,0:T(8,128)(2,1)S(1)}, bf16[2,2,128,128]{3,2,1,0:T(8,128)(2,1)S(1)}, u32[]{:S(2)}, u32[]{:S(2)}) collective-permute-start(bf16[2,2,128,128]{3,2,1,0:T(8,128)(2,1)S(1)} %fusion.12), channel_id=1, source_target_pairs={{0,4},{1,3},{2,6},{3,1},{4,0},{5,7},{6,2},{7,5},{8,12},{9,11},{10,... | collective-permute-start | bytes 393224 | tf_op jit(solution)/shard_map/ppermute | solution.py:21
  82.7 13.0 %collective-permute-start.26 = (f32[16,2048]{1,0:T(8,128)S(1)}, f32[16,2048]{1,0:T(8,128)S(1)}, u32[]{:S(2)}, u32[]{:S(2)}) collective-permute-start(f32[16,2048]{1,0:T(8,128)S(1)} %add.195), channel_id=1, source_target_pairs={{0,2},{1,3},{2,0},{3,1},{4,6},{5,7},{6,4},{7,5},{8,10},{9,11},{10,... | collective-permute-start | bytes 393224 | tf_op jit(solution)/shard_map/ppermute | solution.py:130
  94.6 8.0 %collective-permute-start.14 = (bf16[1,2,128,256]{3,2,1,0:T(8,128)(2,1)}, bf16[1,2,128,256]{3,2,1,0:T(8,128)(2,1)S(1)}, u32[]{:S(2)}, u32[]{:S(2)}) collective-permute-start(bf16[1,2,128,256]{3,2,1,0:T(8,128)(2,1)} %bitcast.234), channel_id=1, source_target_pairs={{0,2},{1,5},{2,0},{3,7},{4,6},{5,1},{6,4},{7,3},{8,10},{9,13},{10,... | collective-permute-start | bytes 393224 | tf_op jit(solution)/shard_map/ppermute | solution.py:21
  95.7 14.8 %collective-permute-start.16 = (bf16[256,1024]{1,0:T(8,128)(2,1)}, bf16[256,1024]{1,0:T(8,128)(2,1)S(1)}, u32[]{:S(2)}, u32[]{:S(2)}) collective-permute-start(bf16[256,1024]{1,0:T(8,128)(2,1)} %get-tuple-element.159), channel_id=1, source_target_pairs={{0,1},{1,0},{2,3},{3,2},{4,5},{5,4},{6,7},{7,6},{8,9},{9,8},{10,11... | collective-permute-start | bytes 1572872 | tf_op jit(solution)/shard_map/ppermute | solution.py:21
  96.7 13.7 %collective-permute-start.17 = (f32[128,1024]{1,0:T(8,128)}, f32[128,1024]{1,0:T(8,128)S(1)}, u32[]{:S(2)}, u32[]{:S(2)}) collective-permute-start(f32[128,1024]{1,0:T(8,128)} %get-tuple-element.160), channel_id=1, source_target_pairs={{0,1},{1,0},{2,3},{3,2},{4,5},{5,4},{6,7},{7,6},{8,9},{9,8},{10,11... | collective-permute-start | bytes 1572872 | tf_op jit(solution)/shard_map/ppermute | solution.py:139
  96.8 13.7 %collective-permute-start.18 = (f32[128,1024]{1,0:T(8,128)}, f32[128,1024]{1,0:T(8,128)}, u32[]{:S(2)}, u32[]{:S(2)}) collective-permute-start(f32[128,1024]{1,0:T(8,128)} %get-tuple-element.161), channel_id=1, source_target_pairs={{1,2},{2,1},{5,6},{6,5},{9,10},{10,9},{13,14},{14,13},{17,18},{18,... | collective-permute-start | bytes 1572872 | tf_op jit(solution)/shard_map/ppermute | solution.py:140
  99.7 10.8 %all-to-all-start.4 = ((f32[32,2,512]{2,1,0:T(2,128)}), f32[32,2,512]{2,1,0:T(2,128)S(1)}, u32[]{:S(2)}, u32[]{:S(2)}) async-start(f32[32,2,512]{2,1,0:T(2,128)} %get-tuple-element.156), calls=%async_computation.4 | async-start | bytes 262144 | tf_op jit(solution)/shard_map/all_to_all | solution.py:32
  102.3 25.0 %collective-permute-start.20 = (bf16[4,2,128,128]{3,2,1,0:T(8,128)(2,1)S(1)}, bf16[4,2,128,128]{3,2,1,0:T(8,128)(2,1)}, u32[]{:S(2)}, u32[]{:S(2)}) collective-permute-start(bf16[4,2,128,128]{3,2,1,0:T(8,128)(2,1)S(1)} %bitcast.212), channel_id=1, source_target_pairs={{0,1},{1,0},{2,3},{3,2},{4,5},{5,4},{6,7},{7,6},{8,9},{9,8},{10,11... | collective-permute-start | bytes 786440 | tf_op jit(solution)/shard_map/ppermute | solution.py:21
  104.2 6.2 %collective-permute-start.15 = (bf16[2,2,128,128]{3,2,1,0:T(8,128)(2,1)}, bf16[2,2,128,128]{3,2,1,0:T(8,128)(2,1)S(1)}, u32[]{:S(2)}, u32[]{:S(2)}) collective-permute-start(bf16[2,2,128,128]{3,2,1,0:T(8,128)(2,1)} %fusion.8), channel_id=1, source_target_pairs={{0,4},{1,3},{2,6},{3,1},{4,0},{5,7},{6,2},{7,5},{8,12},{9,11},{10,... | collective-permute-start | bytes 393224 | tf_op jit(solution)/shard_map/ppermute | solution.py:21
  112.7 21.6 %collective-permute-start.19 = (bf16[256,1024]{1,0:T(8,128)(2,1)}, bf16[256,1024]{1,0:T(8,128)(2,1)}, u32[]{:S(2)}, u32[]{:S(2)}) collective-permute-start(bf16[256,1024]{1,0:T(8,128)(2,1)} %fusion.1), channel_id=1, source_target_pairs={{0,2},{1,5},{2,0},{3,7},{4,6},{5,1},{6,4},{7,3},{8,10},{9,13},{10,... | collective-permute-start | bytes 1572872 | tf_op jit(solution)/shard_map/ppermute | solution.py:21
  114.9 12.5 %collective-permute-start.21 = (bf16[4,2,128,128]{3,2,1,0:T(8,128)(2,1)S(1)}, bf16[4,2,128,128]{3,2,1,0:T(8,128)(2,1)}, u32[]{:S(2)}, u32[]{:S(2)}) collective-permute-start(bf16[4,2,128,128]{3,2,1,0:T(8,128)(2,1)S(1)} %bitcast.214), channel_id=1, source_target_pairs={{0,1},{1,0},{2,3},{3,2},{4,5},{5,4},{6,7},{7,6},{8,9},{9,8},{10,11... | collective-permute-start | bytes 786440 | tf_op jit(solution)/shard_map/ppermute | solution.py:21
  121.6 12.7 %collective-permute-start.22 = (bf16[256,512]{1,0:T(8,128)(2,1)}, bf16[256,512]{1,0:T(8,128)(2,1)}, u32[]{:S(2)}, u32[]{:S(2)}) collective-permute-start(bf16[256,512]{1,0:T(8,128)(2,1)} %get-tuple-element.174), channel_id=1, source_target_pairs={{0,1},{1,0},{2,3},{3,2},{4,5},{5,4},{6,7},{7,6},{8,9},{9,8},{10,11... | collective-permute-start | bytes 786440 | tf_op jit(solution)/shard_map/ppermute | solution.py:21
  122.0 12.3 %all-to-all-start.5 = ((f32[32,2,512]{2,1,0:T(2,128)}), f32[32,2,512]{2,1,0:T(2,128)S(1)}, u32[]{:S(2)}, u32[]{:S(2)}) async-start(f32[32,2,512]{2,1,0:T(2,128)} %get-tuple-element.167), calls=%async_computation.5 | async-start | bytes 262144 | tf_op jit(solution)/shard_map/all_to_all | solution.py:32
  134.9 8.6 %collective-permute-start.24 = (bf16[1152,128]{1,0:T(8,128)(2,1)}, bf16[1152,128]{1,0:T(8,128)(2,1)}, u32[]{:S(2)}, u32[]{:S(2)}) collective-permute-start(bf16[1152,128]{1,0:T(8,128)(2,1)} %bitcast.232), channel_id=1, source_target_pairs={{0,8},{1,9},{2,10},{3,11},{4,12},{5,13},{6,14},{7,15},{8,0},{9,1},... | collective-permute-start | bytes 884744 | tf_op jit(solution)/shard_map/ppermute | solution.py:21
  136.4 5.7 %collective-permute-start.23 = (bf16[128,1024]{1,0:T(8,128)(2,1)S(1)}, bf16[128,1024]{1,0:T(8,128)(2,1)S(1)}, u32[]{:S(2)}, u32[]{:S(2)}) collective-permute-start(bf16[128,1024]{1,0:T(8,128)(2,1)S(1)} %dynamic-slice_convert_fusion.1), channel_id=1, source_target_pairs={{0,4},{1,3},{2,6},{3,1},{4,0},{5,7},{6,2},{7,5},{8,12},{9,11},{10,... | collective-permute-start | bytes 786440 | tf_op jit(solution)/shard_map/ppermute | solution.py:21
  144.6 9.6 %collective-permute-start.28 = (bf16[576,128]{1,0:T(8,128)(2,1)S(1)}, bf16[576,128]{1,0:T(8,128)(2,1)S(1)}, u32[]{:S(2)}, u32[]{:S(2)}) collective-permute-start(bf16[576,128]{1,0:T(8,128)(2,1)S(1)} %dynamic-slice_convert_fusion.2), channel_id=1, source_target_pairs={{0,16},{1,17},{2,18},{3,19},{4,20},{5,21},{6,22},{7,23},{8,24},{9,... | collective-permute-start | bytes 442376 | tf_op jit(solution)/shard_map/ppermute | solution.py:21
  145.2 9.0 %collective-permute-start.29 = (bf16[512,512]{1,0:T(8,128)(2,1)S(1)}, bf16[512,512]{1,0:T(8,128)(2,1)S(1)}, u32[]{:S(2)}, u32[]{:S(2)}) collective-permute-start(bf16[512,512]{1,0:T(8,128)(2,1)S(1)} %convolution_convert_fusion), channel_id=1, source_target_pairs={{0,2},{1,5},{2,0},{3,7},{4,6},{5,1},{6,4},{7,3},{8,10},{9,13},{10,... | collective-permute-start | bytes 1572872 | tf_op jit(solution)/shard_map/ppermute | solution.py:21
  146.5 5.5 %collective-permute-start.27 = (bf16[64,1024]{1,0:T(8,128)(2,1)S(1)}, bf16[64,1024]{1,0:T(8,128)(2,1)S(1)}, u32[]{:S(2)}, u32[]{:S(2)}) collective-permute-start(bf16[64,1024]{1,0:T(8,128)(2,1)S(1)} %dynamic-slice_convert_fusion.4), channel_id=1, source_target_pairs={{0,8},{1,9},{2,10},{3,11},{4,12},{5,13},{6,14},{7,15},{8,0},{9,1},... | collective-permute-start | bytes 393224 | tf_op jit(solution)/shard_map/ppermute | solution.py:21
  154.7 11.9 %collective-permute-start.32 = (bf16[256,512]{1,0:T(8,128)(2,1)S(1)}, bf16[256,512]{1,0:T(8,128)(2,1)S(1)}, u32[]{:S(2)}, u32[]{:S(2)}) collective-permute-start(bf16[256,512]{1,0:T(8,128)(2,1)S(1)} %dynamic-slice_convert_fusion), channel_id=1, source_target_pairs={{0,4},{1,3},{2,6},{3,1},{4,0},{5,7},{6,2},{7,5},{8,12},{9,11},{10,... | collective-permute-start | bytes 786440 | tf_op jit(solution)/shard_map/ppermute | solution.py:21
  154.9 11.7 %collective-permute-start.31 = (bf16[576,128]{1,0:T(8,128)(2,1)S(1)}, bf16[576,128]{1,0:T(8,128)(2,1)S(1)}, u32[]{:S(2)}, u32[]{:S(2)}) collective-permute-start(bf16[576,128]{1,0:T(8,128)(2,1)S(1)} %add_convert_fusion), channel_id=1, source_target_pairs={{0,16},{1,17},{2,18},{3,19},{4,20},{5,21},{6,22},{7,23},{8,24},{9,... | collective-permute-start | bytes 442376 | tf_op jit(solution)/shard_map/ppermute | solution.py:21
  156.2 10.5 %collective-permute-start.30 = (bf16[32,1024]{1,0:T(8,128)(2,1)S(1)}, bf16[32,1024]{1,0:T(8,128)(2,1)S(1)}, u32[]{:S(2)}, u32[]{:S(2)}) collective-permute-start(bf16[32,1024]{1,0:T(8,128)(2,1)S(1)} %dynamic-slice_convert_fusion.6), channel_id=1, source_target_pairs={{0,16},{1,17},{2,18},{3,19},{4,20},{5,21},{6,22},{7,23},{8,24},{9,... | collective-permute-start | bytes 196616 | tf_op jit(solution)/shard_map/ppermute | solution.py:21
  166.7 11.3 %collective-permute-start.34 = (bf16[1152,128]{1,0:T(8,128)(2,1)S(1)}, bf16[1152,128]{1,0:T(8,128)(2,1)S(1)}, u32[]{:S(2)}, u32[]{:S(2)}) collective-permute-start(bf16[1152,128]{1,0:T(8,128)(2,1)S(1)} %bitcast.208), channel_id=1, source_target_pairs={{0,8},{1,9},{2,10},{3,11},{4,12},{5,13},{6,14},{7,15},{8,0},{9,1},... | collective-permute-start | bytes 884744 | tf_op jit(solution)/shard_map/ppermute | solution.py:21
  166.9 11.1 %collective-permute-start.35 = (bf16[128,512]{1,0:T(8,128)(2,1)S(1)}, bf16[128,512]{1,0:T(8,128)(2,1)S(1)}, u32[]{:S(2)}, u32[]{:S(2)}) collective-permute-start(bf16[128,512]{1,0:T(8,128)(2,1)S(1)} %dynamic-slice_convert_fusion.3), channel_id=1, source_target_pairs={{0,8},{1,9},{2,10},{3,11},{4,12},{5,13},{6,14},{7,15},{8,0},{9,1},... | collective-permute-start | bytes 393224 | tf_op jit(solution)/shard_map/ppermute | solution.py:21
  168.4 7.6 %collective-permute-start.33 = (bf16[32,1024]{1,0:T(8,128)(2,1)S(1)}, bf16[32,1024]{1,0:T(8,128)(2,1)S(1)}, u32[]{:S(2)}, u32[]{:S(2)}) collective-permute-start(bf16[32,1024]{1,0:T(8,128)(2,1)S(1)} %add_convert_fusion.2), channel_id=1, source_target_pairs={{0,16},{1,17},{2,18},{3,19},{4,20},{5,21},{6,22},{7,23},{8,24},{9,... | collective-permute-start | bytes 196616 | tf_op jit(solution)/shard_map/ppermute | solution.py:21
  178.1 9.1 %collective-permute-start.37 = (bf16[2304,128]{1,0:T(8,128)(2,1)S(1)}, bf16[2304,128]{1,0:T(8,128)(2,1)S(1)}, u32[]{:S(2)}, u32[]{:S(2)}) collective-permute-start(bf16[2304,128]{1,0:T(8,128)(2,1)S(1)} %bitcast.202), channel_id=1, source_target_pairs={{0,4},{1,3},{2,6},{3,1},{4,0},{5,7},{6,2},{7,5},{8,12},{9,11},{10,... | collective-permute-start | bytes 1769480 | tf_op jit(solution)/shard_map/ppermute | solution.py:21
  179.8 6.0 %collective-permute-start.36 = (bf16[64,1024]{1,0:T(8,128)(2,1)S(1)}, bf16[64,1024]{1,0:T(8,128)(2,1)S(1)}, u32[]{:S(2)}, u32[]{:S(2)}) collective-permute-start(bf16[64,1024]{1,0:T(8,128)(2,1)S(1)} %bitcast.216), channel_id=1, source_target_pairs={{0,8},{1,9},{2,10},{3,11},{4,12},{5,13},{6,14},{7,15},{8,0},{9,1},... | collective-permute-start | bytes 393224 | tf_op jit(solution)/shard_map/ppermute | solution.py:21
  180.9 4.9 %collective-permute-start.38 = (bf16[64,512]{1,0:T(8,128)(2,1)S(1)}, bf16[64,512]{1,0:T(8,128)(2,1)S(1)}, u32[]{:S(2)}, u32[]{:S(2)}) collective-permute-start(bf16[64,512]{1,0:T(8,128)(2,1)S(1)} %dynamic-slice_convert_fusion.5), channel_id=1, source_target_pairs={{0,16},{1,17},{2,18},{3,19},{4,20},{5,21},{6,22},{7,23},{8,24},{9,... | collective-permute-start | bytes 196616 | tf_op jit(solution)/shard_map/ppermute | solution.py:21
  187.5 18.2 %collective-permute-start.40 = (bf16[4608,128]{1,0:T(8,128)(2,1)S(1)}, bf16[4608,128]{1,0:T(8,128)(2,1)S(1)}, u32[]{:S(2)}, u32[]{:S(2)}) collective-permute-start(bf16[4608,128]{1,0:T(8,128)(2,1)S(1)} %bitcast.199), channel_id=1, source_target_pairs={{0,2},{1,5},{2,0},{3,7},{4,6},{5,1},{6,4},{7,3},{8,10},{9,13},{10,... | collective-permute-start | bytes 3538952 | tf_op jit(solution)/shard_map/ppermute | solution.py:21
  188.8 5.9 %collective-permute-start.39 = (bf16[128,1024]{1,0:T(8,128)(2,1)S(1)}, bf16[128,1024]{1,0:T(8,128)(2,1)S(1)}, u32[]{:S(2)}, u32[]{:S(2)}) collective-permute-start(bf16[128,1024]{1,0:T(8,128)(2,1)S(1)} %bitcast.210), channel_id=1, source_target_pairs={{0,4},{1,3},{2,6},{3,1},{4,0},{5,7},{6,2},{7,5},{8,12},{9,11},{10,... | collective-permute-start | bytes 786440 | tf_op jit(solution)/shard_map/ppermute | solution.py:21
  190.3 4.1 %collective-permute-start.41 = (bf16[64,512]{1,0:T(8,128)(2,1)S(1)}, bf16[64,512]{1,0:T(8,128)(2,1)S(1)}, u32[]{:S(2)}, u32[]{:S(2)}) collective-permute-start(bf16[64,512]{1,0:T(8,128)(2,1)S(1)} %add_convert_fusion.1), channel_id=1, source_target_pairs={{0,16},{1,17},{2,18},{3,19},{4,20},{5,21},{6,22},{7,23},{8,24},{9,... | collective-permute-start | bytes 196616 | tf_op jit(solution)/shard_map/ppermute | solution.py:21
  206.2 10.3 %collective-permute-start.43 = (bf16[9216,128]{1,0:T(8,128)(2,1)S(1)}, bf16[9216,128]{1,0:T(8,128)(2,1)S(1)}, u32[]{:S(2)}, u32[]{:S(2)}) collective-permute-start(bf16[9216,128]{1,0:T(8,128)(2,1)S(1)} %bitcast.192), channel_id=1, source_target_pairs={{0,1},{1,0},{2,3},{3,2},{4,5},{5,4},{6,7},{7,6},{8,9},{9,8},{10,11... | collective-permute-start | bytes 7077896 | tf_op jit(solution)/shard_map/ppermute | solution.py:21
  208.1 8.4 %collective-permute-start.42 = (bf16[256,1024]{1,0:T(8,128)(2,1)S(1)}, bf16[256,1024]{1,0:T(8,128)(2,1)S(1)}, u32[]{:S(2)}, u32[]{:S(2)}) collective-permute-start(bf16[256,1024]{1,0:T(8,128)(2,1)S(1)} %bitcast.204), channel_id=1, source_target_pairs={{0,2},{1,5},{2,0},{3,7},{4,6},{5,1},{6,4},{7,3},{8,10},{9,13},{10,... | collective-permute-start | bytes 1572872 | tf_op jit(solution)/shard_map/ppermute | solution.py:21
  209.0 5.2 %collective-permute-start.44 = (bf16[128,512]{1,0:T(8,128)(2,1)S(1)}, bf16[128,512]{1,0:T(8,128)(2,1)S(1)}, u32[]{:S(2)}, u32[]{:S(2)}) collective-permute-start(bf16[128,512]{1,0:T(8,128)(2,1)S(1)} %bitcast.217), channel_id=1, source_target_pairs={{0,8},{1,9},{2,10},{3,11},{4,12},{5,13},{6,14},{7,15},{8,0},{9,1},... | collective-permute-start | bytes 393224 | tf_op jit(solution)/shard_map/ppermute | solution.py:21
  216.7 6.6 %collective-permute-start.45 = (bf16[512,1024]{1,0:T(8,128)(2,1)S(1)}, bf16[512,1024]{1,0:T(8,128)(2,1)S(1)}, u32[]{:S(2)}, u32[]{:S(2)}) collective-permute-start(bf16[512,1024]{1,0:T(8,128)(2,1)S(1)} %bitcast.200), channel_id=1, source_target_pairs={{0,1},{1,0},{2,3},{3,2},{4,5},{5,4},{6,7},{7,6},{8,9},{9,8},{10,11... | collective-permute-start | bytes 3145736 | tf_op jit(solution)/shard_map/ppermute | solution.py:21
  217.7 5.6 %collective-permute-start.46 = (bf16[256,512]{1,0:T(8,128)(2,1)S(1)}, bf16[256,512]{1,0:T(8,128)(2,1)S(1)}, u32[]{:S(2)}, u32[]{:S(2)}) collective-permute-start(bf16[256,512]{1,0:T(8,128)(2,1)S(1)} %bitcast.211), channel_id=1, source_target_pairs={{0,4},{1,3},{2,6},{3,1},{4,0},{5,7},{6,2},{7,5},{8,12},{9,11},{10,... | collective-permute-start | bytes 786440 | tf_op jit(solution)/shard_map/ppermute | solution.py:21
  223.4 8.4 %collective-permute-start.47 = (bf16[512,512]{1,0:T(8,128)(2,1)S(1)}, bf16[512,512]{1,0:T(8,128)(2,1)S(1)}, u32[]{:S(2)}, u32[]{:S(2)}) collective-permute-start(bf16[512,512]{1,0:T(8,128)(2,1)S(1)} %bitcast.205), channel_id=1, source_target_pairs={{0,2},{1,5},{2,0},{3,7},{4,6},{5,1},{6,4},{7,3},{8,10},{9,13},{10,... | collective-permute-start | bytes 1572872 | tf_op jit(solution)/shard_map/ppermute | solution.py:21
  232.0 11.2 %collective-permute-start.48 = (bf16[1024,512]{1,0:T(8,128)(2,1)S(1)}, bf16[1024,512]{1,0:T(8,128)(2,1)S(1)}, u32[]{:S(2)}, u32[]{:S(2)}) collective-permute-start(bf16[1024,512]{1,0:T(8,128)(2,1)S(1)} %bitcast.201), channel_id=1, source_target_pairs={{0,1},{1,0},{2,3},{3,2},{4,5},{5,4},{6,7},{7,6},{8,9},{9,8},{10,11... | collective-permute-start | bytes 3145736 | tf_op jit(solution)/shard_map/ppermute | solution.py:21
  (44 other events, 278.9 us)

commit v5 on v4

--- a/solution.py
+++ b/solution.py
@@ -96,7 +96,7 @@
 
 class Chains:
     def __init__(self):
-        self.running, self.flying, self.results = {}, {}, {}
+        self.running, self.flying, self.results, self.fresh = {}, {}, {}, []
 
     def begin(self, name, chain, spans, sent=None):
         self.running[name] = (chain, list(spans))
@@ -106,22 +106,28 @@
         spans = self.running[name][1]
         self.flying[name] = [sent, None, spans.pop(0) if spans else 1]
 
-    def slot(self, *extra):
-        due = []
+    def slot(self, *extra, held=True):
+        due, fresh = [], list(self.fresh)
         for name, flight in self.flying.items():
             if flight[1] is None:
                 flight[1] = swap(*flight[0])
             flight[2] -= 1
             if flight[2] <= 0:
                 due.append(name)
-        done = tie(*(self.flying[name][1] for name in due), *extra) if due or extra else ()
+        done = [self.flying[name][1] for name in due] + list(extra)
+        if held:
+            done = tie(*done, *(self.results[name] for name in fresh))
+            for name, value in zip(fresh, done[len(due) + len(extra) :]):
+                self.results[name] = value
+            self.fresh = []
         for name, value in zip(due, done):
             try:
                 self.load(name, self.running[name][0].send(value))
             except StopIteration as end:
                 self.results[name] = end.value
+                self.fresh.append(name)
                 del self.running[name], self.flying[name]
-        return done[len(due) :]
+        return done[len(due) : len(due) + len(extra)]
 
 
 def sum_rows_axis(value):
@@ -193,8 +199,8 @@
     top = value[:, 0].reshape(images * width, -1)
     bottom = value[:, height - 1].reshape(images * width, -1)
     odd = place[0, 0] % 2 == 1
-    near[...] = jnp.where(odd, top, bottom)
-    far[...] = jnp.where(odd, bottom, top)
+    near[...] = jnp.where(odd, top, bottom).astype(near.dtype)
+    far[...] = jnp.where(odd, bottom, top).astype(far.dtype)
 
 
 def first_forward(
@@ -448,8 +454,9 @@
     third_sent[...] = jnp.where(odd, one, two)
     third_kept[...] = jnp.where(odd, two, one)
     sums[:, 0] = spread_sum(sums, back)
-    sums[:, 1] = spread_sum(sums, back * ((hidden - average) * inv_std))
-    edges_of(dims, place, jnp.concatenate([back, hidden], axis=1), near, far)
+    normed = (hidden - average) * inv_std
+    sums[:, 1] = spread_sum(sums, back * normed)
+    edges_of(dims, place, jnp.concatenate([back, normed], axis=1), near, far)
 
 
 def mid_weights(
@@ -549,17 +556,16 @@
     average, inv_std, scale, shift = affine(sums_second[...], count, params_mid[0:1], params_mid[1:2])
     mean_grad, mean_gain = totals[0:1] / count, totals[1:2] / count
 
-    def normed_grad(value, hidden, inside):
-        normed = (hidden - average) * inv_std
+    def normed_grad(value, normed, inside):
         return wide(inside[...], value) * scale * (value - (mean_grad + normed * mean_gain))
 
     odd = place[0, 0] % 2 == 1
 
     def beside(one, other, inside):
-        value = jnp.where(odd, one[:, 0:middle], other[:, 0:middle])
-        return normed_grad(value, jnp.where(odd, one[:, middle:], other[:, middle:]), inside)
-
-    centre = normed_grad(grad[...], second[...], mask)
+        value = jnp.where(odd, one[...], other[...]).astype(FULL)
+        return normed_grad(value[:, 0:middle], value[:, middle:], inside)
+
+    centre = normed_grad(grad[...], (second[...] - average) * inv_std, mask)
     above = beside(near, far, mask_above)
     below = beside(far, near, mask_below)
     three = spread(*dims, centre, above, below)
@@ -583,7 +589,22 @@
     sums[:, 1] = spread_sum(sums, total * ((hidden - average) * inv_std))
 
 
-def first_backward(sums_first, came, params, first, grad, mask, first_other, grad_other, mask_other, low, sums_in):
+def contract_in(left, right):
+    return lax.dot_general(left, right, (((0,), (0,)), ((), ())), preferred_element_type=FULL)
+
+
+def put_halves(place, total, sent, kept):
+    half = total.shape[0] // 2
+    high = place[0, 3] == 1
+    one, two = total[0:half], total[half:]
+    sent[...] = jnp.where(high, one, two).astype(LOW)
+    kept[...] = jnp.where(high, two, one)
+
+
+def first_backward(
+    place, sums_first, came, params, first, grad, mask, first_other, grad_other, mask_other, features,
+    low, sums_in, sent, kept, both,
+):
     pixels, middle = first.shape
     count = sums_first[0:1, middle : middle + 1]
     totals = jnp.sum(came[...], axis=0)
@@ -593,7 +614,14 @@
     for k, (hidden, source, inside) in enumerate(pairs):
         normed = (hidden[...] - average) * inv_std
         value = source[...].astype(FULL) - (totals[0:1] + normed * totals[1:2]) / count
-        low[k * pixels : (k + 1) * pixels] = (wide(inside[...], value) * scale * value).astype(LOW)
+        both[k * pixels : (k + 1) * pixels] = (wide(inside[...], value) * scale * value).astype(LOW)
+    low[...] = both[0:pixels]
+    put_halves(place, contract_in(features[...], both[...]), sent, kept)
+
+
+def out_weights(place, act, act_other, third, third_other, sent, kept):
+    total = contract_in(act[...], third[...]) + contract_in(act_other[...], third_other[...])
+    put_halves(place, total, sent, kept)
 
 
 def assemble(odd, mine, other, shape):
@@ -781,16 +809,12 @@
     normed_sent, normed_kept = halves(merge(normed_kept[None], normed_came, steps[1]), steps[2])
     sums_sent, acts, normed_sent = tie(sums_sent, acts, normed_sent)
     features_pair = jnp.concatenate([half_of(flat_features, mine, 1), features_came])
-    features_sent = half_of(features_pair, 1 - steps[1][1], 1)
-    features_kept = half_of(features_pair, steps[1][1], 1)
-    normed = merge(normed_kept, swap(normed_sent, steps[2][0]), steps[2])
-    came, came_other, acts_came, normed, features_sent, features_kept = tie(
+    came, came_other, acts_came, features_pair = tie(
         *everyone_wide(sums_sent, sums_kept, core),
         swap(acts, steps[2][0]),
-        normed,
-        features_sent,
-        features_kept,
-    )
+        features_pair,
+    )
+    normed_came = swap(normed_sent, steps[2][0])
     third_sent, third_kept, grad_second_pre, grads_sent, grads_kept, near, far, sums, sums_out = call(
         lambda *refs: out_backward(dims, *refs),
         [
@@ -799,8 +823,8 @@
             (plane, FULL),
             (half_rows, LOW),
             (half_rows, LOW),
-            ((edge[0], 2 * middle), FULL),
-            ((edge[0], 2 * middle), FULL),
+            ((edge[0], 2 * middle), LOW),
+            ((edge[0], 2 * middle), LOW),
             ((count, 2, middle), FULL),
             (broad, FULL),
         ],
@@ -826,7 +850,16 @@
     sent, kept = halves(merge(grads_kept[None], came, steps[1]), steps[2])
     came = swap(sent, steps[2][0])
     third_came = swap(third_sent, core[0])
-    sums, came, third_came, near, far = tie(sums, came, third_came, near, far)
+    out_sent, out_kept = call(
+        out_weights,
+        [((middle // 2, channels // 2), LOW), ((middle // 2, channels // 2), FULL)],
+        place,
+        second_act,
+        act_other,
+        third_kept,
+        third_came,
+    )
+    sums, came, out_sent, near, far = tie(sums, came, out_sent, near, far)
     grads = merge(kept, came, steps[2])
     grad_first_pre, low_grad, sums, sums_mid = call(
         lambda *refs: mid_backward(dims, *refs),
@@ -849,18 +882,17 @@
         scratch=taps,
         left=(14,),
     )
+    sums, normed_came = tie(sums, normed_came)
+    normed = merge(normed_kept, normed_came, steps[2])
     sums = everyone(sums)
     grad_other = swap(low_grad, core[0])
     grads_came, normed_came = swap(grads, core[0]), swap(normed, core[0])
 
-    def out_rows(which):
-        one, two = (half_of(act, which, 1) for act in (second_act, act_other))
-        return contract(one, third_kept) + contract(two, third_came)
-
     odd = (index % 2).astype(jnp.int32).reshape(1, 1)
+
     def out_chain():
-        came = yield out_rows(1 - steps[1][1]).astype(LOW), steps[1][0]
-        value = out_rows(steps[1][1]) + came.astype(FULL)
+        came = yield out_sent, steps[1][0]
+        value = out_kept + came.astype(FULL)
         value = yield from reduce_chain(value, steps[2:])
         value = yield from gather_chain(value.astype(LOW), steps[:0:-1])
         other = yield value, core[0]
@@ -899,8 +931,8 @@
         return assemble(odd, value, other, (2 * shape[0], *shape[1:]))
 
     def in_chain():
-        came = yield contract(features_sent, grad_first).astype(LOW), steps[1][0]
-        value = contract(features_kept, grad_first) + came.astype(FULL)
+        came = yield in_sent, steps[1][0]
+        value = in_kept + came.astype(FULL)
         value = yield from reduce_chain(value, steps[2:])
         value = yield from gather_chain(value.astype(LOW), steps[:0:-1])
         other = yield value, core[0]
@@ -909,13 +941,18 @@
     chains = Chains()
     mid = mid_chain()
     mid_sent, flips = next(mid)
+    came, mid_sent, grad_other, out_sent = tie(sums, mid_sent, grad_other, out_sent)
     chains.begin("out", out_chain(), ())
-    came, mid_sent, grad_other = chains.slot(sums, mid_sent, grad_other)
     chains.begin("mid", mid, (), (mid_sent, flips))
-    pooled = sum_rows_axis(pooled)
-    grad_first, sums_in = call(
+    grad_first, sums_in, in_sent, in_kept = call(
         first_backward,
-        [((2 * pixels, middle), LOW), (narrow, FULL)],
+        [
+            (plane, LOW),
+            (narrow, FULL),
+            ((channels // 4, middle), LOW),
+            ((channels // 4, middle), FULL),
+        ],
+        place,
         sums_first,
         came,
         params,
@@ -925,14 +962,16 @@
         first_other,
         grad_other,
         mask_other,
-    )
-    entry = in_chain()
-    in_sent, in_flips = next(entry)
-    in_sent, pooled = chains.slot(in_sent, pooled)
-    chains.begin("in", entry, (), (in_sent, in_flips))
-    pooled = pooled / areas[:, :1]
-    grad_features = grad_summed + times_transpose(grad_first[:pixels], weight_in)
+        features_pair,
+        scratch=[pltpu.VMEM((2 * pixels, middle), LOW)],
+    )
+    chains.slot(held=False)
+    chains.begin("in", in_chain(), ())
+    grad_features = grad_summed + times_transpose(grad_first, weight_in)
     (grad_features,) = chains.slot(grad_features)
+    chains.slot()
+    (pooled,) = chains.slot(pooled)
+    (pooled,) = chains.slot(sum_rows_axis(pooled) / areas[:, :1])
     while chains.running:
         chains.slot()
     grad_weight_in, grad_weight_mid, grad_weight_out = (

time: 247 us -> 239 us (0.968)
  waiting for transfers between devices: 82 us -> 68.7 us
  blocking collectives: 0 us -> 11.2 us
  matrix products: 10.5 us -> 2.06 us
  Pallas kernels: 47.6 us -> 51.5 us
  other arithmetic: 17.5 us -> 14.6 us
    ppermute x43, waiting for transfers between devices: 61.3 us -> 45.4 us  [swap(): lax.ppermute(value, AXES, [(i, i ^ flips[i & 1]) for i in range(count)])]
    all_to_all x0 -> x1, blocking collectives: none -> 11.2 us  [everyone_wide(): lax.all_to_all(jnp.broadcast_to(value[None], (count, *value.shape)), AXES...]
    ppermute x2, waiting for transfers between devices: 0.29 us -> 9.09 us  [sum_rows_axis(): lax.ppermute(value, ROWS, [(i, i ^ bit) for i in range(count)])]
    dot_general x6 -> x0, matrix products: 8.4 us -> none  [contract(): lax.dot_general(left, right, (((0,), (0,)), ((), ())), preferred_element_...]
    all_to_all x2 -> x1, starting transfers between devices: 9.1 us -> 3.51 us  [everyone_wide(): lax.all_to_all(jnp.broadcast_to(value[None], (count, *value.shape)), AXES...]
    all_to_all x4, waiting for transfers between devices: 11.3 us -> 6.22 us  [everyone(): return lax.all_to_all(copies, AXES, 0, 0)]
    pallas_call x8 -> x9, Pallas kernels: 41.7 us -> 45.6 us  [call(): pl.pallas_call(kernel, out_shape=[jax.ShapeDtypeStruct(shape, kind) for s...]
    ppermute x43, starting transfers between devices: 42.6 us -> 46 us  [swap(): lax.ppermute(value, AXES, [(i, i ^ flips[i & 1]) for i in range(count)])]
  transfers between devices with their start and end apart: 55 -> 54, of which waited for: 28 -> 24; matrix products, arithmetic and copies ran while one was open for 10% -> 6% of each run, Pallas kernels for 13% -> 13%
where the time goes in v5:
time: 239 us; the launch traced here: 238 us
  starting transfers between devices  79.5 us (33%)
  waiting for transfers between devices  68.7 us (29%)
  Pallas kernels  51.5 us (22%)
  other arithmetic  14.6 us (6%)
  blocking collectives  11.2 us (5%)
  local copies, waits for them, and re-layouts  8.78 us (4%)
    ppermute x43, starting transfers between devices, swap(): lax.ppermute(value, AXES, [(i, i ^ flips[i & 1]) for i in range(count)])  46 us
    pallas_call x9, Pallas kernels, call(): pl.pallas_call(kernel, out_shape=[jax.ShapeDtypeStruct(shape, kind) for s...  45.6 us
    ppermute x43, waiting for transfers between devices, swap(): lax.ppermute(value, AXES, [(i, i ^ flips[i & 1]) for i in range(count)])  45.4 us
    all_to_all x4, starting transfers between devices, everyone(): return lax.all_to_all(copies, AXES, 0, 0)  20.3 us
    all_to_all x1, blocking collectives, everyone_wide(): lax.all_to_all(jnp.broadcast_to(value[None], (count, *value.shape)), AXES...  11.2 us
    ppermute x2, waiting for transfers between devices, sum_rows_axis(): lax.ppermute(value, ROWS, [(i, i ^ bit) for i in range(count)])  9.09 us
    ppermute x2, starting transfers between devices, trade(): lax.ppermute(far, ROWS, pairs + [(b, a) for a, b in pairs])  6.77 us
    all_to_all x4, waiting for transfers between devices, everyone(): return lax.all_to_all(copies, AXES, 0, 0)  6.22 us
  transfers between devices with their start and end apart: 54, of which 24 were waited for; matrix products, arithmetic and copies ran while one was open for 6% of the time, Pallas kernels for 13%

profile of v5, /device:TPU:1, one launch (start us, length us, event | category | flops | bytes accessed | tf_op | source)
XLA Modules:
  0.0 237.9 jit_solution(6660469119630259288)
XLA Ops:
  1.4 4.3 %shard_map.220 = (f32[256,512]{1,0:T(8,128)}, f32[128,512]{1,0:T(8,128)}, f32[128,512]{1,0:T(8,128)}, f32[32,2,640]{2,1,0:T(2,128)}, f32[2,512]{1,0:T(2,128)}, /...) custom-call(s32[1,4]{1,0:T(1,128)} %add_bitcast_fusion.refs_0_.place, ...), custom_call_target="tpu_custom_call" | custom-call | tf_op jit(solution)/shard_map/pallas_call | solution.py:156
  5.6 7.1 %all-to-all-start = ((f32[32,2,640]{2,1,0:T(2,128)}), f32[32,2,640]{2,1,0:T(2,128)S(1)}, u32[]{:S(2)}, u32[]{:S(2)}) async-start(f32[32,2,640]{2,1,0:T(2,128)} %get-tuple-element.120), calls=%async_computation | async-start | bytes 327680 | tf_op jit(solution)/shard_map/all_to_all | solution.py:32
  13.3 3.5 %collective-permute-start.1 = (f32[128,512]{1,0:T(8,128)}, f32[128,512]{1,0:T(8,128)S(1)}, u32[]{:S(2)}, u32[]{:S(2)}) collective-permute-start(f32[128,512]{1,0:T(8,128)} %get-tuple-element.122), channel_id=1, source_target_pairs={{1,2},{2,1},{5,6},{6,5},{9,10},{10,9},{13,14},{14,13},{17,18},{18,... | collective-permute-start | bytes 786440 | tf_op jit(solution)/shard_map/ppermute | solution.py:146
  16.9 4.8 %collective-permute-done.1.refs_5_ = f32[128,512]{1,0:T(8,128)S(1)} collective-permute-done((f32[128,512]{1,0:T(8,128)}, f32[128,512]{1,0:T(8,128)S(1)}, u32[]{:S(2)}, u32[]{:S(2)}) %collective-permute-start.1) | collective-permute-done | bytes 262176 | tf_op jit(solution)/shard_map/ppermute | solution.py:146
  22.4 5.5 %shard_map.221 = (bf16[2,128,512]{2,1,0:T(8,128)(2,1)}, f32[256,512]{1,0:T(8,128)}, f32[32,2,512]{2,1,0:T(2,128)}, f32[2,640]{1,0:T(2,128)}, f32[2,128]{1,0:T(2,128)}) custom-call(s32[1,4]{1,0:T(1,128)} %add_bitcast_fusion.refs_0_.place, f32[32,2,640]{2,1,0:T(2,128)} %copy-done.8, f32[2,512]{1,0:T(2,128)} %get-tuple-element.124.refs_2_.refs_4_.params, ...), custom_call_target="tpu_custom_call" | custom-call | tf_op jit(solution)/shard_map/pallas_call | solution.py:156
  27.9 5.4 %all-to-all-start.1 = ((f32[32,2,512]{2,1,0:T(2,128)}), f32[32,2,512]{2,1,0:T(2,128)S(1)}, u32[]{:S(2)}, u32[]{:S(2)}) async-start(f32[32,2,512]{2,1,0:T(2,128)} %get-tuple-element.132), calls=%async_computation.1 | async-start | bytes 262144 | tf_op jit(solution)/shard_map/all_to_all | solution.py:32
  35.7 5.8 %all-to-all-done.1.refs_2_ = f32[32,2,512]{2,1,0:T(2,128)S(1)} async-done(((f32[32,2,512]{2,1,0:T(2,128)}), f32[32,2,512]{2,1,0:T(2,128)S(1)}, u32[]{:S(2)}, u32[]{:S(2)}) %all-to-all-start.1) | async-done | bytes 131104 | tf_op jit(solution)/shard_map/all_to_all | solution.py:32
  42.2 4.2 %shard_map.222 = (bf16[256,512]{1,0:T(8,128)(2,1)}, bf16[2,128,256]{2,1,0:T(8,128)(2,1)}, bf16[2,128,256]{2,1,0:T(8,128)(2,1)}, f32[256,2048]{1,0:T(8,128)}, f32...) custom-call(s32[1,4]{1,0:T(1,128)} %add_bitcast_fusion.refs_0_.place, ...), custom_call_target="tpu_custom_call" | custom-call | tf_op jit(solution)/shard_map/pallas_call | solution.py:156
  48.5 3.5 %all-to-all-start.2 = ((f32[16,2,1024]{2,1,0:T(2,128)}), f32[16,2,1024]{2,1,0:T(2,128)S(1)}, u32[]{:S(2)}, u32[]{:S(2)}) async-start(f32[16,2,1024]{2,1,0:T(2,128)} %broadcast_in_dim.51), calls=%async_computation.2 | async-start | bytes 262144 | tf_op jit(solution)/shard_map/all_to_all | solution.py:38
  55.6 3.2 %all-to-all-done.2.refs_2_ = f32[16,2,1024]{2,1,0:T(2,128)S(1)} async-done(((f32[16,2,1024]{2,1,0:T(2,128)}), f32[16,2,1024]{2,1,0:T(2,128)S(1)}, u32[]{:S(2)}, u32[]{:S(2)}) %all-to-all-start.2) | async-done | bytes 131104 | tf_op jit(solution)/shard_map/all_to_all | solution.py:38
  58.8 1.6 collective-permute-start.5
  62.1 7.2 %shard_map.223 = (bf16[256,2048]{1,0:T(8,128)(2,1)}, f32[16,2048]{1,0:T(8,128)}, f32[256,2048]{1,0:T(8,128)}, f32[2,1024]{1,0:T(2,128)}, f32[2,1024]{1,0:T(2,128)}, /*index=5*/f32[2,2048]{1,0:T(2,128)}) custom-call(s32[1,4]{1,0:T(1,128)} %add_bitcast_fusion.refs_0_.place, f32[2,640]{1,0:T(2,128)} %get-tuple-element.131.refs_1_.sums_first, ...), custom_call_target="tpu_custom_call" | custom-call | tf_op jit(solution)/shard_map/pallas_call | solution.py:156
  72.9 11.2 %all_to_all.30.refs_4_ = f32[16,2,1024]{2,1,0:T(2,128)S(1)} all-to-all(f32[16,2,1024]{2,1,0:T(2,128)S(1)} %broadcast_in_dim.54), channel_id=1, replica_groups=mesh['img'=8,'half'=2,'low'=2] {'img','half'}, dimensions={0} | all-to-all | bytes 262144 | tf_op jit(solution)/shard_map/all_to_all | solution.py:38
  84.0 1.8 collective-permute-start.11
  87.5 6.0 %shard_map.224 = (bf16[256,1024]{1,0:T(8,128)(2,1)}, bf16[256,1024]{1,0:T(8,128)(2,1)}, f32[256,512]{1,0:T(8,128)}, bf16[2,128,256]{2,1,0:T(8,128)(2,1)}, bf16[2...) custom-call(s32[1,4]{1,0:T(1,128)} %add_bitcast_fusion.refs_0_.place, ...), custom_call_target="tpu_custom_call" | custom-call | tf_op jit(solution)/shard_map/pallas_call | solution.py:156
  94.9 2.5 %all-to-all-start.4 = ((f32[32,2,512]{2,1,0:T(2,128)}), f32[32,2,512]{2,1,0:T(2,128)S(1)}, u32[]{:S(2)}, u32[]{:S(2)}) async-start(f32[32,2,512]{2,1,0:T(2,128)} %get-tuple-element.164), calls=%async_computation.4 | async-start | bytes 262144 | tf_op jit(solution)/shard_map/all_to_all | solution.py:32
  97.8 3.2 %collective-permute-start.17 = (bf16[128,1024]{1,0:T(8,128)(2,1)}, bf16[128,1024]{1,0:T(8,128)(2,1)S(1)}, u32[]{:S(2)}, u32[]{:S(2)}) collective-permute-start(bf16[128,1024]{1,0:T(8,128)(2,1)} %get-tuple-element.169), channel_id=1, source_target_pairs={{1,2},{2,1},{5,6},{6,5},{9,10},{10,9},{13,14},{14,13},{17,18},{18,... | collective-permute-start | bytes 786440 | tf_op jit(solution)/shard_map/ppermute | solution.py:146
  104.4 3.2 %shard_map.225 = (bf16[256,1024]{1,0:T(8,128)(2,1)}, f32[256,1024]{1,0:T(8,128)}) custom-call(s32[1,4]{1,0:T(1,128)} %add_bitcast_fusion.refs_0_.place, bf16[256,512]{1,0:T(8,128)(2,1)} %get-tuple-element.141.act, bf16[256,512]{1,0:T(8,128)(2,1)} %copy-done.26, bf16[256,1024]{1,0:T(8,128)(2,1)} %get-tuple-element.161.third, bf16[256,1024]{1,0:T(8,128)(2,1)} %copy-done.16), custom_call_target="tpu_custom_call" | custom-call | tf_op jit(solution)/shard_map/pallas_call | solution.py:156
  108.5 6.2 %shard_map.226 = (f32[256,512]{1,0:T(8,128)}, bf16[256,512]{1,0:T(8,128)(2,1)}, f32[32,2,512]{2,1,0:T(2,128)}, f32[2,512]{1,0:T(2,128)}) custom-call(s32[1,4]{1,0:T(1,128)} %add_bitcast_fusion.refs_0_.place, f32[2,640]{1,0:T(2,128)} %get-tuple-element.131.refs_1_.sums_first, f32[2,512]{1,0:T(2,128)} %get-tuple-element.148.refs_2_.sums_second, ...), custom_call_target="tpu_custom_call" | custom-call | tf_op jit(solution)/shard_map/pallas_call | solution.py:156
  114.9 5.3 %all-to-all-start.5 = ((f32[32,2,512]{2,1,0:T(2,128)}), f32[32,2,512]{2,1,0:T(2,128)S(1)}, u32[]{:S(2)}, u32[]{:S(2)}) async-start(f32[32,2,512]{2,1,0:T(2,128)} %get-tuple-element.176), calls=%async_computation.5 | async-start | bytes 262144 | tf_op jit(solution)/shard_map/all_to_all | solution.py:32
  123.2 4.8 %shard_map.227 = (bf16[8,9,16,128]{3,2,1,0:T(8,128)(2,1)}, f32[8,9,16,128]{3,2,1,0:T(8,128)}) custom-call(s32[1,4]{1,0:T(1,128)} %add_bitcast_fusion.1.place, s32[2,16]{1,0:T(2,128)} %slice_convert_fusion.sizes, f32[2,640]{1,0:T(2,128)} %get-tuple-element.131.refs_1_.sums_first, f32[2,512]{1,0:T(2,128)} %get-tuple-element.148.refs_2_.sums_second, ...), custom_call_target="tpu_custom_call" | custom-call | tf_op jit(solution)/shard_map/pallas_call | solution.py:156
  130.8 4.3 %shard_map.228 = (bf16[256,512]{1,0:T(8,128)(2,1)}, f32[2,512]{1,0:T(2,128)}, bf16[512,512]{1,0:T(8,128)(2,1)}, f32[512,512]{1,0:T(8,128)}) custom-call(s32[1,4]{1,0:T(1,128)} %add_bitcast_fusion.refs_0_.place, f32[2,640]{1,0:T(2,128)} %get-tuple-element.131.refs_1_.sums_first, f32[32,2,512]{2,1,0:T(2,128)} %copy-done.13, ...), custom_call_target="tpu_custom_call" | custom-call | tf_op jit(solution)/shard_map/pallas_call | solution.py:156
  135.3 1.6 collective-permute-done.24
  137.0 2.3 collective-permute-start.25
  140.8 2.1 convolution_add_fusion
  142.9 3.0 %collective-permute-done.25 = bf16[576,128]{1,0:T(8,128)(2,1)S(1)} collective-permute-done((bf16[576,128]{1,0:T(8,128)(2,1)S(1)}, bf16[576,128]{1,0:T(8,128)(2,1)S(1)}, u32[]{:S(2)}, u32[]{:S(2)}) %collective-permute-start.25) | collective-permute-done | bytes 147488 | tf_op jit(solution)/shard_map/ppermute | solution.py:21
  148.7 1.7 collective-permute-start.28
  150.4 1.7 collective-permute-start.27
  152.1 3.0 %collective-permute-done.27 = bf16[64,1024]{1,0:T(8,128)(2,1)S(1)} collective-permute-done((bf16[64,1024]{1,0:T(8,128)(2,1)S(1)}, bf16[64,1024]{1,0:T(8,128)(2,1)S(1)}, u32[]{:S(2)}, u32[]{:S(2)}) %collective-permute-start.27) | collective-permute-done | bytes 131104 | tf_op jit(solution)/shard_map/ppermute | solution.py:21
  155.0 3.0 %collective-permute-done.28 = bf16[576,128]{1,0:T(8,128)(2,1)S(1)} collective-permute-done((bf16[576,128]{1,0:T(8,128)(2,1)S(1)}, bf16[576,128]{1,0:T(8,128)(2,1)S(1)}, u32[]{:S(2)}, u32[]{:S(2)}) %collective-permute-start.28) | collective-permute-done | bytes 147488 | tf_op jit(solution)/shard_map/ppermute | solution.py:21
  159.9 2.0 collective-permute-start.30
  162.0 5.8 %collective-permute-done.30 = bf16[32,1024]{1,0:T(8,128)(2,1)S(1)} collective-permute-done((bf16[32,1024]{1,0:T(8,128)(2,1)S(1)}, bf16[32,1024]{1,0:T(8,128)(2,1)S(1)}, u32[]{:S(2)}, u32[]{:S(2)}) %collective-permute-start.30) | collective-permute-done | bytes 65568 | tf_op jit(solution)/shard_map/ppermute | solution.py:21
  167.7 1.7 collective-permute-done.31
  169.5 2.3 collective-permute-start.35
  171.8 1.6 collective-permute-start.36
  176.5 8.7 %collective-permute-done.37 = f32[16,2048]{1,0:T(8,128)S(1)} collective-permute-done((f32[16,2048]{1,0:T(8,128)S(1)}, f32[16,2048]{1,0:T(8,128)S(1)}, u32[]{:S(2)}, u32[]{:S(2)}) %collective-permute-start.37) | collective-permute-done | bytes 131104 | tf_op jit(solution)/shard_map/ppermute | solution.py:136
  186.2 1.5 collective-permute-start.39
  187.7 2.1 collective-permute-start.38
  190.8 3.5 %collective-permute-done.40 = bf16[64,512]{1,0:T(8,128)(2,1)S(1)} collective-permute-done((bf16[64,512]{1,0:T(8,128)(2,1)S(1)}, bf16[64,512]{1,0:T(8,128)(2,1)S(1)}, u32[]{:S(2)}, u32[]{:S(2)}) %collective-permute-start.40) | collective-permute-done | bytes 65568 | tf_op jit(solution)/shard_map/ppermute | solution.py:21
  194.4 6.9 %collective-permute-done.39 = bf16[4608,128]{1,0:T(8,128)(2,1)S(1)} collective-permute-done((bf16[4608,128]{1,0:T(8,128)(2,1)S(1)}, bf16[4608,128]{1,0:T(8,128)(2,1)S(1)}, u32[]{:S(2)}, u32[]{:S(2)}) %collective-permute-start.39) | collective-permute-done | bytes 1179680 | tf_op jit(solution)/shard_map/ppermute | solution.py:21
  202.4 1.9 collective-permute-start.43
  204.3 2.7 %collective-permute-done.43 = bf16[128,512]{1,0:T(8,128)(2,1)S(1)} collective-permute-done((bf16[128,512]{1,0:T(8,128)(2,1)S(1)}, bf16[128,512]{1,0:T(8,128)(2,1)S(1)}, u32[]{:S(2)}, u32[]{:S(2)}) %collective-permute-start.43) | collective-permute-done | bytes 131104 | tf_op jit(solution)/shard_map/ppermute | solution.py:21
  209.2 1.6 collective-permute-start.45
  210.8 5.9 %shard_map.229 = f32[9,512,512]{2,1,0:T(8,128)} custom-call(s32[1,1]{1,0:T(1,128)} %bitcast.72.odd, bf16[4,16,9,16,128]{4,3,2,1,0:T(8,128)(2,1)S(1)} %bitcast.186, bf16[4,16,9,16,128]{4,3,2,1,0:T(8,128)(2,1)S(1)} %bitcast.187), custom_call_target="tpu_custom_call" | custom-call | tf_op jit(solution)/shard_map/pallas_call | solution.py:632
  218.3 2.9 %collective-permute-start.46 = (bf16[512,1024]{1,0:T(8,128)(2,1)S(1)}, bf16[512,1024]{1,0:T(8,128)(2,1)S(1)}, u32[]{:S(2)}, u32[]{:S(2)}) collective-permute-start(bf16[512,1024]{1,0:T(8,128)(2,1)S(1)} %bitcast.193), channel_id=1, source_target_pairs={{0,1},{1,0},{2,3},{3,2},{4,5},{5,4},{6,7},{7,6},{8,9},{9,8},{10,11... | collective-permute-start | bytes 3145736 | tf_op jit(solution)/shard_map/ppermute | solution.py:21
  222.0 7.7 %collective-permute-done.47 = bf16[512,512]{1,0:T(8,128)(2,1)S(1)} collective-permute-done((bf16[512,512]{1,0:T(8,128)(2,1)S(1)}, bf16[512,512]{1,0:T(8,128)(2,1)S(1)}, u32[]{:S(2)}, u32[]{:S(2)}) %collective-permute-start.47) | collective-permute-done | bytes 524320 | tf_op jit(solution)/shard_map/ppermute | solution.py:21
  232.2 2.6 %maximum_convert_fusion = f32[512,2048]{1,0:T(8,128)} fusion(bf16[512,1024]{1,0:T(8,128)(2,1)S(1)} %get-tuple-element.233, bf16[512,1024]{1,0:T(8,128)(2,1)S(1)} %get-tuple-element.232), kind=kLoop, calls=%fused_computation.2 | loop fusion | flops 4194304 | bytes 6291456 | tf_op jit(solution)/shard_map/convert_element_type | solution.py:901
  235.2 2.7 %bitcast_convert_fusion = f32[2048,512]{1,0:T(8,128)} fusion(bf16[2,1024,512]{2,1,0:T(8,128)(2,1)S(1)} %pad_maximum_fusion.1), kind=kLoop, calls=%fused_computation.4 | loop fusion | flops 1048576 | bytes 6291456 | tf_op jit(solution)/shard_map/convert_element_type | solution.py:939
  (233 shorter events, 49.5 us)
Async XLA Ops:
  5.6 16.0 %all-to-all-start = ((f32[32,2,640]{2,1,0:T(2,128)}), f32[32,2,640]{2,1,0:T(2,128)S(1)}, u32[]{:S(2)}, u32[]{:S(2)}) async-start(f32[32,2,640]{2,1,0:T(2,128)} %get-tuple-element.120), calls=%async_computation | async-start | bytes 327680 | tf_op jit(solution)/shard_map/all_to_all | solution.py:32
  12.8 22.9 %collective-permute-start.3 = (f32[256,512]{1,0:T(8,128)}, f32[256,512]{1,0:T(8,128)S(1)}, u32[]{:S(2)}, u32[]{:S(2)}) collective-permute-start(f32[256,512]{1,0:T(8,128)} %get-tuple-element.125.refs_3_.refs_10_.first), channel_id=1, source_target_pairs={{0,1},{1,0},{2,3},{3,2},{4,5},{5,4},{6,7},{7,6},{8,9},{9,8},{10,11... | collective-permute-start | bytes 1572872 | tf_op jit(solution)/shard_map/ppermute | solution.py:21
  13.1 3.8 %collective-permute-start = (f32[128,512]{1,0:T(8,128)}, f32[128,512]{1,0:T(8,128)S(1)}, u32[]{:S(2)}, u32[]{:S(2)}) collective-permute-start(f32[128,512]{1,0:T(8,128)} %get-tuple-element.121), channel_id=1, source_target_pairs={{0,1},{1,0},{2,3},{3,2},{4,5},{5,4},{6,7},{7,6},{8,9},{9,8},{10,11... | collective-permute-start | bytes 786440 | tf_op jit(solution)/shard_map/ppermute | solution.py:145
  13.3 8.3 %collective-permute-start.1 = (f32[128,512]{1,0:T(8,128)}, f32[128,512]{1,0:T(8,128)S(1)}, u32[]{:S(2)}, u32[]{:S(2)}) collective-permute-start(f32[128,512]{1,0:T(8,128)} %get-tuple-element.122), channel_id=1, source_target_pairs={{1,2},{2,1},{5,6},{6,5},{9,10},{10,9},{13,14},{14,13},{17,18},{18,... | collective-permute-start | bytes 786440 | tf_op jit(solution)/shard_map/ppermute | solution.py:146
  27.9 13.6 %all-to-all-start.1 = ((f32[32,2,512]{2,1,0:T(2,128)}), f32[32,2,512]{2,1,0:T(2,128)S(1)}, u32[]{:S(2)}, u32[]{:S(2)}) async-start(f32[32,2,512]{2,1,0:T(2,128)} %get-tuple-element.132), calls=%async_computation.1 | async-start | bytes 262144 | tf_op jit(solution)/shard_map/all_to_all | solution.py:32
  46.8 14.2 %collective-permute-start.9 = (bf16[256,1024]{1,0:T(8,128)(2,1)S(1)}, bf16[256,1024]{1,0:T(8,128)(2,1)S(1)}, u32[]{:S(2)}, u32[]{:S(2)}) collective-permute-start(bf16[256,1024]{1,0:T(8,128)(2,1)S(1)} %get-tuple-element.241), channel_id=1, source_target_pairs={{0,1},{1,0},{2,3},{3,2},{4,5},{5,4},{6,7},{7,6},{8,9},{9,8},{10,11... | collective-permute-start | bytes 1572872 | tf_op jit(solution)/shard_map/ppermute | solution.py:21
  48.5 10.3 %all-to-all-start.2 = ((f32[16,2,1024]{2,1,0:T(2,128)}), f32[16,2,1024]{2,1,0:T(2,128)S(1)}, u32[]{:S(2)}, u32[]{:S(2)}) async-start(f32[16,2,1024]{2,1,0:T(2,128)} %broadcast_in_dim.51), calls=%async_computation.2 | async-start | bytes 262144 | tf_op jit(solution)/shard_map/all_to_all | solution.py:38
  52.2 8.9 %collective-permute-start.6 = (bf16[2,2,128,256]{3,2,1,0:T(8,128)(2,1)S(1)}, bf16[2,2,128,256]{3,2,1,0:T(8,128)(2,1)S(1)}, u32[]{:S(2)}, u32[]{:S(2)}) collective-permute-start(bf16[2,2,128,256]{3,2,1,0:T(8,128)(2,1)S(1)} %pad_maximum_fusion.11), channel_id=1, source_target_pairs={{0,2},{1,5},{2,0},{3,7},{4,6},{5,1},{6,4},{7,3},{8,10},{9,13},{10,... | collective-permute-start | bytes 786440 | tf_op jit(solution)/shard_map/ppermute | solution.py:21
  53.5 7.6 %collective-permute-start.8 = (bf16[256,512]{1,0:T(8,128)(2,1)S(1)}, bf16[256,512]{1,0:T(8,128)(2,1)S(1)}, u32[]{:S(2)}, u32[]{:S(2)}) collective-permute-start(bf16[256,512]{1,0:T(8,128)(2,1)S(1)} %copy-done.25), channel_id=1, source_target_pairs={{0,1},{1,0},{2,3},{3,2},{4,5},{5,4},{6,7},{7,6},{8,9},{9,8},{10,11... | collective-permute-start | bytes 786440 | tf_op jit(solution)/shard_map/ppermute | solution.py:21
  54.4 6.7 %collective-permute-start.7 = (bf16[1,2,128,256]{3,2,1,0:T(8,128)(2,1)}, bf16[1,2,128,256]{3,2,1,0:T(8,128)(2,1)S(1)}, u32[]{:S(2)}, u32[]{:S(2)}) collective-permute-start(bf16[1,2,128,256]{3,2,1,0:T(8,128)(2,1)} %bitcast.226), channel_id=1, source_target_pairs={{0,2},{1,5},{2,0},{3,7},{4,6},{5,1},{6,4},{7,3},{8,10},{9,13},{10,... | collective-permute-start | bytes 393224 | tf_op jit(solution)/shard_map/ppermute | solution.py:21
  58.8 2.6 %collective-permute-start.5 = (f32[16,2,1024]{2,1,0:T(2,128)S(1)}, f32[16,2,1024]{2,1,0:T(2,128)S(1)}, u32[]{:S(2)}, u32[]{:S(2)}) collective-permute-start(f32[16,2,1024]{2,1,0:T(2,128)S(1)} %all-to-all-done.2.refs_2_), channel_id=1, source_target_pairs={{0,1},{1,0},{2,3},{3,2},{4,5},{5,4},{6,7},{7,6},{8,9},{9,8},{10,11... | collective-permute-start | bytes 393224 | tf_op jit(solution)/shard_map/ppermute | solution.py:21
  69.3 17.5 %collective-permute-start.12 = (bf16[4,2,128,256]{3,2,1,0:T(8,128)(2,1)S(1)}, bf16[4,2,128,256]{3,2,1,0:T(8,128)(2,1)S(1)}, u32[]{:S(2)}, u32[]{:S(2)}) collective-permute-start(bf16[4,2,128,256]{3,2,1,0:T(8,128)(2,1)S(1)} %bitcast.199), channel_id=1, source_target_pairs={{0,4},{1,3},{2,6},{3,1},{4,0},{5,7},{6,2},{7,5},{8,12},{9,11},{10,... | collective-permute-start | bytes 1572872 | tf_op jit(solution)/shard_map/ppermute | solution.py:21
  84.0 2.8 %collective-permute-start.11 = (f32[16,2,1024]{2,1,0:T(2,128)S(1)}, f32[16,2,1024]{2,1,0:T(2,128)S(1)}, u32[]{:S(2)}, u32[]{:S(2)}) collective-permute-start(f32[16,2,1024]{2,1,0:T(2,128)S(1)} %all_to_all.30.refs_4_), channel_id=1, source_target_pairs={{0,1},{1,0},{2,3},{3,2},{4,5},{5,4},{6,7},{7,6},{8,9},{9,8},{10,11... | collective-permute-start | bytes 393224 | tf_op jit(solution)/shard_map/ppermute | solution.py:21
  93.5 7.6 %collective-permute-start.14 = (bf16[1,2,128,256]{3,2,1,0:T(8,128)(2,1)}, bf16[1,2,128,256]{3,2,1,0:T(8,128)(2,1)S(1)}, u32[]{:S(2)}, u32[]{:S(2)}) collective-permute-start(bf16[1,2,128,256]{3,2,1,0:T(8,128)(2,1)} %bitcast.227), channel_id=1, source_target_pairs={{0,2},{1,5},{2,0},{3,7},{4,6},{5,1},{6,4},{7,3},{8,10},{9,13},{10,... | collective-permute-start | bytes 393224 | tf_op jit(solution)/shard_map/ppermute | solution.py:21
  94.0 9.6 %collective-permute-start.13 = (bf16[256,1024]{1,0:T(8,128)(2,1)}, bf16[256,1024]{1,0:T(8,128)(2,1)S(1)}, u32[]{:S(2)}, u32[]{:S(2)}) collective-permute-start(bf16[256,1024]{1,0:T(8,128)(2,1)} %get-tuple-element.162), channel_id=1, source_target_pairs={{0,1},{1,0},{2,3},{3,2},{4,5},{5,4},{6,7},{7,6},{8,9},{9,8},{10,11... | collective-permute-start | bytes 1572872 | tf_op jit(solution)/shard_map/ppermute | solution.py:21
  94.9 12.7 %all-to-all-start.4 = ((f32[32,2,512]{2,1,0:T(2,128)}), f32[32,2,512]{2,1,0:T(2,128)S(1)}, u32[]{:S(2)}, u32[]{:S(2)}) async-start(f32[32,2,512]{2,1,0:T(2,128)} %get-tuple-element.164), calls=%async_computation.4 | async-start | bytes 262144 | tf_op jit(solution)/shard_map/all_to_all | solution.py:32
  97.4 10.2 %collective-permute-start.16 = (bf16[128,1024]{1,0:T(8,128)(2,1)}, bf16[128,1024]{1,0:T(8,128)(2,1)S(1)}, u32[]{:S(2)}, u32[]{:S(2)}) collective-permute-start(bf16[128,1024]{1,0:T(8,128)(2,1)} %get-tuple-element.168), channel_id=1, source_target_pairs={{0,1},{1,0},{2,3},{3,2},{4,5},{5,4},{6,7},{7,6},{8,9},{9,8},{10,11... | collective-permute-start | bytes 786440 | tf_op jit(solution)/shard_map/ppermute | solution.py:145
  97.8 9.8 %collective-permute-start.17 = (bf16[128,1024]{1,0:T(8,128)(2,1)}, bf16[128,1024]{1,0:T(8,128)(2,1)S(1)}, u32[]{:S(2)}, u32[]{:S(2)}) collective-permute-start(bf16[128,1024]{1,0:T(8,128)(2,1)} %get-tuple-element.169), channel_id=1, source_target_pairs={{1,2},{2,1},{5,6},{6,5},{9,10},{10,9},{13,14},{14,13},{17,18},{18,... | collective-permute-start | bytes 786440 | tf_op jit(solution)/shard_map/ppermute | solution.py:146
  102.0 5.6 %collective-permute-start.15 = (bf16[2,2,128,128]{3,2,1,0:T(8,128)(2,1)S(1)}, bf16[2,2,128,128]{3,2,1,0:T(8,128)(2,1)S(1)}, u32[]{:S(2)}, u32[]{:S(2)}) collective-permute-start(bf16[2,2,128,128]{3,2,1,0:T(8,128)(2,1)S(1)} %fusion.3), channel_id=1, source_target_pairs={{0,4},{1,3},{2,6},{3,1},{4,0},{5,7},{6,2},{7,5},{8,12},{9,11},{10,... | collective-permute-start | bytes 393224 | tf_op jit(solution)/shard_map/ppermute | solution.py:21
  102.1 12.6 %collective-permute-start.18 = (bf16[2,2,128,128]{3,2,1,0:T(8,128)(2,1)S(1)}, bf16[2,2,128,128]{3,2,1,0:T(8,128)(2,1)S(1)}, u32[]{:S(2)}, u32[]{:S(2)}) collective-permute-start(bf16[2,2,128,128]{3,2,1,0:T(8,128)(2,1)S(1)} %fusion.7), channel_id=1, source_target_pairs={{0,4},{1,3},{2,6},{3,1},{4,0},{5,7},{6,2},{7,5},{8,12},{9,11},{10,... | collective-permute-start | bytes 393224 | tf_op jit(solution)/shard_map/ppermute | solution.py:21
  114.9 13.5 %all-to-all-start.5 = ((f32[32,2,512]{2,1,0:T(2,128)}), f32[32,2,512]{2,1,0:T(2,128)S(1)}, u32[]{:S(2)}, u32[]{:S(2)}) async-start(f32[32,2,512]{2,1,0:T(2,128)} %get-tuple-element.176), calls=%async_computation.5 | async-start | bytes 262144 | tf_op jit(solution)/shard_map/all_to_all | solution.py:32
  120.9 7.5 %collective-permute-start.21 = (bf16[256,512]{1,0:T(8,128)(2,1)S(1)}, bf16[256,512]{1,0:T(8,128)(2,1)S(1)}, u32[]{:S(2)}, u32[]{:S(2)}) collective-permute-start(bf16[256,512]{1,0:T(8,128)(2,1)S(1)} %copy-done.42), channel_id=1, source_target_pairs={{0,1},{1,0},{2,3},{3,2},{4,5},{5,4},{6,7},{7,6},{8,9},{9,8},{10,11... | collective-permute-start | bytes 786440 | tf_op jit(solution)/shard_map/ppermute | solution.py:21
  128.4 8.6 %collective-permute-start.24 = (bf16[1152,128]{1,0:T(8,128)(2,1)}, bf16[1152,128]{1,0:T(8,128)(2,1)S(1)}, u32[]{:S(2)}, u32[]{:S(2)}) collective-permute-start(bf16[1152,128]{1,0:T(8,128)(2,1)} %bitcast.225), channel_id=1, source_target_pairs={{0,8},{1,9},{2,10},{3,11},{4,12},{5,13},{6,14},{7,15},{8,0},{9,1},... | collective-permute-start | bytes 884744 | tf_op jit(solution)/shard_map/ppermute | solution.py:21
  129.6 9.7 %collective-permute-start.22 = (bf16[256,1024]{1,0:T(8,128)(2,1)S(1)}, bf16[256,1024]{1,0:T(8,128)(2,1)S(1)}, u32[]{:S(2)}, u32[]{:S(2)}) collective-permute-start(bf16[256,1024]{1,0:T(8,128)(2,1)S(1)} %copy-done.41), channel_id=1, source_target_pairs={{0,2},{1,5},{2,0},{3,7},{4,6},{5,1},{6,4},{7,3},{8,10},{9,13},{10,... | collective-permute-start | bytes 1572872 | tf_op jit(solution)/shard_map/ppermute | solution.py:21
  135.0 10.8 %collective-permute-start.26 = (bf16[512,512]{1,0:T(8,128)(2,1)}, bf16[512,512]{1,0:T(8,128)(2,1)S(1)}, u32[]{:S(2)}, u32[]{:S(2)}) collective-permute-start(bf16[512,512]{1,0:T(8,128)(2,1)} %get-tuple-element.194), channel_id=1, source_target_pairs={{0,2},{1,5},{2,0},{3,7},{4,6},{5,1},{6,4},{7,3},{8,10},{9,13},{10,... | collective-permute-start | bytes 1572872 | tf_op jit(solution)/shard_map/ppermute | solution.py:21
  137.0 8.8 %collective-permute-start.25 = (bf16[576,128]{1,0:T(8,128)(2,1)S(1)}, bf16[576,128]{1,0:T(8,128)(2,1)S(1)}, u32[]{:S(2)}, u32[]{:S(2)}) collective-permute-start(bf16[576,128]{1,0:T(8,128)(2,1)S(1)} %dynamic-slice_convert_fusion.2), channel_id=1, source_target_pairs={{0,16},{1,17},{2,18},{3,19},{4,20},{5,21},{6,22},{7,23},{8,24},{9,... | collective-permute-start | bytes 442376 | tf_op jit(solution)/shard_map/ppermute | solution.py:21
  139.6 7.7 %collective-permute-start.23 = (bf16[128,1024]{1,0:T(8,128)(2,1)S(1)}, bf16[128,1024]{1,0:T(8,128)(2,1)S(1)}, u32[]{:S(2)}, u32[]{:S(2)}) collective-permute-start(bf16[128,1024]{1,0:T(8,128)(2,1)S(1)} %dynamic-slice_convert_fusion.1), channel_id=1, source_target_pairs={{0,4},{1,3},{2,6},{3,1},{4,0},{5,7},{6,2},{7,5},{8,12},{9,11},{10,... | collective-permute-start | bytes 786440 | tf_op jit(solution)/shard_map/ppermute | solution.py:21
  147.5 10.5 %collective-permute-start.29 = (bf16[256,512]{1,0:T(8,128)(2,1)S(1)}, bf16[256,512]{1,0:T(8,128)(2,1)S(1)}, u32[]{:S(2)}, u32[]{:S(2)}) collective-permute-start(bf16[256,512]{1,0:T(8,128)(2,1)S(1)} %dynamic-slice_convert_fusion), channel_id=1, source_target_pairs={{0,4},{1,3},{2,6},{3,1},{4,0},{5,7},{6,2},{7,5},{8,12},{9,11},{10,... | collective-permute-start | bytes 786440 | tf_op jit(solution)/shard_map/ppermute | solution.py:21
  148.7 9.3 %collective-permute-start.28 = (bf16[576,128]{1,0:T(8,128)(2,1)S(1)}, bf16[576,128]{1,0:T(8,128)(2,1)S(1)}, u32[]{:S(2)}, u32[]{:S(2)}) collective-permute-start(bf16[576,128]{1,0:T(8,128)(2,1)S(1)} %add_convert_fusion), channel_id=1, source_target_pairs={{0,16},{1,17},{2,18},{3,19},{4,20},{5,21},{6,22},{7,23},{8,24},{9,... | collective-permute-start | bytes 442376 | tf_op jit(solution)/shard_map/ppermute | solution.py:21
  150.4 4.6 %collective-permute-start.27 = (bf16[64,1024]{1,0:T(8,128)(2,1)S(1)}, bf16[64,1024]{1,0:T(8,128)(2,1)S(1)}, u32[]{:S(2)}, u32[]{:S(2)}) collective-permute-start(bf16[64,1024]{1,0:T(8,128)(2,1)S(1)} %dynamic-slice_convert_fusion.4), channel_id=1, source_target_pairs={{0,8},{1,9},{2,10},{3,11},{4,12},{5,13},{6,14},{7,15},{8,0},{9,1},... | collective-permute-start | bytes 393224 | tf_op jit(solution)/shard_map/ppermute | solution.py:21
  158.2 9.6 %collective-permute-start.32 = (bf16[128,512]{1,0:T(8,128)(2,1)S(1)}, bf16[128,512]{1,0:T(8,128)(2,1)S(1)}, u32[]{:S(2)}, u32[]{:S(2)}) collective-permute-start(bf16[128,512]{1,0:T(8,128)(2,1)S(1)} %dynamic-slice_convert_fusion.3), channel_id=1, source_target_pairs={{0,8},{1,9},{2,10},{3,11},{4,12},{5,13},{6,14},{7,15},{8,0},{9,1},... | collective-permute-start | bytes 393224 | tf_op jit(solution)/shard_map/ppermute | solution.py:21
  158.6 10.9 %collective-permute-start.31 = (bf16[1152,128]{1,0:T(8,128)(2,1)S(1)}, bf16[1152,128]{1,0:T(8,128)(2,1)S(1)}, u32[]{:S(2)}, u32[]{:S(2)}) collective-permute-start(bf16[1152,128]{1,0:T(8,128)(2,1)S(1)} %bitcast.201), channel_id=1, source_target_pairs={{0,8},{1,9},{2,10},{3,11},{4,12},{5,13},{6,14},{7,15},{8,0},{9,1},... | collective-permute-start | bytes 884744 | tf_op jit(solution)/shard_map/ppermute | solution.py:21
  159.9 7.8 %collective-permute-start.30 = (bf16[32,1024]{1,0:T(8,128)(2,1)S(1)}, bf16[32,1024]{1,0:T(8,128)(2,1)S(1)}, u32[]{:S(2)}, u32[]{:S(2)}) collective-permute-start(bf16[32,1024]{1,0:T(8,128)(2,1)S(1)} %dynamic-slice_convert_fusion.6), channel_id=1, source_target_pairs={{0,16},{1,17},{2,18},{3,19},{4,20},{5,21},{6,22},{7,23},{8,24},{9,... | collective-permute-start | bytes 196616 | tf_op jit(solution)/shard_map/ppermute | solution.py:21
  169.5 16.4 %collective-permute-start.35 = (bf16[64,512]{1,0:T(8,128)(2,1)S(1)}, bf16[64,512]{1,0:T(8,128)(2,1)S(1)}, u32[]{:S(2)}, u32[]{:S(2)}) collective-permute-start(bf16[64,512]{1,0:T(8,128)(2,1)S(1)} %dynamic-slice_convert_fusion.5), channel_id=1, source_target_pairs={{0,16},{1,17},{2,18},{3,19},{4,20},{5,21},{6,22},{7,23},{8,24},{9,... | collective-permute-start | bytes 196616 | tf_op jit(solution)/shard_map/ppermute | solution.py:21
  173.6 12.4 %collective-permute-start.34 = (bf16[2304,128]{1,0:T(8,128)(2,1)S(1)}, bf16[2304,128]{1,0:T(8,128)(2,1)S(1)}, u32[]{:S(2)}, u32[]{:S(2)}) collective-permute-start(bf16[2304,128]{1,0:T(8,128)(2,1)S(1)} %bitcast.195), channel_id=1, source_target_pairs={{0,4},{1,3},{2,6},{3,1},{4,0},{5,7},{6,2},{7,5},{8,12},{9,11},{10,... | collective-permute-start | bytes 1769480 | tf_op jit(solution)/shard_map/ppermute | solution.py:21
  174.4 10.7 %collective-permute-start.37 = (f32[16,2048]{1,0:T(8,128)S(1)}, f32[16,2048]{1,0:T(8,128)S(1)}, u32[]{:S(2)}, u32[]{:S(2)}) collective-permute-start(f32[16,2048]{1,0:T(8,128)S(1)} %add.190), channel_id=1, source_target_pairs={{0,2},{1,3},{2,0},{3,1},{4,6},{5,7},{6,4},{7,5},{8,10},{9,11},{10,... | collective-permute-start | bytes 393224 | tf_op jit(solution)/shard_map/ppermute | solution.py:136
  175.2 10.7 %collective-permute-start.33 = (bf16[32,1024]{1,0:T(8,128)(2,1)S(1)}, bf16[32,1024]{1,0:T(8,128)(2,1)S(1)}, u32[]{:S(2)}, u32[]{:S(2)}) collective-permute-start(bf16[32,1024]{1,0:T(8,128)(2,1)S(1)} %add_convert_fusion.2), channel_id=1, source_target_pairs={{0,16},{1,17},{2,18},{3,19},{4,20},{5,21},{6,22},{7,23},{8,24},{9,... | collective-permute-start | bytes 196616 | tf_op jit(solution)/shard_map/ppermute | solution.py:21
  186.2 15.1 %collective-permute-start.39 = (bf16[4608,128]{1,0:T(8,128)(2,1)S(1)}, bf16[4608,128]{1,0:T(8,128)(2,1)S(1)}, u32[]{:S(2)}, u32[]{:S(2)}) collective-permute-start(bf16[4608,128]{1,0:T(8,128)(2,1)S(1)} %bitcast.192), channel_id=1, source_target_pairs={{0,2},{1,5},{2,0},{3,7},{4,6},{5,1},{6,4},{7,3},{8,10},{9,13},{10,... | collective-permute-start | bytes 3538952 | tf_op jit(solution)/shard_map/ppermute | solution.py:21
  187.7 6.6 %collective-permute-start.38 = (bf16[64,1024]{1,0:T(8,128)(2,1)S(1)}, bf16[64,1024]{1,0:T(8,128)(2,1)S(1)}, u32[]{:S(2)}, u32[]{:S(2)}) collective-permute-start(bf16[64,1024]{1,0:T(8,128)(2,1)S(1)} %bitcast.209), channel_id=1, source_target_pairs={{0,8},{1,9},{2,10},{3,11},{4,12},{5,13},{6,14},{7,15},{8,0},{9,1},... | collective-permute-start | bytes 393224 | tf_op jit(solution)/shard_map/ppermute | solution.py:21
  189.8 4.5 %collective-permute-start.40 = (bf16[64,512]{1,0:T(8,128)(2,1)S(1)}, bf16[64,512]{1,0:T(8,128)(2,1)S(1)}, u32[]{:S(2)}, u32[]{:S(2)}) collective-permute-start(bf16[64,512]{1,0:T(8,128)(2,1)S(1)} %add_convert_fusion.1), channel_id=1, source_target_pairs={{0,16},{1,17},{2,18},{3,19},{4,20},{5,21},{6,22},{7,23},{8,24},{9,... | collective-permute-start | bytes 196616 | tf_op jit(solution)/shard_map/ppermute | solution.py:21
  201.8 5.7 %collective-permute-start.42 = (bf16[9216,128]{1,0:T(8,128)(2,1)S(1)}, bf16[9216,128]{1,0:T(8,128)(2,1)S(1)}, u32[]{:S(2)}, u32[]{:S(2)}) collective-permute-start(bf16[9216,128]{1,0:T(8,128)(2,1)S(1)} %bitcast.185), channel_id=1, source_target_pairs={{0,1},{1,0},{2,3},{3,2},{4,5},{5,4},{6,7},{7,6},{8,9},{9,8},{10,11... | collective-permute-start | bytes 7077896 | tf_op jit(solution)/shard_map/ppermute | solution.py:21
  201.9 5.6 %collective-permute-start.41 = (bf16[128,1024]{1,0:T(8,128)(2,1)S(1)}, bf16[128,1024]{1,0:T(8,128)(2,1)S(1)}, u32[]{:S(2)}, u32[]{:S(2)}) collective-permute-start(bf16[128,1024]{1,0:T(8,128)(2,1)S(1)} %bitcast.204), channel_id=1, source_target_pairs={{0,4},{1,3},{2,6},{3,1},{4,0},{5,7},{6,2},{7,5},{8,12},{9,11},{10,... | collective-permute-start | bytes 786440 | tf_op jit(solution)/shard_map/ppermute | solution.py:21
  202.4 4.6 %collective-permute-start.43 = (bf16[128,512]{1,0:T(8,128)(2,1)S(1)}, bf16[128,512]{1,0:T(8,128)(2,1)S(1)}, u32[]{:S(2)}, u32[]{:S(2)}) collective-permute-start(bf16[128,512]{1,0:T(8,128)(2,1)S(1)} %bitcast.210), channel_id=1, source_target_pairs={{0,8},{1,9},{2,10},{3,11},{4,12},{5,13},{6,14},{7,15},{8,0},{9,1},... | collective-permute-start | bytes 393224 | tf_op jit(solution)/shard_map/ppermute | solution.py:21
  207.6 10.4 %collective-permute-start.44 = (bf16[256,1024]{1,0:T(8,128)(2,1)S(1)}, bf16[256,1024]{1,0:T(8,128)(2,1)S(1)}, u32[]{:S(2)}, u32[]{:S(2)}) collective-permute-start(bf16[256,1024]{1,0:T(8,128)(2,1)S(1)} %bitcast.197), channel_id=1, source_target_pairs={{0,2},{1,5},{2,0},{3,7},{4,6},{5,1},{6,4},{7,3},{8,10},{9,13},{10,... | collective-permute-start | bytes 1572872 | tf_op jit(solution)/shard_map/ppermute | solution.py:21
  209.2 7.7 %collective-permute-start.45 = (bf16[256,512]{1,0:T(8,128)(2,1)S(1)}, bf16[256,512]{1,0:T(8,128)(2,1)S(1)}, u32[]{:S(2)}, u32[]{:S(2)}) collective-permute-start(bf16[256,512]{1,0:T(8,128)(2,1)S(1)} %bitcast.203), channel_id=1, source_target_pairs={{0,4},{1,3},{2,6},{3,1},{4,0},{5,7},{6,2},{7,5},{8,12},{9,11},{10,... | collective-permute-start | bytes 786440 | tf_op jit(solution)/shard_map/ppermute | solution.py:21
  218.3 11.4 %collective-permute-start.46 = (bf16[512,1024]{1,0:T(8,128)(2,1)S(1)}, bf16[512,1024]{1,0:T(8,128)(2,1)S(1)}, u32[]{:S(2)}, u32[]{:S(2)}) collective-permute-start(bf16[512,1024]{1,0:T(8,128)(2,1)S(1)} %bitcast.193), channel_id=1, source_target_pairs={{0,1},{1,0},{2,3},{3,2},{4,5},{5,4},{6,7},{7,6},{8,9},{9,8},{10,11... | collective-permute-start | bytes 3145736 | tf_op jit(solution)/shard_map/ppermute | solution.py:21
  221.3 8.4 %collective-permute-start.47 = (bf16[512,512]{1,0:T(8,128)(2,1)S(1)}, bf16[512,512]{1,0:T(8,128)(2,1)S(1)}, u32[]{:S(2)}, u32[]{:S(2)}) collective-permute-start(bf16[512,512]{1,0:T(8,128)(2,1)S(1)} %bitcast.198), channel_id=1, source_target_pairs={{0,2},{1,5},{2,0},{3,7},{4,6},{5,1},{6,4},{7,3},{8,10},{9,13},{10,... | collective-permute-start | bytes 1572872 | tf_op jit(solution)/shard_map/ppermute | solution.py:21
  229.9 4.9 %collective-permute-start.48 = (bf16[1024,512]{1,0:T(8,128)(2,1)S(1)}, bf16[1024,512]{1,0:T(8,128)(2,1)S(1)}, u32[]{:S(2)}, u32[]{:S(2)}) collective-permute-start(bf16[1024,512]{1,0:T(8,128)(2,1)S(1)} %bitcast.194), channel_id=1, source_target_pairs={{0,1},{1,0},{2,3},{3,2},{4,5},{5,4},{6,7},{7,6},{8,9},{9,8},{10,11... | collective-permute-start | bytes 3145736 | tf_op jit(solution)/shard_map/ppermute | solution.py:21
  (49 other events, 272.4 us)

commit v6 on v5

--- a/solution.py
+++ b/solution.py
@@ -971,9 +971,12 @@
     (grad_features,) = chains.slot(grad_features)
     chains.slot()
     (pooled,) = chains.slot(pooled)
-    (pooled,) = chains.slot(sum_rows_axis(pooled) / areas[:, :1])
+    (pooled,) = chains.slot(sum_rows_axis(pooled))
+    pooled = pooled / areas[:, :1]
+    for _ in range(0):
+        chains.slot()
     while chains.running:
-        chains.slot()
+        chains.slot(held=False)
     grad_weight_in, grad_weight_mid, grad_weight_out = (
         chains.results[name] for name in ("in", "mid", "out")
     )

time: 239 us -> 232 us (0.971)
  starting transfers between devices: 79.5 us -> 74.2 us
    ppermute x43, starting transfers between devices: 46 us -> 39.6 us  [swap(): lax.ppermute(value, AXES, [(i, i ^ flips[i & 1]) for i in range(count)])]
    ppermute x2, waiting for transfers between devices: 9.09 us -> 4.31 us  [sum_rows_axis(): lax.ppermute(value, ROWS, [(i, i ^ bit) for i in range(count)])]
    ppermute x43, waiting for transfers between devices: 45.4 us -> 49.2 us  [swap(): lax.ppermute(value, AXES, [(i, i ^ flips[i & 1]) for i in range(count)])]
  transfers between devices with their start and end apart: 54 -> 54, of which waited for: 24 -> 22; matrix products, arithmetic and copies ran while one was open for 6% -> 8% of each run, Pallas kernels for 13% -> 10%
where the time goes in v6:
time: 232 us; the launch traced here: 231 us
  starting transfers between devices  74.2 us (32%)
  waiting for transfers between devices  67.6 us (29%)
  Pallas kernels  51.5 us (22%)
  other arithmetic  14.5 us (6%)
  blocking collectives  11.2 us (5%)
  local copies, waits for them, and re-layouts  8.78 us (4%)
    ppermute x43, waiting for transfers between devices, swap(): lax.ppermute(value, AXES, [(i, i ^ flips[i & 1]) for i in range(count)])  49.2 us
    pallas_call x9, Pallas kernels, call(): pl.pallas_call(kernel, out_shape=[jax.ShapeDtypeStruct(shape, kind) for s...  45.6 us
    ppermute x43, starting transfers between devices, swap(): lax.ppermute(value, AXES, [(i, i ^ flips[i & 1]) for i in range(count)])  39.6 us
    all_to_all x4, starting transfers between devices, everyone(): return lax.all_to_all(copies, AXES, 0, 0)  20.3 us
    all_to_all x1, blocking collectives, everyone_wide(): lax.all_to_all(jnp.broadcast_to(value[None], (count, *value.shape)), AXES...  11.2 us
    ppermute x2, starting transfers between devices, trade(): lax.ppermute(far, ROWS, pairs + [(b, a) for a, b in pairs])  6.77 us
    all_to_all x4, waiting for transfers between devices, everyone(): return lax.all_to_all(copies, AXES, 0, 0)  6.07 us
    pallas_call x1, Pallas kernels, assemble(): pl.pallas_call(mid_assemble, grid=(taps,), out_shape=jax.ShapeDtypeStruct...  5.89 us
  transfers between devices with their start and end apart: 54, of which 22 were waited for; matrix products, arithmetic and copies ran while one was open for 8% of the time, Pallas kernels for 10%

profile of v6, /device:TPU:1, one launch (start us, length us, event | category | flops | bytes accessed | tf_op | source)
XLA Modules:
  0.0 231.5 jit_solution(13064091920270356593)
XLA Ops:
  1.3 4.3 %shard_map.220 = (f32[256,512]{1,0:T(8,128)}, f32[128,512]{1,0:T(8,128)}, f32[128,512]{1,0:T(8,128)}, f32[32,2,640]{2,1,0:T(2,128)}, f32[2,512]{1,0:T(2,128)}, /...) custom-call(s32[1,4]{1,0:T(1,128)} %add_bitcast_fusion.refs_0_.place, ...), custom_call_target="tpu_custom_call" | custom-call | tf_op jit(solution)/shard_map/pallas_call | solution.py:156
  5.6 7.1 %all-to-all-start = ((f32[32,2,640]{2,1,0:T(2,128)}), f32[32,2,640]{2,1,0:T(2,128)S(1)}, u32[]{:S(2)}, u32[]{:S(2)}) async-start(f32[32,2,640]{2,1,0:T(2,128)} %get-tuple-element.107), calls=%async_computation | async-start | bytes 327680 | tf_op jit(solution)/shard_map/all_to_all | solution.py:32
  13.3 3.5 %collective-permute-start.1 = (f32[128,512]{1,0:T(8,128)}, f32[128,512]{1,0:T(8,128)S(1)}, u32[]{:S(2)}, u32[]{:S(2)}) collective-permute-start(f32[128,512]{1,0:T(8,128)} %get-tuple-element.109), channel_id=1, source_target_pairs={{1,2},{2,1},{5,6},{6,5},{9,10},{10,9},{13,14},{14,13},{17,18},{18,... | collective-permute-start | bytes 786440 | tf_op jit(solution)/shard_map/ppermute | solution.py:146
  16.8 4.8 %collective-permute-done.1.refs_5_ = f32[128,512]{1,0:T(8,128)S(1)} collective-permute-done((f32[128,512]{1,0:T(8,128)}, f32[128,512]{1,0:T(8,128)S(1)}, u32[]{:S(2)}, u32[]{:S(2)}) %collective-permute-start.1) | collective-permute-done | bytes 262176 | tf_op jit(solution)/shard_map/ppermute | solution.py:146
  22.4 5.5 %shard_map.221 = (bf16[2,128,512]{2,1,0:T(8,128)(2,1)}, f32[256,512]{1,0:T(8,128)}, f32[32,2,512]{2,1,0:T(2,128)}, f32[2,640]{1,0:T(2,128)}, f32[2,128]{1,0:T(2,128)}) custom-call(s32[1,4]{1,0:T(1,128)} %add_bitcast_fusion.refs_0_.place, f32[32,2,640]{2,1,0:T(2,128)} %copy-done.8, f32[2,512]{1,0:T(2,128)} %get-tuple-element.111.refs_2_.refs_4_.params, ...), custom_call_target="tpu_custom_call" | custom-call | tf_op jit(solution)/shard_map/pallas_call | solution.py:156
  27.8 5.4 %all-to-all-start.1 = ((f32[32,2,512]{2,1,0:T(2,128)}), f32[32,2,512]{2,1,0:T(2,128)S(1)}, u32[]{:S(2)}, u32[]{:S(2)}) async-start(f32[32,2,512]{2,1,0:T(2,128)} %get-tuple-element.119), calls=%async_computation.1 | async-start | bytes 262144 | tf_op jit(solution)/shard_map/all_to_all | solution.py:32
  35.6 5.8 %all-to-all-done.1.refs_2_ = f32[32,2,512]{2,1,0:T(2,128)S(1)} async-done(((f32[32,2,512]{2,1,0:T(2,128)}), f32[32,2,512]{2,1,0:T(2,128)S(1)}, u32[]{:S(2)}, u32[]{:S(2)}) %all-to-all-start.1) | async-done | bytes 131104 | tf_op jit(solution)/shard_map/all_to_all | solution.py:32
  42.1 4.2 %shard_map.222 = (bf16[256,512]{1,0:T(8,128)(2,1)}, bf16[2,128,256]{2,1,0:T(8,128)(2,1)}, bf16[2,128,256]{2,1,0:T(8,128)(2,1)}, f32[256,2048]{1,0:T(8,128)}, f32...) custom-call(s32[1,4]{1,0:T(1,128)} %add_bitcast_fusion.refs_0_.place, ...), custom_call_target="tpu_custom_call" | custom-call | tf_op jit(solution)/shard_map/pallas_call | solution.py:156
  48.5 3.5 %all-to-all-start.2 = ((f32[16,2,1024]{2,1,0:T(2,128)}), f32[16,2,1024]{2,1,0:T(2,128)S(1)}, u32[]{:S(2)}, u32[]{:S(2)}) async-start(f32[16,2,1024]{2,1,0:T(2,128)} %broadcast_in_dim.51), calls=%async_computation.2 | async-start | bytes 262144 | tf_op jit(solution)/shard_map/all_to_all | solution.py:38
  55.5 3.2 %all-to-all-done.2.refs_2_ = f32[16,2,1024]{2,1,0:T(2,128)S(1)} async-done(((f32[16,2,1024]{2,1,0:T(2,128)}), f32[16,2,1024]{2,1,0:T(2,128)S(1)}, u32[]{:S(2)}, u32[]{:S(2)}) %all-to-all-start.2) | async-done | bytes 131104 | tf_op jit(solution)/shard_map/all_to_all | solution.py:38
  58.7 1.6 collective-permute-start.5
  62.0 7.2 %shard_map.223 = (bf16[256,2048]{1,0:T(8,128)(2,1)}, f32[16,2048]{1,0:T(8,128)}, f32[256,2048]{1,0:T(8,128)}, f32[2,1024]{1,0:T(2,128)}, f32[2,1024]{1,0:T(2,128)}, /*index=5*/f32[2,2048]{1,0:T(2,128)}) custom-call(s32[1,4]{1,0:T(1,128)} %add_bitcast_fusion.refs_0_.place, f32[2,640]{1,0:T(2,128)} %get-tuple-element.118.refs_1_.sums_first, ...), custom_call_target="tpu_custom_call" | custom-call | tf_op jit(solution)/shard_map/pallas_call | solution.py:156
  72.8 11.2 %all_to_all.30.refs_4_ = f32[16,2,1024]{2,1,0:T(2,128)S(1)} all-to-all(f32[16,2,1024]{2,1,0:T(2,128)S(1)} %broadcast_in_dim.54), channel_id=1, replica_groups=mesh['img'=8,'half'=2,'low'=2] {'img','half'}, dimensions={0} | all-to-all | bytes 262144 | tf_op jit(solution)/shard_map/all_to_all | solution.py:38
  84.0 1.8 collective-permute-start.11
  87.4 6.0 %shard_map.224 = (bf16[256,1024]{1,0:T(8,128)(2,1)}, bf16[256,1024]{1,0:T(8,128)(2,1)}, f32[256,512]{1,0:T(8,128)}, bf16[2,128,256]{2,1,0:T(8,128)(2,1)}, bf16[2...) custom-call(s32[1,4]{1,0:T(1,128)} %add_bitcast_fusion.refs_0_.place, ...), custom_call_target="tpu_custom_call" | custom-call | tf_op jit(solution)/shard_map/pallas_call | solution.py:156
  94.9 2.5 %all-to-all-start.4 = ((f32[32,2,512]{2,1,0:T(2,128)}), f32[32,2,512]{2,1,0:T(2,128)S(1)}, u32[]{:S(2)}, u32[]{:S(2)}) async-start(f32[32,2,512]{2,1,0:T(2,128)} %get-tuple-element.151), calls=%async_computation.4 | async-start | bytes 262144 | tf_op jit(solution)/shard_map/all_to_all | solution.py:32
  97.7 3.2 %collective-permute-start.17 = (bf16[128,1024]{1,0:T(8,128)(2,1)}, bf16[128,1024]{1,0:T(8,128)(2,1)S(1)}, u32[]{:S(2)}, u32[]{:S(2)}) collective-permute-start(bf16[128,1024]{1,0:T(8,128)(2,1)} %get-tuple-element.156), channel_id=1, source_target_pairs={{1,2},{2,1},{5,6},{6,5},{9,10},{10,9},{13,14},{14,13},{17,18},{18,... | collective-permute-start | bytes 786440 | tf_op jit(solution)/shard_map/ppermute | solution.py:146
  104.3 3.2 %shard_map.225 = (bf16[256,1024]{1,0:T(8,128)(2,1)}, f32[256,1024]{1,0:T(8,128)}) custom-call(s32[1,4]{1,0:T(1,128)} %add_bitcast_fusion.refs_0_.place, bf16[256,512]{1,0:T(8,128)(2,1)} %get-tuple-element.128.act, bf16[256,512]{1,0:T(8,128)(2,1)} %copy-done.26, bf16[256,1024]{1,0:T(8,128)(2,1)} %get-tuple-element.148.third, bf16[256,1024]{1,0:T(8,128)(2,1)} %copy-done.16), custom_call_target="tpu_custom_call" | custom-call | tf_op jit(solution)/shard_map/pallas_call | solution.py:156
  108.4 6.2 %shard_map.226 = (f32[256,512]{1,0:T(8,128)}, bf16[256,512]{1,0:T(8,128)(2,1)}, f32[32,2,512]{2,1,0:T(2,128)}, f32[2,512]{1,0:T(2,128)}) custom-call(s32[1,4]{1,0:T(1,128)} %add_bitcast_fusion.refs_0_.place, f32[2,640]{1,0:T(2,128)} %get-tuple-element.118.refs_1_.sums_first, f32[2,512]{1,0:T(2,128)} %get-tuple-element.135.refs_2_.sums_second, ...), custom_call_target="tpu_custom_call" | custom-call | tf_op jit(solution)/shard_map/pallas_call | solution.py:156
  114.6 5.3 %all-to-all-start.5 = ((f32[32,2,512]{2,1,0:T(2,128)}), f32[32,2,512]{2,1,0:T(2,128)S(1)}, u32[]{:S(2)}, u32[]{:S(2)}) async-start(f32[32,2,512]{2,1,0:T(2,128)} %get-tuple-element.163), calls=%async_computation.5 | async-start | bytes 262144 | tf_op jit(solution)/shard_map/all_to_all | solution.py:32
  123.1 4.8 %shard_map.227 = (bf16[8,9,16,128]{3,2,1,0:T(8,128)(2,1)}, f32[8,9,16,128]{3,2,1,0:T(8,128)}) custom-call(s32[1,4]{1,0:T(1,128)} %add_bitcast_fusion.1.place, s32[2,16]{1,0:T(2,128)} %slice_convert_fusion.sizes, f32[2,640]{1,0:T(2,128)} %get-tuple-element.118.refs_1_.sums_first, f32[2,512]{1,0:T(2,128)} %get-tuple-element.135.refs_2_.sums_second, ...), custom_call_target="tpu_custom_call" | custom-call | tf_op jit(solution)/shard_map/pallas_call | solution.py:156
  130.7 4.3 %shard_map.228 = (bf16[256,512]{1,0:T(8,128)(2,1)}, f32[2,512]{1,0:T(2,128)}, bf16[512,512]{1,0:T(8,128)(2,1)}, f32[512,512]{1,0:T(8,128)}) custom-call(s32[1,4]{1,0:T(1,128)} %add_bitcast_fusion.refs_0_.place, f32[2,640]{1,0:T(2,128)} %get-tuple-element.118.refs_1_.sums_first, f32[32,2,512]{2,1,0:T(2,128)} %copy-done.13, ...), custom_call_target="tpu_custom_call" | custom-call | tf_op jit(solution)/shard_map/pallas_call | solution.py:156
  135.2 1.5 collective-permute-done.24
  136.8 2.4 %collective-permute-start.25 = (bf16[576,128]{1,0:T(8,128)(2,1)S(1)}, bf16[576,128]{1,0:T(8,128)(2,1)S(1)}, u32[]{:S(2)}, u32[]{:S(2)}) collective-permute-start(bf16[576,128]{1,0:T(8,128)(2,1)S(1)} %dynamic-slice_convert_fusion.2), channel_id=1, source_target_pairs={{0,16},{1,17},{2,18},{3,19},{4,20},{5,21},{6,22},{7,23},{8,24},{9,... | collective-permute-start | bytes 442376 | tf_op jit(solution)/shard_map/ppermute | solution.py:21
  140.7 2.1 convolution_add_fusion
  142.8 2.7 %collective-permute-done.25 = bf16[576,128]{1,0:T(8,128)(2,1)S(1)} collective-permute-done((bf16[576,128]{1,0:T(8,128)(2,1)S(1)}, bf16[576,128]{1,0:T(8,128)(2,1)S(1)}, u32[]{:S(2)}, u32[]{:S(2)}) %collective-permute-start.25) | collective-permute-done | bytes 147488 | tf_op jit(solution)/shard_map/ppermute | solution.py:21
  145.5 1.7 collective-permute-done.23
  148.7 1.6 collective-permute-start.28
  150.3 1.7 collective-permute-start.27
  152.1 2.8 %collective-permute-done.27 = bf16[64,1024]{1,0:T(8,128)(2,1)S(1)} collective-permute-done((bf16[64,1024]{1,0:T(8,128)(2,1)S(1)}, bf16[64,1024]{1,0:T(8,128)(2,1)S(1)}, u32[]{:S(2)}, u32[]{:S(2)}) %collective-permute-start.27) | collective-permute-done | bytes 131104 | tf_op jit(solution)/shard_map/ppermute | solution.py:21
  155.0 3.1 %collective-permute-done.28 = bf16[576,128]{1,0:T(8,128)(2,1)S(1)} collective-permute-done((bf16[576,128]{1,0:T(8,128)(2,1)S(1)}, bf16[576,128]{1,0:T(8,128)(2,1)S(1)}, u32[]{:S(2)}, u32[]{:S(2)}) %collective-permute-start.28) | collective-permute-done | bytes 147488 | tf_op jit(solution)/shard_map/ppermute | solution.py:21
  158.2 3.3 %collective-permute-start.31 = (bf16[1152,128]{1,0:T(8,128)(2,1)S(1)}, bf16[1152,128]{1,0:T(8,128)(2,1)S(1)}, u32[]{:S(2)}, u32[]{:S(2)}) collective-permute-start(bf16[1152,128]{1,0:T(8,128)(2,1)S(1)} %bitcast.201), channel_id=1, source_target_pairs={{0,8},{1,9},{2,10},{3,11},{4,12},{5,13},{6,14},{7,15},{8,0},{9,1},... | collective-permute-start | bytes 884744 | tf_op jit(solution)/shard_map/ppermute | solution.py:21
  162.4 9.3 %collective-permute-done.32 = bf16[128,512]{1,0:T(8,128)(2,1)S(1)} collective-permute-done((bf16[128,512]{1,0:T(8,128)(2,1)S(1)}, bf16[128,512]{1,0:T(8,128)(2,1)S(1)}, u32[]{:S(2)}, u32[]{:S(2)}) %collective-permute-start.32) | collective-permute-done | bytes 131104 | tf_op jit(solution)/shard_map/ppermute | solution.py:21
  172.5 3.4 %collective-permute-start.36 = (f32[16,2048]{1,0:T(8,128)S(1)}, f32[16,2048]{1,0:T(8,128)S(1)}, u32[]{:S(2)}, u32[]{:S(2)}) collective-permute-start(f32[16,2048]{1,0:T(8,128)S(1)} %copy-done.30), channel_id=1, source_target_pairs={{0,1},{1,0},{2,3},{3,2},{4,5},{5,4},{6,7},{7,6},{8,9},{9,8},{10,11... | collective-permute-start | bytes 393224 | tf_op jit(solution)/shard_map/ppermute | solution.py:136
  175.9 2.1 collective-permute-start.35
  178.7 4.3 %collective-permute-done.37 = f32[16,2048]{1,0:T(8,128)S(1)} collective-permute-done((f32[16,2048]{1,0:T(8,128)S(1)}, f32[16,2048]{1,0:T(8,128)S(1)}, u32[]{:S(2)}, u32[]{:S(2)}) %collective-permute-start.37) | collective-permute-done | bytes 131104 | tf_op jit(solution)/shard_map/ppermute | solution.py:136
  184.0 1.9 collective-permute-start.43
  188.0 3.7 %collective-permute-done.45 = bf16[64,1024]{1,0:T(8,128)(2,1)S(1)} collective-permute-done((bf16[64,1024]{1,0:T(8,128)(2,1)S(1)}, bf16[64,1024]{1,0:T(8,128)(2,1)S(1)}, u32[]{:S(2)}, u32[]{:S(2)}) %collective-permute-start.45) | collective-permute-done | bytes 131104 | tf_op jit(solution)/shard_map/ppermute | solution.py:21
  191.8 1.6 collective-permute-done.39
  193.5 6.7 %collective-permute-done.46 = bf16[128,1024]{1,0:T(8,128)(2,1)S(1)} collective-permute-done((bf16[128,1024]{1,0:T(8,128)(2,1)S(1)}, bf16[128,1024]{1,0:T(8,128)(2,1)S(1)}, u32[]{:S(2)}, u32[]{:S(2)}) %collective-permute-start.46) | collective-permute-done | bytes 262176 | tf_op jit(solution)/shard_map/ppermute | solution.py:21
  201.1 4.7 %collective-permute-done.40 = bf16[256,512]{1,0:T(8,128)(2,1)S(1)} collective-permute-done((bf16[256,512]{1,0:T(8,128)(2,1)S(1)}, bf16[256,512]{1,0:T(8,128)(2,1)S(1)}, u32[]{:S(2)}, u32[]{:S(2)}) %collective-permute-start.40) | collective-permute-done | bytes 262176 | tf_op jit(solution)/shard_map/ppermute | solution.py:21
  206.2 4.9 %collective-permute-done.47 = bf16[256,1024]{1,0:T(8,128)(2,1)S(1)} collective-permute-done((bf16[256,1024]{1,0:T(8,128)(2,1)S(1)}, bf16[256,1024]{1,0:T(8,128)(2,1)S(1)}, u32[]{:S(2)}, u32[]{:S(2)}) %collective-permute-start.47) | collective-permute-done | bytes 524320 | tf_op jit(solution)/shard_map/ppermute | solution.py:21
  211.3 2.0 collective-permute-start.48
  213.8 2.8 %collective-permute-done.41 = bf16[512,512]{1,0:T(8,128)(2,1)S(1)} collective-permute-done((bf16[512,512]{1,0:T(8,128)(2,1)S(1)}, bf16[512,512]{1,0:T(8,128)(2,1)S(1)}, u32[]{:S(2)}, u32[]{:S(2)}) %collective-permute-start.41) | collective-permute-done | bytes 524320 | tf_op jit(solution)/shard_map/ppermute | solution.py:21
  216.9 2.0 collective-permute-start.42
  219.8 2.6 %maximum_convert_fusion = f32[512,2048]{1,0:T(8,128)} fusion(bf16[512,1024]{1,0:T(8,128)(2,1)S(1)} %get-tuple-element.205, bf16[512,1024]{1,0:T(8,128)(2,1)S(1)} %get-tuple-element.204), kind=kLoop, calls=%fused_computation.3 | loop fusion | flops 4194304 | bytes 6291456 | tf_op jit(solution)/shard_map/convert_element_type | solution.py:901
  222.8 2.7 %bitcast_convert_fusion = f32[2048,512]{1,0:T(8,128)} fusion(bf16[2,1024,512]{2,1,0:T(8,128)(2,1)S(1)} %pad_maximum_fusion.1), kind=kLoop, calls=%fused_computation.4 | loop fusion | flops 1048576 | bytes 6291456 | tf_op jit(solution)/shard_map/convert_element_type | solution.py:939
  225.6 5.9 %shard_map.229 = f32[9,512,512]{2,1,0:T(8,128)} custom-call(s32[1,1]{1,0:T(1,128)} %bitcast.68.odd, bf16[4,16,9,16,128]{4,3,2,1,0:T(8,128)(2,1)S(1)} %bitcast.186, bf16[4,16,9,16,128]{4,3,2,1,0:T(8,128)(2,1)S(1)} %bitcast.187), custom_call_target="tpu_custom_call" | custom-call | tf_op jit(solution)/shard_map/pallas_call | solution.py:632
  (234 shorter events, 41.9 us)
Async XLA Ops:
  5.6 16.0 %all-to-all-start = ((f32[32,2,640]{2,1,0:T(2,128)}), f32[32,2,640]{2,1,0:T(2,128)S(1)}, u32[]{:S(2)}, u32[]{:S(2)}) async-start(f32[32,2,640]{2,1,0:T(2,128)} %get-tuple-element.107), calls=%async_computation | async-start | bytes 327680 | tf_op jit(solution)/shard_map/all_to_all | solution.py:32
  12.7 22.9 %collective-permute-start.3 = (f32[256,512]{1,0:T(8,128)}, f32[256,512]{1,0:T(8,128)S(1)}, u32[]{:S(2)}, u32[]{:S(2)}) collective-permute-start(f32[256,512]{1,0:T(8,128)} %get-tuple-element.112.refs_3_.refs_10_.first), channel_id=1, source_target_pairs={{0,1},{1,0},{2,3},{3,2},{4,5},{5,4},{6,7},{7,6},{8,9},{9,8},{10,11... | collective-permute-start | bytes 1572872 | tf_op jit(solution)/shard_map/ppermute | solution.py:21
  13.0 3.8 %collective-permute-start = (f32[128,512]{1,0:T(8,128)}, f32[128,512]{1,0:T(8,128)S(1)}, u32[]{:S(2)}, u32[]{:S(2)}) collective-permute-start(f32[128,512]{1,0:T(8,128)} %get-tuple-element.108), channel_id=1, source_target_pairs={{0,1},{1,0},{2,3},{3,2},{4,5},{5,4},{6,7},{7,6},{8,9},{9,8},{10,11... | collective-permute-start | bytes 786440 | tf_op jit(solution)/shard_map/ppermute | solution.py:145
  13.3 8.3 %collective-permute-start.1 = (f32[128,512]{1,0:T(8,128)}, f32[128,512]{1,0:T(8,128)S(1)}, u32[]{:S(2)}, u32[]{:S(2)}) collective-permute-start(f32[128,512]{1,0:T(8,128)} %get-tuple-element.109), channel_id=1, source_target_pairs={{1,2},{2,1},{5,6},{6,5},{9,10},{10,9},{13,14},{14,13},{17,18},{18,... | collective-permute-start | bytes 786440 | tf_op jit(solution)/shard_map/ppermute | solution.py:146
  27.8 13.6 %all-to-all-start.1 = ((f32[32,2,512]{2,1,0:T(2,128)}), f32[32,2,512]{2,1,0:T(2,128)S(1)}, u32[]{:S(2)}, u32[]{:S(2)}) async-start(f32[32,2,512]{2,1,0:T(2,128)} %get-tuple-element.119), calls=%async_computation.1 | async-start | bytes 262144 | tf_op jit(solution)/shard_map/all_to_all | solution.py:32
  46.8 14.2 %collective-permute-start.9 = (bf16[256,1024]{1,0:T(8,128)(2,1)S(1)}, bf16[256,1024]{1,0:T(8,128)(2,1)S(1)}, u32[]{:S(2)}, u32[]{:S(2)}) collective-permute-start(bf16[256,1024]{1,0:T(8,128)(2,1)S(1)} %get-tuple-element.215), channel_id=1, source_target_pairs={{0,1},{1,0},{2,3},{3,2},{4,5},{5,4},{6,7},{7,6},{8,9},{9,8},{10,11... | collective-permute-start | bytes 1572872 | tf_op jit(solution)/shard_map/ppermute | solution.py:21
  48.5 10.3 %all-to-all-start.2 = ((f32[16,2,1024]{2,1,0:T(2,128)}), f32[16,2,1024]{2,1,0:T(2,128)S(1)}, u32[]{:S(2)}, u32[]{:S(2)}) async-start(f32[16,2,1024]{2,1,0:T(2,128)} %broadcast_in_dim.51), calls=%async_computation.2 | async-start | bytes 262144 | tf_op jit(solution)/shard_map/all_to_all | solution.py:38
  52.1 8.9 %collective-permute-start.6 = (bf16[2,2,128,256]{3,2,1,0:T(8,128)(2,1)S(1)}, bf16[2,2,128,256]{3,2,1,0:T(8,128)(2,1)S(1)}, u32[]{:S(2)}, u32[]{:S(2)}) collective-permute-start(bf16[2,2,128,256]{3,2,1,0:T(8,128)(2,1)S(1)} %pad_maximum_fusion.11), channel_id=1, source_target_pairs={{0,2},{1,5},{2,0},{3,7},{4,6},{5,1},{6,4},{7,3},{8,10},{9,13},{10,... | collective-permute-start | bytes 786440 | tf_op jit(solution)/shard_map/ppermute | solution.py:21
  53.4 7.6 %collective-permute-start.8 = (bf16[256,512]{1,0:T(8,128)(2,1)S(1)}, bf16[256,512]{1,0:T(8,128)(2,1)S(1)}, u32[]{:S(2)}, u32[]{:S(2)}) collective-permute-start(bf16[256,512]{1,0:T(8,128)(2,1)S(1)} %copy-done.25), channel_id=1, source_target_pairs={{0,1},{1,0},{2,3},{3,2},{4,5},{5,4},{6,7},{7,6},{8,9},{9,8},{10,11... | collective-permute-start | bytes 786440 | tf_op jit(solution)/shard_map/ppermute | solution.py:21
  54.3 6.7 %collective-permute-start.7 = (bf16[1,2,128,256]{3,2,1,0:T(8,128)(2,1)}, bf16[1,2,128,256]{3,2,1,0:T(8,128)(2,1)S(1)}, u32[]{:S(2)}, u32[]{:S(2)}) collective-permute-start(bf16[1,2,128,256]{3,2,1,0:T(8,128)(2,1)} %bitcast.226), channel_id=1, source_target_pairs={{0,2},{1,5},{2,0},{3,7},{4,6},{5,1},{6,4},{7,3},{8,10},{9,13},{10,... | collective-permute-start | bytes 393224 | tf_op jit(solution)/shard_map/ppermute | solution.py:21
  69.3 17.5 %collective-permute-start.12 = (bf16[4,2,128,256]{3,2,1,0:T(8,128)(2,1)S(1)}, bf16[4,2,128,256]{3,2,1,0:T(8,128)(2,1)S(1)}, u32[]{:S(2)}, u32[]{:S(2)}) collective-permute-start(bf16[4,2,128,256]{3,2,1,0:T(8,128)(2,1)S(1)} %bitcast.199), channel_id=1, source_target_pairs={{0,4},{1,3},{2,6},{3,1},{4,0},{5,7},{6,2},{7,5},{8,12},{9,11},{10,... | collective-permute-start | bytes 1572872 | tf_op jit(solution)/shard_map/ppermute | solution.py:21
  84.0 2.8 %collective-permute-start.11 = (f32[16,2,1024]{2,1,0:T(2,128)S(1)}, f32[16,2,1024]{2,1,0:T(2,128)S(1)}, u32[]{:S(2)}, u32[]{:S(2)}) collective-permute-start(f32[16,2,1024]{2,1,0:T(2,128)S(1)} %all_to_all.30.refs_4_), channel_id=1, source_target_pairs={{0,1},{1,0},{2,3},{3,2},{4,5},{5,4},{6,7},{7,6},{8,9},{9,8},{10,11... | collective-permute-start | bytes 393224 | tf_op jit(solution)/shard_map/ppermute | solution.py:21
  93.4 7.6 %collective-permute-start.14 = (bf16[1,2,128,256]{3,2,1,0:T(8,128)(2,1)}, bf16[1,2,128,256]{3,2,1,0:T(8,128)(2,1)S(1)}, u32[]{:S(2)}, u32[]{:S(2)}) collective-permute-start(bf16[1,2,128,256]{3,2,1,0:T(8,128)(2,1)} %bitcast.227), channel_id=1, source_target_pairs={{0,2},{1,5},{2,0},{3,7},{4,6},{5,1},{6,4},{7,3},{8,10},{9,13},{10,... | collective-permute-start | bytes 393224 | tf_op jit(solution)/shard_map/ppermute | solution.py:21
  93.9 9.6 %collective-permute-start.13 = (bf16[256,1024]{1,0:T(8,128)(2,1)}, bf16[256,1024]{1,0:T(8,128)(2,1)S(1)}, u32[]{:S(2)}, u32[]{:S(2)}) collective-permute-start(bf16[256,1024]{1,0:T(8,128)(2,1)} %get-tuple-element.149), channel_id=1, source_target_pairs={{0,1},{1,0},{2,3},{3,2},{4,5},{5,4},{6,7},{7,6},{8,9},{9,8},{10,11... | collective-permute-start | bytes 1572872 | tf_op jit(solution)/shard_map/ppermute | solution.py:21
  94.9 12.7 %all-to-all-start.4 = ((f32[32,2,512]{2,1,0:T(2,128)}), f32[32,2,512]{2,1,0:T(2,128)S(1)}, u32[]{:S(2)}, u32[]{:S(2)}) async-start(f32[32,2,512]{2,1,0:T(2,128)} %get-tuple-element.151), calls=%async_computation.4 | async-start | bytes 262144 | tf_op jit(solution)/shard_map/all_to_all | solution.py:32
  97.4 10.2 %collective-permute-start.16 = (bf16[128,1024]{1,0:T(8,128)(2,1)}, bf16[128,1024]{1,0:T(8,128)(2,1)S(1)}, u32[]{:S(2)}, u32[]{:S(2)}) collective-permute-start(bf16[128,1024]{1,0:T(8,128)(2,1)} %get-tuple-element.155), channel_id=1, source_target_pairs={{0,1},{1,0},{2,3},{3,2},{4,5},{5,4},{6,7},{7,6},{8,9},{9,8},{10,11... | collective-permute-start | bytes 786440 | tf_op jit(solution)/shard_map/ppermute | solution.py:145
  97.7 9.8 %collective-permute-start.17 = (bf16[128,1024]{1,0:T(8,128)(2,1)}, bf16[128,1024]{1,0:T(8,128)(2,1)S(1)}, u32[]{:S(2)}, u32[]{:S(2)}) collective-permute-start(bf16[128,1024]{1,0:T(8,128)(2,1)} %get-tuple-element.156), channel_id=1, source_target_pairs={{1,2},{2,1},{5,6},{6,5},{9,10},{10,9},{13,14},{14,13},{17,18},{18,... | collective-permute-start | bytes 786440 | tf_op jit(solution)/shard_map/ppermute | solution.py:146
  102.0 5.6 %collective-permute-start.15 = (bf16[2,2,128,128]{3,2,1,0:T(8,128)(2,1)S(1)}, bf16[2,2,128,128]{3,2,1,0:T(8,128)(2,1)S(1)}, u32[]{:S(2)}, u32[]{:S(2)}) collective-permute-start(bf16[2,2,128,128]{3,2,1,0:T(8,128)(2,1)S(1)} %fusion.3), channel_id=1, source_target_pairs={{0,4},{1,3},{2,6},{3,1},{4,0},{5,7},{6,2},{7,5},{8,12},{9,11},{10,... | collective-permute-start | bytes 393224 | tf_op jit(solution)/shard_map/ppermute | solution.py:21
  102.0 12.6 %collective-permute-start.18 = (bf16[2,2,128,128]{3,2,1,0:T(8,128)(2,1)S(1)}, bf16[2,2,128,128]{3,2,1,0:T(8,128)(2,1)S(1)}, u32[]{:S(2)}, u32[]{:S(2)}) collective-permute-start(bf16[2,2,128,128]{3,2,1,0:T(8,128)(2,1)S(1)} %fusion.7), channel_id=1, source_target_pairs={{0,4},{1,3},{2,6},{3,1},{4,0},{5,7},{6,2},{7,5},{8,12},{9,11},{10,... | collective-permute-start | bytes 393224 | tf_op jit(solution)/shard_map/ppermute | solution.py:21
  114.6 13.5 %all-to-all-start.5 = ((f32[32,2,512]{2,1,0:T(2,128)}), f32[32,2,512]{2,1,0:T(2,128)S(1)}, u32[]{:S(2)}, u32[]{:S(2)}) async-start(f32[32,2,512]{2,1,0:T(2,128)} %get-tuple-element.163), calls=%async_computation.5 | async-start | bytes 262144 | tf_op jit(solution)/shard_map/all_to_all | solution.py:32
  120.8 7.3 %collective-permute-start.21 = (bf16[256,512]{1,0:T(8,128)(2,1)S(1)}, bf16[256,512]{1,0:T(8,128)(2,1)S(1)}, u32[]{:S(2)}, u32[]{:S(2)}) collective-permute-start(bf16[256,512]{1,0:T(8,128)(2,1)S(1)} %copy-done.42), channel_id=1, source_target_pairs={{0,1},{1,0},{2,3},{3,2},{4,5},{5,4},{6,7},{7,6},{8,9},{9,8},{10,11... | collective-permute-start | bytes 786440 | tf_op jit(solution)/shard_map/ppermute | solution.py:21
  128.1 8.6 %collective-permute-start.24 = (bf16[1152,128]{1,0:T(8,128)(2,1)}, bf16[1152,128]{1,0:T(8,128)(2,1)S(1)}, u32[]{:S(2)}, u32[]{:S(2)}) collective-permute-start(bf16[1152,128]{1,0:T(8,128)(2,1)} %bitcast.225), channel_id=1, source_target_pairs={{0,8},{1,9},{2,10},{3,11},{4,12},{5,13},{6,14},{7,15},{8,0},{9,1},... | collective-permute-start | bytes 884744 | tf_op jit(solution)/shard_map/ppermute | solution.py:21
  129.5 9.7 %collective-permute-start.22 = (bf16[256,1024]{1,0:T(8,128)(2,1)S(1)}, bf16[256,1024]{1,0:T(8,128)(2,1)S(1)}, u32[]{:S(2)}, u32[]{:S(2)}) collective-permute-start(bf16[256,1024]{1,0:T(8,128)(2,1)S(1)} %copy-done.41), channel_id=1, source_target_pairs={{0,2},{1,5},{2,0},{3,7},{4,6},{5,1},{6,4},{7,3},{8,10},{9,13},{10,... | collective-permute-start | bytes 1572872 | tf_op jit(solution)/shard_map/ppermute | solution.py:21
  134.9 10.5 %collective-permute-start.26 = (bf16[512,512]{1,0:T(8,128)(2,1)}, bf16[512,512]{1,0:T(8,128)(2,1)S(1)}, u32[]{:S(2)}, u32[]{:S(2)}) collective-permute-start(bf16[512,512]{1,0:T(8,128)(2,1)} %get-tuple-element.181), channel_id=1, source_target_pairs={{0,2},{1,5},{2,0},{3,7},{4,6},{5,1},{6,4},{7,3},{8,10},{9,13},{10,... | collective-permute-start | bytes 1572872 | tf_op jit(solution)/shard_map/ppermute | solution.py:21
  136.8 8.7 %collective-permute-start.25 = (bf16[576,128]{1,0:T(8,128)(2,1)S(1)}, bf16[576,128]{1,0:T(8,128)(2,1)S(1)}, u32[]{:S(2)}, u32[]{:S(2)}) collective-permute-start(bf16[576,128]{1,0:T(8,128)(2,1)S(1)} %dynamic-slice_convert_fusion.2), channel_id=1, source_target_pairs={{0,16},{1,17},{2,18},{3,19},{4,20},{5,21},{6,22},{7,23},{8,24},{9,... | collective-permute-start | bytes 442376 | tf_op jit(solution)/shard_map/ppermute | solution.py:21
  139.4 7.7 %collective-permute-start.23 = (bf16[128,1024]{1,0:T(8,128)(2,1)S(1)}, bf16[128,1024]{1,0:T(8,128)(2,1)S(1)}, u32[]{:S(2)}, u32[]{:S(2)}) collective-permute-start(bf16[128,1024]{1,0:T(8,128)(2,1)S(1)} %dynamic-slice_convert_fusion.1), channel_id=1, source_target_pairs={{0,4},{1,3},{2,6},{3,1},{4,0},{5,7},{6,2},{7,5},{8,12},{9,11},{10,... | collective-permute-start | bytes 786440 | tf_op jit(solution)/shard_map/ppermute | solution.py:21
  147.5 10.5 %collective-permute-start.29 = (bf16[256,512]{1,0:T(8,128)(2,1)S(1)}, bf16[256,512]{1,0:T(8,128)(2,1)S(1)}, u32[]{:S(2)}, u32[]{:S(2)}) collective-permute-start(bf16[256,512]{1,0:T(8,128)(2,1)S(1)} %dynamic-slice_convert_fusion), channel_id=1, source_target_pairs={{0,4},{1,3},{2,6},{3,1},{4,0},{5,7},{6,2},{7,5},{8,12},{9,11},{10,... | collective-permute-start | bytes 786440 | tf_op jit(solution)/shard_map/ppermute | solution.py:21
  148.7 9.3 %collective-permute-start.28 = (bf16[576,128]{1,0:T(8,128)(2,1)S(1)}, bf16[576,128]{1,0:T(8,128)(2,1)S(1)}, u32[]{:S(2)}, u32[]{:S(2)}) collective-permute-start(bf16[576,128]{1,0:T(8,128)(2,1)S(1)} %add_convert_fusion), channel_id=1, source_target_pairs={{0,16},{1,17},{2,18},{3,19},{4,20},{5,21},{6,22},{7,23},{8,24},{9,... | collective-permute-start | bytes 442376 | tf_op jit(solution)/shard_map/ppermute | solution.py:21
  150.3 4.7 %collective-permute-start.27 = (bf16[64,1024]{1,0:T(8,128)(2,1)S(1)}, bf16[64,1024]{1,0:T(8,128)(2,1)S(1)}, u32[]{:S(2)}, u32[]{:S(2)}) collective-permute-start(bf16[64,1024]{1,0:T(8,128)(2,1)S(1)} %dynamic-slice_convert_fusion.4), channel_id=1, source_target_pairs={{0,8},{1,9},{2,10},{3,11},{4,12},{5,13},{6,14},{7,15},{8,0},{9,1},... | collective-permute-start | bytes 393224 | tf_op jit(solution)/shard_map/ppermute | solution.py:21
  158.1 4.3 %collective-permute-start.30 = (bf16[32,1024]{1,0:T(8,128)(2,1)S(1)}, bf16[32,1024]{1,0:T(8,128)(2,1)S(1)}, u32[]{:S(2)}, u32[]{:S(2)}) collective-permute-start(bf16[32,1024]{1,0:T(8,128)(2,1)S(1)} %dynamic-slice_convert_fusion.6), channel_id=1, source_target_pairs={{0,16},{1,17},{2,18},{3,19},{4,20},{5,21},{6,22},{7,23},{8,24},{9,... | collective-permute-start | bytes 196616 | tf_op jit(solution)/shard_map/ppermute | solution.py:21
  158.2 13.4 %collective-permute-start.31 = (bf16[1152,128]{1,0:T(8,128)(2,1)S(1)}, bf16[1152,128]{1,0:T(8,128)(2,1)S(1)}, u32[]{:S(2)}, u32[]{:S(2)}) collective-permute-start(bf16[1152,128]{1,0:T(8,128)(2,1)S(1)} %bitcast.201), channel_id=1, source_target_pairs={{0,8},{1,9},{2,10},{3,11},{4,12},{5,13},{6,14},{7,15},{8,0},{9,1},... | collective-permute-start | bytes 884744 | tf_op jit(solution)/shard_map/ppermute | solution.py:21
  161.7 10.0 %collective-permute-start.32 = (bf16[128,512]{1,0:T(8,128)(2,1)S(1)}, bf16[128,512]{1,0:T(8,128)(2,1)S(1)}, u32[]{:S(2)}, u32[]{:S(2)}) collective-permute-start(bf16[128,512]{1,0:T(8,128)(2,1)S(1)} %dynamic-slice_convert_fusion.3), channel_id=1, source_target_pairs={{0,8},{1,9},{2,10},{3,11},{4,12},{5,13},{6,14},{7,15},{8,0},{9,1},... | collective-permute-start | bytes 393224 | tf_op jit(solution)/shard_map/ppermute | solution.py:21
  171.8 11.3 %collective-permute-start.34 = (bf16[2304,128]{1,0:T(8,128)(2,1)S(1)}, bf16[2304,128]{1,0:T(8,128)(2,1)S(1)}, u32[]{:S(2)}, u32[]{:S(2)}) collective-permute-start(bf16[2304,128]{1,0:T(8,128)(2,1)S(1)} %bitcast.195), channel_id=1, source_target_pairs={{0,4},{1,3},{2,6},{3,1},{4,0},{5,7},{6,2},{7,5},{8,12},{9,11},{10,... | collective-permute-start | bytes 1769480 | tf_op jit(solution)/shard_map/ppermute | solution.py:21
  171.9 11.1 %collective-permute-start.33 = (bf16[32,1024]{1,0:T(8,128)(2,1)S(1)}, bf16[32,1024]{1,0:T(8,128)(2,1)S(1)}, u32[]{:S(2)}, u32[]{:S(2)}) collective-permute-start(bf16[32,1024]{1,0:T(8,128)(2,1)S(1)} %add_convert_fusion.2), channel_id=1, source_target_pairs={{0,16},{1,17},{2,18},{3,19},{4,20},{5,21},{6,22},{7,23},{8,24},{9,... | collective-permute-start | bytes 196616 | tf_op jit(solution)/shard_map/ppermute | solution.py:21
  172.5 5.5 %collective-permute-start.36 = (f32[16,2048]{1,0:T(8,128)S(1)}, f32[16,2048]{1,0:T(8,128)S(1)}, u32[]{:S(2)}, u32[]{:S(2)}) collective-permute-start(f32[16,2048]{1,0:T(8,128)S(1)} %copy-done.30), channel_id=1, source_target_pairs={{0,1},{1,0},{2,3},{3,2},{4,5},{5,4},{6,7},{7,6},{8,9},{9,8},{10,11... | collective-permute-start | bytes 393224 | tf_op jit(solution)/shard_map/ppermute | solution.py:136
  175.9 7.1 %collective-permute-start.35 = (bf16[64,512]{1,0:T(8,128)(2,1)S(1)}, bf16[64,512]{1,0:T(8,128)(2,1)S(1)}, u32[]{:S(2)}, u32[]{:S(2)}) collective-permute-start(bf16[64,512]{1,0:T(8,128)(2,1)S(1)} %dynamic-slice_convert_fusion.5), channel_id=1, source_target_pairs={{0,16},{1,17},{2,18},{3,19},{4,20},{5,21},{6,22},{7,23},{8,24},{9,... | collective-permute-start | bytes 196616 | tf_op jit(solution)/shard_map/ppermute | solution.py:21
  178.0 5.0 %collective-permute-start.37 = (f32[16,2048]{1,0:T(8,128)S(1)}, f32[16,2048]{1,0:T(8,128)S(1)}, u32[]{:S(2)}, u32[]{:S(2)}) collective-permute-start(f32[16,2048]{1,0:T(8,128)S(1)} %add.190), channel_id=1, source_target_pairs={{0,2},{1,3},{2,0},{3,1},{4,6},{5,7},{6,4},{7,5},{8,10},{9,11},{10,... | collective-permute-start | bytes 393224 | tf_op jit(solution)/shard_map/ppermute | solution.py:136
  183.1 4.8 %collective-permute-start.38 = (bf16[64,512]{1,0:T(8,128)(2,1)S(1)}, bf16[64,512]{1,0:T(8,128)(2,1)S(1)}, u32[]{:S(2)}, u32[]{:S(2)}) collective-permute-start(bf16[64,512]{1,0:T(8,128)(2,1)S(1)} %add_convert_fusion.1), channel_id=1, source_target_pairs={{0,16},{1,17},{2,18},{3,19},{4,20},{5,21},{6,22},{7,23},{8,24},{9,... | collective-permute-start | bytes 196616 | tf_op jit(solution)/shard_map/ppermute | solution.py:21
  184.0 29.3 %collective-permute-start.43 = (bf16[4608,128]{1,0:T(8,128)(2,1)S(1)}, bf16[4608,128]{1,0:T(8,128)(2,1)S(1)}, u32[]{:S(2)}, u32[]{:S(2)}) collective-permute-start(bf16[4608,128]{1,0:T(8,128)(2,1)S(1)} %bitcast.192), channel_id=1, source_target_pairs={{0,2},{1,5},{2,0},{3,7},{4,6},{5,1},{6,4},{7,3},{8,10},{9,13},{10,... | collective-permute-start | bytes 3538952 | tf_op jit(solution)/shard_map/ppermute | solution.py:21
  186.0 5.7 %collective-permute-start.45 = (bf16[64,1024]{1,0:T(8,128)(2,1)S(1)}, bf16[64,1024]{1,0:T(8,128)(2,1)S(1)}, u32[]{:S(2)}, u32[]{:S(2)}) collective-permute-start(bf16[64,1024]{1,0:T(8,128)(2,1)S(1)} %bitcast.209), channel_id=1, source_target_pairs={{0,8},{1,9},{2,10},{3,11},{4,12},{5,13},{6,14},{7,15},{8,0},{9,1},... | collective-permute-start | bytes 393224 | tf_op jit(solution)/shard_map/ppermute | solution.py:21
  187.9 5.5 %collective-permute-start.39 = (bf16[128,512]{1,0:T(8,128)(2,1)S(1)}, bf16[128,512]{1,0:T(8,128)(2,1)S(1)}, u32[]{:S(2)}, u32[]{:S(2)}) collective-permute-start(bf16[128,512]{1,0:T(8,128)(2,1)S(1)} %bitcast.210), channel_id=1, source_target_pairs={{0,8},{1,9},{2,10},{3,11},{4,12},{5,13},{6,14},{7,15},{8,0},{9,1},... | collective-permute-start | bytes 393224 | tf_op jit(solution)/shard_map/ppermute | solution.py:21
  191.8 8.5 %collective-permute-start.46 = (bf16[128,1024]{1,0:T(8,128)(2,1)S(1)}, bf16[128,1024]{1,0:T(8,128)(2,1)S(1)}, u32[]{:S(2)}, u32[]{:S(2)}) collective-permute-start(bf16[128,1024]{1,0:T(8,128)(2,1)S(1)} %bitcast.204), channel_id=1, source_target_pairs={{0,4},{1,3},{2,6},{3,1},{4,0},{5,7},{6,2},{7,5},{8,12},{9,11},{10,... | collective-permute-start | bytes 786440 | tf_op jit(solution)/shard_map/ppermute | solution.py:21
  193.5 12.4 %collective-permute-start.40 = (bf16[256,512]{1,0:T(8,128)(2,1)S(1)}, bf16[256,512]{1,0:T(8,128)(2,1)S(1)}, u32[]{:S(2)}, u32[]{:S(2)}) collective-permute-start(bf16[256,512]{1,0:T(8,128)(2,1)S(1)} %bitcast.203), channel_id=1, source_target_pairs={{0,4},{1,3},{2,6},{3,1},{4,0},{5,7},{6,2},{7,5},{8,12},{9,11},{10,... | collective-permute-start | bytes 786440 | tf_op jit(solution)/shard_map/ppermute | solution.py:21
  200.3 10.7 %collective-permute-start.47 = (bf16[256,1024]{1,0:T(8,128)(2,1)S(1)}, bf16[256,1024]{1,0:T(8,128)(2,1)S(1)}, u32[]{:S(2)}, u32[]{:S(2)}) collective-permute-start(bf16[256,1024]{1,0:T(8,128)(2,1)S(1)} %bitcast.198), channel_id=1, source_target_pairs={{0,2},{1,5},{2,0},{3,7},{4,6},{5,1},{6,4},{7,3},{8,10},{9,13},{10,... | collective-permute-start | bytes 1572872 | tf_op jit(solution)/shard_map/ppermute | solution.py:21
  205.9 10.7 %collective-permute-start.41 = (bf16[512,512]{1,0:T(8,128)(2,1)S(1)}, bf16[512,512]{1,0:T(8,128)(2,1)S(1)}, u32[]{:S(2)}, u32[]{:S(2)}) collective-permute-start(bf16[512,512]{1,0:T(8,128)(2,1)S(1)} %bitcast.197), channel_id=1, source_target_pairs={{0,2},{1,5},{2,0},{3,7},{4,6},{5,1},{6,4},{7,3},{8,10},{9,13},{10,... | collective-permute-start | bytes 1572872 | tf_op jit(solution)/shard_map/ppermute | solution.py:21
  211.3 8.4 %collective-permute-start.48 = (bf16[512,1024]{1,0:T(8,128)(2,1)S(1)}, bf16[512,1024]{1,0:T(8,128)(2,1)S(1)}, u32[]{:S(2)}, u32[]{:S(2)}) collective-permute-start(bf16[512,1024]{1,0:T(8,128)(2,1)S(1)} %bitcast.193), channel_id=1, source_target_pairs={{0,1},{1,0},{2,3},{3,2},{4,5},{5,4},{6,7},{7,6},{8,9},{9,8},{10,11... | collective-permute-start | bytes 3145736 | tf_op jit(solution)/shard_map/ppermute | solution.py:21
  213.7 11.8 %collective-permute-start.44 = (bf16[9216,128]{1,0:T(8,128)(2,1)S(1)}, bf16[9216,128]{1,0:T(8,128)(2,1)S(1)}, u32[]{:S(2)}, u32[]{:S(2)}) collective-permute-start(bf16[9216,128]{1,0:T(8,128)(2,1)S(1)} %bitcast.185), channel_id=1, source_target_pairs={{0,1},{1,0},{2,3},{3,2},{4,5},{5,4},{6,7},{7,6},{8,9},{9,8},{10,11... | collective-permute-start | bytes 7077896 | tf_op jit(solution)/shard_map/ppermute | solution.py:21
  216.9 5.5 %collective-permute-start.42 = (bf16[1024,512]{1,0:T(8,128)(2,1)S(1)}, bf16[1024,512]{1,0:T(8,128)(2,1)S(1)}, u32[]{:S(2)}, u32[]{:S(2)}) collective-permute-start(bf16[1024,512]{1,0:T(8,128)(2,1)S(1)} %bitcast.194), channel_id=1, source_target_pairs={{0,1},{1,0},{2,3},{3,2},{4,5},{5,4},{6,7},{7,6},{8,9},{9,8},{10,11... | collective-permute-start | bytes 3145736 | tf_op jit(solution)/shard_map/ppermute | solution.py:21
  (49 other events, 274.1 us)

commit v7 on v6

--- a/solution.py
+++ b/solution.py
@@ -533,15 +533,16 @@
 
 
 def mid_assemble(odd, mine, other, total):
-    quarters, groups, _, size, lanes = mine.shape
+    quarters, groups, taps, size, lanes = mine.shape
     half = groups * size
     swapped = odd[0, 0] == 1
-    for q, turned in enumerate((0, 2, 1, 3)):
-        span = pl.ds(q * lanes, lanes)
-        even = jnp.where(swapped, other[q, :, 0], mine[q, :, 0])
-        total[0, 0:half, span] = even.astype(FULL).reshape(half, lanes)
-        uneven = jnp.where(swapped, mine[turned, :, 0], other[turned, :, 0])
-        total[0, half:, span] = uneven.astype(FULL).reshape(half, lanes)
+    for t in range(taps):
+        for q, turned in enumerate((0, 2, 1, 3)):
+            span = pl.ds(q * lanes, lanes)
+            even = jnp.where(swapped, other[q, :, t], mine[q, :, t])
+            total[t, 0:half, span] = even.astype(FULL).reshape(half, lanes)
+            uneven = jnp.where(swapped, mine[turned, :, t], other[turned, :, t])
+            total[t, half:, span] = uneven.astype(FULL).reshape(half, lanes)
 
 
 def mid_backward(
@@ -628,13 +629,14 @@
     groups, taps, size, lanes = shape
     quarters = mine.shape[0] // (groups * taps * size)
     channels = quarters * lanes
-    pieces = pl.BlockSpec((quarters, groups, 1, size, lanes), lambda t: (0, 0, t, 0, 0))
+    step = 3
+    pieces = pl.BlockSpec((quarters, groups, step, size, lanes), lambda t: (0, 0, t, 0, 0))
     return pl.pallas_call(
         mid_assemble,
-        grid=(taps,),
+        grid=(taps // step,),
         out_shape=jax.ShapeDtypeStruct((taps, channels, channels), FULL),
         in_specs=[pl.BlockSpec(memory_space=pltpu.SMEM), pieces, pieces],
-        out_specs=pl.BlockSpec((1, channels, channels), lambda t: (t, 0, 0)),
+        out_specs=pl.BlockSpec((step, channels, channels), lambda t: (t, 0, 0)),
         compiler_params=pltpu.CompilerParams(vmem_limit_bytes=48 * MIB),
     )(
         odd,

time: 232 us -> 231 us (level)
  no operation moved by 1% of the time
where the time goes in v7:
time: 231 us; the launch traced here: 230 us
  starting transfers between devices  74.2 us (32%)
  waiting for transfers between devices  67.6 us (29%)
  Pallas kernels  50.1 us (22%)
  other arithmetic  14.5 us (6%)
  blocking collectives  11.2 us (5%)
  local copies, waits for them, and re-layouts  8.78 us (4%)
    ppermute x43, waiting for transfers between devices, swap(): lax.ppermute(value, AXES, [(i, i ^ flips[i & 1]) for i in range(count)])  49.2 us
    pallas_call x9, Pallas kernels, call(): pl.pallas_call(kernel, out_shape=[jax.ShapeDtypeStruct(shape, kind) for s...  45.6 us
    ppermute x43, starting transfers between devices, swap(): lax.ppermute(value, AXES, [(i, i ^ flips[i & 1]) for i in range(count)])  39.6 us
    all_to_all x4, starting transfers between devices, everyone(): return lax.all_to_all(copies, AXES, 0, 0)  20.3 us
    all_to_all x1, blocking collectives, everyone_wide(): lax.all_to_all(jnp.broadcast_to(value[None], (count, *value.shape)), AXES...  11.2 us
    ppermute x2, starting transfers between devices, trade(): lax.ppermute(far, ROWS, pairs + [(b, a) for a, b in pairs])  6.77 us
    all_to_all x4, waiting for transfers between devices, everyone(): return lax.all_to_all(copies, AXES, 0, 0)  6.07 us
    unnamed x86, local copies, waits for them, and re-layouts  4.98 us
  transfers between devices with their start and end apart: 54, of which 22 were waited for; matrix products, arithmetic and copies ran while one was open for 8% of the time, Pallas kernels for 10%

profile of v7, /device:TPU:1, one launch (start us, length us, event | category | flops | bytes accessed | tf_op | source)
XLA Modules:
  0.0 230.1 jit_solution(162051327663464732)
XLA Ops:
  1.3 4.3 %shard_map.220 = (f32[256,512]{1,0:T(8,128)}, f32[128,512]{1,0:T(8,128)}, f32[128,512]{1,0:T(8,128)}, f32[32,2,640]{2,1,0:T(2,128)}, f32[2,512]{1,0:T(2,128)}, /...) custom-call(s32[1,4]{1,0:T(1,128)} %add_bitcast_fusion.refs_0_.place, ...), custom_call_target="tpu_custom_call" | custom-call | tf_op jit(solution)/shard_map/pallas_call | solution.py:156
  5.6 7.1 %all-to-all-start = ((f32[32,2,640]{2,1,0:T(2,128)}), f32[32,2,640]{2,1,0:T(2,128)S(1)}, u32[]{:S(2)}, u32[]{:S(2)}) async-start(f32[32,2,640]{2,1,0:T(2,128)} %get-tuple-element.107), calls=%async_computation | async-start | bytes 327680 | tf_op jit(solution)/shard_map/all_to_all | solution.py:32
  13.3 3.5 %collective-permute-start.1 = (f32[128,512]{1,0:T(8,128)}, f32[128,512]{1,0:T(8,128)S(1)}, u32[]{:S(2)}, u32[]{:S(2)}) collective-permute-start(f32[128,512]{1,0:T(8,128)} %get-tuple-element.109), channel_id=1, source_target_pairs={{1,2},{2,1},{5,6},{6,5},{9,10},{10,9},{13,14},{14,13},{17,18},{18,... | collective-permute-start | bytes 786440 | tf_op jit(solution)/shard_map/ppermute | solution.py:146
  16.8 4.8 %collective-permute-done.1.refs_5_ = f32[128,512]{1,0:T(8,128)S(1)} collective-permute-done((f32[128,512]{1,0:T(8,128)}, f32[128,512]{1,0:T(8,128)S(1)}, u32[]{:S(2)}, u32[]{:S(2)}) %collective-permute-start.1) | collective-permute-done | bytes 262176 | tf_op jit(solution)/shard_map/ppermute | solution.py:146
  22.4 5.5 %shard_map.221 = (bf16[2,128,512]{2,1,0:T(8,128)(2,1)}, f32[256,512]{1,0:T(8,128)}, f32[32,2,512]{2,1,0:T(2,128)}, f32[2,640]{1,0:T(2,128)}, f32[2,128]{1,0:T(2,128)}) custom-call(s32[1,4]{1,0:T(1,128)} %add_bitcast_fusion.refs_0_.place, f32[32,2,640]{2,1,0:T(2,128)} %copy-done.8, f32[2,512]{1,0:T(2,128)} %get-tuple-element.111.refs_2_.refs_4_.params, ...), custom_call_target="tpu_custom_call" | custom-call | tf_op jit(solution)/shard_map/pallas_call | solution.py:156
  27.8 5.4 %all-to-all-start.1 = ((f32[32,2,512]{2,1,0:T(2,128)}), f32[32,2,512]{2,1,0:T(2,128)S(1)}, u32[]{:S(2)}, u32[]{:S(2)}) async-start(f32[32,2,512]{2,1,0:T(2,128)} %get-tuple-element.119), calls=%async_computation.1 | async-start | bytes 262144 | tf_op jit(solution)/shard_map/all_to_all | solution.py:32
  35.6 5.8 %all-to-all-done.1.refs_2_ = f32[32,2,512]{2,1,0:T(2,128)S(1)} async-done(((f32[32,2,512]{2,1,0:T(2,128)}), f32[32,2,512]{2,1,0:T(2,128)S(1)}, u32[]{:S(2)}, u32[]{:S(2)}) %all-to-all-start.1) | async-done | bytes 131104 | tf_op jit(solution)/shard_map/all_to_all | solution.py:32
  42.1 4.2 %shard_map.222 = (bf16[256,512]{1,0:T(8,128)(2,1)}, bf16[2,128,256]{2,1,0:T(8,128)(2,1)}, bf16[2,128,256]{2,1,0:T(8,128)(2,1)}, f32[256,2048]{1,0:T(8,128)}, f32...) custom-call(s32[1,4]{1,0:T(1,128)} %add_bitcast_fusion.refs_0_.place, ...), custom_call_target="tpu_custom_call" | custom-call | tf_op jit(solution)/shard_map/pallas_call | solution.py:156
  48.5 3.5 %all-to-all-start.2 = ((f32[16,2,1024]{2,1,0:T(2,128)}), f32[16,2,1024]{2,1,0:T(2,128)S(1)}, u32[]{:S(2)}, u32[]{:S(2)}) async-start(f32[16,2,1024]{2,1,0:T(2,128)} %broadcast_in_dim.51), calls=%async_computation.2 | async-start | bytes 262144 | tf_op jit(solution)/shard_map/all_to_all | solution.py:38
  55.5 3.2 %all-to-all-done.2.refs_2_ = f32[16,2,1024]{2,1,0:T(2,128)S(1)} async-done(((f32[16,2,1024]{2,1,0:T(2,128)}), f32[16,2,1024]{2,1,0:T(2,128)S(1)}, u32[]{:S(2)}, u32[]{:S(2)}) %all-to-all-start.2) | async-done | bytes 131104 | tf_op jit(solution)/shard_map/all_to_all | solution.py:38
  58.7 1.6 collective-permute-start.5
  62.0 7.2 %shard_map.223 = (bf16[256,2048]{1,0:T(8,128)(2,1)}, f32[16,2048]{1,0:T(8,128)}, f32[256,2048]{1,0:T(8,128)}, f32[2,1024]{1,0:T(2,128)}, f32[2,1024]{1,0:T(2,128)}, /*index=5*/f32[2,2048]{1,0:T(2,128)}) custom-call(s32[1,4]{1,0:T(1,128)} %add_bitcast_fusion.refs_0_.place, f32[2,640]{1,0:T(2,128)} %get-tuple-element.118.refs_1_.sums_first, ...), custom_call_target="tpu_custom_call" | custom-call | tf_op jit(solution)/shard_map/pallas_call | solution.py:156
  72.8 11.2 %all_to_all.30.refs_4_ = f32[16,2,1024]{2,1,0:T(2,128)S(1)} all-to-all(f32[16,2,1024]{2,1,0:T(2,128)S(1)} %broadcast_in_dim.54), channel_id=1, replica_groups=mesh['img'=8,'half'=2,'low'=2] {'img','half'}, dimensions={0} | all-to-all | bytes 262144 | tf_op jit(solution)/shard_map/all_to_all | solution.py:38
  84.0 1.8 collective-permute-start.11
  87.4 6.0 %shard_map.224 = (bf16[256,1024]{1,0:T(8,128)(2,1)}, bf16[256,1024]{1,0:T(8,128)(2,1)}, f32[256,512]{1,0:T(8,128)}, bf16[2,128,256]{2,1,0:T(8,128)(2,1)}, bf16[2...) custom-call(s32[1,4]{1,0:T(1,128)} %add_bitcast_fusion.refs_0_.place, ...), custom_call_target="tpu_custom_call" | custom-call | tf_op jit(solution)/shard_map/pallas_call | solution.py:156
  94.9 2.5 %all-to-all-start.4 = ((f32[32,2,512]{2,1,0:T(2,128)}), f32[32,2,512]{2,1,0:T(2,128)S(1)}, u32[]{:S(2)}, u32[]{:S(2)}) async-start(f32[32,2,512]{2,1,0:T(2,128)} %get-tuple-element.151), calls=%async_computation.4 | async-start | bytes 262144 | tf_op jit(solution)/shard_map/all_to_all | solution.py:32
  97.7 3.2 %collective-permute-start.17 = (bf16[128,1024]{1,0:T(8,128)(2,1)}, bf16[128,1024]{1,0:T(8,128)(2,1)S(1)}, u32[]{:S(2)}, u32[]{:S(2)}) collective-permute-start(bf16[128,1024]{1,0:T(8,128)(2,1)} %get-tuple-element.156), channel_id=1, source_target_pairs={{1,2},{2,1},{5,6},{6,5},{9,10},{10,9},{13,14},{14,13},{17,18},{18,... | collective-permute-start | bytes 786440 | tf_op jit(solution)/shard_map/ppermute | solution.py:146
  104.3 3.2 %shard_map.225 = (bf16[256,1024]{1,0:T(8,128)(2,1)}, f32[256,1024]{1,0:T(8,128)}) custom-call(s32[1,4]{1,0:T(1,128)} %add_bitcast_fusion.refs_0_.place, bf16[256,512]{1,0:T(8,128)(2,1)} %get-tuple-element.128.act, bf16[256,512]{1,0:T(8,128)(2,1)} %copy-done.26, bf16[256,1024]{1,0:T(8,128)(2,1)} %get-tuple-element.148.third, bf16[256,1024]{1,0:T(8,128)(2,1)} %copy-done.16), custom_call_target="tpu_custom_call" | custom-call | tf_op jit(solution)/shard_map/pallas_call | solution.py:156
  108.4 6.2 %shard_map.226 = (f32[256,512]{1,0:T(8,128)}, bf16[256,512]{1,0:T(8,128)(2,1)}, f32[32,2,512]{2,1,0:T(2,128)}, f32[2,512]{1,0:T(2,128)}) custom-call(s32[1,4]{1,0:T(1,128)} %add_bitcast_fusion.refs_0_.place, f32[2,640]{1,0:T(2,128)} %get-tuple-element.118.refs_1_.sums_first, f32[2,512]{1,0:T(2,128)} %get-tuple-element.135.refs_2_.sums_second, ...), custom_call_target="tpu_custom_call" | custom-call | tf_op jit(solution)/shard_map/pallas_call | solution.py:156
  114.6 5.3 %all-to-all-start.5 = ((f32[32,2,512]{2,1,0:T(2,128)}), f32[32,2,512]{2,1,0:T(2,128)S(1)}, u32[]{:S(2)}, u32[]{:S(2)}) async-start(f32[32,2,512]{2,1,0:T(2,128)} %get-tuple-element.163), calls=%async_computation.5 | async-start | bytes 262144 | tf_op jit(solution)/shard_map/all_to_all | solution.py:32
  123.1 4.8 %shard_map.227 = (bf16[8,9,16,128]{3,2,1,0:T(8,128)(2,1)}, f32[8,9,16,128]{3,2,1,0:T(8,128)}) custom-call(s32[1,4]{1,0:T(1,128)} %add_bitcast_fusion.1.place, s32[2,16]{1,0:T(2,128)} %slice_convert_fusion.sizes, f32[2,640]{1,0:T(2,128)} %get-tuple-element.118.refs_1_.sums_first, f32[2,512]{1,0:T(2,128)} %get-tuple-element.135.refs_2_.sums_second, ...), custom_call_target="tpu_custom_call" | custom-call | tf_op jit(solution)/shard_map/pallas_call | solution.py:156
  130.7 4.3 %shard_map.228 = (bf16[256,512]{1,0:T(8,128)(2,1)}, f32[2,512]{1,0:T(2,128)}, bf16[512,512]{1,0:T(8,128)(2,1)}, f32[512,512]{1,0:T(8,128)}) custom-call(s32[1,4]{1,0:T(1,128)} %add_bitcast_fusion.refs_0_.place, f32[2,640]{1,0:T(2,128)} %get-tuple-element.118.refs_1_.sums_first, f32[32,2,512]{2,1,0:T(2,128)} %copy-done.13, ...), custom_call_target="tpu_custom_call" | custom-call | tf_op jit(solution)/shard_map/pallas_call | solution.py:156
  135.2 1.5 collective-permute-done.24
  136.8 2.4 %collective-permute-start.25 = (bf16[576,128]{1,0:T(8,128)(2,1)S(1)}, bf16[576,128]{1,0:T(8,128)(2,1)S(1)}, u32[]{:S(2)}, u32[]{:S(2)}) collective-permute-start(bf16[576,128]{1,0:T(8,128)(2,1)S(1)} %dynamic-slice_convert_fusion.2), channel_id=1, source_target_pairs={{0,16},{1,17},{2,18},{3,19},{4,20},{5,21},{6,22},{7,23},{8,24},{9,... | collective-permute-start | bytes 442376 | tf_op jit(solution)/shard_map/ppermute | solution.py:21
  140.7 2.1 convolution_add_fusion
  142.8 2.7 %collective-permute-done.25 = bf16[576,128]{1,0:T(8,128)(2,1)S(1)} collective-permute-done((bf16[576,128]{1,0:T(8,128)(2,1)S(1)}, bf16[576,128]{1,0:T(8,128)(2,1)S(1)}, u32[]{:S(2)}, u32[]{:S(2)}) %collective-permute-start.25) | collective-permute-done | bytes 147488 | tf_op jit(solution)/shard_map/ppermute | solution.py:21
  145.5 1.7 collective-permute-done.23
  148.7 1.6 collective-permute-start.28
  150.3 1.7 collective-permute-start.27
  152.1 2.8 %collective-permute-done.27 = bf16[64,1024]{1,0:T(8,128)(2,1)S(1)} collective-permute-done((bf16[64,1024]{1,0:T(8,128)(2,1)S(1)}, bf16[64,1024]{1,0:T(8,128)(2,1)S(1)}, u32[]{:S(2)}, u32[]{:S(2)}) %collective-permute-start.27) | collective-permute-done | bytes 131104 | tf_op jit(solution)/shard_map/ppermute | solution.py:21
  155.0 3.1 %collective-permute-done.28 = bf16[576,128]{1,0:T(8,128)(2,1)S(1)} collective-permute-done((bf16[576,128]{1,0:T(8,128)(2,1)S(1)}, bf16[576,128]{1,0:T(8,128)(2,1)S(1)}, u32[]{:S(2)}, u32[]{:S(2)}) %collective-permute-start.28) | collective-permute-done | bytes 147488 | tf_op jit(solution)/shard_map/ppermute | solution.py:21
  158.2 3.3 %collective-permute-start.31 = (bf16[1152,128]{1,0:T(8,128)(2,1)S(1)}, bf16[1152,128]{1,0:T(8,128)(2,1)S(1)}, u32[]{:S(2)}, u32[]{:S(2)}) collective-permute-start(bf16[1152,128]{1,0:T(8,128)(2,1)S(1)} %bitcast.201), channel_id=1, source_target_pairs={{0,8},{1,9},{2,10},{3,11},{4,12},{5,13},{6,14},{7,15},{8,0},{9,1},... | collective-permute-start | bytes 884744 | tf_op jit(solution)/shard_map/ppermute | solution.py:21
  162.4 9.3 %collective-permute-done.32 = bf16[128,512]{1,0:T(8,128)(2,1)S(1)} collective-permute-done((bf16[128,512]{1,0:T(8,128)(2,1)S(1)}, bf16[128,512]{1,0:T(8,128)(2,1)S(1)}, u32[]{:S(2)}, u32[]{:S(2)}) %collective-permute-start.32) | collective-permute-done | bytes 131104 | tf_op jit(solution)/shard_map/ppermute | solution.py:21
  172.5 3.4 %collective-permute-start.36 = (f32[16,2048]{1,0:T(8,128)S(1)}, f32[16,2048]{1,0:T(8,128)S(1)}, u32[]{:S(2)}, u32[]{:S(2)}) collective-permute-start(f32[16,2048]{1,0:T(8,128)S(1)} %copy-done.30), channel_id=1, source_target_pairs={{0,1},{1,0},{2,3},{3,2},{4,5},{5,4},{6,7},{7,6},{8,9},{9,8},{10,11... | collective-permute-start | bytes 393224 | tf_op jit(solution)/shard_map/ppermute | solution.py:136
  175.9 2.1 collective-permute-start.35
  178.7 4.3 %collective-permute-done.37 = f32[16,2048]{1,0:T(8,128)S(1)} collective-permute-done((f32[16,2048]{1,0:T(8,128)S(1)}, f32[16,2048]{1,0:T(8,128)S(1)}, u32[]{:S(2)}, u32[]{:S(2)}) %collective-permute-start.37) | collective-permute-done | bytes 131104 | tf_op jit(solution)/shard_map/ppermute | solution.py:136
  184.0 1.9 collective-permute-start.43
  188.0 3.7 %collective-permute-done.45 = bf16[64,1024]{1,0:T(8,128)(2,1)S(1)} collective-permute-done((bf16[64,1024]{1,0:T(8,128)(2,1)S(1)}, bf16[64,1024]{1,0:T(8,128)(2,1)S(1)}, u32[]{:S(2)}, u32[]{:S(2)}) %collective-permute-start.45) | collective-permute-done | bytes 131104 | tf_op jit(solution)/shard_map/ppermute | solution.py:21
  191.8 1.6 collective-permute-done.39
  193.5 6.7 %collective-permute-done.46 = bf16[128,1024]{1,0:T(8,128)(2,1)S(1)} collective-permute-done((bf16[128,1024]{1,0:T(8,128)(2,1)S(1)}, bf16[128,1024]{1,0:T(8,128)(2,1)S(1)}, u32[]{:S(2)}, u32[]{:S(2)}) %collective-permute-start.46) | collective-permute-done | bytes 262176 | tf_op jit(solution)/shard_map/ppermute | solution.py:21
  201.1 4.7 %collective-permute-done.40 = bf16[256,512]{1,0:T(8,128)(2,1)S(1)} collective-permute-done((bf16[256,512]{1,0:T(8,128)(2,1)S(1)}, bf16[256,512]{1,0:T(8,128)(2,1)S(1)}, u32[]{:S(2)}, u32[]{:S(2)}) %collective-permute-start.40) | collective-permute-done | bytes 262176 | tf_op jit(solution)/shard_map/ppermute | solution.py:21
  206.2 4.9 %collective-permute-done.47 = bf16[256,1024]{1,0:T(8,128)(2,1)S(1)} collective-permute-done((bf16[256,1024]{1,0:T(8,128)(2,1)S(1)}, bf16[256,1024]{1,0:T(8,128)(2,1)S(1)}, u32[]{:S(2)}, u32[]{:S(2)}) %collective-permute-start.47) | collective-permute-done | bytes 524320 | tf_op jit(solution)/shard_map/ppermute | solution.py:21
  211.3 2.0 collective-permute-start.48
  213.8 2.8 %collective-permute-done.41 = bf16[512,512]{1,0:T(8,128)(2,1)S(1)} collective-permute-done((bf16[512,512]{1,0:T(8,128)(2,1)S(1)}, bf16[512,512]{1,0:T(8,128)(2,1)S(1)}, u32[]{:S(2)}, u32[]{:S(2)}) %collective-permute-start.41) | collective-permute-done | bytes 524320 | tf_op jit(solution)/shard_map/ppermute | solution.py:21
  216.9 2.0 collective-permute-start.42
  219.8 2.6 %maximum_convert_fusion = f32[512,2048]{1,0:T(8,128)} fusion(bf16[512,1024]{1,0:T(8,128)(2,1)S(1)} %get-tuple-element.205, bf16[512,1024]{1,0:T(8,128)(2,1)S(1)} %get-tuple-element.204), kind=kLoop, calls=%fused_computation.3 | loop fusion | flops 4194304 | bytes 6291456 | tf_op jit(solution)/shard_map/convert_element_type | solution.py:903
  222.8 2.7 %bitcast_convert_fusion = f32[2048,512]{1,0:T(8,128)} fusion(bf16[2,1024,512]{2,1,0:T(8,128)(2,1)S(1)} %pad_maximum_fusion.1), kind=kLoop, calls=%fused_computation.4 | loop fusion | flops 1048576 | bytes 6291456 | tf_op jit(solution)/shard_map/convert_element_type | solution.py:941
  225.6 4.5 %shard_map.229 = f32[9,512,512]{2,1,0:T(8,128)} custom-call(s32[1,1]{1,0:T(1,128)} %bitcast.68.odd, bf16[4,16,9,16,128]{4,3,2,1,0:T(8,128)(2,1)S(1)} %bitcast.186, bf16[4,16,9,16,128]{4,3,2,1,0:T(8,128)(2,1)S(1)} %bitcast.187), custom_call_target="tpu_custom_call" | custom-call | tf_op jit(solution)/shard_map/pallas_call | solution.py:634
  (234 shorter events, 41.9 us)
Async XLA Ops:
  5.6 16.0 %all-to-all-start = ((f32[32,2,640]{2,1,0:T(2,128)}), f32[32,2,640]{2,1,0:T(2,128)S(1)}, u32[]{:S(2)}, u32[]{:S(2)}) async-start(f32[32,2,640]{2,1,0:T(2,128)} %get-tuple-element.107), calls=%async_computation | async-start | bytes 327680 | tf_op jit(solution)/shard_map/all_to_all | solution.py:32
  12.7 22.9 %collective-permute-start.3 = (f32[256,512]{1,0:T(8,128)}, f32[256,512]{1,0:T(8,128)S(1)}, u32[]{:S(2)}, u32[]{:S(2)}) collective-permute-start(f32[256,512]{1,0:T(8,128)} %get-tuple-element.112.refs_3_.refs_10_.first), channel_id=1, source_target_pairs={{0,1},{1,0},{2,3},{3,2},{4,5},{5,4},{6,7},{7,6},{8,9},{9,8},{10,11... | collective-permute-start | bytes 1572872 | tf_op jit(solution)/shard_map/ppermute | solution.py:21
  13.0 3.8 %collective-permute-start = (f32[128,512]{1,0:T(8,128)}, f32[128,512]{1,0:T(8,128)S(1)}, u32[]{:S(2)}, u32[]{:S(2)}) collective-permute-start(f32[128,512]{1,0:T(8,128)} %get-tuple-element.108), channel_id=1, source_target_pairs={{0,1},{1,0},{2,3},{3,2},{4,5},{5,4},{6,7},{7,6},{8,9},{9,8},{10,11... | collective-permute-start | bytes 786440 | tf_op jit(solution)/shard_map/ppermute | solution.py:145
  13.3 8.3 %collective-permute-start.1 = (f32[128,512]{1,0:T(8,128)}, f32[128,512]{1,0:T(8,128)S(1)}, u32[]{:S(2)}, u32[]{:S(2)}) collective-permute-start(f32[128,512]{1,0:T(8,128)} %get-tuple-element.109), channel_id=1, source_target_pairs={{1,2},{2,1},{5,6},{6,5},{9,10},{10,9},{13,14},{14,13},{17,18},{18,... | collective-permute-start | bytes 786440 | tf_op jit(solution)/shard_map/ppermute | solution.py:146
  27.8 13.6 %all-to-all-start.1 = ((f32[32,2,512]{2,1,0:T(2,128)}), f32[32,2,512]{2,1,0:T(2,128)S(1)}, u32[]{:S(2)}, u32[]{:S(2)}) async-start(f32[32,2,512]{2,1,0:T(2,128)} %get-tuple-element.119), calls=%async_computation.1 | async-start | bytes 262144 | tf_op jit(solution)/shard_map/all_to_all | solution.py:32
  46.8 14.2 %collective-permute-start.9 = (bf16[256,1024]{1,0:T(8,128)(2,1)S(1)}, bf16[256,1024]{1,0:T(8,128)(2,1)S(1)}, u32[]{:S(2)}, u32[]{:S(2)}) collective-permute-start(bf16[256,1024]{1,0:T(8,128)(2,1)S(1)} %get-tuple-element.215), channel_id=1, source_target_pairs={{0,1},{1,0},{2,3},{3,2},{4,5},{5,4},{6,7},{7,6},{8,9},{9,8},{10,11... | collective-permute-start | bytes 1572872 | tf_op jit(solution)/shard_map/ppermute | solution.py:21
  48.5 10.3 %all-to-all-start.2 = ((f32[16,2,1024]{2,1,0:T(2,128)}), f32[16,2,1024]{2,1,0:T(2,128)S(1)}, u32[]{:S(2)}, u32[]{:S(2)}) async-start(f32[16,2,1024]{2,1,0:T(2,128)} %broadcast_in_dim.51), calls=%async_computation.2 | async-start | bytes 262144 | tf_op jit(solution)/shard_map/all_to_all | solution.py:38
  52.1 8.9 %collective-permute-start.6 = (bf16[2,2,128,256]{3,2,1,0:T(8,128)(2,1)S(1)}, bf16[2,2,128,256]{3,2,1,0:T(8,128)(2,1)S(1)}, u32[]{:S(2)}, u32[]{:S(2)}) collective-permute-start(bf16[2,2,128,256]{3,2,1,0:T(8,128)(2,1)S(1)} %pad_maximum_fusion.11), channel_id=1, source_target_pairs={{0,2},{1,5},{2,0},{3,7},{4,6},{5,1},{6,4},{7,3},{8,10},{9,13},{10,... | collective-permute-start | bytes 786440 | tf_op jit(solution)/shard_map/ppermute | solution.py:21
  53.4 7.6 %collective-permute-start.8 = (bf16[256,512]{1,0:T(8,128)(2,1)S(1)}, bf16[256,512]{1,0:T(8,128)(2,1)S(1)}, u32[]{:S(2)}, u32[]{:S(2)}) collective-permute-start(bf16[256,512]{1,0:T(8,128)(2,1)S(1)} %copy-done.25), channel_id=1, source_target_pairs={{0,1},{1,0},{2,3},{3,2},{4,5},{5,4},{6,7},{7,6},{8,9},{9,8},{10,11... | collective-permute-start | bytes 786440 | tf_op jit(solution)/shard_map/ppermute | solution.py:21
  54.3 6.7 %collective-permute-start.7 = (bf16[1,2,128,256]{3,2,1,0:T(8,128)(2,1)}, bf16[1,2,128,256]{3,2,1,0:T(8,128)(2,1)S(1)}, u32[]{:S(2)}, u32[]{:S(2)}) collective-permute-start(bf16[1,2,128,256]{3,2,1,0:T(8,128)(2,1)} %bitcast.226), channel_id=1, source_target_pairs={{0,2},{1,5},{2,0},{3,7},{4,6},{5,1},{6,4},{7,3},{8,10},{9,13},{10,... | collective-permute-start | bytes 393224 | tf_op jit(solution)/shard_map/ppermute | solution.py:21
  69.3 17.5 %collective-permute-start.12 = (bf16[4,2,128,256]{3,2,1,0:T(8,128)(2,1)S(1)}, bf16[4,2,128,256]{3,2,1,0:T(8,128)(2,1)S(1)}, u32[]{:S(2)}, u32[]{:S(2)}) collective-permute-start(bf16[4,2,128,256]{3,2,1,0:T(8,128)(2,1)S(1)} %bitcast.199), channel_id=1, source_target_pairs={{0,4},{1,3},{2,6},{3,1},{4,0},{5,7},{6,2},{7,5},{8,12},{9,11},{10,... | collective-permute-start | bytes 1572872 | tf_op jit(solution)/shard_map/ppermute | solution.py:21
  84.0 2.8 %collective-permute-start.11 = (f32[16,2,1024]{2,1,0:T(2,128)S(1)}, f32[16,2,1024]{2,1,0:T(2,128)S(1)}, u32[]{:S(2)}, u32[]{:S(2)}) collective-permute-start(f32[16,2,1024]{2,1,0:T(2,128)S(1)} %all_to_all.30.refs_4_), channel_id=1, source_target_pairs={{0,1},{1,0},{2,3},{3,2},{4,5},{5,4},{6,7},{7,6},{8,9},{9,8},{10,11... | collective-permute-start | bytes 393224 | tf_op jit(solution)/shard_map/ppermute | solution.py:21
  93.4 7.6 %collective-permute-start.14 = (bf16[1,2,128,256]{3,2,1,0:T(8,128)(2,1)}, bf16[1,2,128,256]{3,2,1,0:T(8,128)(2,1)S(1)}, u32[]{:S(2)}, u32[]{:S(2)}) collective-permute-start(bf16[1,2,128,256]{3,2,1,0:T(8,128)(2,1)} %bitcast.227), channel_id=1, source_target_pairs={{0,2},{1,5},{2,0},{3,7},{4,6},{5,1},{6,4},{7,3},{8,10},{9,13},{10,... | collective-permute-start | bytes 393224 | tf_op jit(solution)/shard_map/ppermute | solution.py:21
  93.9 9.6 %collective-permute-start.13 = (bf16[256,1024]{1,0:T(8,128)(2,1)}, bf16[256,1024]{1,0:T(8,128)(2,1)S(1)}, u32[]{:S(2)}, u32[]{:S(2)}) collective-permute-start(bf16[256,1024]{1,0:T(8,128)(2,1)} %get-tuple-element.149), channel_id=1, source_target_pairs={{0,1},{1,0},{2,3},{3,2},{4,5},{5,4},{6,7},{7,6},{8,9},{9,8},{10,11... | collective-permute-start | bytes 1572872 | tf_op jit(solution)/shard_map/ppermute | solution.py:21
  94.9 12.7 %all-to-all-start.4 = ((f32[32,2,512]{2,1,0:T(2,128)}), f32[32,2,512]{2,1,0:T(2,128)S(1)}, u32[]{:S(2)}, u32[]{:S(2)}) async-start(f32[32,2,512]{2,1,0:T(2,128)} %get-tuple-element.151), calls=%async_computation.4 | async-start | bytes 262144 | tf_op jit(solution)/shard_map/all_to_all | solution.py:32
  97.4 10.2 %collective-permute-start.16 = (bf16[128,1024]{1,0:T(8,128)(2,1)}, bf16[128,1024]{1,0:T(8,128)(2,1)S(1)}, u32[]{:S(2)}, u32[]{:S(2)}) collective-permute-start(bf16[128,1024]{1,0:T(8,128)(2,1)} %get-tuple-element.155), channel_id=1, source_target_pairs={{0,1},{1,0},{2,3},{3,2},{4,5},{5,4},{6,7},{7,6},{8,9},{9,8},{10,11... | collective-permute-start | bytes 786440 | tf_op jit(solution)/shard_map/ppermute | solution.py:145
  97.7 9.8 %collective-permute-start.17 = (bf16[128,1024]{1,0:T(8,128)(2,1)}, bf16[128,1024]{1,0:T(8,128)(2,1)S(1)}, u32[]{:S(2)}, u32[]{:S(2)}) collective-permute-start(bf16[128,1024]{1,0:T(8,128)(2,1)} %get-tuple-element.156), channel_id=1, source_target_pairs={{1,2},{2,1},{5,6},{6,5},{9,10},{10,9},{13,14},{14,13},{17,18},{18,... | collective-permute-start | bytes 786440 | tf_op jit(solution)/shard_map/ppermute | solution.py:146
  102.0 5.6 %collective-permute-start.15 = (bf16[2,2,128,128]{3,2,1,0:T(8,128)(2,1)S(1)}, bf16[2,2,128,128]{3,2,1,0:T(8,128)(2,1)S(1)}, u32[]{:S(2)}, u32[]{:S(2)}) collective-permute-start(bf16[2,2,128,128]{3,2,1,0:T(8,128)(2,1)S(1)} %fusion.3), channel_id=1, source_target_pairs={{0,4},{1,3},{2,6},{3,1},{4,0},{5,7},{6,2},{7,5},{8,12},{9,11},{10,... | collective-permute-start | bytes 393224 | tf_op jit(solution)/shard_map/ppermute | solution.py:21
  102.0 12.6 %collective-permute-start.18 = (bf16[2,2,128,128]{3,2,1,0:T(8,128)(2,1)S(1)}, bf16[2,2,128,128]{3,2,1,0:T(8,128)(2,1)S(1)}, u32[]{:S(2)}, u32[]{:S(2)}) collective-permute-start(bf16[2,2,128,128]{3,2,1,0:T(8,128)(2,1)S(1)} %fusion.7), channel_id=1, source_target_pairs={{0,4},{1,3},{2,6},{3,1},{4,0},{5,7},{6,2},{7,5},{8,12},{9,11},{10,... | collective-permute-start | bytes 393224 | tf_op jit(solution)/shard_map/ppermute | solution.py:21
  114.6 13.5 %all-to-all-start.5 = ((f32[32,2,512]{2,1,0:T(2,128)}), f32[32,2,512]{2,1,0:T(2,128)S(1)}, u32[]{:S(2)}, u32[]{:S(2)}) async-start(f32[32,2,512]{2,1,0:T(2,128)} %get-tuple-element.163), calls=%async_computation.5 | async-start | bytes 262144 | tf_op jit(solution)/shard_map/all_to_all | solution.py:32
  120.8 7.3 %collective-permute-start.21 = (bf16[256,512]{1,0:T(8,128)(2,1)S(1)}, bf16[256,512]{1,0:T(8,128)(2,1)S(1)}, u32[]{:S(2)}, u32[]{:S(2)}) collective-permute-start(bf16[256,512]{1,0:T(8,128)(2,1)S(1)} %copy-done.42), channel_id=1, source_target_pairs={{0,1},{1,0},{2,3},{3,2},{4,5},{5,4},{6,7},{7,6},{8,9},{9,8},{10,11... | collective-permute-start | bytes 786440 | tf_op jit(solution)/shard_map/ppermute | solution.py:21
  128.1 8.6 %collective-permute-start.24 = (bf16[1152,128]{1,0:T(8,128)(2,1)}, bf16[1152,128]{1,0:T(8,128)(2,1)S(1)}, u32[]{:S(2)}, u32[]{:S(2)}) collective-permute-start(bf16[1152,128]{1,0:T(8,128)(2,1)} %bitcast.225), channel_id=1, source_target_pairs={{0,8},{1,9},{2,10},{3,11},{4,12},{5,13},{6,14},{7,15},{8,0},{9,1},... | collective-permute-start | bytes 884744 | tf_op jit(solution)/shard_map/ppermute | solution.py:21
  129.5 9.7 %collective-permute-start.22 = (bf16[256,1024]{1,0:T(8,128)(2,1)S(1)}, bf16[256,1024]{1,0:T(8,128)(2,1)S(1)}, u32[]{:S(2)}, u32[]{:S(2)}) collective-permute-start(bf16[256,1024]{1,0:T(8,128)(2,1)S(1)} %copy-done.41), channel_id=1, source_target_pairs={{0,2},{1,5},{2,0},{3,7},{4,6},{5,1},{6,4},{7,3},{8,10},{9,13},{10,... | collective-permute-start | bytes 1572872 | tf_op jit(solution)/shard_map/ppermute | solution.py:21
  134.9 10.5 %collective-permute-start.26 = (bf16[512,512]{1,0:T(8,128)(2,1)}, bf16[512,512]{1,0:T(8,128)(2,1)S(1)}, u32[]{:S(2)}, u32[]{:S(2)}) collective-permute-start(bf16[512,512]{1,0:T(8,128)(2,1)} %get-tuple-element.181), channel_id=1, source_target_pairs={{0,2},{1,5},{2,0},{3,7},{4,6},{5,1},{6,4},{7,3},{8,10},{9,13},{10,... | collective-permute-start | bytes 1572872 | tf_op jit(solution)/shard_map/ppermute | solution.py:21
  136.8 8.7 %collective-permute-start.25 = (bf16[576,128]{1,0:T(8,128)(2,1)S(1)}, bf16[576,128]{1,0:T(8,128)(2,1)S(1)}, u32[]{:S(2)}, u32[]{:S(2)}) collective-permute-start(bf16[576,128]{1,0:T(8,128)(2,1)S(1)} %dynamic-slice_convert_fusion.2), channel_id=1, source_target_pairs={{0,16},{1,17},{2,18},{3,19},{4,20},{5,21},{6,22},{7,23},{8,24},{9,... | collective-permute-start | bytes 442376 | tf_op jit(solution)/shard_map/ppermute | solution.py:21
  139.4 7.7 %collective-permute-start.23 = (bf16[128,1024]{1,0:T(8,128)(2,1)S(1)}, bf16[128,1024]{1,0:T(8,128)(2,1)S(1)}, u32[]{:S(2)}, u32[]{:S(2)}) collective-permute-start(bf16[128,1024]{1,0:T(8,128)(2,1)S(1)} %dynamic-slice_convert_fusion.1), channel_id=1, source_target_pairs={{0,4},{1,3},{2,6},{3,1},{4,0},{5,7},{6,2},{7,5},{8,12},{9,11},{10,... | collective-permute-start | bytes 786440 | tf_op jit(solution)/shard_map/ppermute | solution.py:21
  147.5 10.5 %collective-permute-start.29 = (bf16[256,512]{1,0:T(8,128)(2,1)S(1)}, bf16[256,512]{1,0:T(8,128)(2,1)S(1)}, u32[]{:S(2)}, u32[]{:S(2)}) collective-permute-start(bf16[256,512]{1,0:T(8,128)(2,1)S(1)} %dynamic-slice_convert_fusion), channel_id=1, source_target_pairs={{0,4},{1,3},{2,6},{3,1},{4,0},{5,7},{6,2},{7,5},{8,12},{9,11},{10,... | collective-permute-start | bytes 786440 | tf_op jit(solution)/shard_map/ppermute | solution.py:21
  148.7 9.3 %collective-permute-start.28 = (bf16[576,128]{1,0:T(8,128)(2,1)S(1)}, bf16[576,128]{1,0:T(8,128)(2,1)S(1)}, u32[]{:S(2)}, u32[]{:S(2)}) collective-permute-start(bf16[576,128]{1,0:T(8,128)(2,1)S(1)} %add_convert_fusion), channel_id=1, source_target_pairs={{0,16},{1,17},{2,18},{3,19},{4,20},{5,21},{6,22},{7,23},{8,24},{9,... | collective-permute-start | bytes 442376 | tf_op jit(solution)/shard_map/ppermute | solution.py:21
  150.3 4.7 %collective-permute-start.27 = (bf16[64,1024]{1,0:T(8,128)(2,1)S(1)}, bf16[64,1024]{1,0:T(8,128)(2,1)S(1)}, u32[]{:S(2)}, u32[]{:S(2)}) collective-permute-start(bf16[64,1024]{1,0:T(8,128)(2,1)S(1)} %dynamic-slice_convert_fusion.4), channel_id=1, source_target_pairs={{0,8},{1,9},{2,10},{3,11},{4,12},{5,13},{6,14},{7,15},{8,0},{9,1},... | collective-permute-start | bytes 393224 | tf_op jit(solution)/shard_map/ppermute | solution.py:21
  158.1 4.3 %collective-permute-start.30 = (bf16[32,1024]{1,0:T(8,128)(2,1)S(1)}, bf16[32,1024]{1,0:T(8,128)(2,1)S(1)}, u32[]{:S(2)}, u32[]{:S(2)}) collective-permute-start(bf16[32,1024]{1,0:T(8,128)(2,1)S(1)} %dynamic-slice_convert_fusion.6), channel_id=1, source_target_pairs={{0,16},{1,17},{2,18},{3,19},{4,20},{5,21},{6,22},{7,23},{8,24},{9,... | collective-permute-start | bytes 196616 | tf_op jit(solution)/shard_map/ppermute | solution.py:21
  158.2 13.4 %collective-permute-start.31 = (bf16[1152,128]{1,0:T(8,128)(2,1)S(1)}, bf16[1152,128]{1,0:T(8,128)(2,1)S(1)}, u32[]{:S(2)}, u32[]{:S(2)}) collective-permute-start(bf16[1152,128]{1,0:T(8,128)(2,1)S(1)} %bitcast.201), channel_id=1, source_target_pairs={{0,8},{1,9},{2,10},{3,11},{4,12},{5,13},{6,14},{7,15},{8,0},{9,1},... | collective-permute-start | bytes 884744 | tf_op jit(solution)/shard_map/ppermute | solution.py:21
  161.7 10.0 %collective-permute-start.32 = (bf16[128,512]{1,0:T(8,128)(2,1)S(1)}, bf16[128,512]{1,0:T(8,128)(2,1)S(1)}, u32[]{:S(2)}, u32[]{:S(2)}) collective-permute-start(bf16[128,512]{1,0:T(8,128)(2,1)S(1)} %dynamic-slice_convert_fusion.3), channel_id=1, source_target_pairs={{0,8},{1,9},{2,10},{3,11},{4,12},{5,13},{6,14},{7,15},{8,0},{9,1},... | collective-permute-start | bytes 393224 | tf_op jit(solution)/shard_map/ppermute | solution.py:21
  171.8 11.3 %collective-permute-start.34 = (bf16[2304,128]{1,0:T(8,128)(2,1)S(1)}, bf16[2304,128]{1,0:T(8,128)(2,1)S(1)}, u32[]{:S(2)}, u32[]{:S(2)}) collective-permute-start(bf16[2304,128]{1,0:T(8,128)(2,1)S(1)} %bitcast.195), channel_id=1, source_target_pairs={{0,4},{1,3},{2,6},{3,1},{4,0},{5,7},{6,2},{7,5},{8,12},{9,11},{10,... | collective-permute-start | bytes 1769480 | tf_op jit(solution)/shard_map/ppermute | solution.py:21
  171.9 11.1 %collective-permute-start.33 = (bf16[32,1024]{1,0:T(8,128)(2,1)S(1)}, bf16[32,1024]{1,0:T(8,128)(2,1)S(1)}, u32[]{:S(2)}, u32[]{:S(2)}) collective-permute-start(bf16[32,1024]{1,0:T(8,128)(2,1)S(1)} %add_convert_fusion.2), channel_id=1, source_target_pairs={{0,16},{1,17},{2,18},{3,19},{4,20},{5,21},{6,22},{7,23},{8,24},{9,... | collective-permute-start | bytes 196616 | tf_op jit(solution)/shard_map/ppermute | solution.py:21
  172.5 5.5 %collective-permute-start.36 = (f32[16,2048]{1,0:T(8,128)S(1)}, f32[16,2048]{1,0:T(8,128)S(1)}, u32[]{:S(2)}, u32[]{:S(2)}) collective-permute-start(f32[16,2048]{1,0:T(8,128)S(1)} %copy-done.30), channel_id=1, source_target_pairs={{0,1},{1,0},{2,3},{3,2},{4,5},{5,4},{6,7},{7,6},{8,9},{9,8},{10,11... | collective-permute-start | bytes 393224 | tf_op jit(solution)/shard_map/ppermute | solution.py:136
  175.9 7.1 %collective-permute-start.35 = (bf16[64,512]{1,0:T(8,128)(2,1)S(1)}, bf16[64,512]{1,0:T(8,128)(2,1)S(1)}, u32[]{:S(2)}, u32[]{:S(2)}) collective-permute-start(bf16[64,512]{1,0:T(8,128)(2,1)S(1)} %dynamic-slice_convert_fusion.5), channel_id=1, source_target_pairs={{0,16},{1,17},{2,18},{3,19},{4,20},{5,21},{6,22},{7,23},{8,24},{9,... | collective-permute-start | bytes 196616 | tf_op jit(solution)/shard_map/ppermute | solution.py:21
  178.0 5.0 %collective-permute-start.37 = (f32[16,2048]{1,0:T(8,128)S(1)}, f32[16,2048]{1,0:T(8,128)S(1)}, u32[]{:S(2)}, u32[]{:S(2)}) collective-permute-start(f32[16,2048]{1,0:T(8,128)S(1)} %add.190), channel_id=1, source_target_pairs={{0,2},{1,3},{2,0},{3,1},{4,6},{5,7},{6,4},{7,5},{8,10},{9,11},{10,... | collective-permute-start | bytes 393224 | tf_op jit(solution)/shard_map/ppermute | solution.py:136
  183.1 4.8 %collective-permute-start.38 = (bf16[64,512]{1,0:T(8,128)(2,1)S(1)}, bf16[64,512]{1,0:T(8,128)(2,1)S(1)}, u32[]{:S(2)}, u32[]{:S(2)}) collective-permute-start(bf16[64,512]{1,0:T(8,128)(2,1)S(1)} %add_convert_fusion.1), channel_id=1, source_target_pairs={{0,16},{1,17},{2,18},{3,19},{4,20},{5,21},{6,22},{7,23},{8,24},{9,... | collective-permute-start | bytes 196616 | tf_op jit(solution)/shard_map/ppermute | solution.py:21
  184.0 29.3 %collective-permute-start.43 = (bf16[4608,128]{1,0:T(8,128)(2,1)S(1)}, bf16[4608,128]{1,0:T(8,128)(2,1)S(1)}, u32[]{:S(2)}, u32[]{:S(2)}) collective-permute-start(bf16[4608,128]{1,0:T(8,128)(2,1)S(1)} %bitcast.192), channel_id=1, source_target_pairs={{0,2},{1,5},{2,0},{3,7},{4,6},{5,1},{6,4},{7,3},{8,10},{9,13},{10,... | collective-permute-start | bytes 3538952 | tf_op jit(solution)/shard_map/ppermute | solution.py:21
  186.0 5.7 %collective-permute-start.45 = (bf16[64,1024]{1,0:T(8,128)(2,1)S(1)}, bf16[64,1024]{1,0:T(8,128)(2,1)S(1)}, u32[]{:S(2)}, u32[]{:S(2)}) collective-permute-start(bf16[64,1024]{1,0:T(8,128)(2,1)S(1)} %bitcast.209), channel_id=1, source_target_pairs={{0,8},{1,9},{2,10},{3,11},{4,12},{5,13},{6,14},{7,15},{8,0},{9,1},... | collective-permute-start | bytes 393224 | tf_op jit(solution)/shard_map/ppermute | solution.py:21
  187.9 5.5 %collective-permute-start.39 = (bf16[128,512]{1,0:T(8,128)(2,1)S(1)}, bf16[128,512]{1,0:T(8,128)(2,1)S(1)}, u32[]{:S(2)}, u32[]{:S(2)}) collective-permute-start(bf16[128,512]{1,0:T(8,128)(2,1)S(1)} %bitcast.210), channel_id=1, source_target_pairs={{0,8},{1,9},{2,10},{3,11},{4,12},{5,13},{6,14},{7,15},{8,0},{9,1},... | collective-permute-start | bytes 393224 | tf_op jit(solution)/shard_map/ppermute | solution.py:21
  191.8 8.5 %collective-permute-start.46 = (bf16[128,1024]{1,0:T(8,128)(2,1)S(1)}, bf16[128,1024]{1,0:T(8,128)(2,1)S(1)}, u32[]{:S(2)}, u32[]{:S(2)}) collective-permute-start(bf16[128,1024]{1,0:T(8,128)(2,1)S(1)} %bitcast.204), channel_id=1, source_target_pairs={{0,4},{1,3},{2,6},{3,1},{4,0},{5,7},{6,2},{7,5},{8,12},{9,11},{10,... | collective-permute-start | bytes 786440 | tf_op jit(solution)/shard_map/ppermute | solution.py:21
  193.5 12.4 %collective-permute-start.40 = (bf16[256,512]{1,0:T(8,128)(2,1)S(1)}, bf16[256,512]{1,0:T(8,128)(2,1)S(1)}, u32[]{:S(2)}, u32[]{:S(2)}) collective-permute-start(bf16[256,512]{1,0:T(8,128)(2,1)S(1)} %bitcast.203), channel_id=1, source_target_pairs={{0,4},{1,3},{2,6},{3,1},{4,0},{5,7},{6,2},{7,5},{8,12},{9,11},{10,... | collective-permute-start | bytes 786440 | tf_op jit(solution)/shard_map/ppermute | solution.py:21
  200.3 10.7 %collective-permute-start.47 = (bf16[256,1024]{1,0:T(8,128)(2,1)S(1)}, bf16[256,1024]{1,0:T(8,128)(2,1)S(1)}, u32[]{:S(2)}, u32[]{:S(2)}) collective-permute-start(bf16[256,1024]{1,0:T(8,128)(2,1)S(1)} %bitcast.198), channel_id=1, source_target_pairs={{0,2},{1,5},{2,0},{3,7},{4,6},{5,1},{6,4},{7,3},{8,10},{9,13},{10,... | collective-permute-start | bytes 1572872 | tf_op jit(solution)/shard_map/ppermute | solution.py:21
  205.9 10.7 %collective-permute-start.41 = (bf16[512,512]{1,0:T(8,128)(2,1)S(1)}, bf16[512,512]{1,0:T(8,128)(2,1)S(1)}, u32[]{:S(2)}, u32[]{:S(2)}) collective-permute-start(bf16[512,512]{1,0:T(8,128)(2,1)S(1)} %bitcast.197), channel_id=1, source_target_pairs={{0,2},{1,5},{2,0},{3,7},{4,6},{5,1},{6,4},{7,3},{8,10},{9,13},{10,... | collective-permute-start | bytes 1572872 | tf_op jit(solution)/shard_map/ppermute | solution.py:21
  211.3 8.4 %collective-permute-start.48 = (bf16[512,1024]{1,0:T(8,128)(2,1)S(1)}, bf16[512,1024]{1,0:T(8,128)(2,1)S(1)}, u32[]{:S(2)}, u32[]{:S(2)}) collective-permute-start(bf16[512,1024]{1,0:T(8,128)(2,1)S(1)} %bitcast.193), channel_id=1, source_target_pairs={{0,1},{1,0},{2,3},{3,2},{4,5},{5,4},{6,7},{7,6},{8,9},{9,8},{10,11... | collective-permute-start | bytes 3145736 | tf_op jit(solution)/shard_map/ppermute | solution.py:21
  213.7 11.8 %collective-permute-start.44 = (bf16[9216,128]{1,0:T(8,128)(2,1)S(1)}, bf16[9216,128]{1,0:T(8,128)(2,1)S(1)}, u32[]{:S(2)}, u32[]{:S(2)}) collective-permute-start(bf16[9216,128]{1,0:T(8,128)(2,1)S(1)} %bitcast.185), channel_id=1, source_target_pairs={{0,1},{1,0},{2,3},{3,2},{4,5},{5,4},{6,7},{7,6},{8,9},{9,8},{10,11... | collective-permute-start | bytes 7077896 | tf_op jit(solution)/shard_map/ppermute | solution.py:21
  216.9 5.5 %collective-permute-start.42 = (bf16[1024,512]{1,0:T(8,128)(2,1)S(1)}, bf16[1024,512]{1,0:T(8,128)(2,1)S(1)}, u32[]{:S(2)}, u32[]{:S(2)}) collective-permute-start(bf16[1024,512]{1,0:T(8,128)(2,1)S(1)} %bitcast.194), channel_id=1, source_target_pairs={{0,1},{1,0},{2,3},{3,2},{4,5},{5,4},{6,7},{7,6},{8,9},{9,8},{10,11... | collective-permute-start | bytes 3145736 | tf_op jit(solution)/shard_map/ppermute | solution.py:21
  (49 other events, 274.1 us)

commit v8 on v7

--- a/solution.py
+++ b/solution.py
@@ -33,9 +33,7 @@
 
 
 def everyone_wide(sent, kept, low_step):
-    value = kept + swap(sent, low_step[0])
-    count = lax.axis_size(AXES[:2])
-    mine = lax.all_to_all(jnp.broadcast_to(value[None], (count, *value.shape)), AXES[:2], 0, 0)
+    mine = lax.all_to_all(kept + swap(sent, low_step[0])[None], AXES[:2], 0, 0)
     return mine, swap(mine, low_step[0])
 
 
@@ -301,7 +299,8 @@
     mine = (place[0, 0] % 2 == 1) == (at >= half)
     for k, value in enumerate((values, others)):
         total = jnp.sum(value, axis=0, keepdims=True)
-        kept[k : k + 1, span] = jnp.where(mine, total, kept[k : k + 1, span])
+        held = jnp.where(mine, total, kept[0, k : k + 1, span])
+        kept[:, k, span] = jnp.broadcast_to(held, (kept.shape[0], chunk))
         sent[k : k + 1, span] = jnp.where(mine, sent[k : k + 1, span], total)
 
 
@@ -415,7 +414,7 @@
         gate = logistic(summed)
         value = summed * gate * inside
         result[:, span] = value.astype(LOW)
-        pooled[:, span] = jnp.sum(value.reshape(images, height * width, chunk), axis=1)
+        pooled[:, span] = jnp.sum(value.reshape(images, height * width, chunk), axis=1) / area
         share = (pool_grad[:, span] / area)[:, None]
         total = out_grad[:, span].astype(FULL).reshape(images, height * width, chunk) + share
         total = total.reshape(inside.shape) * inside * (gate * (1.0 + summed * (1.0 - gate)))
@@ -693,6 +692,7 @@
     plane, narrow, broad, large = (pixels, middle), (2, middle), (2, channels), (pixels, channels)
     edge, split_rows = (images * width, middle), (height, images * width, middle)
     half_broad = (2, channels // 2)
+    many_broad = (lax.axis_size(AXES[:2]), *half_broad)
     half_rows = (height, images * width, middle // 2)
     taps = [pltpu.VMEM(weight_mid.shape, LOW), pltpu.SemaphoreType.DMA((3, 3))]
 
@@ -764,7 +764,7 @@
             (half_rows, LOW),
             (large, FULL),
             (half_broad, FULL),
-            (half_broad, FULL),
+            (many_broad, FULL),
             (narrow, FULL),
         ],
         place,
@@ -791,7 +791,7 @@
             ((images, channels), FULL),
             (large, FULL),
             (half_broad, FULL),
-            (half_broad, FULL),
+            (many_broad, FULL),
             (broad, FULL),
         ],
         place,
@@ -974,7 +974,6 @@
     chains.slot()
     (pooled,) = chains.slot(pooled)
     (pooled,) = chains.slot(sum_rows_axis(pooled))
-    pooled = pooled / areas[:, :1]
     for _ in range(0):
         chains.slot()
     while chains.running:

time: 231 us -> 231 us (level)
  waiting for transfers between devices: 67.6 us -> 61.4 us
  starting transfers between devices: 74.2 us -> 79.1 us
    ppermute x43, waiting for transfers between devices: 49.2 us -> 44 us  [swap(): lax.ppermute(value, AXES, [(i, i ^ flips[i & 1]) for i in range(count)])]
    ppermute x43, starting transfers between devices: 39.6 us -> 44.5 us  [swap(): lax.ppermute(value, AXES, [(i, i ^ flips[i & 1]) for i in range(count)])]
    unnamed x86 -> x88, local copies, waits for them, and re-layouts: 4.98 us -> 5.02 us
  transfers between devices with their start and end apart: 54 -> 54, of which waited for: 22 -> 23; matrix products, arithmetic and copies ran while one was open for 8% -> 9% of each run, Pallas kernels for 10% -> 10%
where the time goes in v8:
time: 231 us; the launch traced here: 230 us
  starting transfers between devices  79.1 us (34%)
  waiting for transfers between devices  61.4 us (27%)
  Pallas kernels  50.2 us (22%)
  other arithmetic  16.1 us (7%)
  blocking collectives  12 us (5%)
  local copies, waits for them, and re-layouts  7.97 us (3%)
    pallas_call x9, Pallas kernels, call(): pl.pallas_call(kernel, out_shape=[jax.ShapeDtypeStruct(shape, kind) for s...  45.7 us
    ppermute x43, starting transfers between devices, swap(): lax.ppermute(value, AXES, [(i, i ^ flips[i & 1]) for i in range(count)])  44.5 us
    ppermute x43, waiting for transfers between devices, swap(): lax.ppermute(value, AXES, [(i, i ^ flips[i & 1]) for i in range(count)])  44 us
    all_to_all x4, starting transfers between devices, everyone(): return lax.all_to_all(copies, AXES, 0, 0)  20.1 us
    all_to_all x1, blocking collectives, everyone_wide(): mine = lax.all_to_all(kept + swap(sent, low_step[0])[None], AXES[:2], 0, 0)  12 us
    ppermute x2, starting transfers between devices, trade(): lax.ppermute(far, ROWS, pairs + [(b, a) for a, b in pairs])  7 us
    all_to_all x4, waiting for transfers between devices, everyone(): return lax.all_to_all(copies, AXES, 0, 0)  6.1 us
    unnamed x88, local copies, waits for them, and re-layouts  5.02 us
  transfers between devices with their start and end apart: 54, of which 23 were waited for; matrix products, arithmetic and copies ran while one was open for 9% of the time, Pallas kernels for 10%

profile of v8, /device:TPU:1, one launch (start us, length us, event | category | flops | bytes accessed | tf_op | source)
XLA Modules:
  0.0 230.4 jit_solution(9764990468765085688)
XLA Ops:
  1.3 4.3 %shard_map.220 = (f32[256,512]{1,0:T(8,128)}, f32[128,512]{1,0:T(8,128)}, f32[128,512]{1,0:T(8,128)}, f32[32,2,640]{2,1,0:T(2,128)}, f32[2,512]{1,0:T(2,128)}, /...) custom-call(s32[1,4]{1,0:T(1,128)} %add_bitcast_fusion.refs_0_.place, ...), custom_call_target="tpu_custom_call" | custom-call | tf_op jit(solution)/shard_map/pallas_call | solution.py:154
  5.6 7.1 %all-to-all-start = ((f32[32,2,640]{2,1,0:T(2,128)}), f32[32,2,640]{2,1,0:T(2,128)S(1)}, u32[]{:S(2)}, u32[]{:S(2)}) async-start(f32[32,2,640]{2,1,0:T(2,128)} %get-tuple-element.107), calls=%async_computation | async-start | bytes 327680 | tf_op jit(solution)/shard_map/all_to_all | solution.py:32
  13.3 3.5 %collective-permute-start.1 = (f32[128,512]{1,0:T(8,128)}, f32[128,512]{1,0:T(8,128)S(1)}, u32[]{:S(2)}, u32[]{:S(2)}) collective-permute-start(f32[128,512]{1,0:T(8,128)} %get-tuple-element.109), channel_id=1, source_target_pairs={{1,2},{2,1},{5,6},{6,5},{9,10},{10,9},{13,14},{14,13},{17,18},{18,... | collective-permute-start | bytes 786440 | tf_op jit(solution)/shard_map/ppermute | solution.py:144
  16.8 4.8 %collective-permute-done.1.refs_5_ = f32[128,512]{1,0:T(8,128)S(1)} collective-permute-done((f32[128,512]{1,0:T(8,128)}, f32[128,512]{1,0:T(8,128)S(1)}, u32[]{:S(2)}, u32[]{:S(2)}) %collective-permute-start.1) | collective-permute-done | bytes 262176 | tf_op jit(solution)/shard_map/ppermute | solution.py:144
  22.4 5.5 %shard_map.221 = (bf16[2,128,512]{2,1,0:T(8,128)(2,1)}, f32[256,512]{1,0:T(8,128)}, f32[32,2,512]{2,1,0:T(2,128)}, f32[2,640]{1,0:T(2,128)}, f32[2,128]{1,0:T(2,128)}) custom-call(s32[1,4]{1,0:T(1,128)} %add_bitcast_fusion.refs_0_.place, f32[32,2,640]{2,1,0:T(2,128)} %copy-done.8, f32[2,512]{1,0:T(2,128)} %get-tuple-element.111.refs_2_.refs_4_.params, ...), custom_call_target="tpu_custom_call" | custom-call | tf_op jit(solution)/shard_map/pallas_call | solution.py:154
  27.8 5.4 %all-to-all-start.1 = ((f32[32,2,512]{2,1,0:T(2,128)}), f32[32,2,512]{2,1,0:T(2,128)S(1)}, u32[]{:S(2)}, u32[]{:S(2)}) async-start(f32[32,2,512]{2,1,0:T(2,128)} %get-tuple-element.119), calls=%async_computation.1 | async-start | bytes 262144 | tf_op jit(solution)/shard_map/all_to_all | solution.py:32
  35.6 5.8 %all-to-all-done.1.refs_2_ = f32[32,2,512]{2,1,0:T(2,128)S(1)} async-done(((f32[32,2,512]{2,1,0:T(2,128)}), f32[32,2,512]{2,1,0:T(2,128)S(1)}, u32[]{:S(2)}, u32[]{:S(2)}) %all-to-all-start.1) | async-done | bytes 131104 | tf_op jit(solution)/shard_map/all_to_all | solution.py:32
  42.1 4.2 %shard_map.222 = (bf16[256,512]{1,0:T(8,128)(2,1)}, bf16[2,128,256]{2,1,0:T(8,128)(2,1)}, bf16[2,128,256]{2,1,0:T(8,128)(2,1)}, f32[256,2048]{1,0:T(8,128)}, f32...) custom-call(s32[1,4]{1,0:T(1,128)} %add_bitcast_fusion.refs_0_.place, ...), custom_call_target="tpu_custom_call" | custom-call | tf_op jit(solution)/shard_map/pallas_call | solution.py:154
  48.5 3.5 %all-to-all-start.2 = ((f32[16,2,1024]{2,1,0:T(2,128)}), f32[16,2,1024]{2,1,0:T(2,128)S(1)}, u32[]{:S(2)}, u32[]{:S(2)}) async-start(f32[16,2,1024]{2,1,0:T(2,128)} %bitcast.187), calls=%async_computation.2 | async-start | bytes 262144 | tf_op jit(solution)/shard_map/all_to_all | solution.py:36
  56.4 2.4 %all-to-all-done.2.refs_2_ = f32[16,2,1024]{2,1,0:T(2,128)S(1)} async-done(((f32[16,2,1024]{2,1,0:T(2,128)}), f32[16,2,1024]{2,1,0:T(2,128)S(1)}, u32[]{:S(2)}, u32[]{:S(2)}) %all-to-all-start.2) | async-done | bytes 131104 | tf_op jit(solution)/shard_map/all_to_all | solution.py:36
  58.8 1.6 collective-permute-start.5
  62.0 7.2 %shard_map.223 = (bf16[256,2048]{1,0:T(8,128)(2,1)}, f32[16,2048]{1,0:T(8,128)}, f32[256,2048]{1,0:T(8,128)}, f32[2,1024]{1,0:T(2,128)}, f32[16,2,1024]{2,1,0:T(2,128)}, /*index=5*/f32[2,2048]{1,0:T(2,128)}) custom-call(s32[1,4]{1,0:T(1,128)} %add_bitcast_fusion.refs_0_.place, f32[2,640]{1,0:T(2,128)} %get-tuple-element.118.refs_1_.sums_first, ...), custom_call_target="tpu_custom_call" | custom-call | tf_op jit(solution)/shard_map/pallas_call | solution.py:154
  72.2 12.0 %all_to_all.30.refs_4_ = f32[16,2,1024]{2,1,0:T(2,128)S(1)} all-to-all(f32[16,2,1024]{2,1,0:T(2,128)S(1)} %bitcast.217), channel_id=1, replica_groups=mesh['img'=8,'half'=2,'low'=2] {'img','half'}, dimensions={0} | all-to-all | bytes 262144 | tf_op jit(solution)/shard_map/all_to_all | solution.py:36
  84.2 1.8 collective-permute-start.11
  87.7 6.0 %shard_map.224 = (bf16[256,1024]{1,0:T(8,128)(2,1)}, bf16[256,1024]{1,0:T(8,128)(2,1)}, f32[256,512]{1,0:T(8,128)}, bf16[2,128,256]{2,1,0:T(8,128)(2,1)}, bf16[2...) custom-call(s32[1,4]{1,0:T(1,128)} %add_bitcast_fusion.refs_0_.place, ...), custom_call_target="tpu_custom_call" | custom-call | tf_op jit(solution)/shard_map/pallas_call | solution.py:154
  95.2 2.3 %all-to-all-start.4 = ((f32[32,2,512]{2,1,0:T(2,128)}), f32[32,2,512]{2,1,0:T(2,128)S(1)}, u32[]{:S(2)}, u32[]{:S(2)}) async-start(f32[32,2,512]{2,1,0:T(2,128)} %get-tuple-element.151), calls=%async_computation.4 | async-start | bytes 262144 | tf_op jit(solution)/shard_map/all_to_all | solution.py:32
  97.9 3.5 %collective-permute-start.17 = (bf16[128,1024]{1,0:T(8,128)(2,1)}, bf16[128,1024]{1,0:T(8,128)(2,1)S(1)}, u32[]{:S(2)}, u32[]{:S(2)}) collective-permute-start(bf16[128,1024]{1,0:T(8,128)(2,1)} %get-tuple-element.156), channel_id=1, source_target_pairs={{1,2},{2,1},{5,6},{6,5},{9,10},{10,9},{13,14},{14,13},{17,18},{18,... | collective-permute-start | bytes 786440 | tf_op jit(solution)/shard_map/ppermute | solution.py:144
  104.7 3.2 %shard_map.225 = (bf16[256,1024]{1,0:T(8,128)(2,1)}, f32[256,1024]{1,0:T(8,128)}) custom-call(s32[1,4]{1,0:T(1,128)} %add_bitcast_fusion.refs_0_.place, bf16[256,512]{1,0:T(8,128)(2,1)} %get-tuple-element.128.act, bf16[256,512]{1,0:T(8,128)(2,1)} %copy-done.26, bf16[256,1024]{1,0:T(8,128)(2,1)} %get-tuple-element.148.third, bf16[256,1024]{1,0:T(8,128)(2,1)} %copy-done.16), custom_call_target="tpu_custom_call" | custom-call | tf_op jit(solution)/shard_map/pallas_call | solution.py:154
  108.7 6.2 %shard_map.226 = (f32[256,512]{1,0:T(8,128)}, bf16[256,512]{1,0:T(8,128)(2,1)}, f32[32,2,512]{2,1,0:T(2,128)}, f32[2,512]{1,0:T(2,128)}) custom-call(s32[1,4]{1,0:T(1,128)} %add_bitcast_fusion.refs_0_.place, f32[2,640]{1,0:T(2,128)} %get-tuple-element.118.refs_1_.sums_first, f32[2,512]{1,0:T(2,128)} %get-tuple-element.135.refs_2_.sums_second, ...), custom_call_target="tpu_custom_call" | custom-call | tf_op jit(solution)/shard_map/pallas_call | solution.py:154
  115.0 5.2 %all-to-all-start.5 = ((f32[32,2,512]{2,1,0:T(2,128)}), f32[32,2,512]{2,1,0:T(2,128)S(1)}, u32[]{:S(2)}, u32[]{:S(2)}) async-start(f32[32,2,512]{2,1,0:T(2,128)} %get-tuple-element.163), calls=%async_computation.5 | async-start | bytes 262144 | tf_op jit(solution)/shard_map/all_to_all | solution.py:32
  123.3 4.8 %shard_map.227 = (bf16[8,9,16,128]{3,2,1,0:T(8,128)(2,1)}, f32[8,9,16,128]{3,2,1,0:T(8,128)}) custom-call(s32[1,4]{1,0:T(1,128)} %add_bitcast_fusion.1.place, s32[2,16]{1,0:T(2,128)} %slice_convert_fusion.sizes, f32[2,640]{1,0:T(2,128)} %get-tuple-element.118.refs_1_.sums_first, f32[2,512]{1,0:T(2,128)} %get-tuple-element.135.refs_2_.sums_second, ...), custom_call_target="tpu_custom_call" | custom-call | tf_op jit(solution)/shard_map/pallas_call | solution.py:154
  130.9 4.2 %shard_map.228 = (bf16[256,512]{1,0:T(8,128)(2,1)}, f32[2,512]{1,0:T(2,128)}, bf16[512,512]{1,0:T(8,128)(2,1)}, f32[512,512]{1,0:T(8,128)}) custom-call(s32[1,4]{1,0:T(1,128)} %add_bitcast_fusion.refs_0_.place, f32[2,640]{1,0:T(2,128)} %get-tuple-element.118.refs_1_.sums_first, f32[32,2,512]{2,1,0:T(2,128)} %copy-done.13, ...), custom_call_target="tpu_custom_call" | custom-call | tf_op jit(solution)/shard_map/pallas_call | solution.py:154
  137.1 2.4 %collective-permute-start.25 = (bf16[576,128]{1,0:T(8,128)(2,1)S(1)}, bf16[576,128]{1,0:T(8,128)(2,1)S(1)}, u32[]{:S(2)}, u32[]{:S(2)}) collective-permute-start(bf16[576,128]{1,0:T(8,128)(2,1)S(1)} %dynamic-slice_convert_fusion.2), channel_id=1, source_target_pairs={{0,16},{1,17},{2,18},{3,19},{4,20},{5,21},{6,22},{7,23},{8,24},{9,... | collective-permute-start | bytes 442376 | tf_op jit(solution)/shard_map/ppermute | solution.py:21
  140.9 2.1 convolution_add_fusion
  143.0 2.8 %collective-permute-done.25 = bf16[576,128]{1,0:T(8,128)(2,1)S(1)} collective-permute-done((bf16[576,128]{1,0:T(8,128)(2,1)S(1)}, bf16[576,128]{1,0:T(8,128)(2,1)S(1)}, u32[]{:S(2)}, u32[]{:S(2)}) %collective-permute-start.25) | collective-permute-done | bytes 147488 | tf_op jit(solution)/shard_map/ppermute | solution.py:21
  145.8 1.6 collective-permute-done.23
  150.5 1.7 collective-permute-start.27
  152.2 3.0 %collective-permute-done.27 = bf16[64,1024]{1,0:T(8,128)(2,1)S(1)} collective-permute-done((bf16[64,1024]{1,0:T(8,128)(2,1)S(1)}, bf16[64,1024]{1,0:T(8,128)(2,1)S(1)}, u32[]{:S(2)}, u32[]{:S(2)}) %collective-permute-start.27) | collective-permute-done | bytes 131104 | tf_op jit(solution)/shard_map/ppermute | solution.py:21
  155.2 3.0 %collective-permute-done.28 = bf16[576,128]{1,0:T(8,128)(2,1)S(1)} collective-permute-done((bf16[576,128]{1,0:T(8,128)(2,1)S(1)}, bf16[576,128]{1,0:T(8,128)(2,1)S(1)}, u32[]{:S(2)}, u32[]{:S(2)}) %collective-permute-start.28) | collective-permute-done | bytes 147488 | tf_op jit(solution)/shard_map/ppermute | solution.py:21
  160.1 1.9 collective-permute-start.30
  162.0 5.7 %collective-permute-done.30 = bf16[32,1024]{1,0:T(8,128)(2,1)S(1)} collective-permute-done((bf16[32,1024]{1,0:T(8,128)(2,1)S(1)}, bf16[32,1024]{1,0:T(8,128)(2,1)S(1)}, u32[]{:S(2)}, u32[]{:S(2)}) %collective-permute-start.30) | collective-permute-done | bytes 65568 | tf_op jit(solution)/shard_map/ppermute | solution.py:21
  167.7 1.8 collective-permute-done.32
  172.0 3.4 %collective-permute-start.36 = (f32[16,2048]{1,0:T(8,128)S(1)}, f32[16,2048]{1,0:T(8,128)S(1)}, u32[]{:S(2)}, u32[]{:S(2)}) collective-permute-start(f32[16,2048]{1,0:T(8,128)S(1)} %copy-done.30), channel_id=1, source_target_pairs={{0,1},{1,0},{2,3},{3,2},{4,5},{5,4},{6,7},{7,6},{8,9},{9,8},{10,11... | collective-permute-start | bytes 393224 | tf_op jit(solution)/shard_map/ppermute | solution.py:134
  178.0 3.2 %collective-permute-done.37 = f32[16,2048]{1,0:T(8,128)S(1)} collective-permute-done((f32[16,2048]{1,0:T(8,128)S(1)}, f32[16,2048]{1,0:T(8,128)S(1)}, u32[]{:S(2)}, u32[]{:S(2)}) %collective-permute-start.37) | collective-permute-done | bytes 131104 | tf_op jit(solution)/shard_map/ppermute | solution.py:134
  181.9 2.0 collective-permute-start.38
  184.1 1.8 collective-permute-start.43
  186.0 2.3 collective-permute-start.45
  189.6 2.3 %collective-permute-done.45 = bf16[64,1024]{1,0:T(8,128)(2,1)S(1)} collective-permute-done((bf16[64,1024]{1,0:T(8,128)(2,1)S(1)}, bf16[64,1024]{1,0:T(8,128)(2,1)S(1)}, u32[]{:S(2)}, u32[]{:S(2)}) %collective-permute-start.45) | collective-permute-done | bytes 131104 | tf_op jit(solution)/shard_map/ppermute | solution.py:21
  192.1 2.7 %collective-permute-done.39 = bf16[128,512]{1,0:T(8,128)(2,1)S(1)} collective-permute-done((bf16[128,512]{1,0:T(8,128)(2,1)S(1)}, bf16[128,512]{1,0:T(8,128)(2,1)S(1)}, u32[]{:S(2)}, u32[]{:S(2)}) %collective-permute-start.39) | collective-permute-done | bytes 131104 | tf_op jit(solution)/shard_map/ppermute | solution.py:21
  194.9 5.6 %collective-permute-done.46 = bf16[128,1024]{1,0:T(8,128)(2,1)S(1)} collective-permute-done((bf16[128,1024]{1,0:T(8,128)(2,1)S(1)}, bf16[128,1024]{1,0:T(8,128)(2,1)S(1)}, u32[]{:S(2)}, u32[]{:S(2)}) %collective-permute-start.46) | collective-permute-done | bytes 262176 | tf_op jit(solution)/shard_map/ppermute | solution.py:21
  201.7 4.4 %collective-permute-done.40 = bf16[256,512]{1,0:T(8,128)(2,1)S(1)} collective-permute-done((bf16[256,512]{1,0:T(8,128)(2,1)S(1)}, bf16[256,512]{1,0:T(8,128)(2,1)S(1)}, u32[]{:S(2)}, u32[]{:S(2)}) %collective-permute-start.40) | collective-permute-done | bytes 262176 | tf_op jit(solution)/shard_map/ppermute | solution.py:21
  206.7 4.4 %collective-permute-done.47 = bf16[256,1024]{1,0:T(8,128)(2,1)S(1)} collective-permute-done((bf16[256,1024]{1,0:T(8,128)(2,1)S(1)}, bf16[256,1024]{1,0:T(8,128)(2,1)S(1)}, u32[]{:S(2)}, u32[]{:S(2)}) %collective-permute-start.47) | collective-permute-done | bytes 524320 | tf_op jit(solution)/shard_map/ppermute | solution.py:21
  211.3 1.9 collective-permute-start.48
  213.8 2.9 %collective-permute-done.41 = bf16[512,512]{1,0:T(8,128)(2,1)S(1)} collective-permute-done((bf16[512,512]{1,0:T(8,128)(2,1)S(1)}, bf16[512,512]{1,0:T(8,128)(2,1)S(1)}, u32[]{:S(2)}, u32[]{:S(2)}) %collective-permute-start.41) | collective-permute-done | bytes 524320 | tf_op jit(solution)/shard_map/ppermute | solution.py:21
  216.9 1.9 collective-permute-start.42
  220.2 2.5 %maximum_convert_fusion = f32[512,2048]{1,0:T(8,128)} fusion(bf16[512,1024]{1,0:T(8,128)(2,1)S(1)} %get-tuple-element.205, bf16[512,1024]{1,0:T(8,128)(2,1)S(1)} %get-tuple-element.204), kind=kLoop, calls=%fused_computation.3 | loop fusion | flops 4194304 | bytes 6291456 | tf_op jit(solution)/shard_map/convert_element_type | solution.py:903
  223.2 2.7 %bitcast_convert_fusion = f32[2048,512]{1,0:T(8,128)} fusion(bf16[2,1024,512]{2,1,0:T(8,128)(2,1)S(1)} %pad_maximum_fusion.1), kind=kLoop, calls=%fused_computation.4 | loop fusion | flops 1048576 | bytes 6291456 | tf_op jit(solution)/shard_map/convert_element_type | solution.py:941
  225.9 4.5 %shard_map.229 = f32[9,512,512]{2,1,0:T(8,128)} custom-call(s32[1,1]{1,0:T(1,128)} %bitcast.68.odd, bf16[4,16,9,16,128]{4,3,2,1,0:T(8,128)(2,1)S(1)} %bitcast.192, bf16[4,16,9,16,128]{4,3,2,1,0:T(8,128)(2,1)S(1)} %bitcast.193), custom_call_target="tpu_custom_call" | custom-call | tf_op jit(solution)/shard_map/pallas_call | solution.py:633
  (232 shorter events, 49.6 us)
Async XLA Ops:
  5.6 16.0 %all-to-all-start = ((f32[32,2,640]{2,1,0:T(2,128)}), f32[32,2,640]{2,1,0:T(2,128)S(1)}, u32[]{:S(2)}, u32[]{:S(2)}) async-start(f32[32,2,640]{2,1,0:T(2,128)} %get-tuple-element.107), calls=%async_computation | async-start | bytes 327680 | tf_op jit(solution)/shard_map/all_to_all | solution.py:32
  12.7 22.9 %collective-permute-start.3 = (f32[256,512]{1,0:T(8,128)}, f32[256,512]{1,0:T(8,128)S(1)}, u32[]{:S(2)}, u32[]{:S(2)}) collective-permute-start(f32[256,512]{1,0:T(8,128)} %get-tuple-element.112.refs_3_.refs_10_.first), channel_id=1, source_target_pairs={{0,1},{1,0},{2,3},{3,2},{4,5},{5,4},{6,7},{7,6},{8,9},{9,8},{10,11... | collective-permute-start | bytes 1572872 | tf_op jit(solution)/shard_map/ppermute | solution.py:21
  13.0 3.8 %collective-permute-start = (f32[128,512]{1,0:T(8,128)}, f32[128,512]{1,0:T(8,128)S(1)}, u32[]{:S(2)}, u32[]{:S(2)}) collective-permute-start(f32[128,512]{1,0:T(8,128)} %get-tuple-element.108), channel_id=1, source_target_pairs={{0,1},{1,0},{2,3},{3,2},{4,5},{5,4},{6,7},{7,6},{8,9},{9,8},{10,11... | collective-permute-start | bytes 786440 | tf_op jit(solution)/shard_map/ppermute | solution.py:143
  13.3 8.3 %collective-permute-start.1 = (f32[128,512]{1,0:T(8,128)}, f32[128,512]{1,0:T(8,128)S(1)}, u32[]{:S(2)}, u32[]{:S(2)}) collective-permute-start(f32[128,512]{1,0:T(8,128)} %get-tuple-element.109), channel_id=1, source_target_pairs={{1,2},{2,1},{5,6},{6,5},{9,10},{10,9},{13,14},{14,13},{17,18},{18,... | collective-permute-start | bytes 786440 | tf_op jit(solution)/shard_map/ppermute | solution.py:144
  27.8 13.6 %all-to-all-start.1 = ((f32[32,2,512]{2,1,0:T(2,128)}), f32[32,2,512]{2,1,0:T(2,128)S(1)}, u32[]{:S(2)}, u32[]{:S(2)}) async-start(f32[32,2,512]{2,1,0:T(2,128)} %get-tuple-element.119), calls=%async_computation.1 | async-start | bytes 262144 | tf_op jit(solution)/shard_map/all_to_all | solution.py:32
  46.8 14.2 %collective-permute-start.9 = (bf16[256,1024]{1,0:T(8,128)(2,1)S(1)}, bf16[256,1024]{1,0:T(8,128)(2,1)S(1)}, u32[]{:S(2)}, u32[]{:S(2)}) collective-permute-start(bf16[256,1024]{1,0:T(8,128)(2,1)S(1)} %get-tuple-element.215), channel_id=1, source_target_pairs={{0,1},{1,0},{2,3},{3,2},{4,5},{5,4},{6,7},{7,6},{8,9},{9,8},{10,11... | collective-permute-start | bytes 1572872 | tf_op jit(solution)/shard_map/ppermute | solution.py:21
  48.5 10.3 %all-to-all-start.2 = ((f32[16,2,1024]{2,1,0:T(2,128)}), f32[16,2,1024]{2,1,0:T(2,128)S(1)}, u32[]{:S(2)}, u32[]{:S(2)}) async-start(f32[16,2,1024]{2,1,0:T(2,128)} %bitcast.187), calls=%async_computation.2 | async-start | bytes 262144 | tf_op jit(solution)/shard_map/all_to_all | solution.py:36
  53.0 8.0 %collective-permute-start.6 = (bf16[2,2,128,256]{3,2,1,0:T(8,128)(2,1)S(1)}, bf16[2,2,128,256]{3,2,1,0:T(8,128)(2,1)S(1)}, u32[]{:S(2)}, u32[]{:S(2)}) collective-permute-start(bf16[2,2,128,256]{3,2,1,0:T(8,128)(2,1)S(1)} %pad_maximum_fusion.11), channel_id=1, source_target_pairs={{0,2},{1,5},{2,0},{3,7},{4,6},{5,1},{6,4},{7,3},{8,10},{9,13},{10,... | collective-permute-start | bytes 786440 | tf_op jit(solution)/shard_map/ppermute | solution.py:21
  54.4 6.7 %collective-permute-start.8 = (bf16[256,512]{1,0:T(8,128)(2,1)S(1)}, bf16[256,512]{1,0:T(8,128)(2,1)S(1)}, u32[]{:S(2)}, u32[]{:S(2)}) collective-permute-start(bf16[256,512]{1,0:T(8,128)(2,1)S(1)} %copy-done.25), channel_id=1, source_target_pairs={{0,1},{1,0},{2,3},{3,2},{4,5},{5,4},{6,7},{7,6},{8,9},{9,8},{10,11... | collective-permute-start | bytes 786440 | tf_op jit(solution)/shard_map/ppermute | solution.py:21
  55.2 5.9 %collective-permute-start.7 = (bf16[1,2,128,256]{3,2,1,0:T(8,128)(2,1)}, bf16[1,2,128,256]{3,2,1,0:T(8,128)(2,1)S(1)}, u32[]{:S(2)}, u32[]{:S(2)}) collective-permute-start(bf16[1,2,128,256]{3,2,1,0:T(8,128)(2,1)} %bitcast.237), channel_id=1, source_target_pairs={{0,2},{1,5},{2,0},{3,7},{4,6},{5,1},{6,4},{7,3},{8,10},{9,13},{10,... | collective-permute-start | bytes 393224 | tf_op jit(solution)/shard_map/ppermute | solution.py:21
  70.1 17.0 %collective-permute-start.12 = (bf16[4,2,128,256]{3,2,1,0:T(8,128)(2,1)S(1)}, bf16[4,2,128,256]{3,2,1,0:T(8,128)(2,1)S(1)}, u32[]{:S(2)}, u32[]{:S(2)}) collective-permute-start(bf16[4,2,128,256]{3,2,1,0:T(8,128)(2,1)S(1)} %bitcast.205), channel_id=1, source_target_pairs={{0,4},{1,3},{2,6},{3,1},{4,0},{5,7},{6,2},{7,5},{8,12},{9,11},{10,... | collective-permute-start | bytes 1572872 | tf_op jit(solution)/shard_map/ppermute | solution.py:21
  84.2 2.8 %collective-permute-start.11 = (f32[16,2,1024]{2,1,0:T(2,128)S(1)}, f32[16,2,1024]{2,1,0:T(2,128)S(1)}, u32[]{:S(2)}, u32[]{:S(2)}) collective-permute-start(f32[16,2,1024]{2,1,0:T(2,128)S(1)} %all_to_all.30.refs_4_), channel_id=1, source_target_pairs={{0,1},{1,0},{2,3},{3,2},{4,5},{5,4},{6,7},{7,6},{8,9},{9,8},{10,11... | collective-permute-start | bytes 393224 | tf_op jit(solution)/shard_map/ppermute | solution.py:21
  93.7 7.6 %collective-permute-start.14 = (bf16[1,2,128,256]{3,2,1,0:T(8,128)(2,1)}, bf16[1,2,128,256]{3,2,1,0:T(8,128)(2,1)S(1)}, u32[]{:S(2)}, u32[]{:S(2)}) collective-permute-start(bf16[1,2,128,256]{3,2,1,0:T(8,128)(2,1)} %bitcast.238), channel_id=1, source_target_pairs={{0,2},{1,5},{2,0},{3,7},{4,6},{5,1},{6,4},{7,3},{8,10},{9,13},{10,... | collective-permute-start | bytes 393224 | tf_op jit(solution)/shard_map/ppermute | solution.py:21
  94.2 9.6 %collective-permute-start.13 = (bf16[256,1024]{1,0:T(8,128)(2,1)}, bf16[256,1024]{1,0:T(8,128)(2,1)S(1)}, u32[]{:S(2)}, u32[]{:S(2)}) collective-permute-start(bf16[256,1024]{1,0:T(8,128)(2,1)} %get-tuple-element.149), channel_id=1, source_target_pairs={{0,1},{1,0},{2,3},{3,2},{4,5},{5,4},{6,7},{7,6},{8,9},{9,8},{10,11... | collective-permute-start | bytes 1572872 | tf_op jit(solution)/shard_map/ppermute | solution.py:21
  95.2 12.7 %all-to-all-start.4 = ((f32[32,2,512]{2,1,0:T(2,128)}), f32[32,2,512]{2,1,0:T(2,128)S(1)}, u32[]{:S(2)}, u32[]{:S(2)}) async-start(f32[32,2,512]{2,1,0:T(2,128)} %get-tuple-element.151), calls=%async_computation.4 | async-start | bytes 262144 | tf_op jit(solution)/shard_map/all_to_all | solution.py:32
  97.5 10.4 %collective-permute-start.16 = (bf16[128,1024]{1,0:T(8,128)(2,1)}, bf16[128,1024]{1,0:T(8,128)(2,1)S(1)}, u32[]{:S(2)}, u32[]{:S(2)}) collective-permute-start(bf16[128,1024]{1,0:T(8,128)(2,1)} %get-tuple-element.155), channel_id=1, source_target_pairs={{0,1},{1,0},{2,3},{3,2},{4,5},{5,4},{6,7},{7,6},{8,9},{9,8},{10,11... | collective-permute-start | bytes 786440 | tf_op jit(solution)/shard_map/ppermute | solution.py:143
  97.9 10.1 %collective-permute-start.17 = (bf16[128,1024]{1,0:T(8,128)(2,1)}, bf16[128,1024]{1,0:T(8,128)(2,1)S(1)}, u32[]{:S(2)}, u32[]{:S(2)}) collective-permute-start(bf16[128,1024]{1,0:T(8,128)(2,1)} %get-tuple-element.156), channel_id=1, source_target_pairs={{1,2},{2,1},{5,6},{6,5},{9,10},{10,9},{13,14},{14,13},{17,18},{18,... | collective-permute-start | bytes 786440 | tf_op jit(solution)/shard_map/ppermute | solution.py:144
  102.3 5.6 %collective-permute-start.15 = (bf16[2,2,128,128]{3,2,1,0:T(8,128)(2,1)S(1)}, bf16[2,2,128,128]{3,2,1,0:T(8,128)(2,1)S(1)}, u32[]{:S(2)}, u32[]{:S(2)}) collective-permute-start(bf16[2,2,128,128]{3,2,1,0:T(8,128)(2,1)S(1)} %fusion.3), channel_id=1, source_target_pairs={{0,4},{1,3},{2,6},{3,1},{4,0},{5,7},{6,2},{7,5},{8,12},{9,11},{10,... | collective-permute-start | bytes 393224 | tf_op jit(solution)/shard_map/ppermute | solution.py:21
  102.4 12.6 %collective-permute-start.18 = (bf16[2,2,128,128]{3,2,1,0:T(8,128)(2,1)S(1)}, bf16[2,2,128,128]{3,2,1,0:T(8,128)(2,1)S(1)}, u32[]{:S(2)}, u32[]{:S(2)}) collective-permute-start(bf16[2,2,128,128]{3,2,1,0:T(8,128)(2,1)S(1)} %fusion.7), channel_id=1, source_target_pairs={{0,4},{1,3},{2,6},{3,1},{4,0},{5,7},{6,2},{7,5},{8,12},{9,11},{10,... | collective-permute-start | bytes 393224 | tf_op jit(solution)/shard_map/ppermute | solution.py:21
  115.0 13.4 %all-to-all-start.5 = ((f32[32,2,512]{2,1,0:T(2,128)}), f32[32,2,512]{2,1,0:T(2,128)S(1)}, u32[]{:S(2)}, u32[]{:S(2)}) async-start(f32[32,2,512]{2,1,0:T(2,128)} %get-tuple-element.163), calls=%async_computation.5 | async-start | bytes 262144 | tf_op jit(solution)/shard_map/all_to_all | solution.py:32
  121.1 7.3 %collective-permute-start.21 = (bf16[256,512]{1,0:T(8,128)(2,1)S(1)}, bf16[256,512]{1,0:T(8,128)(2,1)S(1)}, u32[]{:S(2)}, u32[]{:S(2)}) collective-permute-start(bf16[256,512]{1,0:T(8,128)(2,1)S(1)} %copy-done.42), channel_id=1, source_target_pairs={{0,1},{1,0},{2,3},{3,2},{4,5},{5,4},{6,7},{7,6},{8,9},{9,8},{10,11... | collective-permute-start | bytes 786440 | tf_op jit(solution)/shard_map/ppermute | solution.py:21
  128.4 8.6 %collective-permute-start.24 = (bf16[1152,128]{1,0:T(8,128)(2,1)}, bf16[1152,128]{1,0:T(8,128)(2,1)S(1)}, u32[]{:S(2)}, u32[]{:S(2)}) collective-permute-start(bf16[1152,128]{1,0:T(8,128)(2,1)} %bitcast.236), channel_id=1, source_target_pairs={{0,8},{1,9},{2,10},{3,11},{4,12},{5,13},{6,14},{7,15},{8,0},{9,1},... | collective-permute-start | bytes 884744 | tf_op jit(solution)/shard_map/ppermute | solution.py:21
  129.7 9.7 %collective-permute-start.22 = (bf16[256,1024]{1,0:T(8,128)(2,1)S(1)}, bf16[256,1024]{1,0:T(8,128)(2,1)S(1)}, u32[]{:S(2)}, u32[]{:S(2)}) collective-permute-start(bf16[256,1024]{1,0:T(8,128)(2,1)S(1)} %copy-done.41), channel_id=1, source_target_pairs={{0,2},{1,5},{2,0},{3,7},{4,6},{5,1},{6,4},{7,3},{8,10},{9,13},{10,... | collective-permute-start | bytes 1572872 | tf_op jit(solution)/shard_map/ppermute | solution.py:21
  135.2 10.6 %collective-permute-start.26 = (bf16[512,512]{1,0:T(8,128)(2,1)}, bf16[512,512]{1,0:T(8,128)(2,1)S(1)}, u32[]{:S(2)}, u32[]{:S(2)}) collective-permute-start(bf16[512,512]{1,0:T(8,128)(2,1)} %get-tuple-element.181), channel_id=1, source_target_pairs={{0,2},{1,5},{2,0},{3,7},{4,6},{5,1},{6,4},{7,3},{8,10},{9,13},{10,... | collective-permute-start | bytes 1572872 | tf_op jit(solution)/shard_map/ppermute | solution.py:21
  137.1 8.7 %collective-permute-start.25 = (bf16[576,128]{1,0:T(8,128)(2,1)S(1)}, bf16[576,128]{1,0:T(8,128)(2,1)S(1)}, u32[]{:S(2)}, u32[]{:S(2)}) collective-permute-start(bf16[576,128]{1,0:T(8,128)(2,1)S(1)} %dynamic-slice_convert_fusion.2), channel_id=1, source_target_pairs={{0,16},{1,17},{2,18},{3,19},{4,20},{5,21},{6,22},{7,23},{8,24},{9,... | collective-permute-start | bytes 442376 | tf_op jit(solution)/shard_map/ppermute | solution.py:21
  139.7 7.7 %collective-permute-start.23 = (bf16[128,1024]{1,0:T(8,128)(2,1)S(1)}, bf16[128,1024]{1,0:T(8,128)(2,1)S(1)}, u32[]{:S(2)}, u32[]{:S(2)}) collective-permute-start(bf16[128,1024]{1,0:T(8,128)(2,1)S(1)} %dynamic-slice_convert_fusion.1), channel_id=1, source_target_pairs={{0,4},{1,3},{2,6},{3,1},{4,0},{5,7},{6,2},{7,5},{8,12},{9,11},{10,... | collective-permute-start | bytes 786440 | tf_op jit(solution)/shard_map/ppermute | solution.py:21
  147.7 10.5 %collective-permute-start.29 = (bf16[256,512]{1,0:T(8,128)(2,1)S(1)}, bf16[256,512]{1,0:T(8,128)(2,1)S(1)}, u32[]{:S(2)}, u32[]{:S(2)}) collective-permute-start(bf16[256,512]{1,0:T(8,128)(2,1)S(1)} %dynamic-slice_convert_fusion), channel_id=1, source_target_pairs={{0,4},{1,3},{2,6},{3,1},{4,0},{5,7},{6,2},{7,5},{8,12},{9,11},{10,... | collective-permute-start | bytes 786440 | tf_op jit(solution)/shard_map/ppermute | solution.py:21
  148.9 9.3 %collective-permute-start.28 = (bf16[576,128]{1,0:T(8,128)(2,1)S(1)}, bf16[576,128]{1,0:T(8,128)(2,1)S(1)}, u32[]{:S(2)}, u32[]{:S(2)}) collective-permute-start(bf16[576,128]{1,0:T(8,128)(2,1)S(1)} %add_convert_fusion), channel_id=1, source_target_pairs={{0,16},{1,17},{2,18},{3,19},{4,20},{5,21},{6,22},{7,23},{8,24},{9,... | collective-permute-start | bytes 442376 | tf_op jit(solution)/shard_map/ppermute | solution.py:21
  150.5 4.7 %collective-permute-start.27 = (bf16[64,1024]{1,0:T(8,128)(2,1)S(1)}, bf16[64,1024]{1,0:T(8,128)(2,1)S(1)}, u32[]{:S(2)}, u32[]{:S(2)}) collective-permute-start(bf16[64,1024]{1,0:T(8,128)(2,1)S(1)} %dynamic-slice_convert_fusion.4), channel_id=1, source_target_pairs={{0,8},{1,9},{2,10},{3,11},{4,12},{5,13},{6,14},{7,15},{8,0},{9,1},... | collective-permute-start | bytes 393224 | tf_op jit(solution)/shard_map/ppermute | solution.py:21
  158.3 11.2 %collective-permute-start.31 = (bf16[1152,128]{1,0:T(8,128)(2,1)S(1)}, bf16[1152,128]{1,0:T(8,128)(2,1)S(1)}, u32[]{:S(2)}, u32[]{:S(2)}) collective-permute-start(bf16[1152,128]{1,0:T(8,128)(2,1)S(1)} %bitcast.207), channel_id=1, source_target_pairs={{0,8},{1,9},{2,10},{3,11},{4,12},{5,13},{6,14},{7,15},{8,0},{9,1},... | collective-permute-start | bytes 884744 | tf_op jit(solution)/shard_map/ppermute | solution.py:21
  158.6 10.9 %collective-permute-start.32 = (bf16[128,512]{1,0:T(8,128)(2,1)S(1)}, bf16[128,512]{1,0:T(8,128)(2,1)S(1)}, u32[]{:S(2)}, u32[]{:S(2)}) collective-permute-start(bf16[128,512]{1,0:T(8,128)(2,1)S(1)} %dynamic-slice_convert_fusion.3), channel_id=1, source_target_pairs={{0,8},{1,9},{2,10},{3,11},{4,12},{5,13},{6,14},{7,15},{8,0},{9,1},... | collective-permute-start | bytes 393224 | tf_op jit(solution)/shard_map/ppermute | solution.py:21
  160.1 7.6 %collective-permute-start.30 = (bf16[32,1024]{1,0:T(8,128)(2,1)S(1)}, bf16[32,1024]{1,0:T(8,128)(2,1)S(1)}, u32[]{:S(2)}, u32[]{:S(2)}) collective-permute-start(bf16[32,1024]{1,0:T(8,128)(2,1)S(1)} %dynamic-slice_convert_fusion.6), channel_id=1, source_target_pairs={{0,16},{1,17},{2,18},{3,19},{4,20},{5,21},{6,22},{7,23},{8,24},{9,... | collective-permute-start | bytes 196616 | tf_op jit(solution)/shard_map/ppermute | solution.py:21
  169.6 12.2 %collective-permute-start.34 = (bf16[2304,128]{1,0:T(8,128)(2,1)S(1)}, bf16[2304,128]{1,0:T(8,128)(2,1)S(1)}, u32[]{:S(2)}, u32[]{:S(2)}) collective-permute-start(bf16[2304,128]{1,0:T(8,128)(2,1)S(1)} %bitcast.201), channel_id=1, source_target_pairs={{0,4},{1,3},{2,6},{3,1},{4,0},{5,7},{6,2},{7,5},{8,12},{9,11},{10,... | collective-permute-start | bytes 1769480 | tf_op jit(solution)/shard_map/ppermute | solution.py:21
  170.4 11.5 %collective-permute-start.33 = (bf16[32,1024]{1,0:T(8,128)(2,1)S(1)}, bf16[32,1024]{1,0:T(8,128)(2,1)S(1)}, u32[]{:S(2)}, u32[]{:S(2)}) collective-permute-start(bf16[32,1024]{1,0:T(8,128)(2,1)S(1)} %add_convert_fusion.2), channel_id=1, source_target_pairs={{0,16},{1,17},{2,18},{3,19},{4,20},{5,21},{6,22},{7,23},{8,24},{9,... | collective-permute-start | bytes 196616 | tf_op jit(solution)/shard_map/ppermute | solution.py:21
  172.0 4.4 %collective-permute-start.36 = (f32[16,2048]{1,0:T(8,128)S(1)}, f32[16,2048]{1,0:T(8,128)S(1)}, u32[]{:S(2)}, u32[]{:S(2)}) collective-permute-start(f32[16,2048]{1,0:T(8,128)S(1)} %copy-done.30), channel_id=1, source_target_pairs={{0,1},{1,0},{2,3},{3,2},{4,5},{5,4},{6,7},{7,6},{8,9},{9,8},{10,11... | collective-permute-start | bytes 393224 | tf_op jit(solution)/shard_map/ppermute | solution.py:134
  176.4 4.8 %collective-permute-start.37 = (f32[16,2048]{1,0:T(8,128)S(1)}, f32[16,2048]{1,0:T(8,128)S(1)}, u32[]{:S(2)}, u32[]{:S(2)}) collective-permute-start(f32[16,2048]{1,0:T(8,128)S(1)} %add.202), channel_id=1, source_target_pairs={{0,2},{1,3},{2,0},{3,1},{4,6},{5,7},{6,4},{7,5},{8,10},{9,11},{10,... | collective-permute-start | bytes 393224 | tf_op jit(solution)/shard_map/ppermute | solution.py:134
  176.5 5.4 %collective-permute-start.35 = (bf16[64,512]{1,0:T(8,128)(2,1)S(1)}, bf16[64,512]{1,0:T(8,128)(2,1)S(1)}, u32[]{:S(2)}, u32[]{:S(2)}) collective-permute-start(bf16[64,512]{1,0:T(8,128)(2,1)S(1)} %dynamic-slice_convert_fusion.5), channel_id=1, source_target_pairs={{0,16},{1,17},{2,18},{3,19},{4,20},{5,21},{6,22},{7,23},{8,24},{9,... | collective-permute-start | bytes 196616 | tf_op jit(solution)/shard_map/ppermute | solution.py:21
  181.9 6.3 %collective-permute-start.38 = (bf16[64,512]{1,0:T(8,128)(2,1)S(1)}, bf16[64,512]{1,0:T(8,128)(2,1)S(1)}, u32[]{:S(2)}, u32[]{:S(2)}) collective-permute-start(bf16[64,512]{1,0:T(8,128)(2,1)S(1)} %add_convert_fusion.1), channel_id=1, source_target_pairs={{0,16},{1,17},{2,18},{3,19},{4,20},{5,21},{6,22},{7,23},{8,24},{9,... | collective-permute-start | bytes 196616 | tf_op jit(solution)/shard_map/ppermute | solution.py:21
  184.1 29.1 %collective-permute-start.43 = (bf16[4608,128]{1,0:T(8,128)(2,1)S(1)}, bf16[4608,128]{1,0:T(8,128)(2,1)S(1)}, u32[]{:S(2)}, u32[]{:S(2)}) collective-permute-start(bf16[4608,128]{1,0:T(8,128)(2,1)S(1)} %bitcast.198), channel_id=1, source_target_pairs={{0,2},{1,5},{2,0},{3,7},{4,6},{5,1},{6,4},{7,3},{8,10},{9,13},{10,... | collective-permute-start | bytes 3538952 | tf_op jit(solution)/shard_map/ppermute | solution.py:21
  186.0 5.9 %collective-permute-start.45 = (bf16[64,1024]{1,0:T(8,128)(2,1)S(1)}, bf16[64,1024]{1,0:T(8,128)(2,1)S(1)}, u32[]{:S(2)}, u32[]{:S(2)}) collective-permute-start(bf16[64,1024]{1,0:T(8,128)(2,1)S(1)} %bitcast.215), channel_id=1, source_target_pairs={{0,8},{1,9},{2,10},{3,11},{4,12},{5,13},{6,14},{7,15},{8,0},{9,1},... | collective-permute-start | bytes 393224 | tf_op jit(solution)/shard_map/ppermute | solution.py:21
  188.3 6.4 %collective-permute-start.39 = (bf16[128,512]{1,0:T(8,128)(2,1)S(1)}, bf16[128,512]{1,0:T(8,128)(2,1)S(1)}, u32[]{:S(2)}, u32[]{:S(2)}) collective-permute-start(bf16[128,512]{1,0:T(8,128)(2,1)S(1)} %bitcast.216), channel_id=1, source_target_pairs={{0,8},{1,9},{2,10},{3,11},{4,12},{5,13},{6,14},{7,15},{8,0},{9,1},... | collective-permute-start | bytes 393224 | tf_op jit(solution)/shard_map/ppermute | solution.py:21
  192.0 8.5 %collective-permute-start.46 = (bf16[128,1024]{1,0:T(8,128)(2,1)S(1)}, bf16[128,1024]{1,0:T(8,128)(2,1)S(1)}, u32[]{:S(2)}, u32[]{:S(2)}) collective-permute-start(bf16[128,1024]{1,0:T(8,128)(2,1)S(1)} %bitcast.210), channel_id=1, source_target_pairs={{0,4},{1,3},{2,6},{3,1},{4,0},{5,7},{6,2},{7,5},{8,12},{9,11},{10,... | collective-permute-start | bytes 786440 | tf_op jit(solution)/shard_map/ppermute | solution.py:21
  194.8 11.3 %collective-permute-start.40 = (bf16[256,512]{1,0:T(8,128)(2,1)S(1)}, bf16[256,512]{1,0:T(8,128)(2,1)S(1)}, u32[]{:S(2)}, u32[]{:S(2)}) collective-permute-start(bf16[256,512]{1,0:T(8,128)(2,1)S(1)} %bitcast.209), channel_id=1, source_target_pairs={{0,4},{1,3},{2,6},{3,1},{4,0},{5,7},{6,2},{7,5},{8,12},{9,11},{10,... | collective-permute-start | bytes 786440 | tf_op jit(solution)/shard_map/ppermute | solution.py:21
  200.6 10.5 %collective-permute-start.47 = (bf16[256,1024]{1,0:T(8,128)(2,1)S(1)}, bf16[256,1024]{1,0:T(8,128)(2,1)S(1)}, u32[]{:S(2)}, u32[]{:S(2)}) collective-permute-start(bf16[256,1024]{1,0:T(8,128)(2,1)S(1)} %bitcast.204), channel_id=1, source_target_pairs={{0,2},{1,5},{2,0},{3,7},{4,6},{5,1},{6,4},{7,3},{8,10},{9,13},{10,... | collective-permute-start | bytes 1572872 | tf_op jit(solution)/shard_map/ppermute | solution.py:21
  206.2 10.5 %collective-permute-start.41 = (bf16[512,512]{1,0:T(8,128)(2,1)S(1)}, bf16[512,512]{1,0:T(8,128)(2,1)S(1)}, u32[]{:S(2)}, u32[]{:S(2)}) collective-permute-start(bf16[512,512]{1,0:T(8,128)(2,1)S(1)} %bitcast.203), channel_id=1, source_target_pairs={{0,2},{1,5},{2,0},{3,7},{4,6},{5,1},{6,4},{7,3},{8,10},{9,13},{10,... | collective-permute-start | bytes 1572872 | tf_op jit(solution)/shard_map/ppermute | solution.py:21
  211.3 8.7 %collective-permute-start.48 = (bf16[512,1024]{1,0:T(8,128)(2,1)S(1)}, bf16[512,1024]{1,0:T(8,128)(2,1)S(1)}, u32[]{:S(2)}, u32[]{:S(2)}) collective-permute-start(bf16[512,1024]{1,0:T(8,128)(2,1)S(1)} %bitcast.199), channel_id=1, source_target_pairs={{0,1},{1,0},{2,3},{3,2},{4,5},{5,4},{6,7},{7,6},{8,9},{9,8},{10,11... | collective-permute-start | bytes 3145736 | tf_op jit(solution)/shard_map/ppermute | solution.py:21
  213.7 12.2 %collective-permute-start.44 = (bf16[9216,128]{1,0:T(8,128)(2,1)S(1)}, bf16[9216,128]{1,0:T(8,128)(2,1)S(1)}, u32[]{:S(2)}, u32[]{:S(2)}) collective-permute-start(bf16[9216,128]{1,0:T(8,128)(2,1)S(1)} %bitcast.191), channel_id=1, source_target_pairs={{0,1},{1,0},{2,3},{3,2},{4,5},{5,4},{6,7},{7,6},{8,9},{9,8},{10,11... | collective-permute-start | bytes 7077896 | tf_op jit(solution)/shard_map/ppermute | solution.py:21
  216.9 5.9 %collective-permute-start.42 = (bf16[1024,512]{1,0:T(8,128)(2,1)S(1)}, bf16[1024,512]{1,0:T(8,128)(2,1)S(1)}, u32[]{:S(2)}, u32[]{:S(2)}) collective-permute-start(bf16[1024,512]{1,0:T(8,128)(2,1)S(1)} %bitcast.200), channel_id=1, source_target_pairs={{0,1},{1,0},{2,3},{3,2},{4,5},{5,4},{6,7},{7,6},{8,9},{9,8},{10,11... | collective-permute-start | bytes 3145736 | tf_op jit(solution)/shard_map/ppermute | solution.py:21
  (49 other events, 260.8 us)
